TPU v7x, 32 devices: a whole 2x2x4 slice. The times are simulated.
32 devices in a mesh: row: 4 (over x, core), col: 8 (over z, y).
Axes of the slice: x: 2, y: 2, z: 4, core: 2. Of those that a mesh axis runs over, the one named last changes fastest.
Arguments:
- embeddings: float32 [16384, 1024], P(('row', 'col')), may hold values from -6 to 6
- dest_pos: int32 [16384], P(('row', 'col')), may hold values from 0 to 16383, as said below
- cluster_ids: int32 [4, 4096], P('row', 'col'), may hold values from 0 to 7, as said below
Outputs:
- best_match: float32 [4, 4096], P('row', 'col')
Inputs may be any that keep to these rules, and one draw needn't show every extreme that they name: dest_pos is a permutation; of the 512 rows stored on one device at most 32 have positions in one device's block of 512 positions, and exactly 32 for some pairs of devices. In each group cluster_ids never falls along the positions; every cluster holds 102 to 2560 positions, and one cluster of each group exactly 2560.
All inputs are finite; a program needn't handle non-finite values.
Results may differ from a plain program's by a relative error of at most 0.0013.
Values may be sent and summed in bfloat16 or wider, within the bound.
No kernel may reach another device: no remote copies, remote signals or barrier semaphores. Data moves between devices by JAX's collectives and lax.ppermute only.
A program may use at most 64 MiB of HBM per device.

v0:
```python
import jax
import jax.numpy as jnp
from jax import lax
from jax.sharding import PartitionSpec as P


def normalize(rows):
    scale = lax.rsqrt(jnp.sum(rows * rows, axis=1, keepdims=True) + 1e-06)
    return (rows * scale).astype(jnp.bfloat16)


def masked_sims(left, left_labels, right, right_labels, keep_extra):
    sims = lax.dot_general(
        left, right, (((1,), (1,)), ((), ())), preferred_element_type=jnp.float32
    )
    keep = (left_labels[:, None] == right_labels[None, :]) & keep_extra
    return jnp.where(keep, sims, jnp.float32(-1.0))


def shards(embeddings, dest_pos, cluster_ids):
    rows_dev, width = embeddings.shape
    devs = lax.axis_size("row") * lax.axis_size("col")
    slots = max(4, 2 * rows_dev // devs)
    unit = normalize(embeddings)
    target = dest_pos // rows_dev
    place = dest_pos % rows_dev
    onehot = (target[:, None] == jnp.arange(devs, dtype=jnp.int32)[None, :]).astype(jnp.int32)
    slot = jnp.sum(jnp.cumsum(onehot, axis=0) * onehot, axis=1) - 1
    send_rows = jnp.zeros((devs, slots, width), jnp.bfloat16).at[target, slot].set(unit)
    send_places = jnp.full((devs, slots), rows_dev, jnp.int32).at[target, slot].set(place)
    got_rows, got_places = (
        lax.all_to_all(send_rows, ("row", "col"), split_axis=0, concat_axis=0, tiled=True),
        lax.all_to_all(send_places, ("row", "col"), split_axis=0, concat_axis=0, tiled=True),
    )
    mine = (
        jnp.zeros((rows_dev, width), jnp.bfloat16)
        .at[got_places.reshape(-1)]
        .set(got_rows.reshape(-1, width), mode="drop")
    )
    labels = cluster_ids.reshape(rows_dev)
    local_index = jnp.arange(rows_dev, dtype=jnp.int32)
    my_start = lax.axis_index("col") * rows_dev
    my_places = my_start + local_index
    init = jnp.full((rows_dev,), -1.0, jnp.float32)
    other = lax.all_gather(mine, "col", axis=0, tiled=True)
    other_labels = lax.all_gather(labels, "col", axis=0, tiled=True)
    columns = jnp.arange(other.shape[0], dtype=jnp.int32)
    sims = masked_sims(mine, labels, other, other_labels, my_places[:, None] != columns[None, :])
    best = jnp.maximum(init, jnp.max(sims, axis=1))
    return best.reshape(1, rows_dev)


def solution(mesh):
    return jax.shard_map(
        shards,
        mesh=mesh,
        in_specs=(P(("row", "col"), None), P(("row", "col")), P("row", "col")),
        out_specs=P("row", "col"),
        check_vma=False,
    )
```

profile of v0, /device:TPU:0, one launch (start us, length us, event | category | flops | bytes accessed | tf_op | source)
XLA Modules:
  0.0 358.4 jit_solution(15550475129570466350)
XLA Ops:
  6.5 0.7 compare_select_fusion.2
  7.2 1.2 reduce-window.6
  8.4 0.2 slice_reduce_fusion
  8.7 0.1 fusion.4
  8.8 0.6 broadcast_in_dim.14
  9.4 0.0 copy-start
  9.4 66.1 %scatter_fusion = s32[32,32]{1,0:T(8,128)} fusion(s32[32,32]{1,0:T(8,128)} %broadcast_in_dim.14, s32[512]{0:T(512)S(1)} %bitcast.33, s32[512]{0:T(512)S(1)} %get-tuple-element.7), kind=kCustom, calls=%fused_computation | custom fusion | bytes 10240 | tf_op jit(solution)/shard_map/scatter | solution.py:30
  75.5 7.5 %all-to-all-start = ((s32[32,1,32]{2,1,0:T(1,128)}), s32[32,1,32]{2,1,0:T(1,128)S(1)}, u32[]{:S(2)}, u32[]{:S(2)}) async-start(s32[32,1,32]{2,1,0:T(1,128)} %bitcast.9), calls=%async_computation | async-start | bytes 32768 | tf_op jit(solution)/shard_map/all_to_all | solution.py:33
  83.0 0.0 copy-done
  83.0 0.2 multiply_reduce_fusion
  83.2 0.2 multiply_convert_fusion
  83.4 1.6 broadcast_in_dim.32
  85.0 71.6 %scatter_fusion.1 = bf16[32,32,1024]{2,1,0:T(8,128)(2,1)} fusion(bf16[32,32,1024]{2,1,0:T(8,128)(2,1)} %broadcast_in_dim.32, s32[512]{0:T(512)S(1)} %bitcast.34, bf16[512,1024]{1,0:T(8,128)(2,1)S(1)} %multiply_convert_fusion), kind=kCustom, calls=%fused_computation.1 | custom fusion | bytes 3149824 | tf_op jit(solution)/shard_map/scatter | solution.py:29
  156.6 0.0 all-to-all-done
  156.6 5.8 %all-to-all-start.1 = ((bf16[32,32,1024]{2,1,0:T(8,128)(2,1)}), bf16[32,32,1024]{2,1,0:T(8,128)(2,1)S(1)}, u32[]{:S(2)}, u32[]{:S(2)}) async-start(bf16[32,32,1024]{2,1,0:T(8,128)(2,1)} %scatter_fusion.1), calls=%async_computation.1 | async-start | bytes 4194304 | tf_op jit(solution)/shard_map/all_to_all | solution.py:32
  162.5 0.0 copy-start.1
  162.5 0.0 all-gather.3.cloned.1.call-start
  162.5 0.5 broadcast.155
  163.0 0.7 reduce.5
  163.7 0.1 reshape.97
  163.8 48.7 %all-to-all-done.1 = bf16[32,32,1024]{2,1,0:T(8,128)(2,1)S(1)} async-done(((bf16[32,32,1024]{2,1,0:T(8,128)(2,1)}), bf16[32,32,1024]{2,1,0:T(8,128)(2,1)S(1)}, u32[]{:S(2)}, u32[]{:S(2)}) %all-to-all-start.1) | async-done | bytes 2097184 | tf_op jit(solution)/shard_map/all_to_all | solution.py:32
  212.6 6.3 %scatter_custom_fusion.2 = bf16[512,1024]{1,0:T(8,128)(2,1)} fusion(s32[1024]{0:T(1024)S(1)} %bitcast.41, bf16[1024,1024]{1,0:T(8,128)(2,1)S(1)} %bitcast.35, bf16[]{:T(256)} %constant.47.clone.1), kind=kCustom, calls=%fused_computation.8 | custom fusion | bytes 1048578 | tf_op jit(solution)/shard_map/scatter | solution.py:38
  218.9 0.0 all-gather.3.cloned.1.call-update
  218.9 0.0 copy-done.1
  218.9 26.6 %all-gather = s32[1,4096]{1,0:T(1,128)S(1)} all-gather(s32[1,512]{1,0:T(1,128)S(1)} %copy-done.1), channel_id=2, replica_groups=mesh['row'=4,'col'=8] {'col'}, dimensions={1}, use_global_device_ids=true | all-gather | bytes 18432 | tf_op jit(solution)/shard_map/all_gather | solution.py:46
  245.5 96.6 %all-gather.3.cloned.1.call-done = bf16[4096,1024]{1,0:T(8,128)(2,1)} async-done(((bf16[512,1024]{1,0:T(8,128)(2,1)}), bf16[4096,1024]{1,0:T(8,128)(2,1)}) %all-gather.3.cloned.1.call-update) | async-done | bytes 8388624 | tf_op jit(solution)/shard_map/all_gather | solution.py:45
  342.0 9.0 %select_reduce_fusion = f32[512]{0:T(512)S(1)} fusion(bf16[512,1024]{1,0:T(8,128)(2,1)} %scatter_custom_fusion.2, bf16[4096,1024]{1,0:T(8,128)(2,1)} %all-gather.3.cloned.1.call-done, s32[512]{0:T(512)S(1)} %iota_add_fusion, s32[4096]{0:T(1024)S(1)} %bitcast.37, s32[512]{0:T(512)S(1)} %bitcast.42), kind=kOutput, calls=%fused_computation.3 | convolution fusion | flops 4305452544 | bytes 9459712 | tf_op jit(solution)/shard_map/dot_general | solution.py:13
  351.0 0.6 broadcast_maximum_fusion
  (8 shorter events, 0.1 us)
Async XLA Ops:
  9.4 73.6 %copy-start = (f32[512,1024]{1,0:T(8,128)S(1)}, f32[512,1024]{1,0:T(8,128)}, u32[]{:S(2)}) copy-start(f32[512,1024]{1,0:T(8,128)} %param.3) | copy-start | bytes 6291460
  75.5 81.1 %all-to-all-start = ((s32[32,1,32]{2,1,0:T(1,128)}), s32[32,1,32]{2,1,0:T(1,128)S(1)}, u32[]{:S(2)}, u32[]{:S(2)}) async-start(s32[32,1,32]{2,1,0:T(1,128)} %bitcast.9), calls=%async_computation | async-start | bytes 32768 | tf_op jit(solution)/shard_map/all_to_all | solution.py:33
  156.6 55.9 %all-to-all-start.1 = ((bf16[32,32,1024]{2,1,0:T(8,128)(2,1)}), bf16[32,32,1024]{2,1,0:T(8,128)(2,1)S(1)}, u32[]{:S(2)}, u32[]{:S(2)}) async-start(bf16[32,32,1024]{2,1,0:T(8,128)(2,1)} %scatter_fusion.1), calls=%async_computation.1 | async-start | bytes 4194304 | tf_op jit(solution)/shard_map/all_to_all | solution.py:32
  162.5 56.4 %copy-start.1 = (s32[1,512]{1,0:T(1,128)S(1)}, s32[1,512]{1,0:T(1,128)}, u32[]{:S(2)}) copy-start(s32[1,512]{1,0:T(1,128)} %param.5) | copy-start | bytes 6148
  162.5 179.6 %all-gather.3.cloned.1.call-start = ((), (), s32[]{:S(2)}) async-start(), calls=%async_computation.2 | async-start | bytes 9437184 | tf_op jit(solution)/shard_map/all_gather | solution.py:45
Sparse Core Ops, SparseCore 0:
  219.0 122.9 all-gather.2
where the time goes:
time: 363 us; the launch traced here: 358 us
  local copies, waits for them, and re-layouts  147 us (40%)
  waiting for transfers between devices  145 us (40%)
  blocking collectives  26.6 us (7%)
  between operations  13.5 us (4%)
  starting transfers between devices  13.3 us (4%)
  matrix products  8.96 us (2%)
  other arithmetic  3.72 us (1%)
    all_gather x1, waiting for transfers between devices, shards(): other = lax.all_gather(mine, 'col', axis=0, tiled=True)  96.6 us
    scatter x1, local copies, waits for them, and re-layouts, shards(): jnp.zeros((devs, slots, width), jnp.bfloat16).at[target, slot].set(unit)  71.6 us
    scatter x1, local copies, waits for them, and re-layouts, shards(): jnp.full((devs, slots), rows_dev, jnp.int32).at[target, slot].set(place)  66.1 us
    all_to_all x1, waiting for transfers between devices, shards(): lax.all_to_all(send_rows, ('row', 'col'), split_axis=0, concat_axis=0, ti...  48.7 us
    all_gather x1, blocking collectives, shards(): other_labels = lax.all_gather(labels, 'col', axis=0, tiled=True)  26.6 us
    dot_general x1, matrix products, masked_sims(): lax.dot_general(left, right, (((1,), (1,)), ((), ())), preferred_element_...  8.96 us
    all_to_all x1, starting transfers between devices, shards(): lax.all_to_all(send_places, ('row', 'col'), split_axis=0, concat_axis=0,...  7.46 us
  transfers between devices with their start and end apart: 3, of which 2 were waited for; matrix products, arithmetic and copies ran while one was open for 21% of the time, Pallas kernels for 0%

commit v1 on v0

v1 whole, which is shorter than its diff:
```python
import functools
import itertools

import jax
import jax.numpy as jnp
import numpy as np
from jax import lax
from jax.experimental import pallas as pl
from jax.experimental.pallas import tpu as pltpu
from jax.sharding import PartitionSpec as P

AXES = ("row", "col")
LEVELS = 16
NT = (((1,), (1,)), ((), ()))
VMEM = pl.BlockSpec(memory_space=pltpu.VMEM)


def kernel_params(mebibytes):
    return pltpu.CompilerParams(vmem_limit_bytes=mebibytes * 2**20)


def plane_plan(n_row, wide):
    n = n_row * wide
    if n_row == 4 and wide == 2:
        chips = [(0, 0), (0, 1), (1, 1), (1, 0)]

        def dev(chip, core):
            x, y = chips[chip % 4]
            return (x * 2 + core) * wide + y

        held = np.zeros((4, n), np.int64)
        for chip, core in itertools.product(range(4), range(2)):
            i = dev(chip, core)
            crossed = 1 - core if chip in (1, 2) else core
            held[:, i] = i, dev(chip, 1 - core), dev(chip + 1, core), dev(chip + 3, crossed)
        pairs = [(0, 0), (0, 1), (0, 2), (1, 2), (2, 3)]
    else:
        def covered(cover):
            return {(b - a) % n for a in cover for b in cover}

        size = 1
        while True:
            found = [c for c in itertools.combinations(range(n), size) if c[0] == 0 and len(covered(c)) == n]
            if found:
                break
            size += 1
        cover = found[0]
        held = (np.arange(n)[None, :] + np.array(cover)[:, None]) % n
        pairs, seen = [], set()
        for j, k in itertools.combinations_with_replacement(range(size), 2):
            delta = (cover[k] - cover[j]) % n
            if delta not in seen:
                seen |= {delta, (n - delta) % n}
                pairs.append((j, k))
    met = set()
    for j, k in pairs:
        for i in range(n):
            met |= {(held[j, i], held[k, i]), (held[k, i], held[j, i])}
    assert len(met) == n * n
    return held, pairs


def write_chunks(slot, unit, cap, chunk_refs, numbers):
    for ref, k in zip(chunk_refs, numbers):
        index = lax.broadcasted_iota(jnp.int32, (cap, unit.shape[0]), 0) + k * cap
        pick = (index == slot).astype(jnp.bfloat16)
        ref[...] = jnp.dot(pick, unit, preferred_element_type=jnp.float32).astype(jnp.bfloat16)


def unit_kernel(groups, cap, group_size, numbers, plane_ref, dest_ref, emb_ref, unit_ref, slot_ref, *chunk_refs):
    rows_dev = emb_ref.shape[0]
    dest = dest_ref[...]
    group = jnp.zeros_like(dest)
    for g in range(1, groups):
        group += (dest >= g * group_size).astype(jnp.int32)
    group = jnp.bitwise_xor(group, plane_ref[0])
    pad = -(-groups // 16) * 16
    member = lax.broadcasted_iota(jnp.int32, (pad, rows_dev), 0) == group
    earlier = lax.broadcasted_iota(jnp.int32, (rows_dev, rows_dev), 0) < lax.broadcasted_iota(
        jnp.int32, (rows_dev, rows_dev), 1
    )
    before = jnp.dot(member.astype(jnp.bfloat16), earlier.astype(jnp.bfloat16), preferred_element_type=jnp.float32)
    rank = jnp.sum(jnp.where(member, before, 0.0), axis=0, keepdims=True).astype(jnp.int32)
    slot = jnp.where(rank < cap, group * cap + rank, groups * cap)
    slot_ref[...] = slot
    x = emb_ref[...]
    unit = (x * lax.rsqrt(jnp.sum(x * x, axis=1, keepdims=True) + 1e-06)).astype(jnp.bfloat16)
    unit_ref[...] = unit
    write_chunks(slot, unit, cap, chunk_refs, numbers)


def rest_kernel(groups, cap, group_size, numbers, dest_ref, slot_ref, unit_ref, place_ref, *chunk_refs):
    rows_dev = unit_ref.shape[0]
    slot = slot_ref[...]
    write_chunks(slot, unit_ref[...], cap, chunk_refs, numbers)
    dest = dest_ref[...]
    place = dest
    for g in range(1, groups):
        place -= jnp.where(dest >= g * group_size, group_size, 0)
    high = lax.shift_right_logical(place, 7)
    low = jnp.bitwise_and(place, 127)
    kind = lax.broadcasted_iota(jnp.int32, (16, rows_dev), 0)
    facts = jnp.where(kind == 0, high, jnp.where(kind == 1, low, jnp.where(kind == 2, 1, 0)))
    facts = facts.astype(jnp.float32).astype(jnp.bfloat16)
    pick = (lax.broadcasted_iota(jnp.int32, (groups * cap, rows_dev), 0) == slot).astype(jnp.bfloat16)
    got = lax.dot_general(facts, pick, NT, preferred_element_type=jnp.float32).astype(jnp.int32)
    there = got[2:3, :] > 0
    place_ref[...] = jnp.where(there, got[0:1, :] * 128 + got[1:2, :], group_size)


class Best:
    def __init__(self, start):
        self.row, self.column = start, None

    def add_row(self, row):
        self.row = jnp.maximum(self.row, row)

    def add_column(self, column):
        self.column = column if self.column is None else jnp.maximum(self.column, column)

    def as_row(self):
        if self.column is None:
            return self.row
        n = self.column.shape[0]
        eye = lax.broadcasted_iota(jnp.int32, (n, n), 0) == lax.broadcasted_iota(jnp.int32, (n, n), 1)
        return jnp.maximum(self.row, jnp.max(jnp.where(eye, self.column, -1.0), axis=0, keepdims=True))


def similar(left, right, left_label, right_label, shift=None):
    sims = lax.dot_general(left, right, NT, preferred_element_type=jnp.float32)
    keep = left_label == right_label
    if shift is not None:
        keep &= lax.broadcasted_iota(jnp.int32, sims.shape, 0) != lax.broadcasted_iota(jnp.int32, sims.shape, 1) + shift
    return jnp.where(keep, sims, -1.0)


def row_max(sims):
    return jnp.max(sims, axis=1, keepdims=True)


def column_max(sims):
    return jnp.max(sims, axis=0, keepdims=True)


def loader(chunks, count, blocks, sems):
    number = len(chunks) // count
    cap = chunks[0].shape[0]

    def copy(j, k):
        return pltpu.make_async_copy(chunks[j * number + k], blocks.at[j, pl.ds(k * cap, cap)], sems.at[j, k])

    for j, k in itertools.product(range(count), range(number)):
        copy(j, k).start()
    here = set()

    def need(*wanted):
        for j in sorted(set(wanted) - here):
            for k in range(number):
                copy(j, k).wait()
            here.add(j)

    return need


def early_kernel(pairs, count, *refs):
    *chunks, label_ref, label_col_ref, out_ref, blocks, sems = refs
    need = loader(chunks, count, blocks, sems)
    best = [Best(jnp.full((1, blocks.shape[1]), -1.0, jnp.float32)) for _ in range(count)]
    for j, k in pairs:
        need(j, k)
        sims = similar(
            blocks[j], blocks[k], label_col_ref[:, j : j + 1], label_ref[k : k + 1, :], 0 if j == k else None
        )
        best[k].add_row(column_max(sims))
        if j != k:
            best[j].add_column(row_max(sims))
    for j in range(count):
        out_ref[j : j + 1, :] = best[j].as_row()


def late_kernel(pairs, count, group_size, *refs):
    plane_ref, *chunks, best_ref, place_ref, last_place_ref, label_ref, last_label_ref, label_col_ref, out_ref, blocks, sems = refs
    need = loader(chunks, count, blocks, sems)
    cap = chunks[0].shape[0]
    first = blocks.shape[1] - cap
    early = [Best(best_ref[j : j + 1, :]) for j in range(count)]
    late = [Best(jnp.full((1, cap), -1.0, jnp.float32)) for _ in range(count)]
    for j, k in pairs:
        need(j, k)
        sims = similar(
            blocks[j],
            blocks[k, first:],
            label_col_ref[:, j : j + 1],
            last_label_ref[k : k + 1, :],
            first if j == k else None,
        )
        column = row_max(sims)
        early[j].add_column(column[:first])
        late[k].add_row(column_max(sims))
        if j != k:
            late[j].add_column(column[first:])
            sims = similar(
                blocks[j, first:], blocks[k, :first], label_col_ref[first:, j : j + 1], label_ref[k : k + 1, :]
            )
            early[k].add_row(column_max(sims))
            late[j].add_column(row_max(sims))
    tall = group_size // 128
    pieces = [(early[j], place_ref[j : j + 1, :]) for j in range(count)]
    pieces += [(late[j], last_place_ref[j : j + 1, :]) for j in range(count)]
    spread = jnp.zeros((4 * tall, 128), jnp.float32)
    for best, place in pieces:
        best = best.as_row()
        slots = best.shape[1]
        high = lax.broadcasted_iota(jnp.int32, (tall, slots), 0) == lax.shift_right_logical(place, 7)
        low = lax.broadcasted_iota(jnp.int32, (128, slots), 0) == jnp.bitwise_and(place, 127)
        parts, rest = [], best
        for _ in range(3):
            part = rest.astype(jnp.bfloat16).astype(jnp.float32)
            rest = rest - part
            parts.append(part)
        parts.append(jnp.ones_like(best))
        stack = jnp.concatenate([jnp.where(high, part, 0.0) for part in parts], axis=0).astype(jnp.bfloat16)
        spread += lax.dot_general(stack, low.astype(jnp.bfloat16), NT, preferred_element_type=jnp.float32)
    value = spread[:tall] + spread[tall : 2 * tall] + spread[2 * tall : 3 * tall]
    value = jnp.where(spread[3 * tall :] > 0.5, value, -1.0)
    n_row, n_col, lines, _ = out_ref.shape
    for r in range(n_row):
        here = jnp.where(plane_ref[0] == r, value, -1.0)
        for c in range(n_col):
            out_ref[r, c] = here[c * lines : (c + 1) * lines]


def best_matches(cap, embeddings, dest_pos, cluster_ids):
    n_row, n_col = lax.axis_size("row"), lax.axis_size("col")
    devs = n_row * n_col
    groups, wide = n_row, n_col // n_row
    rows_dev, width = embeddings.shape
    group_size = rows_dev * n_col
    slots = groups * cap
    held, pairs = plane_plan(n_row, wide)
    count = len(held)

    assert groups & (groups - 1) == 0
    row, col = lax.axis_index("row"), lax.axis_index("col")
    plane, index = col // wide, row * wide + col % wide

    def device(i, h):
        return (i // wide) * n_col + h * wide + i % wide

    planes = [(i, h) for h in range(groups) for i in range(n_row * wide)]
    numbers = tuple(range(1, min(3, groups)))
    others = tuple(k for k in range(groups) if k not in numbers)
    chunk_shape = jax.ShapeDtypeStruct((cap, width), jnp.bfloat16)
    dest_row = dest_pos.reshape(1, rows_dev)
    plane_ref = plane.astype(jnp.int32).reshape(1)
    unit, slot, *made = pl.pallas_call(
        functools.partial(unit_kernel, groups, cap, group_size, numbers),
        out_shape=[
            jax.ShapeDtypeStruct((rows_dev, width), jnp.bfloat16),
            jax.ShapeDtypeStruct((1, rows_dev), jnp.int32),
            *[chunk_shape] * len(numbers),
        ],
        in_specs=[pl.BlockSpec(memory_space=pltpu.SMEM), VMEM, VMEM],
        out_specs=[VMEM] * (2 + len(numbers)),
        compiler_params=kernel_params(20),
    )(plane_ref, dest_row, embeddings)
    place, *more = pl.pallas_call(
        functools.partial(rest_kernel, groups, cap, group_size, others),
        out_shape=[jax.ShapeDtypeStruct((1, slots), jnp.int32), *[chunk_shape] * len(others)],
        in_specs=[VMEM] * 3,
        out_specs=[VMEM] * (1 + len(others)),
        compiler_params=kernel_params(20),
    )(dest_row, slot, unit)
    parts = dict(zip(numbers + others, made + more))

    def across(part, k):
        return lax.ppermute(part, AXES, [(device(i, h ^ k), device(i, h)) for i, h in planes])

    def inside(part, j):
        return lax.ppermute(part, AXES, [(device(int(held[j, i]), h), device(i, h)) for i, h in planes])

    def after(values, *done):
        return lax.optimization_barrier((values, done))[0]

    own = [parts[0]] + [across(parts[k], k) for k in numbers]
    rounds = [[inside(own[0], j) for j in range(1, count)]]
    place, rest = after((place, [parts[k] for k in others[1:]]), *rounds[0])
    own += [across(part, k) for k, part in zip(others[1:], rest)]
    for k in range(1, groups):
        part = own[k] if k == 1 else after(own[k], *rounds[-1])
        rounds.append([inside(part, j) for j in range(1, count)])
    blocks = [own] + [[moved[j - 1] for moved in rounds] for j in range(1, count)]

    planes_i = jnp.arange(groups, dtype=jnp.int32)
    swap = (planes_i[:, None] ^ planes_i[None, :]) == plane

    def by_plane(array):
        return jnp.sum(jnp.where(swap[:, :, None], array[None, :, :], 0), axis=1)

    levels = jnp.arange(LEVELS, dtype=jnp.int32)
    counts = jnp.sum((cluster_ids.reshape(1, rows_dev) <= levels[:, None]).astype(jnp.int32), axis=1)
    target_group = dest_pos // group_size
    most = jnp.max(jnp.sum((target_group[None, :] == jnp.arange(groups)[:, None]).astype(jnp.int32), axis=1))
    tail = jnp.concatenate([counts, (most > cap).astype(jnp.int32).reshape(1)])
    length = -(-(cap + LEVELS + 1) // 128) * 128
    facts = jnp.concatenate(
        [
            by_plane(place.reshape(groups, cap)),
            jnp.broadcast_to(tail[None, :], (groups, LEVELS + 1)),
            jnp.zeros((groups, length - cap - LEVELS - 1), jnp.int32),
        ],
        axis=1,
    )
    facts = jnp.broadcast_to(facts[None, :, None, :], (n_row, groups, wide, length)).reshape(devs, length)
    facts = lax.all_to_all(facts, AXES, split_axis=0, concat_axis=0, tiled=True)
    over = jnp.max(facts[:, cap + LEVELS]) > 0
    facts = facts.reshape(n_row, groups, wide, length)

    in_plane = (jnp.arange(n_row, dtype=jnp.int32) == plane).astype(jnp.int32)
    ends = jnp.sum(facts[..., cap : cap + LEVELS] * in_plane[:, None, None, None], axis=(0, 1, 2))
    places = by_plane(facts[..., :cap].transpose(1, 0, 2, 3).reshape(groups, n_row * wide * cap))
    places = places.reshape(groups, n_row * wide, cap).transpose(1, 0, 2).reshape(n_row * wide, slots)
    mine = jnp.sum(
        jnp.where(jnp.arange(n_row * wide)[None, :] == index, jnp.asarray(held, jnp.int32), 0), axis=1
    )
    mine = (mine[:, None] == jnp.arange(n_row * wide)[None, :]).astype(jnp.int32)
    places = jnp.sum(mine[:, :, None] * places[None, :, :], axis=1)
    labels = jnp.sum((places[:, None, :] >= ends[None, :, None]).astype(jnp.int32), axis=1)
    labels = jnp.where(places < group_size, labels, -1)

    early = slots - cap
    any_space = pl.BlockSpec(memory_space=pl.ANY)
    label_cols = labels.T
    area = 4 * slots * slots

    def scratch(number):
        return [
            pltpu.VMEM((count, number * cap, width), jnp.bfloat16),
            pltpu.SemaphoreType.DMA((count, number)),
        ]

    limit = 8 + (2 * count * slots * width + 5 * area) // 2**20
    first_best = pl.pallas_call(
        functools.partial(early_kernel, pairs, count),
        out_shape=jax.ShapeDtypeStruct((count, early), jnp.float32),
        in_specs=[any_space] * (count * (groups - 1)) + [VMEM] * 2,
        out_specs=VMEM,
        scratch_shapes=scratch(groups - 1),
        compiler_params=kernel_params(limit),
        cost_estimate=pl.CostEstimate(
            flops=2 * len(pairs) * early * early * width, bytes_accessed=2 * count * early * width, transcendentals=0
        ),
    )(*[part for block in blocks for part in block[:-1]], labels[:, :early], label_cols[:early])
    best = pl.pallas_call(
        functools.partial(late_kernel, pairs, count, group_size),
        out_shape=jax.ShapeDtypeStruct((n_row, n_col, rows_dev // 128, 128), jnp.float32),
        in_specs=[pl.BlockSpec(memory_space=pltpu.SMEM)] + [any_space] * (count * groups) + [VMEM] * 6,
        out_specs=VMEM,
        scratch_shapes=scratch(groups),
        compiler_params=kernel_params(limit),
    )(
        plane_ref,
        *itertools.chain(*blocks),
        first_best,
        places[:, :early],
        places[:, early:],
        labels[:, :early],
        labels[:, early:],
        label_cols,
    )

    best = lax.all_to_all(best.reshape(devs, -1, 128), AXES, split_axis=0, concat_axis=0, tiled=True)
    return jnp.max(best, axis=0).reshape(1, rows_dev), over


def shards(embeddings, dest_pos, cluster_ids):
    n_row, n_col = lax.axis_size("row"), lax.axis_size("col")
    rows_dev = embeddings.shape[0]
    devs = n_row * n_col
    most = min(rows_dev, n_col * max(4, 2 * rows_dev // devs))
    usual = min(most, -(-(rows_dev // n_row) * 11 // 8 // 16) * 16)
    args = (embeddings, dest_pos, cluster_ids)
    best, over = best_matches(usual, *args)
    if usual == most:
        return best
    return lax.cond(over, lambda: best_matches(most, *args)[0], lambda: best)


def solution(mesh):
    return jax.shard_map(
        shards,
        mesh=mesh,
        in_specs=(P(("row", "col"), None), P(("row", "col")), P("row", "col")),
        out_specs=P("row", "col"),
        check_vma=False,
    )
```

time: 363 us -> 84.6 us (0.23); the launches traced: 358 us -> 84.3 us
  local copies, waits for them, and re-layouts: 147 us -> 6.04 us
  waiting for transfers between devices: 145 us -> 27.3 us
  blocking collectives: 26.6 us -> 0 us
  Pallas kernels: 0 us -> 19.4 us
  starting transfers between devices: 13.3 us -> 26 us
  between operations: 13.5 us -> 1.67 us
  matrix products: 8.96 us -> 0 us
    scatter x3 -> x0, local copies, waits for them, and re-layouts: 144 us -> none  [the longest x1 71.6 us: shards(): jnp.zeros((devs, slots, width), jnp.bfloat16).at[target, slot].set(unit)]
    all_gather x1 -> x0, waiting for transfers between devices: 96.6 us -> none  [shards(): other = lax.all_gather(mine, 'col', axis=0, tiled=True)]
    all_to_all x2, waiting for transfers between devices: 48.7 us -> 15.1 us  [the longest x1 9.26 us: best_matches(): facts = lax.all_to_all(facts, AXES, split_axis=0, concat_axis=0, tiled=True)]
    all_gather x1 -> x0, blocking collectives: 26.6 us -> none  [shards(): other_labels = lax.all_gather(labels, 'col', axis=0, tiled=True)]
    pallas_call x0 -> x4, Pallas kernels: none -> 19.4 us  [the longest x1 7.78 us: best_matches(): pl.pallas_call(functools.partial(late_kernel, pairs, count, group_size),...]
    ppermute x0 -> x15, starting transfers between devices: none -> 17.5 us  [the longest x12 9.23 us: inside(): lax.ppermute(part, AXES, [(device(int(held[j, i]), h), device(i, h)) for...]
    ppermute x0 -> x15, waiting for transfers between devices: none -> 12.1 us  [the longest x12 12.1 us: inside(): lax.ppermute(part, AXES, [(device(int(held[j, i]), h), device(i, h)) for...]
    dot_general x1 -> x0, matrix products: 8.96 us -> none  [masked_sims(): lax.dot_general(left, right, (((1,), (1,)), ((), ())), preferred_element_...]
  transfers between devices with their start and end apart: 3 -> 17, of which waited for: 2 -> 6; matrix products, arithmetic and copies ran while one was open for 21% -> 9% of each run, Pallas kernels for 0% -> 8%
where the time goes in v1:
time: 84.6 us; the launch traced here: 84.3 us
  waiting for transfers between devices  27.3 us (32%)
  starting transfers between devices  26 us (31%)
  Pallas kernels  19.4 us (23%)
  local copies, waits for them, and re-layouts  6.04 us (7%)
  other arithmetic  3.68 us (4%)
  between operations  1.67 us (2%)
    ppermute x12, waiting for transfers between devices, inside(): lax.ppermute(part, AXES, [(device(int(held[j, i]), h), device(i, h)) for...  12.1 us
    all_to_all x1, waiting for transfers between devices, best_matches(): facts = lax.all_to_all(facts, AXES, split_axis=0, concat_axis=0, tiled=True)  9.26 us
    ppermute x12, starting transfers between devices, inside(): lax.ppermute(part, AXES, [(device(int(held[j, i]), h), device(i, h)) for...  9.23 us
    ppermute x3, starting transfers between devices, across(): lax.ppermute(part, AXES, [(device(i, h ^ k), device(i, h)) for i, h in pl...  8.24 us
    pallas_call x1, Pallas kernels, best_matches(): pl.pallas_call(functools.partial(late_kernel, pairs, count, group_size),...  7.78 us
    pallas_call x1, Pallas kernels, best_matches(): pl.pallas_call(functools.partial(early_kernel, pairs, count), out_shape=j...  7.16 us
    all_to_all x1, waiting for transfers between devices, best_matches(): lax.all_to_all(best.reshape(devs, -1, 128), AXES, split_axis=0, concat_ax...  5.88 us
    all_to_all x1, starting transfers between devices, best_matches(): facts = lax.all_to_all(facts, AXES, split_axis=0, concat_axis=0, tiled=True)  4.89 us
  transfers between devices with their start and end apart: 17, of which 6 were waited for; matrix products, arithmetic and copies ran while one was open for 9% of the time, Pallas kernels for 8%

profile of v1, /device:TPU:0, one launch (start us, length us, event | category | flops | bytes accessed | tf_op | source)
XLA Modules:
  0.0 84.3 jit_solution(3228428332996758060)
XLA Ops:
  0.0 3.2 %shard_map.57 = (bf16[512,1024]{1,0:T(8,128)(2,1)S(1)}, s32[1,512]{1,0:T(1,128)S(1)}, bf16[176,1024]{1,0:T(8,128)(2,1)S(1)}, bf16[176,1024]{1,0:T(8,128)(2,1)}) custom-call(s32[1]{0:T(128)} %bitcast.13.plane_ref.refs_0_, s32[1,512]{1,0:T(1,128)} %bitcast.38, f32[512,1024]{1,0:T(8,128)} %emb_ref.1), custom_call_target="tpu_custom_call" | custom-call | tf_op jit(solution)/shard_map/pallas_call | solution.py:256
  3.2 1.3 %shard_map.58 = (s32[1,704]{1,0:T(1,128)S(1)}, bf16[176,1024]{1,0:T(8,128)(2,1)S(1)}, bf16[176,1024]{1,0:T(8,128)(2,1)}) custom-call(s32[1,512]{1,0:T(1,128)S(1)} %bitcast.39, s32[1,512]{1,0:T(1,128)S(1)} %get-tuple-element.47.slot_ref, bf16[512,1024]{1,0:T(8,128)(2,1)S(1)} %get-tuple-element.48.unit_ref), custom_call_target="tpu_custom_call" | custom-call | tf_op jit(solution)/shard_map/pallas_call | solution.py:267
  4.5 2.4 %collective-permute-start.17 = (bf16[176,1024]{1,0:T(8,128)(2,1)S(1)}, bf16[176,1024]{1,0:T(8,128)(2,1)S(1)}, u32[]{:S(2)}, u32[]{:S(2)}) collective-permute-start(bf16[176,1024]{1,0:T(8,128)(2,1)S(1)} %get-tuple-element.51.refs_0_.refs_1_), channel_id=1, source_target_pairs={{16,0},{8,1},{24,8},{0,9},{17,16},{9,17},{25,24},{1,25},{18,2},{10... | collective-permute-start | bytes 1081352 | tf_op jit(solution)/shard_map/ppermute | solution.py:280
  6.9 0.5 collective-permute-start.16
  7.4 0.1 collective-permute-start.15
  7.5 2.0 %collective-permute-start.18 = (bf16[176,1024]{1,0:T(8,128)(2,1)S(1)}, bf16[176,1024]{1,0:T(8,128)(2,1)S(1)}, u32[]{:S(2)}, u32[]{:S(2)}) collective-permute-start(bf16[176,1024]{1,0:T(8,128)(2,1)S(1)} %get-tuple-element.53), channel_id=1, source_target_pairs={{2,0},{3,1},{10,8},{11,9},{18,16},{19,17},{26,24},{27,25},{0,2},{1... | collective-permute-start | bytes 1081352 | tf_op jit(solution)/shard_map/ppermute | solution.py:277
  9.5 2.6 %collective-permute-start.19 = (bf16[176,1024]{1,0:T(8,128)(2,1)}, bf16[176,1024]{1,0:T(8,128)(2,1)S(1)}, u32[]{:S(2)}, u32[]{:S(2)}) collective-permute-start(bf16[176,1024]{1,0:T(8,128)(2,1)} %get-tuple-element.54), channel_id=1, source_target_pairs={{4,0},{5,1},{12,8},{13,9},{20,16},{21,17},{28,24},{29,25},{6,2},{7... | collective-permute-start | bytes 1081352 | tf_op jit(solution)/shard_map/ppermute | solution.py:277
  12.2 0.1 convert_reduce_fusion.4
  12.3 0.1 convert_reduce_fusion.5
  12.4 0.7 reduce_max.46
  13.8 0.1 pad_add_fusion.1
  13.9 0.1 pad.7.clone
  14.0 0.1 pad.6.clone
  14.0 0.1 select_reduce_fusion.5
  14.2 0.1 fusion.7
  14.2 1.6 %collective-permute-done.17.refs_9_.refs_13_ = bf16[176,1024]{1,0:T(8,128)(2,1)S(1)} collective-permute-done((bf16[176,1024]{1,0:T(8,128)(2,1)S(1)}, bf16[176,1024]{1,0:T(8,128)(2,1)S(1)}, u32[]{:S(2)}, u32[]{:S(2)}) %collective-permute-start.17) | collective-permute-done | bytes 360480 | tf_op jit(solution)/shard_map/ppermute | solution.py:280
  15.8 2.1 %collective-permute-done.16.refs_6_.refs_9_ = bf16[176,1024]{1,0:T(8,128)(2,1)S(1)} collective-permute-done((bf16[176,1024]{1,0:T(8,128)(2,1)S(1)}, bf16[176,1024]{1,0:T(8,128)(2,1)S(1)}, u32[]{:S(2)}, u32[]{:S(2)}) %collective-permute-start.16) | collective-permute-done | bytes 360480 | tf_op jit(solution)/shard_map/ppermute | solution.py:280
  17.9 0.0 collective-permute-done.15.refs_3_.refs_5_
  17.9 0.1 broadcast_in_dim.172
  18.0 0.1 select_reduce_fusion.4
  18.1 0.7 all_to_all.21
  18.7 4.9 %all-to-all-start.2 = ((s32[32,1,256]{2,1,0:T(1,128)}), s32[32,1,256]{2,1,0:T(1,128)S(1)}, u32[]{:S(2)}, u32[]{:S(2)}) async-start(s32[32,1,256]{2,1,0:T(1,128)} %all_to_all.21), calls=%async_computation.2 | async-start | bytes 65536 | tf_op jit(solution)/shard_map/all_to_all | solution.py:315
  23.7 3.7 %collective-permute-start.20 = (bf16[176,1024]{1,0:T(8,128)(2,1)}, bf16[176,1024]{1,0:T(8,128)(2,1)S(1)}, u32[]{:S(2)}, u32[]{:S(2)}) collective-permute-start(bf16[176,1024]{1,0:T(8,128)(2,1)} %get-tuple-element.55), channel_id=1, source_target_pairs={{6,0},{7,1},{14,8},{15,9},{22,16},{23,17},{30,24},{31,25},{4,2},{5... | collective-permute-start | bytes 1081352 | tf_op jit(solution)/shard_map/ppermute | solution.py:277
  27.3 0.0 collective-permute-done.18.refs_1_.refs_2_
  27.3 1.0 %collective-permute-start.23 = (bf16[176,1024]{1,0:T(8,128)(2,1)S(1)}, bf16[176,1024]{1,0:T(8,128)(2,1)S(1)}, u32[]{:S(2)}, u32[]{:S(2)}) collective-permute-start(bf16[176,1024]{1,0:T(8,128)(2,1)S(1)} %collective-permute-done.18.refs_1_.refs_2_), channel_id=1, source_target_pairs={{16,0},{8,1},{24,8},{0,9},{17,16},{9,17},{25,24},{1,25},{18,2},{10... | collective-permute-start | bytes 1081352 | tf_op jit(solution)/shard_map/ppermute | solution.py:280
  28.3 1.1 %collective-permute-start.22 = (bf16[176,1024]{1,0:T(8,128)(2,1)S(1)}, bf16[176,1024]{1,0:T(8,128)(2,1)S(1)}, u32[]{:S(2)}, u32[]{:S(2)}) collective-permute-start(bf16[176,1024]{1,0:T(8,128)(2,1)S(1)} %collective-permute-done.18.refs_1_.refs_2_), channel_id=1, source_target_pairs={{1,0},{17,1},{9,8},{25,9},{0,16},{16,17},{8,24},{24,25},{3,2},{19,... | collective-permute-start | bytes 1081352 | tf_op jit(solution)/shard_map/ppermute | solution.py:280
  29.4 9.3 %all-to-all-done.2 = s32[32,1,256]{2,1,0:T(1,128)S(1)} async-done(((s32[32,1,256]{2,1,0:T(1,128)}), s32[32,1,256]{2,1,0:T(1,128)S(1)}, u32[]{:S(2)}, u32[]{:S(2)}) %all-to-all-start.2) | async-done | bytes 32800 | tf_op jit(solution)/shard_map/all_to_all | solution.py:315
  38.6 0.1 reduce.4
  38.8 0.1 broadcast_in_dim.181
  38.9 0.1 select_reduce_fusion.3
  39.0 0.1 reshape.175
  39.1 0.1 mul.54
  39.2 0.1 multiply_reduce_fusion.1
  39.3 0.0 collective-permute-done.19.refs_2_.refs_3_
  39.4 0.0 collective-permute-done.23.refs_10_.refs_14_
  39.4 0.0 collective-permute-done.21.refs_4_.refs_6_
  39.4 1.1 %collective-permute-start.26 = (bf16[176,1024]{1,0:T(8,128)(2,1)S(1)}, bf16[176,1024]{1,0:T(8,128)(2,1)}, u32[]{:S(2)}, u32[]{:S(2)}) collective-permute-start(bf16[176,1024]{1,0:T(8,128)(2,1)S(1)} %collective-permute-done.19.refs_2_.refs_3_), channel_id=1, source_target_pairs={{16,0},{8,1},{24,8},{0,9},{17,16},{9,17},{25,24},{1,25},{18,2},{10... | collective-permute-start | bytes 1081352 | tf_op jit(solution)/shard_map/ppermute | solution.py:280
  40.5 1.0 %collective-permute-start.25 = (bf16[176,1024]{1,0:T(8,128)(2,1)S(1)}, bf16[176,1024]{1,0:T(8,128)(2,1)}, u32[]{:S(2)}, u32[]{:S(2)}) collective-permute-start(bf16[176,1024]{1,0:T(8,128)(2,1)S(1)} %collective-permute-done.19.refs_2_.refs_3_), channel_id=1, source_target_pairs={{1,0},{17,1},{9,8},{25,9},{0,16},{16,17},{8,24},{24,25},{3,2},{19,... | collective-permute-start | bytes 1081352 | tf_op jit(solution)/shard_map/ppermute | solution.py:280
  41.5 0.2 copy.85
  41.7 0.1 fusion.4
  41.8 0.1 convert_reduce_fusion.3
  42.0 0.9 %copy.86 = s32[4,704]{0,1:T(8,128)} copy(s32[4,704]{1,0:T(4,128)S(1)} %convert_reduce_fusion.3) | data formatting | bytes 22528 | tf_op jit(solution)/shard_map/reduce_sum | solution.py:328
  42.9 7.1 %collective-permute-done.26.refs_11_.refs_15_ = bf16[176,1024]{1,0:T(8,128)(2,1)} collective-permute-done((bf16[176,1024]{1,0:T(8,128)(2,1)S(1)}, bf16[176,1024]{1,0:T(8,128)(2,1)}, u32[]{:S(2)}, u32[]{:S(2)}) %collective-permute-start.26) | collective-permute-done | bytes 360480 | tf_op jit(solution)/shard_map/ppermute | solution.py:280
  50.0 1.4 %collective-permute-done.25.refs_8_.refs_11_ = bf16[176,1024]{1,0:T(8,128)(2,1)} collective-permute-done((bf16[176,1024]{1,0:T(8,128)(2,1)S(1)}, bf16[176,1024]{1,0:T(8,128)(2,1)}, u32[]{:S(2)}, u32[]{:S(2)}) %collective-permute-start.25) | collective-permute-done | bytes 360480 | tf_op jit(solution)/shard_map/ppermute | solution.py:280
  51.4 0.0 collective-permute-done.24.refs_5_.refs_7_
  51.4 2.0 %collective-permute-start.28 = (bf16[176,1024]{1,0:T(8,128)(2,1)S(1)}, bf16[176,1024]{1,0:T(8,128)(2,1)}, u32[]{:S(2)}, u32[]{:S(2)}) collective-permute-start(bf16[176,1024]{1,0:T(8,128)(2,1)S(1)} %collective-permute-done.20.refs_4_), channel_id=1, source_target_pairs={{1,0},{17,1},{9,8},{25,9},{0,16},{16,17},{8,24},{24,25},{3,2},{19,... | collective-permute-start | bytes 1081352 | tf_op jit(solution)/shard_map/ppermute | solution.py:280
  53.4 0.0 collective-permute-start.27
  53.4 1.0 %broadcast_select_fusion.1 = s32[4,704]{0,1:T(8,128)S(1)} fusion(pred[4,704]{0,1:T(8,128)(4,1)S(1)} %copy.85, s32[4,704]{0,1:T(8,128)} %copy.86), kind=kLoop, calls=%fused_computation.30 | loop fusion | flops 2816 | bytes 25344 | tf_op jit(solution)/shard_map/jit(_where)/select_n | solution.py:329
  54.4 0.1 slice.68.refs_19_
  54.5 0.8 slice.65
  55.3 0.1 copy.94.refs_21_
  55.4 1.1 %copy.87.refs_12_.refs_20_ = s32[4,528]{1,0:T(4,128)S(1)} copy(s32[4,528]{0,1:T(8,128)} %slice.65) | data formatting | bytes 16896 | tf_op jit(solution)/shard_map/slice | solution.py:353
  56.5 1.0 %copy-done.4 = bf16[176,1024]{1,0:T(8,128)(2,1)S(1)} copy-done((bf16[176,1024]{1,0:T(8,128)(2,1)S(1)}, bf16[176,1024]{1,0:T(8,128)(2,1)}, u32[]{:S(2)}) %copy-start.4) | copy-done | bytes 360472
  57.5 7.2 %shard_map.59.refs_17_ = f32[4,528]{1,0:T(4,128)S(1)} custom-call(bf16[176,1024]{1,0:T(8,128)(2,1)S(1)} %get-tuple-element.51.refs_0_.refs_1_, bf16[176,1024]{1,0:T(8,128)(2,1)S(1)} %collective-permute-done.18.refs_1_.refs_2_, bf16[176,1024]{1,0:T(8,128)(2,1)S(1)} %collective-permute-done.19.refs_2_.refs_3_, ...), custom_call_target="tpu_custom_call" | custom-call | flops 2854748160 | bytes 4325376 | tf_op jit(solution)/shard_map/pallas_call | solution.py:343
  64.7 0.0 copy-start.14
  64.7 0.0 collective-permute-done.28.refs_12_
  64.7 0.0 collective-permute-done.27.refs_8_
  64.7 7.8 %shard_map.60 = f32[4,8,4,128]{3,2,1,0:T(4,128)} custom-call(s32[1]{0:T(128)} %bitcast.13.plane_ref.refs_0_, bf16[176,1024]{1,0:T(8,128)(2,1)S(1)} %get-tuple-element.51.refs_0_.refs_1_, bf16[176,1024]{1,0:T(8,128)(2,1)S(1)} %collective-permute-done.18.refs_1_.refs_2_, bf16[176,1024]{1,0:T(8,128)(2,1)S(1)} %collective-permute-done.19.refs_2_.refs_3_, ...), custom_call_target="tpu_custom_call" | custom-call | tf_op jit(solution)/shard_map/pallas_call | solution.py:354
  72.5 3.6 %all-to-all-start.3 = ((f32[32,4,128]{2,1,0:T(4,128)}), f32[32,4,128]{2,1,0:T(4,128)S(1)}, u32[]{:S(2)}, u32[]{:S(2)}) async-start(f32[32,4,128]{2,1,0:T(4,128)} %bitcast.19), calls=%async_computation.3 | async-start | bytes 131072 | tf_op jit(solution)/shard_map/all_to_all | solution.py:372
  76.1 0.7 slice_reduce_fusion
  77.5 5.9 %all-to-all-done.3 = f32[32,4,128]{2,1,0:T(4,128)S(1)} async-done(((f32[32,4,128]{2,1,0:T(4,128)}), f32[32,4,128]{2,1,0:T(4,128)S(1)}, u32[]{:S(2)}, u32[]{:S(2)}) %all-to-all-start.3) | async-done | bytes 65568 | tf_op jit(solution)/shard_map/all_to_all | solution.py:372
  83.4 0.3 conditional.1
  83.7 0.0 copy-start.15
  83.7 0.6 copy-done.15
  (40 shorter events, 0.2 us)
Async XLA Ops:
  0.0 14.0 %copy-start.13 = (s32[4,8]{1,0:T(4,128)S(1)}, s32[4,8]{1,0:T(4,128)}, u32[]{:S(2)}) copy-start(s32[4,8]{1,0:T(4,128)} %constant.109.clone) | copy-start | bytes 388
  0.0 3.2 %copy-start.11 = (s32[512]{0:T(512)S(1)}, s32[512]{0:T(512)}, u32[]{:S(2)}) copy-start(s32[512]{0:T(512)} %param.8) | copy-start | bytes 6148
  0.0 12.1 %copy-start.12 = (s32[1,512]{1,0:T(1,128)S(1)}, s32[1,512]{1,0:T(1,128)}, u32[]{:S(2)}) copy-start(s32[1,512]{1,0:T(1,128)} %param.9) | copy-start | bytes 6148
  4.5 11.3 %collective-permute-start.17 = (bf16[176,1024]{1,0:T(8,128)(2,1)S(1)}, bf16[176,1024]{1,0:T(8,128)(2,1)S(1)}, u32[]{:S(2)}, u32[]{:S(2)}) collective-permute-start(bf16[176,1024]{1,0:T(8,128)(2,1)S(1)} %get-tuple-element.51.refs_0_.refs_1_), channel_id=1, source_target_pairs={{16,0},{8,1},{24,8},{0,9},{17,16},{9,17},{25,24},{1,25},{18,2},{10... | collective-permute-start | bytes 1081352 | tf_op jit(solution)/shard_map/ppermute | solution.py:280
  6.9 11.0 %collective-permute-start.16 = (bf16[176,1024]{1,0:T(8,128)(2,1)S(1)}, bf16[176,1024]{1,0:T(8,128)(2,1)S(1)}, u32[]{:S(2)}, u32[]{:S(2)}) collective-permute-start(bf16[176,1024]{1,0:T(8,128)(2,1)S(1)} %get-tuple-element.51.refs_0_.refs_1_), channel_id=1, source_target_pairs={{1,0},{17,1},{9,8},{25,9},{0,16},{16,17},{8,24},{24,25},{3,2},{19,... | collective-permute-start | bytes 1081352 | tf_op jit(solution)/shard_map/ppermute | solution.py:280
  7.4 10.5 %collective-permute-start.15 = (bf16[176,1024]{1,0:T(8,128)(2,1)S(1)}, bf16[176,1024]{1,0:T(8,128)(2,1)S(1)}, u32[]{:S(2)}, u32[]{:S(2)}) collective-permute-start(bf16[176,1024]{1,0:T(8,128)(2,1)S(1)} %get-tuple-element.51.refs_0_.refs_1_), channel_id=1, source_target_pairs={{8,0},{9,1},{0,8},{1,9},{24,16},{25,17},{16,24},{17,25},{10,2},{11... | collective-permute-start | bytes 1081352 | tf_op jit(solution)/shard_map/ppermute | solution.py:280
  7.5 19.8 %collective-permute-start.18 = (bf16[176,1024]{1,0:T(8,128)(2,1)S(1)}, bf16[176,1024]{1,0:T(8,128)(2,1)S(1)}, u32[]{:S(2)}, u32[]{:S(2)}) collective-permute-start(bf16[176,1024]{1,0:T(8,128)(2,1)S(1)} %get-tuple-element.53), channel_id=1, source_target_pairs={{2,0},{3,1},{10,8},{11,9},{18,16},{19,17},{26,24},{27,25},{0,2},{1... | collective-permute-start | bytes 1081352 | tf_op jit(solution)/shard_map/ppermute | solution.py:277
  9.5 29.8 %collective-permute-start.19 = (bf16[176,1024]{1,0:T(8,128)(2,1)}, bf16[176,1024]{1,0:T(8,128)(2,1)S(1)}, u32[]{:S(2)}, u32[]{:S(2)}) collective-permute-start(bf16[176,1024]{1,0:T(8,128)(2,1)} %get-tuple-element.54), channel_id=1, source_target_pairs={{4,0},{5,1},{12,8},{13,9},{20,16},{21,17},{28,24},{29,25},{6,2},{7... | collective-permute-start | bytes 1081352 | tf_op jit(solution)/shard_map/ppermute | solution.py:277
  18.7 19.9 %all-to-all-start.2 = ((s32[32,1,256]{2,1,0:T(1,128)}), s32[32,1,256]{2,1,0:T(1,128)S(1)}, u32[]{:S(2)}, u32[]{:S(2)}) async-start(s32[32,1,256]{2,1,0:T(1,128)} %all_to_all.21), calls=%async_computation.2 | async-start | bytes 65536 | tf_op jit(solution)/shard_map/all_to_all | solution.py:315
  23.7 19.2 %collective-permute-start.20 = (bf16[176,1024]{1,0:T(8,128)(2,1)}, bf16[176,1024]{1,0:T(8,128)(2,1)S(1)}, u32[]{:S(2)}, u32[]{:S(2)}) collective-permute-start(bf16[176,1024]{1,0:T(8,128)(2,1)} %get-tuple-element.55), channel_id=1, source_target_pairs={{6,0},{7,1},{14,8},{15,9},{22,16},{23,17},{30,24},{31,25},{4,2},{5... | collective-permute-start | bytes 1081352 | tf_op jit(solution)/shard_map/ppermute | solution.py:277
  27.3 12.0 %collective-permute-start.23 = (bf16[176,1024]{1,0:T(8,128)(2,1)S(1)}, bf16[176,1024]{1,0:T(8,128)(2,1)S(1)}, u32[]{:S(2)}, u32[]{:S(2)}) collective-permute-start(bf16[176,1024]{1,0:T(8,128)(2,1)S(1)} %collective-permute-done.18.refs_1_.refs_2_), channel_id=1, source_target_pairs={{16,0},{8,1},{24,8},{0,9},{17,16},{9,17},{25,24},{1,25},{18,2},{10... | collective-permute-start | bytes 1081352 | tf_op jit(solution)/shard_map/ppermute | solution.py:280
  28.3 11.0 %collective-permute-start.22 = (bf16[176,1024]{1,0:T(8,128)(2,1)S(1)}, bf16[176,1024]{1,0:T(8,128)(2,1)S(1)}, u32[]{:S(2)}, u32[]{:S(2)}) collective-permute-start(bf16[176,1024]{1,0:T(8,128)(2,1)S(1)} %collective-permute-done.18.refs_1_.refs_2_), channel_id=1, source_target_pairs={{1,0},{17,1},{9,8},{25,9},{0,16},{16,17},{8,24},{24,25},{3,2},{19,... | collective-permute-start | bytes 1081352 | tf_op jit(solution)/shard_map/ppermute | solution.py:280
  29.4 10.0 %collective-permute-start.21 = (bf16[176,1024]{1,0:T(8,128)(2,1)S(1)}, bf16[176,1024]{1,0:T(8,128)(2,1)}, u32[]{:S(2)}, u32[]{:S(2)}) collective-permute-start(bf16[176,1024]{1,0:T(8,128)(2,1)S(1)} %collective-permute-done.18.refs_1_.refs_2_), channel_id=1, source_target_pairs={{8,0},{9,1},{0,8},{1,9},{24,16},{25,17},{16,24},{17,25},{10,2},{11... | collective-permute-start | bytes 1081352 | tf_op jit(solution)/shard_map/ppermute | solution.py:280
  38.6 2.8 %copy-start.9 = (s32[32,1,256]{2,1,0:T(1,128)}, s32[32,1,256]{2,1,0:T(1,128)S(1)}, u32[]{:S(2)}) copy-start(s32[32,1,256]{2,1,0:T(1,128)S(1)} %all-to-all-done.2) | copy-start | bytes 98308
  39.4 14.0 %copy-start.3 = (bf16[176,1024]{1,0:T(8,128)(2,1)}, bf16[176,1024]{1,0:T(8,128)(2,1)S(1)}, u32[]{:S(2)}) copy-start(bf16[176,1024]{1,0:T(8,128)(2,1)S(1)} %collective-permute-done.22.refs_7_.refs_10_) | copy-start | bytes 1081348
  39.4 10.6 %collective-permute-start.26 = (bf16[176,1024]{1,0:T(8,128)(2,1)S(1)}, bf16[176,1024]{1,0:T(8,128)(2,1)}, u32[]{:S(2)}, u32[]{:S(2)}) collective-permute-start(bf16[176,1024]{1,0:T(8,128)(2,1)S(1)} %collective-permute-done.19.refs_2_.refs_3_), channel_id=1, source_target_pairs={{16,0},{8,1},{24,8},{0,9},{17,16},{9,17},{25,24},{1,25},{18,2},{10... | collective-permute-start | bytes 1081352 | tf_op jit(solution)/shard_map/ppermute | solution.py:280
  40.5 10.9 %collective-permute-start.25 = (bf16[176,1024]{1,0:T(8,128)(2,1)S(1)}, bf16[176,1024]{1,0:T(8,128)(2,1)}, u32[]{:S(2)}, u32[]{:S(2)}) collective-permute-start(bf16[176,1024]{1,0:T(8,128)(2,1)S(1)} %collective-permute-done.19.refs_2_.refs_3_), channel_id=1, source_target_pairs={{1,0},{17,1},{9,8},{25,9},{0,16},{16,17},{8,24},{24,25},{3,2},{19,... | collective-permute-start | bytes 1081352 | tf_op jit(solution)/shard_map/ppermute | solution.py:280
  41.5 9.9 %collective-permute-start.24 = (bf16[176,1024]{1,0:T(8,128)(2,1)S(1)}, bf16[176,1024]{1,0:T(8,128)(2,1)}, u32[]{:S(2)}, u32[]{:S(2)}) collective-permute-start(bf16[176,1024]{1,0:T(8,128)(2,1)S(1)} %collective-permute-done.19.refs_2_.refs_3_), channel_id=1, source_target_pairs={{8,0},{9,1},{0,8},{1,9},{24,16},{25,17},{16,24},{17,25},{10,2},{11... | collective-permute-start | bytes 1081352 | tf_op jit(solution)/shard_map/ppermute | solution.py:280
  51.4 13.3 %collective-permute-start.29 = (bf16[176,1024]{1,0:T(8,128)(2,1)S(1)}, bf16[176,1024]{1,0:T(8,128)(2,1)}, u32[]{:S(2)}, u32[]{:S(2)}) collective-permute-start(bf16[176,1024]{1,0:T(8,128)(2,1)S(1)} %collective-permute-done.20.refs_4_), channel_id=1, source_target_pairs={{16,0},{8,1},{24,8},{0,9},{17,16},{9,17},{25,24},{1,25},{18,2},{10... | collective-permute-start | bytes 1081352 | tf_op jit(solution)/shard_map/ppermute | solution.py:280
  51.4 13.3 %collective-permute-start.28 = (bf16[176,1024]{1,0:T(8,128)(2,1)S(1)}, bf16[176,1024]{1,0:T(8,128)(2,1)}, u32[]{:S(2)}, u32[]{:S(2)}) collective-permute-start(bf16[176,1024]{1,0:T(8,128)(2,1)S(1)} %collective-permute-done.20.refs_4_), channel_id=1, source_target_pairs={{1,0},{17,1},{9,8},{25,9},{0,16},{16,17},{8,24},{24,25},{3,2},{19,... | collective-permute-start | bytes 1081352 | tf_op jit(solution)/shard_map/ppermute | solution.py:280
  53.4 11.3 %collective-permute-start.27 = (bf16[176,1024]{1,0:T(8,128)(2,1)S(1)}, bf16[176,1024]{1,0:T(8,128)(2,1)}, u32[]{:S(2)}, u32[]{:S(2)}) collective-permute-start(bf16[176,1024]{1,0:T(8,128)(2,1)S(1)} %collective-permute-done.20.refs_4_), channel_id=1, source_target_pairs={{8,0},{9,1},{0,8},{1,9},{24,16},{25,17},{16,24},{17,25},{10,2},{11... | collective-permute-start | bytes 1081352 | tf_op jit(solution)/shard_map/ppermute | solution.py:280
  56.5 1.0 %copy-start.4 = (bf16[176,1024]{1,0:T(8,128)(2,1)S(1)}, bf16[176,1024]{1,0:T(8,128)(2,1)}, u32[]{:S(2)}) copy-start(bf16[176,1024]{1,0:T(8,128)(2,1)} %copy-done.3) | copy-start | bytes 1081348
  57.5 7.2 %copy-start.5 = (bf16[176,1024]{1,0:T(8,128)(2,1)S(1)}, bf16[176,1024]{1,0:T(8,128)(2,1)}, u32[]{:S(2)}) copy-start(bf16[176,1024]{1,0:T(8,128)(2,1)} %copy-done.3) | copy-start | bytes 1081348
  64.7 11.5 %copy-start.10 = (s32[32,1,256]{2,1,0:T(1,128)S(1)}, s32[32,1,256]{2,1,0:T(1,128)}, u32[]{:S(2)}) copy-start(s32[32,1,256]{2,1,0:T(1,128)} %copy-done.9) | copy-start | bytes 98308
  64.7 12.8 %copy-start.14 = (s32[4,8]{1,0:T(4,128)S(1)}, s32[4,8]{1,0:T(4,128)}, u32[]{:S(2)}) copy-start(s32[4,8]{1,0:T(4,128)} %constant.109.clone) | copy-start | bytes 388
  72.5 10.9 %all-to-all-start.3 = ((f32[32,4,128]{2,1,0:T(4,128)}), f32[32,4,128]{2,1,0:T(4,128)S(1)}, u32[]{:S(2)}, u32[]{:S(2)}) async-start(f32[32,4,128]{2,1,0:T(4,128)} %bitcast.19), calls=%async_computation.3 | async-start | bytes 131072 | tf_op jit(solution)/shard_map/all_to_all | solution.py:372
  83.7 0.6 copy-start.15

commit v2 on v1

--- a/solution.py
+++ b/solution.py
@@ -248,8 +248,7 @@
         return (i // wide) * n_col + h * wide + i % wide
 
     planes = [(i, h) for h in range(groups) for i in range(n_row * wide)]
-    numbers = tuple(range(1, min(3, groups)))
-    others = tuple(k for k in range(groups) if k not in numbers)
+    numbers, others = (0,), tuple(range(1, groups))
     chunk_shape = jax.ShapeDtypeStruct((cap, width), jnp.bfloat16)
     dest_row = dest_pos.reshape(1, rows_dev)
     plane_ref = plane.astype(jnp.int32).reshape(1)
@@ -282,14 +281,15 @@
     def after(values, *done):
         return lax.optimization_barrier((values, done))[0]
 
-    own = [parts[0]] + [across(parts[k], k) for k in numbers]
+    own = [parts[0]] + [across(parts[k], k) for k in range(1, min(3, groups))]
     rounds = [[inside(own[0], j) for j in range(1, count)]]
-    place, rest = after((place, [parts[k] for k in others[1:]]), *rounds[0])
-    own += [across(part, k) for k, part in zip(others[1:], rest)]
-    for k in range(1, groups):
-        part = own[k] if k == 1 else after(own[k], *rounds[-1])
-        rounds.append([inside(part, j) for j in range(1, count)])
-    blocks = [own] + [[moved[j - 1] for moved in rounds] for j in range(1, count)]
+    place = after(place, rounds[0][0])
+    rest = after([parts[k] for k in range(3, groups)], own[1])
+    own += [across(part, k) for k, part in zip(range(3, groups), rest)]
+    for k in range(1, groups - 1):
+        near, *far = rounds[-1]
+        part = after(own[k], near, *([] if k > 1 else far))
+        rounds.append([inside(after(part, *far), 1), *[inside(part, j) for j in range(2, count)]])
 
     planes_i = jnp.arange(groups, dtype=jnp.int32)
     swap = (planes_i[:, None] ^ planes_i[None, :]) == plane
@@ -313,6 +313,7 @@
     )
     facts = jnp.broadcast_to(facts[None, :, None, :], (n_row, groups, wide, length)).reshape(devs, length)
     facts = lax.all_to_all(facts, AXES, split_axis=0, concat_axis=0, tiled=True)
+    facts = after(facts, *rounds[1])
     over = jnp.max(facts[:, cap + LEVELS]) > 0
     facts = facts.reshape(n_row, groups, wide, length)
 
@@ -329,8 +330,13 @@
     labels = jnp.where(places < group_size, labels, -1)
 
     early = slots - cap
+    label_cols = labels.T
+    facts = places[:, :early], places[:, early:], labels[:, :early], labels[:, early:], label_cols[:early], label_cols
+    facts, last = lax.optimization_barrier((facts, after(own[-1], *rounds[-1][:1], *rounds[-2])))
+    rounds.append([inside(last, j) for j in range(1, count)])
+    place, last_place, label, last_label, label_col, label_cols = facts
+    blocks = [own] + [[moved[j - 1] for moved in rounds] for j in range(1, count)]
     any_space = pl.BlockSpec(memory_space=pl.ANY)
-    label_cols = labels.T
     area = 4 * slots * slots
 
     def scratch(number):
@@ -350,7 +356,7 @@
         cost_estimate=pl.CostEstimate(
             flops=2 * len(pairs) * early * early * width, bytes_accessed=2 * count * early * width, transcendentals=0
         ),
-    )(*[part for block in blocks for part in block[:-1]], labels[:, :early], label_cols[:early])
+    )(*[part for block in blocks for part in block[:-1]], label, label_col)
     best = pl.pallas_call(
         functools.partial(late_kernel, pairs, count, group_size),
         out_shape=jax.ShapeDtypeStruct((n_row, n_col, rows_dev // 128, 128), jnp.float32),
@@ -362,10 +368,10 @@
         plane_ref,
         *itertools.chain(*blocks),
         first_best,
-        places[:, :early],
-        places[:, early:],
-        labels[:, :early],
-        labels[:, early:],
+        place,
+        last_place,
+        label,
+        last_label,
         label_cols,
     )
 

time: 84.6 us -> 85.4 us (level)
  waiting for transfers between devices: 27.3 us -> 22.3 us
  starting transfers between devices: 26 us -> 30.1 us
  local copies, waits for them, and re-layouts: 6.04 us -> 8.26 us
    ppermute x3, waiting for transfers between devices: 0.01 us -> 11.8 us  [across(): lax.ppermute(part, AXES, [(device(i, h ^ k), device(i, h)) for i, h in pl...]
    ppermute x12, waiting for transfers between devices: 12.1 us -> 1.02 us  [inside(): lax.ppermute(part, AXES, [(device(int(held[j, i]), h), device(i, h)) for...]
    all_to_all x1, waiting for transfers between devices: 9.26 us -> 3.58 us  [best_matches(): facts = lax.all_to_all(facts, AXES, split_axis=0, concat_axis=0, tiled=True)]
    all_to_all x1, starting transfers between devices: 3.59 us -> 8.23 us  [best_matches(): lax.all_to_all(best.reshape(devs, -1, 128), AXES, split_axis=0, concat_ax...]
    optimization_barrier x0 -> x2, local copies, waits for them, and re-layouts: none -> 2.07 us  [best_matches(): lax.optimization_barrier((facts, after(own[-1], *rounds[-1][:1], *rounds[...]
    slice x2 -> x1, local copies, waits for them, and re-layouts: 1.83 us -> 0.75 us  [best_matches(): labels[:, :early]]
    pallas_call x1, Pallas kernels: 3.16 us -> 2.22 us  [best_matches(): pl.pallas_call(functools.partial(unit_kernel, groups, cap, group_size, nu...]
    unnamed x22 -> x23, local copies, waits for them, and re-layouts: 1.69 us -> 2.33 us
  transfers between devices with their start and end apart: 17 -> 17, of which waited for: 6 -> 4; matrix products, arithmetic and copies ran while one was open for 9% -> 10% of each run, Pallas kernels for 8% -> 10%
where the time goes in v2:
time: 85.4 us; the launch traced here: 85 us
  starting transfers between devices  30.1 us (35%)
  waiting for transfers between devices  22.3 us (26%)
  Pallas kernels  18.8 us (22%)
  local copies, waits for them, and re-layouts  8.26 us (10%)
  other arithmetic  3.6 us (4%)
  between operations  1.69 us (2%)
    ppermute x3, waiting for transfers between devices, across(): lax.ppermute(part, AXES, [(device(i, h ^ k), device(i, h)) for i, h in pl...  11.8 us
    ppermute x12, starting transfers between devices, inside(): lax.ppermute(part, AXES, [(device(int(held[j, i]), h), device(i, h)) for...  9.49 us
    ppermute x3, starting transfers between devices, across(): lax.ppermute(part, AXES, [(device(i, h ^ k), device(i, h)) for i, h in pl...  8.23 us
    all_to_all x1, starting transfers between devices, best_matches(): lax.all_to_all(best.reshape(devs, -1, 128), AXES, split_axis=0, concat_ax...  8.23 us
    pallas_call x1, Pallas kernels, best_matches(): pl.pallas_call(functools.partial(late_kernel, pairs, count, group_size),...  7.83 us
    pallas_call x1, Pallas kernels, best_matches(): pl.pallas_call(functools.partial(early_kernel, pairs, count), out_shape=j...  7.3 us
    all_to_all x1, waiting for transfers between devices, best_matches(): lax.all_to_all(best.reshape(devs, -1, 128), AXES, split_axis=0, concat_ax...  5.9 us
    all_to_all x1, starting transfers between devices, best_matches(): facts = lax.all_to_all(facts, AXES, split_axis=0, concat_axis=0, tiled=True)  4.14 us
  transfers between devices with their start and end apart: 17, of which 4 were waited for; matrix products, arithmetic and copies ran while one was open for 10% of the time, Pallas kernels for 10%

profile of v2, /device:TPU:0, one launch (start us, length us, event | category | flops | bytes accessed | tf_op | source)
XLA Modules:
  0.0 85.0 jit_solution(5075917793802729654)
XLA Ops:
  0.0 2.2 %shard_map.57 = (bf16[512,1024]{1,0:T(8,128)(2,1)S(1)}, s32[1,512]{1,0:T(1,128)S(1)}, bf16[176,1024]{1,0:T(8,128)(2,1)S(1)}) custom-call(s32[1]{0:T(128)} %bitcast.13.plane_ref.refs_0_, s32[1,512]{1,0:T(1,128)} %bitcast.43, f32[512,1024]{1,0:T(8,128)} %emb_ref.1), custom_call_target="tpu_custom_call" | custom-call | tf_op jit(solution)/shard_map/pallas_call | solution.py:255
  2.2 2.5 %collective-permute-start.18 = (bf16[176,1024]{1,0:T(8,128)(2,1)S(1)}, bf16[176,1024]{1,0:T(8,128)(2,1)S(1)}, u32[]{:S(2)}, u32[]{:S(2)}) collective-permute-start(bf16[176,1024]{1,0:T(8,128)(2,1)S(1)} %get-tuple-element.72.refs_0_.refs_1_), channel_id=1, source_target_pairs={{16,0},{8,1},{24,8},{0,9},{17,16},{9,17},{25,24},{1,25},{18,2},{10... | collective-permute-start | bytes 1081352 | tf_op jit(solution)/shard_map/ppermute | solution.py:279
  4.7 0.6 collective-permute-start.17
  5.3 0.1 collective-permute-start.15
  5.4 1.5 %shard_map.58 = (s32[1,704]{1,0:T(1,128)S(1)}, bf16[176,1024]{1,0:T(8,128)(2,1)S(1)}, bf16[176,1024]{1,0:T(8,128)(2,1)}, bf16[176,1024]{1,0:T(8,128)(2,1)S(1)}) custom-call(s32[1,512]{1,0:T(1,128)S(1)} %bitcast.44, s32[1,512]{1,0:T(1,128)S(1)} %get-tuple-element.69.slot_ref, bf16[512,1024]{1,0:T(8,128)(2,1)S(1)} %get-tuple-element.70.unit_ref), custom_call_target="tpu_custom_call" | custom-call | tf_op jit(solution)/shard_map/pallas_call | solution.py:266
  6.9 0.7 copy-done.9
  7.6 2.0 %collective-permute-start.16 = (bf16[176,1024]{1,0:T(8,128)(2,1)S(1)}, bf16[176,1024]{1,0:T(8,128)(2,1)S(1)}, u32[]{:S(2)}, u32[]{:S(2)}) collective-permute-start(bf16[176,1024]{1,0:T(8,128)(2,1)S(1)} %get-tuple-element.74), channel_id=1, source_target_pairs={{2,0},{3,1},{10,8},{11,9},{18,16},{19,17},{26,24},{27,25},{0,2},{1... | collective-permute-start | bytes 1081352 | tf_op jit(solution)/shard_map/ppermute | solution.py:276
  9.6 2.6 %collective-permute-start.22 = (bf16[176,1024]{1,0:T(8,128)(2,1)}, bf16[176,1024]{1,0:T(8,128)(2,1)S(1)}, u32[]{:S(2)}, u32[]{:S(2)}) collective-permute-start(bf16[176,1024]{1,0:T(8,128)(2,1)} %get-tuple-element.78), channel_id=1, source_target_pairs={{4,0},{5,1},{12,8},{13,9},{20,16},{21,17},{28,24},{29,25},{6,2},{7... | collective-permute-start | bytes 1081352 | tf_op jit(solution)/shard_map/ppermute | solution.py:276
  12.2 0.1 convert_reduce_fusion.4
  12.3 0.1 convert_reduce_fusion.5
  12.4 0.7 reduce_max.46
  13.9 0.1 pad_add_fusion.1
  13.9 0.1 pad.7.clone
  14.0 0.1 pad.6.clone
  14.1 0.1 select_reduce_fusion.5
  14.2 0.1 fusion.7
  14.3 11.8 %collective-permute-done.16.refs_1_.refs_2_ = bf16[176,1024]{1,0:T(8,128)(2,1)S(1)} collective-permute-done((bf16[176,1024]{1,0:T(8,128)(2,1)S(1)}, bf16[176,1024]{1,0:T(8,128)(2,1)S(1)}, u32[]{:S(2)}, u32[]{:S(2)}) %collective-permute-start.16) | collective-permute-done | bytes 360480 | tf_op jit(solution)/shard_map/ppermute | solution.py:276
  26.1 0.0 collective-permute-done.18.refs_9_.refs_13_
  26.1 0.0 collective-permute-done.17.refs_6_.refs_9_
  26.1 0.0 collective-permute-done.15.refs_3_.refs_5_
  26.1 0.1 collective-permute-start.21
  26.1 2.0 %collective-permute-start.20 = (bf16[176,1024]{1,0:T(8,128)(2,1)S(1)}, bf16[176,1024]{1,0:T(8,128)(2,1)S(1)}, u32[]{:S(2)}, u32[]{:S(2)}) collective-permute-start(bf16[176,1024]{1,0:T(8,128)(2,1)S(1)} %collective-permute-done.16.refs_1_.refs_2_), channel_id=1, source_target_pairs={{1,0},{17,1},{9,8},{25,9},{0,16},{16,17},{8,24},{24,25},{3,2},{19,... | collective-permute-start | bytes 1081352 | tf_op jit(solution)/shard_map/ppermute | solution.py:279
  28.2 0.1 broadcast_in_dim.172
  28.2 0.0 collective-permute-start.19
  28.3 0.1 select_reduce_fusion.4
  28.4 0.7 all_to_all.23
  29.1 4.1 %all-to-all-start.2 = ((s32[32,1,256]{2,1,0:T(1,128)}), s32[32,1,256]{2,1,0:T(1,128)S(1)}, u32[]{:S(2)}, u32[]{:S(2)}) async-start(s32[32,1,256]{2,1,0:T(1,128)} %all_to_all.23), calls=%async_computation.2 | async-start | bytes 65536 | tf_op jit(solution)/shard_map/all_to_all | solution.py:315
  33.2 3.7 %collective-permute-start.23 = (bf16[176,1024]{1,0:T(8,128)(2,1)}, bf16[176,1024]{1,0:T(8,128)(2,1)}, u32[]{:S(2)}, u32[]{:S(2)}) collective-permute-start(bf16[176,1024]{1,0:T(8,128)(2,1)} %copy-done.9), channel_id=1, source_target_pairs={{6,0},{7,1},{14,8},{15,9},{22,16},{23,17},{30,24},{31,25},{4,2},{5... | collective-permute-start | bytes 1081352 | tf_op jit(solution)/shard_map/ppermute | solution.py:276
  36.9 3.6 %all-to-all-done.2 = s32[32,1,256]{2,1,0:T(1,128)S(1)} async-done(((s32[32,1,256]{2,1,0:T(1,128)}), s32[32,1,256]{2,1,0:T(1,128)S(1)}, u32[]{:S(2)}, u32[]{:S(2)}) %all-to-all-start.2) | async-done | bytes 32800 | tf_op jit(solution)/shard_map/all_to_all | solution.py:315
  40.5 0.6 collective-permute-start.28
  41.1 1.5 %collective-permute-start.26 = (bf16[176,1024]{1,0:T(8,128)(2,1)S(1)}, bf16[176,1024]{1,0:T(8,128)(2,1)}, u32[]{:S(2)}, u32[]{:S(2)}) collective-permute-start(bf16[176,1024]{1,0:T(8,128)(2,1)S(1)} %collective-permute-done.22.refs_2_.refs_3_), channel_id=1, source_target_pairs={{1,0},{17,1},{9,8},{25,9},{0,16},{16,17},{8,24},{24,25},{3,2},{19,... | collective-permute-start | bytes 1081352 | tf_op jit(solution)/shard_map/ppermute | solution.py:279
  42.6 0.0 collective-permute-done.21.refs_10_.refs_14_
  42.6 0.0 collective-permute-done.20.refs_7_.refs_10_
  42.7 0.1 broadcast_in_dim.181
  42.8 0.1 select_reduce_fusion.3
  42.9 0.1 reshape.173
  43.0 0.1 mul.54
  43.1 0.1 multiply_reduce_fusion.1
  43.2 0.1 collective-permute-start.24
  43.3 0.1 fusion.4
  43.4 0.1 convert_reduce_fusion.3
  43.5 0.1 slice.62.refs_19_
  43.6 0.2 copy.85
  43.9 0.9 %copy.86 = s32[4,704]{0,1:T(8,128)} copy(s32[4,704]{1,0:T(4,128)S(1)} %convert_reduce_fusion.3) | data formatting | bytes 22528 | tf_op jit(solution)/shard_map/reduce_sum | solution.py:329
  44.8 1.0 %broadcast_select_fusion.1 = s32[4,704]{0,1:T(8,128)S(1)} fusion(pred[4,704]{0,1:T(8,128)(4,1)S(1)} %copy.85, s32[4,704]{0,1:T(8,128)} %copy.86), kind=kLoop, calls=%fused_computation.31 | loop fusion | flops 2816 | bytes 25344 | tf_op jit(solution)/shard_map/jit(_where)/select_n | solution.py:330
  45.8 0.6 slice.65
  46.4 0.8 slice.64
  47.2 0.0 collective-permute-done.23.refs_4_
  47.2 0.7 collective-permute-start.29
  47.9 1.4 %collective-permute-start.27 = (bf16[176,1024]{1,0:T(8,128)(2,1)}, bf16[176,1024]{1,0:T(8,128)(2,1)}, u32[]{:S(2)}, u32[]{:S(2)}) collective-permute-start(bf16[176,1024]{1,0:T(8,128)(2,1)} %collective-permute-done.23.refs_4_), channel_id=1, source_target_pairs={{1,0},{17,1},{9,8},{25,9},{0,16},{16,17},{8,24},{24,25},{3,2},{19,... | collective-permute-start | bytes 1081352 | tf_op jit(solution)/shard_map/ppermute | solution.py:279
  49.3 1.1 %copy.87.refs_12_.refs_20_ = s32[4,528]{1,0:T(4,128)S(1)} copy(s32[4,528]{0,1:T(8,128)} %slice.64) | data formatting | bytes 16896 | tf_op jit(solution)/shard_map/optimization_barrier | solution.py:335
  50.4 1.0 %copy.89.refs_21_ = s32[4,176]{1,0:T(4,128)S(1)} copy(s32[4,176]{0,1:T(8,128)} %slice.65) | data formatting | bytes 5632 | tf_op jit(solution)/shard_map/optimization_barrier | solution.py:335
  51.4 0.0 collective-permute-done.28.refs_11_.refs_15_
  51.4 1.0 %collective-permute-done.26.refs_8_.refs_11_ = bf16[176,1024]{1,0:T(8,128)(2,1)} collective-permute-done((bf16[176,1024]{1,0:T(8,128)(2,1)S(1)}, bf16[176,1024]{1,0:T(8,128)(2,1)}, u32[]{:S(2)}, u32[]{:S(2)}) %collective-permute-start.26) | collective-permute-done | bytes 360480 | tf_op jit(solution)/shard_map/ppermute | solution.py:279
  52.4 1.0 %copy-done.4 = bf16[176,1024]{1,0:T(8,128)(2,1)S(1)} copy-done((bf16[176,1024]{1,0:T(8,128)(2,1)S(1)}, bf16[176,1024]{1,0:T(8,128)(2,1)}, u32[]{:S(2)}) %copy-start.4) | copy-done | bytes 360472
  53.4 7.3 %shard_map.59.refs_17_ = f32[4,528]{1,0:T(4,128)S(1)} custom-call(bf16[176,1024]{1,0:T(8,128)(2,1)S(1)} %get-tuple-element.72.refs_0_.refs_1_, bf16[176,1024]{1,0:T(8,128)(2,1)S(1)} %collective-permute-done.16.refs_1_.refs_2_, bf16[176,1024]{1,0:T(8,128)(2,1)S(1)} %collective-permute-done.22.refs_2_.refs_3_, ...), custom_call_target="tpu_custom_call" | custom-call | flops 2854748160 | bytes 4325376 | tf_op jit(solution)/shard_map/pallas_call | solution.py:349
  60.7 0.0 copy-start.15
  60.8 7.8 %shard_map.60 = f32[4,8,4,128]{3,2,1,0:T(4,128)} custom-call(s32[1]{0:T(128)} %bitcast.13.plane_ref.refs_0_, bf16[176,1024]{1,0:T(8,128)(2,1)S(1)} %get-tuple-element.72.refs_0_.refs_1_, bf16[176,1024]{1,0:T(8,128)(2,1)S(1)} %collective-permute-done.16.refs_1_.refs_2_, bf16[176,1024]{1,0:T(8,128)(2,1)S(1)} %collective-permute-done.22.refs_2_.refs_3_, ...), custom_call_target="tpu_custom_call" | custom-call | tf_op jit(solution)/shard_map/pallas_call | solution.py:360
  68.6 8.2 %all-to-all-start.3 = ((f32[32,4,128]{2,1,0:T(4,128)}), f32[32,4,128]{2,1,0:T(4,128)S(1)}, u32[]{:S(2)}, u32[]{:S(2)}) async-start(f32[32,4,128]{2,1,0:T(4,128)} %bitcast.19), calls=%async_computation.3 | async-start | bytes 131072 | tf_op jit(solution)/shard_map/all_to_all | solution.py:378
  76.8 0.7 slice_reduce_fusion
  78.2 5.9 %all-to-all-done.3 = f32[32,4,128]{2,1,0:T(4,128)S(1)} async-done(((f32[32,4,128]{2,1,0:T(4,128)}), f32[32,4,128]{2,1,0:T(4,128)S(1)}, u32[]{:S(2)}, u32[]{:S(2)}) %all-to-all-start.3) | async-done | bytes 65568 | tf_op jit(solution)/shard_map/all_to_all | solution.py:378
  84.1 0.3 conditional.1
  84.4 0.0 copy-start.16
  84.4 0.6 copy-done.16
  (41 shorter events, 0.2 us)
Async XLA Ops:
  0.0 14.1 %copy-start.14 = (s32[4,8]{1,0:T(4,128)S(1)}, s32[4,8]{1,0:T(4,128)}, u32[]{:S(2)}) copy-start(s32[4,8]{1,0:T(4,128)} %constant.109.clone) | copy-start | bytes 388
  0.0 5.4 %copy-start.12 = (s32[512]{0:T(512)S(1)}, s32[512]{0:T(512)}, u32[]{:S(2)}) copy-start(s32[512]{0:T(512)} %param.8) | copy-start | bytes 6148
  0.0 12.2 %copy-start.13 = (s32[1,512]{1,0:T(1,128)S(1)}, s32[1,512]{1,0:T(1,128)}, u32[]{:S(2)}) copy-start(s32[1,512]{1,0:T(1,128)} %param.9) | copy-start | bytes 6148
  2.2 23.8 %collective-permute-start.18 = (bf16[176,1024]{1,0:T(8,128)(2,1)S(1)}, bf16[176,1024]{1,0:T(8,128)(2,1)S(1)}, u32[]{:S(2)}, u32[]{:S(2)}) collective-permute-start(bf16[176,1024]{1,0:T(8,128)(2,1)S(1)} %get-tuple-element.72.refs_0_.refs_1_), channel_id=1, source_target_pairs={{16,0},{8,1},{24,8},{0,9},{17,16},{9,17},{25,24},{1,25},{18,2},{10... | collective-permute-start | bytes 1081352 | tf_op jit(solution)/shard_map/ppermute | solution.py:279
  4.7 21.4 %collective-permute-start.17 = (bf16[176,1024]{1,0:T(8,128)(2,1)S(1)}, bf16[176,1024]{1,0:T(8,128)(2,1)S(1)}, u32[]{:S(2)}, u32[]{:S(2)}) collective-permute-start(bf16[176,1024]{1,0:T(8,128)(2,1)S(1)} %get-tuple-element.72.refs_0_.refs_1_), channel_id=1, source_target_pairs={{1,0},{17,1},{9,8},{25,9},{0,16},{16,17},{8,24},{24,25},{3,2},{19,... | collective-permute-start | bytes 1081352 | tf_op jit(solution)/shard_map/ppermute | solution.py:279
  5.3 20.8 %collective-permute-start.15 = (bf16[176,1024]{1,0:T(8,128)(2,1)S(1)}, bf16[176,1024]{1,0:T(8,128)(2,1)S(1)}, u32[]{:S(2)}, u32[]{:S(2)}) collective-permute-start(bf16[176,1024]{1,0:T(8,128)(2,1)S(1)} %get-tuple-element.72.refs_0_.refs_1_), channel_id=1, source_target_pairs={{8,0},{9,1},{0,8},{1,9},{24,16},{25,17},{16,24},{17,25},{10,2},{11... | collective-permute-start | bytes 1081352 | tf_op jit(solution)/shard_map/ppermute | solution.py:279
  6.9 0.7 copy-start.9
  7.6 18.4 %collective-permute-start.16 = (bf16[176,1024]{1,0:T(8,128)(2,1)S(1)}, bf16[176,1024]{1,0:T(8,128)(2,1)S(1)}, u32[]{:S(2)}, u32[]{:S(2)}) collective-permute-start(bf16[176,1024]{1,0:T(8,128)(2,1)S(1)} %get-tuple-element.74), channel_id=1, source_target_pairs={{2,0},{3,1},{10,8},{11,9},{18,16},{19,17},{26,24},{27,25},{0,2},{1... | collective-permute-start | bytes 1081352 | tf_op jit(solution)/shard_map/ppermute | solution.py:276
  9.6 30.9 %collective-permute-start.22 = (bf16[176,1024]{1,0:T(8,128)(2,1)}, bf16[176,1024]{1,0:T(8,128)(2,1)S(1)}, u32[]{:S(2)}, u32[]{:S(2)}) collective-permute-start(bf16[176,1024]{1,0:T(8,128)(2,1)} %get-tuple-element.78), channel_id=1, source_target_pairs={{4,0},{5,1},{12,8},{13,9},{20,16},{21,17},{28,24},{29,25},{6,2},{7... | collective-permute-start | bytes 1081352 | tf_op jit(solution)/shard_map/ppermute | solution.py:276
  26.1 16.5 %collective-permute-start.21 = (bf16[176,1024]{1,0:T(8,128)(2,1)S(1)}, bf16[176,1024]{1,0:T(8,128)(2,1)S(1)}, u32[]{:S(2)}, u32[]{:S(2)}) collective-permute-start(bf16[176,1024]{1,0:T(8,128)(2,1)S(1)} %collective-permute-done.16.refs_1_.refs_2_), channel_id=1, source_target_pairs={{16,0},{8,1},{24,8},{0,9},{17,16},{9,17},{25,24},{1,25},{18,2},{10... | collective-permute-start | bytes 1081352 | tf_op jit(solution)/shard_map/ppermute | solution.py:279
  26.1 16.5 %collective-permute-start.20 = (bf16[176,1024]{1,0:T(8,128)(2,1)S(1)}, bf16[176,1024]{1,0:T(8,128)(2,1)S(1)}, u32[]{:S(2)}, u32[]{:S(2)}) collective-permute-start(bf16[176,1024]{1,0:T(8,128)(2,1)S(1)} %collective-permute-done.16.refs_1_.refs_2_), channel_id=1, source_target_pairs={{1,0},{17,1},{9,8},{25,9},{0,16},{16,17},{8,24},{24,25},{3,2},{19,... | collective-permute-start | bytes 1081352 | tf_op jit(solution)/shard_map/ppermute | solution.py:279
  28.2 12.2 %collective-permute-start.19 = (bf16[176,1024]{1,0:T(8,128)(2,1)S(1)}, bf16[176,1024]{1,0:T(8,128)(2,1)S(1)}, u32[]{:S(2)}, u32[]{:S(2)}) collective-permute-start(bf16[176,1024]{1,0:T(8,128)(2,1)S(1)} %collective-permute-done.16.refs_1_.refs_2_), channel_id=1, source_target_pairs={{8,0},{9,1},{0,8},{1,9},{24,16},{25,17},{16,24},{17,25},{10,2},{11... | collective-permute-start | bytes 1081352 | tf_op jit(solution)/shard_map/ppermute | solution.py:279
  29.1 11.4 %all-to-all-start.2 = ((s32[32,1,256]{2,1,0:T(1,128)}), s32[32,1,256]{2,1,0:T(1,128)S(1)}, u32[]{:S(2)}, u32[]{:S(2)}) async-start(s32[32,1,256]{2,1,0:T(1,128)} %all_to_all.23), calls=%async_computation.2 | async-start | bytes 65536 | tf_op jit(solution)/shard_map/all_to_all | solution.py:315
  33.2 14.0 %collective-permute-start.23 = (bf16[176,1024]{1,0:T(8,128)(2,1)}, bf16[176,1024]{1,0:T(8,128)(2,1)}, u32[]{:S(2)}, u32[]{:S(2)}) collective-permute-start(bf16[176,1024]{1,0:T(8,128)(2,1)} %copy-done.9), channel_id=1, source_target_pairs={{6,0},{7,1},{14,8},{15,9},{22,16},{23,17},{30,24},{31,25},{4,2},{5... | collective-permute-start | bytes 1081352 | tf_op jit(solution)/shard_map/ppermute | solution.py:276
  40.5 2.9 %copy-start.10 = (s32[32,1,256]{2,0,1:T(8,128)}, s32[32,1,256]{2,0,1:T(8,128)S(1)}, u32[]{:S(2)}) copy-start(s32[32,1,256]{2,0,1:T(8,128)S(1)} %copy.98) | copy-start | bytes 98308
  40.5 3.4 %copy-start.3 = (bf16[176,1024]{1,0:T(8,128)(2,1)}, bf16[176,1024]{1,0:T(8,128)(2,1)S(1)}, u32[]{:S(2)}) copy-start(bf16[176,1024]{1,0:T(8,128)(2,1)S(1)} %collective-permute-done.19.refs_4_.refs_6_) | copy-start | bytes 1081348
  40.5 10.9 %collective-permute-start.28 = (bf16[176,1024]{1,0:T(8,128)(2,1)S(1)}, bf16[176,1024]{1,0:T(8,128)(2,1)}, u32[]{:S(2)}, u32[]{:S(2)}) collective-permute-start(bf16[176,1024]{1,0:T(8,128)(2,1)S(1)} %collective-permute-done.22.refs_2_.refs_3_), channel_id=1, source_target_pairs={{16,0},{8,1},{24,8},{0,9},{17,16},{9,17},{25,24},{1,25},{18,2},{10... | collective-permute-start | bytes 1081352 | tf_op jit(solution)/shard_map/ppermute | solution.py:279
  41.1 11.3 %collective-permute-start.26 = (bf16[176,1024]{1,0:T(8,128)(2,1)S(1)}, bf16[176,1024]{1,0:T(8,128)(2,1)}, u32[]{:S(2)}, u32[]{:S(2)}) collective-permute-start(bf16[176,1024]{1,0:T(8,128)(2,1)S(1)} %collective-permute-done.22.refs_2_.refs_3_), channel_id=1, source_target_pairs={{1,0},{17,1},{9,8},{25,9},{0,16},{16,17},{8,24},{24,25},{3,2},{19,... | collective-permute-start | bytes 1081352 | tf_op jit(solution)/shard_map/ppermute | solution.py:279
  43.2 4.0 %collective-permute-start.24 = (bf16[176,1024]{1,0:T(8,128)(2,1)S(1)}, bf16[176,1024]{1,0:T(8,128)(2,1)}, u32[]{:S(2)}, u32[]{:S(2)}) collective-permute-start(bf16[176,1024]{1,0:T(8,128)(2,1)S(1)} %collective-permute-done.22.refs_2_.refs_3_), channel_id=1, source_target_pairs={{8,0},{9,1},{0,8},{1,9},{24,16},{25,17},{16,24},{17,25},{10,2},{11... | collective-permute-start | bytes 1081352 | tf_op jit(solution)/shard_map/ppermute | solution.py:279
  47.2 13.5 %collective-permute-start.29 = (bf16[176,1024]{1,0:T(8,128)(2,1)}, bf16[176,1024]{1,0:T(8,128)(2,1)}, u32[]{:S(2)}, u32[]{:S(2)}) collective-permute-start(bf16[176,1024]{1,0:T(8,128)(2,1)} %collective-permute-done.23.refs_4_), channel_id=1, source_target_pairs={{16,0},{8,1},{24,8},{0,9},{17,16},{9,17},{25,24},{1,25},{18,2},{10... | collective-permute-start | bytes 1081352 | tf_op jit(solution)/shard_map/ppermute | solution.py:279
  47.9 12.8 %collective-permute-start.27 = (bf16[176,1024]{1,0:T(8,128)(2,1)}, bf16[176,1024]{1,0:T(8,128)(2,1)}, u32[]{:S(2)}, u32[]{:S(2)}) collective-permute-start(bf16[176,1024]{1,0:T(8,128)(2,1)} %collective-permute-done.23.refs_4_), channel_id=1, source_target_pairs={{1,0},{17,1},{9,8},{25,9},{0,16},{16,17},{8,24},{24,25},{3,2},{19,... | collective-permute-start | bytes 1081352 | tf_op jit(solution)/shard_map/ppermute | solution.py:279
  49.3 11.4 %collective-permute-start.25 = (bf16[176,1024]{1,0:T(8,128)(2,1)}, bf16[176,1024]{1,0:T(8,128)(2,1)}, u32[]{:S(2)}, u32[]{:S(2)}) collective-permute-start(bf16[176,1024]{1,0:T(8,128)(2,1)} %collective-permute-done.23.refs_4_), channel_id=1, source_target_pairs={{8,0},{9,1},{0,8},{1,9},{24,16},{25,17},{16,24},{17,25},{10,2},{11... | collective-permute-start | bytes 1081352 | tf_op jit(solution)/shard_map/ppermute | solution.py:279
  52.4 1.0 %copy-start.4 = (bf16[176,1024]{1,0:T(8,128)(2,1)S(1)}, bf16[176,1024]{1,0:T(8,128)(2,1)}, u32[]{:S(2)}) copy-start(bf16[176,1024]{1,0:T(8,128)(2,1)} %copy-done.3) | copy-start | bytes 1081348
  53.4 7.4 %copy-start.5 = (bf16[176,1024]{1,0:T(8,128)(2,1)S(1)}, bf16[176,1024]{1,0:T(8,128)(2,1)}, u32[]{:S(2)}) copy-start(bf16[176,1024]{1,0:T(8,128)(2,1)} %copy-done.3) | copy-start | bytes 1081348
  60.7 16.1 %copy-start.11 = (s32[32,1,256]{2,0,1:T(8,128)S(1)}, s32[32,1,256]{2,0,1:T(8,128)}, u32[]{:S(2)}) copy-start(s32[32,1,256]{2,0,1:T(8,128)} %copy-done.10) | copy-start | bytes 98308
  60.7 17.5 %copy-start.15 = (s32[4,8]{1,0:T(4,128)S(1)}, s32[4,8]{1,0:T(4,128)}, u32[]{:S(2)}) copy-start(s32[4,8]{1,0:T(4,128)} %constant.109.clone) | copy-start | bytes 388
  68.6 15.5 %all-to-all-start.3 = ((f32[32,4,128]{2,1,0:T(4,128)}), f32[32,4,128]{2,1,0:T(4,128)S(1)}, u32[]{:S(2)}, u32[]{:S(2)}) async-start(f32[32,4,128]{2,1,0:T(4,128)} %bitcast.19), calls=%async_computation.3 | async-start | bytes 131072 | tf_op jit(solution)/shard_map/all_to_all | solution.py:378
  84.4 0.6 copy-start.16

commit v3 on v2

--- a/solution.py
+++ b/solution.py
@@ -248,7 +248,7 @@
         return (i // wide) * n_col + h * wide + i % wide
 
     planes = [(i, h) for h in range(groups) for i in range(n_row * wide)]
-    numbers, others = (0,), tuple(range(1, groups))
+    numbers, others = tuple(range(min(3, groups))), tuple(range(3, groups))
     chunk_shape = jax.ShapeDtypeStruct((cap, width), jnp.bfloat16)
     dest_row = dest_pos.reshape(1, rows_dev)
     plane_ref = plane.astype(jnp.int32).reshape(1)
@@ -282,14 +282,9 @@
         return lax.optimization_barrier((values, done))[0]
 
     own = [parts[0]] + [across(parts[k], k) for k in range(1, min(3, groups))]
-    rounds = [[inside(own[0], j) for j in range(1, count)]]
-    place = after(place, rounds[0][0])
-    rest = after([parts[k] for k in range(3, groups)], own[1])
-    own += [across(part, k) for k, part in zip(range(3, groups), rest)]
-    for k in range(1, groups - 1):
-        near, *far = rounds[-1]
-        part = after(own[k], near, *([] if k > 1 else far))
-        rounds.append([inside(after(part, *far), 1), *[inside(part, j) for j in range(2, count)]])
+    near = inside(own[0], 1)
+    rounds = [[near] + [inside(after(own[0], near), j) for j in range(2, count)]]
+    place, rest = after((place, [parts[k] for k in range(3, groups)]), near)
 
     planes_i = jnp.arange(groups, dtype=jnp.int32)
     swap = (planes_i[:, None] ^ planes_i[None, :]) == plane
@@ -313,7 +308,13 @@
     )
     facts = jnp.broadcast_to(facts[None, :, None, :], (n_row, groups, wide, length)).reshape(devs, length)
     facts = lax.all_to_all(facts, AXES, split_axis=0, concat_axis=0, tiled=True)
-    facts = after(facts, *rounds[1])
+    rest = after(rest, near)
+    own += [across(part, k) for k, part in zip(range(3, groups), rest)]
+    for k in range(1, groups - 1):
+        part = after(own[k], facts, *rounds[0]) if k == 1 else after(own[k], rounds[-1][0], *rounds[-2])
+        near = after(part, own[k + 1]) if k > 1 else part
+        rounds.append([inside(near, 1), *[inside(part, j) for j in range(2, count)]])
+
     over = jnp.max(facts[:, cap + LEVELS]) > 0
     facts = facts.reshape(n_row, groups, wide, length)
 
@@ -332,11 +333,11 @@
     early = slots - cap
     label_cols = labels.T
     facts = places[:, :early], places[:, early:], labels[:, :early], labels[:, early:], label_cols[:early], label_cols
-    facts, last = lax.optimization_barrier((facts, after(own[-1], *rounds[-1][:1], *rounds[-2])))
-    rounds.append([inside(last, j) for j in range(1, count)])
+    facts, last = lax.optimization_barrier((facts, after(own[-1], *rounds[-2])))
+    rounds.append([inside(after(last, rounds[-1][0]), 1), *[inside(last, j) for j in range(2, count)]])
     place, last_place, label, last_label, label_col, label_cols = facts
     blocks = [own] + [[moved[j - 1] for moved in rounds] for j in range(1, count)]
-    any_space = pl.BlockSpec(memory_space=pl.ANY)
+    any_space = pl.BlockSpec(memory_space=pltpu.HBM)
     area = 4 * slots * slots
 
     def scratch(number):

time: 85.4 us -> 84.9 us (level)
  waiting for transfers between devices: 22.3 us -> 31.3 us
  starting transfers between devices: 30.1 us -> 25.4 us
  local copies, waits for them, and re-layouts: 8.26 us -> 5.47 us
  Pallas kernels: 18.8 us -> 17.8 us
  other arithmetic: 3.6 us -> 2.69 us
    ppermute x3, waiting for transfers between devices: 11.8 us -> 0.01 us  [across(): lax.ppermute(part, AXES, [(device(i, h ^ k), device(i, h)) for i, h in pl...]
    ppermute x12, waiting for transfers between devices: 1.02 us -> 12 us  [inside(): lax.ppermute(part, AXES, [(device(int(held[j, i]), h), device(i, h)) for...]
    all_to_all x1, waiting for transfers between devices: 3.58 us -> 13.4 us  [best_matches(): facts = lax.all_to_all(facts, AXES, split_axis=0, concat_axis=0, tiled=True)]
    all_to_all x1, starting transfers between devices: 8.23 us -> 4.84 us  [best_matches(): lax.all_to_all(best.reshape(devs, -1, 128), AXES, split_axis=0, concat_ax...]
    optimization_barrier x2, local copies, waits for them, and re-layouts: 2.07 us -> 0.23 us  [best_matches(): facts, last = lax.optimization_barrier((facts, after(own[-1], *rounds[-2])))]
    ppermute x12, starting transfers between devices: 9.49 us -> 8.24 us  [inside(): lax.ppermute(part, AXES, [(device(int(held[j, i]), h), device(i, h)) for...]
    all_to_all x1, starting transfers between devices: 4.14 us -> 2.92 us  [best_matches(): facts = lax.all_to_all(facts, AXES, split_axis=0, concat_axis=0, tiled=True)]
    unnamed x23 -> x19, local copies, waits for them, and re-layouts: 2.33 us -> 3.48 us
  transfers between devices with their start and end apart: 17 -> 17, of which waited for: 4 -> 6; matrix products, arithmetic and copies ran while one was open for 10% -> 5% of each run, Pallas kernels for 10% -> 9%
where the time goes in v3:
time: 84.9 us; the launch traced here: 84.6 us
  waiting for transfers between devices  31.3 us (37%)
  starting transfers between devices  25.4 us (30%)
  Pallas kernels  17.8 us (21%)
  local copies, waits for them, and re-layouts  5.47 us (6%)
  other arithmetic  2.69 us (3%)
  between operations  1.7 us (2%)
    all_to_all x1, waiting for transfers between devices, best_matches(): facts = lax.all_to_all(facts, AXES, split_axis=0, concat_axis=0, tiled=True)  13.4 us
    ppermute x12, waiting for transfers between devices, inside(): lax.ppermute(part, AXES, [(device(int(held[j, i]), h), device(i, h)) for...  12 us
    ppermute x3, starting transfers between devices, across(): lax.ppermute(part, AXES, [(device(i, h ^ k), device(i, h)) for i, h in pl...  9.36 us
    ppermute x12, starting transfers between devices, inside(): lax.ppermute(part, AXES, [(device(int(held[j, i]), h), device(i, h)) for...  8.24 us
    pallas_call x1, Pallas kernels, best_matches(): pl.pallas_call(functools.partial(late_kernel, pairs, count, group_size),...  7.65 us
    pallas_call x1, Pallas kernels, best_matches(): pl.pallas_call(functools.partial(early_kernel, pairs, count), out_shape=j...  7.01 us
    all_to_all x1, waiting for transfers between devices, best_matches(): lax.all_to_all(best.reshape(devs, -1, 128), AXES, split_axis=0, concat_ax...  5.91 us
    all_to_all x1, starting transfers between devices, best_matches(): lax.all_to_all(best.reshape(devs, -1, 128), AXES, split_axis=0, concat_ax...  4.84 us
  transfers between devices with their start and end apart: 17, of which 6 were waited for; matrix products, arithmetic and copies ran while one was open for 5% of the time, Pallas kernels for 9%

profile of v3, /device:TPU:0, one launch (start us, length us, event | category | flops | bytes accessed | tf_op | source)
XLA Modules:
  0.0 84.6 jit_solution(14744208763394153029)
XLA Ops:
  0.0 2.6 %shard_map.57 = (bf16[512,1024]{1,0:T(8,128)(2,1)S(1)}, s32[1,512]{1,0:T(1,128)S(1)}, bf16[176,1024]{1,0:T(8,128)(2,1)S(1)}, bf16[176,1024]{1,0:T(8,128)(2,1)S(1)}, bf16[176,1024]{1,0:T(8,128)(2,1)S(1)}) custom-call(s32[1]{0:T(128)} %bitcast.13.plane_ref.refs_0_, s32[1,512]{1,0:T(1,128)} %bitcast.38, f32[512,1024]{1,0:T(8,128)} %emb_ref.1), custom_call_target="tpu_custom_call" | custom-call | tf_op jit(solution)/shard_map/pallas_call | solution.py:255
  2.6 3.1 %collective-permute-start.16 = (bf16[176,1024]{1,0:T(8,128)(2,1)S(1)}, bf16[176,1024]{1,0:T(8,128)(2,1)S(1)}, u32[]{:S(2)}, u32[]{:S(2)}) collective-permute-start(bf16[176,1024]{1,0:T(8,128)(2,1)S(1)} %get-tuple-element.77), channel_id=1, source_target_pairs={{2,0},{3,1},{10,8},{11,9},{18,16},{19,17},{26,24},{27,25},{0,2},{1... | collective-permute-start | bytes 1081352 | tf_op jit(solution)/shard_map/ppermute | solution.py:276
  5.7 2.6 %collective-permute-start.17 = (bf16[176,1024]{1,0:T(8,128)(2,1)S(1)}, bf16[176,1024]{1,0:T(8,128)(2,1)S(1)}, u32[]{:S(2)}, u32[]{:S(2)}) collective-permute-start(bf16[176,1024]{1,0:T(8,128)(2,1)S(1)} %get-tuple-element.78), channel_id=1, source_target_pairs={{4,0},{5,1},{12,8},{13,9},{20,16},{21,17},{28,24},{29,25},{6,2},{7... | collective-permute-start | bytes 1081352 | tf_op jit(solution)/shard_map/ppermute | solution.py:276
  8.4 0.1 convert_reduce_fusion.4
  8.5 0.1 convert_reduce_fusion.5
  8.6 0.7 reduce_max.46
  10.0 0.1 pad_add_fusion.1
  10.1 0.1 pad.7.clone
  10.2 0.1 pad.6.clone
  10.3 0.5 shard_map.58
  10.8 0.1 select_reduce_fusion.5
  10.9 0.1 fusion.7
  11.0 0.5 copy-done.9
  11.5 1.6 %collective-permute-start.20 = (bf16[176,1024]{1,0:T(8,128)(2,1)S(1)}, bf16[176,1024]{1,0:T(8,128)(2,1)S(1)}, u32[]{:S(2)}, u32[]{:S(2)}) collective-permute-start(bf16[176,1024]{1,0:T(8,128)(2,1)S(1)} %get-tuple-element.81.refs_0_.refs_1_), channel_id=1, source_target_pairs={{16,0},{8,1},{24,8},{0,9},{17,16},{9,17},{25,24},{1,25},{18,2},{10... | collective-permute-start | bytes 1081352 | tf_op jit(solution)/shard_map/ppermute | solution.py:279
  13.2 0.4 collective-permute-start.19
  13.6 0.1 broadcast_in_dim.172
  13.7 0.1 select_reduce_fusion.4
  13.8 0.7 all_to_all.21
  14.4 2.9 %all-to-all-start.2 = ((s32[32,1,256]{2,1,0:T(1,128)}), s32[32,1,256]{2,1,0:T(1,128)S(1)}, u32[]{:S(2)}, u32[]{:S(2)}) async-start(s32[32,1,256]{2,1,0:T(1,128)} %all_to_all.21), calls=%async_computation.2 | async-start | bytes 65536 | tf_op jit(solution)/shard_map/all_to_all | solution.py:310
  17.4 3.7 %collective-permute-start.18 = (bf16[176,1024]{1,0:T(8,128)(2,1)}, bf16[176,1024]{1,0:T(8,128)(2,1)S(1)}, u32[]{:S(2)}, u32[]{:S(2)}) collective-permute-start(bf16[176,1024]{1,0:T(8,128)(2,1)} %copy-done.9), channel_id=1, source_target_pairs={{6,0},{7,1},{14,8},{15,9},{22,16},{23,17},{30,24},{31,25},{4,2},{5... | collective-permute-start | bytes 1081352 | tf_op jit(solution)/shard_map/ppermute | solution.py:276
  21.1 13.4 %all-to-all-done.2 = s32[32,1,256]{2,1,0:T(1,128)S(1)} async-done(((s32[32,1,256]{2,1,0:T(1,128)}), s32[32,1,256]{2,1,0:T(1,128)S(1)}, u32[]{:S(2)}, u32[]{:S(2)}) %all-to-all-start.2) | async-done | bytes 32800 | tf_op jit(solution)/shard_map/all_to_all | solution.py:310
  34.5 0.1 reduce.4
  34.6 0.1 broadcast_in_dim.181
  34.8 0.6 copy.97
  35.4 0.1 select_reduce_fusion.3
  35.5 0.0 collective-permute-done.16.refs_1_.refs_2_
  35.5 0.0 collective-permute-done.19.refs_6_.refs_9_
  35.5 0.1 collective-permute-start.21
  35.6 0.1 fusion.4
  35.7 0.1 reshape.175
  35.8 0.1 mul.54
  35.9 0.1 multiply_reduce_fusion.1
  36.0 0.7 collective-permute-start.24
  36.8 1.3 %collective-permute-start.23 = (bf16[176,1024]{1,0:T(8,128)(2,1)S(1)}, bf16[176,1024]{1,0:T(8,128)(2,1)}, u32[]{:S(2)}, u32[]{:S(2)}) collective-permute-start(bf16[176,1024]{1,0:T(8,128)(2,1)S(1)} %collective-permute-done.16.refs_1_.refs_2_), channel_id=1, source_target_pairs={{1,0},{17,1},{9,8},{25,9},{0,16},{16,17},{8,24},{24,25},{3,2},{19,... | collective-permute-start | bytes 1081352 | tf_op jit(solution)/shard_map/ppermute | solution.py:279
  38.1 0.8 copy-done.3
  38.9 0.2 collective-permute-start.28
  39.0 1.9 %collective-permute-start.26 = (bf16[176,1024]{1,0:T(8,128)(2,1)S(1)}, bf16[176,1024]{1,0:T(8,128)(2,1)}, u32[]{:S(2)}, u32[]{:S(2)}) collective-permute-start(bf16[176,1024]{1,0:T(8,128)(2,1)S(1)} %collective-permute-done.17.refs_2_.refs_3_), channel_id=1, source_target_pairs={{1,0},{17,1},{9,8},{25,9},{0,16},{16,17},{8,24},{24,25},{3,2},{19,... | collective-permute-start | bytes 1081352 | tf_op jit(solution)/shard_map/ppermute | solution.py:279
  40.9 0.0 collective-permute-done.18.refs_4_
  40.9 0.0 collective-permute-start.22
  40.9 0.1 convert_reduce_fusion.3
  41.0 0.1 slice.63.refs_19_
  41.1 0.2 copy.85
  41.3 0.2 copy.86
  41.6 5.8 %collective-permute-done.24.refs_10_.refs_14_ = bf16[176,1024]{1,0:T(8,128)(2,1)} collective-permute-done((bf16[176,1024]{1,0:T(8,128)(2,1)S(1)}, bf16[176,1024]{1,0:T(8,128)(2,1)}, u32[]{:S(2)}, u32[]{:S(2)}) %collective-permute-start.24) | collective-permute-done | bytes 360480 | tf_op jit(solution)/shard_map/ppermute | solution.py:279
  47.4 0.7 collective-permute-done.23.refs_7_.refs_10_
  48.1 0.0 collective-permute-start.29
  48.1 2.0 %collective-permute-start.27 = (bf16[176,1024]{1,0:T(8,128)(2,1)S(1)}, bf16[176,1024]{1,0:T(8,128)(2,1)}, u32[]{:S(2)}, u32[]{:S(2)}) collective-permute-start(bf16[176,1024]{1,0:T(8,128)(2,1)S(1)} %collective-permute-done.18.refs_4_), channel_id=1, source_target_pairs={{1,0},{17,1},{9,8},{25,9},{0,16},{16,17},{8,24},{24,25},{3,2},{19,... | collective-permute-start | bytes 1081352 | tf_op jit(solution)/shard_map/ppermute | solution.py:279
  50.2 0.0 collective-permute-done.22.refs_5_.refs_7_
  50.2 0.0 collective-permute-start.25
  50.2 0.1 copy.87.refs_12_.refs_20_
  50.3 0.1 copy.89.refs_21_
  50.4 4.7 %collective-permute-done.28.refs_11_.refs_15_ = bf16[176,1024]{1,0:T(8,128)(2,1)} collective-permute-done((bf16[176,1024]{1,0:T(8,128)(2,1)S(1)}, bf16[176,1024]{1,0:T(8,128)(2,1)}, u32[]{:S(2)}, u32[]{:S(2)}) %collective-permute-start.28) | collective-permute-done | bytes 360480 | tf_op jit(solution)/shard_map/ppermute | solution.py:279
  55.1 0.7 collective-permute-done.26.refs_8_.refs_11_
  55.9 1.0 %copy-done.4 = bf16[176,1024]{1,0:T(8,128)(2,1)S(1)} copy-done((bf16[176,1024]{1,0:T(8,128)(2,1)S(1)}, bf16[176,1024]{1,0:T(8,128)(2,1)}, u32[]{:S(2)}) %copy-start.4) | copy-done | bytes 360472
  56.9 7.0 %shard_map.59.refs_17_ = f32[4,528]{1,0:T(4,128)S(1)} custom-call(bf16[176,1024]{1,0:T(8,128)(2,1)S(1)} %get-tuple-element.81.refs_0_.refs_1_, bf16[176,1024]{1,0:T(8,128)(2,1)S(1)} %collective-permute-done.16.refs_1_.refs_2_, bf16[176,1024]{1,0:T(8,128)(2,1)S(1)} %collective-permute-done.17.refs_2_.refs_3_, ...), custom_call_target="tpu_custom_call" | custom-call | flops 2854748160 | bytes 4325376 | tf_op jit(solution)/shard_map/pallas_call | solution.py:350
  63.9 0.0 collective-permute-done.29.refs_16_
  63.9 0.0 collective-permute-done.25.refs_8_
  63.9 7.6 %shard_map.60 = f32[4,8,4,128]{3,2,1,0:T(4,128)} custom-call(s32[1]{0:T(128)} %bitcast.13.plane_ref.refs_0_, bf16[176,1024]{1,0:T(8,128)(2,1)S(1)} %get-tuple-element.81.refs_0_.refs_1_, bf16[176,1024]{1,0:T(8,128)(2,1)S(1)} %collective-permute-done.16.refs_1_.refs_2_, bf16[176,1024]{1,0:T(8,128)(2,1)S(1)} %collective-permute-done.17.refs_2_.refs_3_, ...), custom_call_target="tpu_custom_call" | custom-call | tf_op jit(solution)/shard_map/pallas_call | solution.py:361
  71.6 4.8 %all-to-all-start.3 = ((f32[32,4,128]{2,1,0:T(4,128)}), f32[32,4,128]{2,1,0:T(4,128)S(1)}, u32[]{:S(2)}, u32[]{:S(2)}) async-start(f32[32,4,128]{2,1,0:T(4,128)} %bitcast.19), calls=%async_computation.3 | async-start | bytes 131072 | tf_op jit(solution)/shard_map/all_to_all | solution.py:379
  76.4 0.7 slice_reduce_fusion
  77.8 5.9 %all-to-all-done.3 = f32[32,4,128]{2,1,0:T(4,128)S(1)} async-done(((f32[32,4,128]{2,1,0:T(4,128)}), f32[32,4,128]{2,1,0:T(4,128)S(1)}, u32[]{:S(2)}, u32[]{:S(2)}) %all-to-all-start.3) | async-done | bytes 65568 | tf_op jit(solution)/shard_map/all_to_all | solution.py:379
  83.7 0.3 conditional.1
  84.0 0.0 copy-start.14
  84.0 0.6 copy-done.14
  (38 shorter events, 0.3 us)
Async XLA Ops:
  0.0 10.8 %copy-start.13 = (s32[4,8]{1,0:T(4,128)S(1)}, s32[4,8]{1,0:T(4,128)}, u32[]{:S(2)}) copy-start(s32[4,8]{1,0:T(4,128)} %constant.109.clone) | copy-start | bytes 388
  0.0 8.3 %copy-start.11 = (s32[512]{0:T(512)S(1)}, s32[512]{0:T(512)}, u32[]{:S(2)}) copy-start(s32[512]{0:T(512)} %param.8) | copy-start | bytes 6148
  0.0 8.4 %copy-start.12 = (s32[1,512]{1,0:T(1,128)S(1)}, s32[1,512]{1,0:T(1,128)}, u32[]{:S(2)}) copy-start(s32[1,512]{1,0:T(1,128)} %param.9) | copy-start | bytes 6148
  2.6 32.9 %collective-permute-start.16 = (bf16[176,1024]{1,0:T(8,128)(2,1)S(1)}, bf16[176,1024]{1,0:T(8,128)(2,1)S(1)}, u32[]{:S(2)}, u32[]{:S(2)}) collective-permute-start(bf16[176,1024]{1,0:T(8,128)(2,1)S(1)} %get-tuple-element.77), channel_id=1, source_target_pairs={{2,0},{3,1},{10,8},{11,9},{18,16},{19,17},{26,24},{27,25},{0,2},{1... | collective-permute-start | bytes 1081352 | tf_op jit(solution)/shard_map/ppermute | solution.py:276
  5.7 32.4 %collective-permute-start.17 = (bf16[176,1024]{1,0:T(8,128)(2,1)S(1)}, bf16[176,1024]{1,0:T(8,128)(2,1)S(1)}, u32[]{:S(2)}, u32[]{:S(2)}) collective-permute-start(bf16[176,1024]{1,0:T(8,128)(2,1)S(1)} %get-tuple-element.78), channel_id=1, source_target_pairs={{4,0},{5,1},{12,8},{13,9},{20,16},{21,17},{28,24},{29,25},{6,2},{7... | collective-permute-start | bytes 1081352 | tf_op jit(solution)/shard_map/ppermute | solution.py:276
  8.3 2.7 %collective-permute-start.15 = (bf16[176,1024]{1,0:T(8,128)(2,1)S(1)}, bf16[176,1024]{1,0:T(8,128)(2,1)S(1)}, u32[]{:S(2)}, u32[]{:S(2)}) collective-permute-start(bf16[176,1024]{1,0:T(8,128)(2,1)S(1)} %get-tuple-element.81.refs_0_.refs_1_), channel_id=1, source_target_pairs={{8,0},{9,1},{0,8},{1,9},{24,16},{25,17},{16,24},{17,25},{10,2},{11... | collective-permute-start | bytes 1081352 | tf_op jit(solution)/shard_map/ppermute | solution.py:279
  10.8 0.7 copy-start.9
  11.5 24.0 %collective-permute-start.20 = (bf16[176,1024]{1,0:T(8,128)(2,1)S(1)}, bf16[176,1024]{1,0:T(8,128)(2,1)S(1)}, u32[]{:S(2)}, u32[]{:S(2)}) collective-permute-start(bf16[176,1024]{1,0:T(8,128)(2,1)S(1)} %get-tuple-element.81.refs_0_.refs_1_), channel_id=1, source_target_pairs={{16,0},{8,1},{24,8},{0,9},{17,16},{9,17},{25,24},{1,25},{18,2},{10... | collective-permute-start | bytes 1081352 | tf_op jit(solution)/shard_map/ppermute | solution.py:279
  13.2 22.4 %collective-permute-start.19 = (bf16[176,1024]{1,0:T(8,128)(2,1)S(1)}, bf16[176,1024]{1,0:T(8,128)(2,1)S(1)}, u32[]{:S(2)}, u32[]{:S(2)}) collective-permute-start(bf16[176,1024]{1,0:T(8,128)(2,1)S(1)} %get-tuple-element.81.refs_0_.refs_1_), channel_id=1, source_target_pairs={{1,0},{17,1},{9,8},{25,9},{0,16},{16,17},{8,24},{24,25},{3,2},{19,... | collective-permute-start | bytes 1081352 | tf_op jit(solution)/shard_map/ppermute | solution.py:279
  14.4 20.1 %all-to-all-start.2 = ((s32[32,1,256]{2,1,0:T(1,128)}), s32[32,1,256]{2,1,0:T(1,128)S(1)}, u32[]{:S(2)}, u32[]{:S(2)}) async-start(s32[32,1,256]{2,1,0:T(1,128)} %all_to_all.21), calls=%async_computation.2 | async-start | bytes 65536 | tf_op jit(solution)/shard_map/all_to_all | solution.py:310
  17.4 23.5 %collective-permute-start.18 = (bf16[176,1024]{1,0:T(8,128)(2,1)}, bf16[176,1024]{1,0:T(8,128)(2,1)S(1)}, u32[]{:S(2)}, u32[]{:S(2)}) collective-permute-start(bf16[176,1024]{1,0:T(8,128)(2,1)} %copy-done.9), channel_id=1, source_target_pairs={{6,0},{7,1},{14,8},{15,9},{22,16},{23,17},{30,24},{31,25},{4,2},{5... | collective-permute-start | bytes 1081352 | tf_op jit(solution)/shard_map/ppermute | solution.py:276
  35.5 2.6 %collective-permute-start.21 = (bf16[176,1024]{1,0:T(8,128)(2,1)S(1)}, bf16[176,1024]{1,0:T(8,128)(2,1)S(1)}, u32[]{:S(2)}, u32[]{:S(2)}) collective-permute-start(bf16[176,1024]{1,0:T(8,128)(2,1)S(1)} %collective-permute-done.16.refs_1_.refs_2_), channel_id=1, source_target_pairs={{8,0},{9,1},{0,8},{1,9},{24,16},{25,17},{16,24},{17,25},{10,2},{11... | collective-permute-start | bytes 1081352 | tf_op jit(solution)/shard_map/ppermute | solution.py:279
  36.0 11.4 %collective-permute-start.24 = (bf16[176,1024]{1,0:T(8,128)(2,1)S(1)}, bf16[176,1024]{1,0:T(8,128)(2,1)}, u32[]{:S(2)}, u32[]{:S(2)}) collective-permute-start(bf16[176,1024]{1,0:T(8,128)(2,1)S(1)} %collective-permute-done.16.refs_1_.refs_2_), channel_id=1, source_target_pairs={{16,0},{8,1},{24,8},{0,9},{17,16},{9,17},{25,24},{1,25},{18,2},{10... | collective-permute-start | bytes 1081352 | tf_op jit(solution)/shard_map/ppermute | solution.py:279
  36.8 11.4 %collective-permute-start.23 = (bf16[176,1024]{1,0:T(8,128)(2,1)S(1)}, bf16[176,1024]{1,0:T(8,128)(2,1)}, u32[]{:S(2)}, u32[]{:S(2)}) collective-permute-start(bf16[176,1024]{1,0:T(8,128)(2,1)S(1)} %collective-permute-done.16.refs_1_.refs_2_), channel_id=1, source_target_pairs={{1,0},{17,1},{9,8},{25,9},{0,16},{16,17},{8,24},{24,25},{3,2},{19,... | collective-permute-start | bytes 1081352 | tf_op jit(solution)/shard_map/ppermute | solution.py:279
  38.1 0.8 copy-start.3
  38.9 16.2 %collective-permute-start.28 = (bf16[176,1024]{1,0:T(8,128)(2,1)S(1)}, bf16[176,1024]{1,0:T(8,128)(2,1)}, u32[]{:S(2)}, u32[]{:S(2)}) collective-permute-start(bf16[176,1024]{1,0:T(8,128)(2,1)S(1)} %collective-permute-done.17.refs_2_.refs_3_), channel_id=1, source_target_pairs={{16,0},{8,1},{24,8},{0,9},{17,16},{9,17},{25,24},{1,25},{18,2},{10... | collective-permute-start | bytes 1081352 | tf_op jit(solution)/shard_map/ppermute | solution.py:279
  39.0 16.8 %collective-permute-start.26 = (bf16[176,1024]{1,0:T(8,128)(2,1)S(1)}, bf16[176,1024]{1,0:T(8,128)(2,1)}, u32[]{:S(2)}, u32[]{:S(2)}) collective-permute-start(bf16[176,1024]{1,0:T(8,128)(2,1)S(1)} %collective-permute-done.17.refs_2_.refs_3_), channel_id=1, source_target_pairs={{1,0},{17,1},{9,8},{25,9},{0,16},{16,17},{8,24},{24,25},{3,2},{19,... | collective-permute-start | bytes 1081352 | tf_op jit(solution)/shard_map/ppermute | solution.py:279
  40.9 9.3 %collective-permute-start.22 = (bf16[176,1024]{1,0:T(8,128)(2,1)S(1)}, bf16[176,1024]{1,0:T(8,128)(2,1)}, u32[]{:S(2)}, u32[]{:S(2)}) collective-permute-start(bf16[176,1024]{1,0:T(8,128)(2,1)S(1)} %collective-permute-done.17.refs_2_.refs_3_), channel_id=1, source_target_pairs={{8,0},{9,1},{0,8},{1,9},{24,16},{25,17},{16,24},{17,25},{10,2},{11... | collective-permute-start | bytes 1081352 | tf_op jit(solution)/shard_map/ppermute | solution.py:279
  48.1 15.7 %collective-permute-start.29 = (bf16[176,1024]{1,0:T(8,128)(2,1)S(1)}, bf16[176,1024]{1,0:T(8,128)(2,1)}, u32[]{:S(2)}, u32[]{:S(2)}) collective-permute-start(bf16[176,1024]{1,0:T(8,128)(2,1)S(1)} %collective-permute-done.18.refs_4_), channel_id=1, source_target_pairs={{16,0},{8,1},{24,8},{0,9},{17,16},{9,17},{25,24},{1,25},{18,2},{10... | collective-permute-start | bytes 1081352 | tf_op jit(solution)/shard_map/ppermute | solution.py:279
  48.1 15.8 %collective-permute-start.27 = (bf16[176,1024]{1,0:T(8,128)(2,1)S(1)}, bf16[176,1024]{1,0:T(8,128)(2,1)}, u32[]{:S(2)}, u32[]{:S(2)}) collective-permute-start(bf16[176,1024]{1,0:T(8,128)(2,1)S(1)} %collective-permute-done.18.refs_4_), channel_id=1, source_target_pairs={{1,0},{17,1},{9,8},{25,9},{0,16},{16,17},{8,24},{24,25},{3,2},{19,... | collective-permute-start | bytes 1081352 | tf_op jit(solution)/shard_map/ppermute | solution.py:279
  50.2 13.7 %collective-permute-start.25 = (bf16[176,1024]{1,0:T(8,128)(2,1)S(1)}, bf16[176,1024]{1,0:T(8,128)(2,1)}, u32[]{:S(2)}, u32[]{:S(2)}) collective-permute-start(bf16[176,1024]{1,0:T(8,128)(2,1)S(1)} %collective-permute-done.18.refs_4_), channel_id=1, source_target_pairs={{8,0},{9,1},{0,8},{1,9},{24,16},{25,17},{16,24},{17,25},{10,2},{11... | collective-permute-start | bytes 1081352 | tf_op jit(solution)/shard_map/ppermute | solution.py:279
  55.9 1.0 %copy-start.4 = (bf16[176,1024]{1,0:T(8,128)(2,1)S(1)}, bf16[176,1024]{1,0:T(8,128)(2,1)}, u32[]{:S(2)}) copy-start(bf16[176,1024]{1,0:T(8,128)(2,1)} %copy-done.3) | copy-start | bytes 1081348
  56.9 7.1 %copy-start.5 = (bf16[176,1024]{1,0:T(8,128)(2,1)S(1)}, bf16[176,1024]{1,0:T(8,128)(2,1)}, u32[]{:S(2)}) copy-start(bf16[176,1024]{1,0:T(8,128)(2,1)} %copy-done.3) | copy-start | bytes 1081348
  63.9 12.6 %copy-start.10 = (s32[32,1,256]{2,0,1:T(8,128)S(1)}, s32[32,1,256]{2,0,1:T(8,128)}, u32[]{:S(2)}) copy-start(s32[32,1,256]{2,0,1:T(8,128)} %copy.97) | copy-start | bytes 98308
  71.6 12.1 %all-to-all-start.3 = ((f32[32,4,128]{2,1,0:T(4,128)}), f32[32,4,128]{2,1,0:T(4,128)S(1)}, u32[]{:S(2)}, u32[]{:S(2)}) async-start(f32[32,4,128]{2,1,0:T(4,128)} %bitcast.19), calls=%async_computation.3 | async-start | bytes 131072 | tf_op jit(solution)/shard_map/all_to_all | solution.py:379
  84.0 0.6 copy-start.14

commit v4 on v3

--- a/solution.py
+++ b/solution.py
@@ -284,7 +284,17 @@
     own = [parts[0]] + [across(parts[k], k) for k in range(1, min(3, groups))]
     near = inside(own[0], 1)
     rounds = [[near] + [inside(after(own[0], near), j) for j in range(2, count)]]
-    place, rest = after((place, [parts[k] for k in range(3, groups)]), near)
+    rest = after([parts[k] for k in range(3, groups)], near)
+
+    own += [across(part, k) for k, part in zip(range(3, groups), rest)]
+    for k in range(1, groups - 1):
+        part = after(own[k], *rounds[0]) if k == 1 else after(own[k], rounds[-1][0], *rounds[-2])
+        near = after(part, own[k + 1]) if k > 1 else part
+        rounds.append([inside(near, 1), *[inside(part, j) for j in range(2, count)]])
+
+    last = after(own[-1], *rounds[-2])
+    rounds.append([inside(after(last, rounds[-1][0]), 1), *[inside(last, j) for j in range(2, count)]])
+    place = after(place, rounds[1][0])
 
     planes_i = jnp.arange(groups, dtype=jnp.int32)
     swap = (planes_i[:, None] ^ planes_i[None, :]) == plane
@@ -308,13 +318,6 @@
     )
     facts = jnp.broadcast_to(facts[None, :, None, :], (n_row, groups, wide, length)).reshape(devs, length)
     facts = lax.all_to_all(facts, AXES, split_axis=0, concat_axis=0, tiled=True)
-    rest = after(rest, near)
-    own += [across(part, k) for k, part in zip(range(3, groups), rest)]
-    for k in range(1, groups - 1):
-        part = after(own[k], facts, *rounds[0]) if k == 1 else after(own[k], rounds[-1][0], *rounds[-2])
-        near = after(part, own[k + 1]) if k > 1 else part
-        rounds.append([inside(near, 1), *[inside(part, j) for j in range(2, count)]])
-
     over = jnp.max(facts[:, cap + LEVELS]) > 0
     facts = facts.reshape(n_row, groups, wide, length)
 
@@ -333,8 +336,6 @@
     early = slots - cap
     label_cols = labels.T
     facts = places[:, :early], places[:, early:], labels[:, :early], labels[:, early:], label_cols[:early], label_cols
-    facts, last = lax.optimization_barrier((facts, after(own[-1], *rounds[-2])))
-    rounds.append([inside(after(last, rounds[-1][0]), 1), *[inside(last, j) for j in range(2, count)]])
     place, last_place, label, last_label, label_col, label_cols = facts
     blocks = [own] + [[moved[j - 1] for moved in rounds] for j in range(1, count)]
     any_space = pl.BlockSpec(memory_space=pltpu.HBM)

time: 84.9 us -> 77 us (0.907)
  waiting for transfers between devices: 31.3 us -> 23.9 us
  Pallas kernels: 17.8 us -> 19.4 us
  local copies, waits for them, and re-layouts: 5.47 us -> 4.3 us
    ppermute x3, waiting for transfers between devices: 0.01 us -> 11.9 us  [across(): lax.ppermute(part, AXES, [(device(i, h ^ k), device(i, h)) for i, h in pl...]
    all_to_all x1, waiting for transfers between devices: 13.4 us -> 3.31 us  [best_matches(): facts = lax.all_to_all(facts, AXES, split_axis=0, concat_axis=0, tiled=True)]
    ppermute x12, waiting for transfers between devices: 12 us -> 2.78 us  [inside(): lax.ppermute(part, AXES, [(device(int(held[j, i]), h), device(i, h)) for...]
    ppermute x3, starting transfers between devices: 9.36 us -> 7.81 us  [across(): lax.ppermute(part, AXES, [(device(i, h ^ k), device(i, h)) for i, h in pl...]
    unnamed x19 -> x20, local copies, waits for them, and re-layouts: 3.48 us -> 2.4 us
  transfers between devices with their start and end apart: 17 -> 17, of which waited for: 6 -> 7; matrix products, arithmetic and copies ran while one was open for 5% -> 5% of each run, Pallas kernels for 9% -> 11%
where the time goes in v4:
time: 77 us; the launch traced here: 76.7 us
  starting transfers between devices  24.7 us (32%)
  waiting for transfers between devices  23.9 us (31%)
  Pallas kernels  19.4 us (25%)
  local copies, waits for them, and re-layouts  4.3 us (6%)
  other arithmetic  2.62 us (3%)
  between operations  1.59 us (2%)
    ppermute x3, waiting for transfers between devices, across(): lax.ppermute(part, AXES, [(device(i, h ^ k), device(i, h)) for i, h in pl...  11.9 us
    ppermute x12, starting transfers between devices, inside(): lax.ppermute(part, AXES, [(device(int(held[j, i]), h), device(i, h)) for...  8.86 us
    pallas_call x1, Pallas kernels, best_matches(): pl.pallas_call(functools.partial(late_kernel, pairs, count, group_size),...  7.83 us
    ppermute x3, starting transfers between devices, across(): lax.ppermute(part, AXES, [(device(i, h ^ k), device(i, h)) for i, h in pl...  7.81 us
    pallas_call x1, Pallas kernels, best_matches(): pl.pallas_call(functools.partial(early_kernel, pairs, count), out_shape=j...  7.16 us
    all_to_all x1, waiting for transfers between devices, best_matches(): lax.all_to_all(best.reshape(devs, -1, 128), AXES, split_axis=0, concat_ax...  5.9 us
    all_to_all x1, starting transfers between devices, best_matches(): lax.all_to_all(best.reshape(devs, -1, 128), AXES, split_axis=0, concat_ax...  4.57 us
    all_to_all x1, starting transfers between devices, best_matches(): facts = lax.all_to_all(facts, AXES, split_axis=0, concat_axis=0, tiled=True)  3.42 us
  transfers between devices with their start and end apart: 17, of which 7 were waited for; matrix products, arithmetic and copies ran while one was open for 5% of the time, Pallas kernels for 11%

profile of v4, /device:TPU:0, one launch (start us, length us, event | category | flops | bytes accessed | tf_op | source)
XLA Modules:
  0.0 76.7 jit_solution(847887194438622101)
XLA Ops:
  0.0 3.3 %shard_map.57 = (bf16[512,1024]{1,0:T(8,128)(2,1)S(1)}, s32[1,512]{1,0:T(1,128)S(1)}, bf16[176,1024]{1,0:T(8,128)(2,1)S(1)}, bf16[176,1024]{1,0:T(8,128)(2,1)}, bf16[176,1024]{1,0:T(8,128)(2,1)}) custom-call(s32[1]{0:T(128)} %bitcast.13.plane_ref.refs_0_, s32[1,512]{1,0:T(1,128)} %bitcast.38, f32[512,1024]{1,0:T(8,128)} %emb_ref.1), custom_call_target="tpu_custom_call" | custom-call | tf_op jit(solution)/shard_map/pallas_call | solution.py:255
  3.4 0.5 collective-permute-start.16
  3.8 2.6 %collective-permute-start.15 = (bf16[176,1024]{1,0:T(8,128)(2,1)}, bf16[176,1024]{1,0:T(8,128)(2,1)S(1)}, u32[]{:S(2)}, u32[]{:S(2)}) collective-permute-start(bf16[176,1024]{1,0:T(8,128)(2,1)} %get-tuple-element.58), channel_id=1, source_target_pairs={{2,0},{3,1},{10,8},{11,9},{18,16},{19,17},{26,24},{27,25},{0,2},{1... | collective-permute-start | bytes 1081352 | tf_op jit(solution)/shard_map/ppermute | solution.py:276
  6.4 2.6 %collective-permute-start.20 = (bf16[176,1024]{1,0:T(8,128)(2,1)}, bf16[176,1024]{1,0:T(8,128)(2,1)S(1)}, u32[]{:S(2)}, u32[]{:S(2)}) collective-permute-start(bf16[176,1024]{1,0:T(8,128)(2,1)} %get-tuple-element.63), channel_id=1, source_target_pairs={{4,0},{5,1},{12,8},{13,9},{20,16},{21,17},{28,24},{29,25},{6,2},{7... | collective-permute-start | bytes 1081352 | tf_op jit(solution)/shard_map/ppermute | solution.py:276
  9.0 0.0 collective-permute-done.16.refs_3_.refs_5_
  9.0 1.1 %collective-permute-start.18 = (bf16[176,1024]{1,0:T(8,128)(2,1)S(1)}, bf16[176,1024]{1,0:T(8,128)(2,1)S(1)}, u32[]{:S(2)}, u32[]{:S(2)}) collective-permute-start(bf16[176,1024]{1,0:T(8,128)(2,1)S(1)} %get-tuple-element.60.refs_0_.refs_1_), channel_id=1, source_target_pairs={{16,0},{8,1},{24,8},{0,9},{17,16},{9,17},{25,24},{1,25},{18,2},{10... | collective-permute-start | bytes 1081352 | tf_op jit(solution)/shard_map/ppermute | solution.py:279
  10.1 1.0 %collective-permute-start.17 = (bf16[176,1024]{1,0:T(8,128)(2,1)S(1)}, bf16[176,1024]{1,0:T(8,128)(2,1)S(1)}, u32[]{:S(2)}, u32[]{:S(2)}) collective-permute-start(bf16[176,1024]{1,0:T(8,128)(2,1)S(1)} %get-tuple-element.60.refs_0_.refs_1_), channel_id=1, source_target_pairs={{1,0},{17,1},{9,8},{25,9},{0,16},{16,17},{8,24},{24,25},{3,2},{19,... | collective-permute-start | bytes 1081352 | tf_op jit(solution)/shard_map/ppermute | solution.py:279
  11.1 0.1 convert_reduce_fusion.5
  11.2 0.6 reduce_max.46
  12.5 0.1 convert_reduce_fusion.4
  12.6 10.6 %collective-permute-done.15.refs_1_.refs_2_ = bf16[176,1024]{1,0:T(8,128)(2,1)S(1)} collective-permute-done((bf16[176,1024]{1,0:T(8,128)(2,1)}, bf16[176,1024]{1,0:T(8,128)(2,1)S(1)}, u32[]{:S(2)}, u32[]{:S(2)}) %collective-permute-start.15) | collective-permute-done | bytes 360480 | tf_op jit(solution)/shard_map/ppermute | solution.py:276
  23.3 0.0 collective-permute-done.18.refs_9_.refs_13_
  23.3 0.0 collective-permute-done.17.refs_6_.refs_9_
  23.3 0.0 collective-permute-start.19
  23.3 0.1 pad_add_fusion.1
  23.4 0.1 pad.7.clone
  23.5 0.1 pad.6.clone
  23.5 1.1 %shard_map.58 = (s32[1,704]{1,0:T(1,128)S(1)}, bf16[176,1024]{1,0:T(8,128)(2,1)}) custom-call(s32[1,512]{1,0:T(1,128)S(1)} %bitcast.39, s32[1,512]{1,0:T(1,128)S(1)} %get-tuple-element.55.slot_ref, bf16[512,1024]{1,0:T(8,128)(2,1)S(1)} %get-tuple-element.56.unit_ref), custom_call_target="tpu_custom_call" | custom-call | tf_op jit(solution)/shard_map/pallas_call | solution.py:266
  24.6 0.1 select_reduce_fusion.5
  24.7 0.1 fusion.7
  24.8 2.6 %collective-permute-start.21 = (bf16[176,1024]{1,0:T(8,128)(2,1)}, bf16[176,1024]{1,0:T(8,128)(2,1)}, u32[]{:S(2)}, u32[]{:S(2)}) collective-permute-start(bf16[176,1024]{1,0:T(8,128)(2,1)} %get-tuple-element.65), channel_id=1, source_target_pairs={{6,0},{7,1},{14,8},{15,9},{22,16},{23,17},{30,24},{31,25},{4,2},{5... | collective-permute-start | bytes 1081352 | tf_op jit(solution)/shard_map/ppermute | solution.py:276
  27.5 1.3 %collective-permute-start.24 = (bf16[176,1024]{1,0:T(8,128)(2,1)S(1)}, bf16[176,1024]{1,0:T(8,128)(2,1)S(1)}, u32[]{:S(2)}, u32[]{:S(2)}) collective-permute-start(bf16[176,1024]{1,0:T(8,128)(2,1)S(1)} %collective-permute-done.15.refs_1_.refs_2_), channel_id=1, source_target_pairs={{16,0},{8,1},{24,8},{0,9},{17,16},{9,17},{25,24},{1,25},{18,2},{10... | collective-permute-start | bytes 1081352 | tf_op jit(solution)/shard_map/ppermute | solution.py:279
  28.8 0.7 collective-permute-start.23
  29.5 0.7 copy-done.3
  30.3 0.1 broadcast_in_dim.172
  30.3 0.1 select_reduce_fusion.4
  30.5 0.6 all_to_all.21
  31.1 3.4 %all-to-all-start.2 = ((s32[32,1,256]{2,1,0:T(1,128)}), s32[32,1,256]{2,1,0:T(1,128)S(1)}, u32[]{:S(2)}, u32[]{:S(2)}) async-start(s32[32,1,256]{2,1,0:T(1,128)} %all_to_all.21), calls=%async_computation.2 | async-start | bytes 65536 | tf_op jit(solution)/shard_map/all_to_all | solution.py:320
  34.6 1.6 %collective-permute-start.28 = (bf16[176,1024]{1,0:T(8,128)(2,1)S(1)}, bf16[176,1024]{1,0:T(8,128)(2,1)}, u32[]{:S(2)}, u32[]{:S(2)}) collective-permute-start(bf16[176,1024]{1,0:T(8,128)(2,1)S(1)} %collective-permute-done.20.refs_2_.refs_3_), channel_id=1, source_target_pairs={{16,0},{8,1},{24,8},{0,9},{17,16},{9,17},{25,24},{1,25},{18,2},{10... | collective-permute-start | bytes 1081352 | tf_op jit(solution)/shard_map/ppermute | solution.py:279
  36.2 0.5 collective-permute-start.26
  36.7 1.2 %collective-permute-done.21.refs_4_ = bf16[176,1024]{1,0:T(8,128)(2,1)} collective-permute-done((bf16[176,1024]{1,0:T(8,128)(2,1)}, bf16[176,1024]{1,0:T(8,128)(2,1)}, u32[]{:S(2)}, u32[]{:S(2)}) %collective-permute-start.21) | collective-permute-done | bytes 360480 | tf_op jit(solution)/shard_map/ppermute | solution.py:276
  37.9 0.7 collective-permute-done.24.refs_10_.refs_14_
  38.6 1.4 %collective-permute-done.23.refs_7_.refs_10_ = bf16[176,1024]{1,0:T(8,128)(2,1)} collective-permute-done((bf16[176,1024]{1,0:T(8,128)(2,1)S(1)}, bf16[176,1024]{1,0:T(8,128)(2,1)}, u32[]{:S(2)}, u32[]{:S(2)}) %collective-permute-start.23) | collective-permute-done | bytes 360480 | tf_op jit(solution)/shard_map/ppermute | solution.py:279
  39.9 0.2 collective-permute-start.29
  40.1 1.8 %collective-permute-start.27 = (bf16[176,1024]{1,0:T(8,128)(2,1)}, bf16[176,1024]{1,0:T(8,128)(2,1)}, u32[]{:S(2)}, u32[]{:S(2)}) collective-permute-start(bf16[176,1024]{1,0:T(8,128)(2,1)} %collective-permute-done.21.refs_4_), channel_id=1, source_target_pairs={{1,0},{17,1},{9,8},{25,9},{0,16},{16,17},{8,24},{24,25},{3,2},{19,... | collective-permute-start | bytes 1081352 | tf_op jit(solution)/shard_map/ppermute | solution.py:279
  42.0 0.0 collective-permute-start.22
  42.0 3.3 %all-to-all-done.2 = s32[32,1,256]{2,1,0:T(1,128)S(1)} async-done(((s32[32,1,256]{2,1,0:T(1,128)}), s32[32,1,256]{2,1,0:T(1,128)S(1)}, u32[]{:S(2)}, u32[]{:S(2)}) %all-to-all-start.2) | async-done | bytes 32800 | tf_op jit(solution)/shard_map/all_to_all | solution.py:320
  45.3 0.1 reduce.4
  45.4 0.1 broadcast_in_dim.181
  45.5 0.1 select_reduce_fusion.3
  45.7 0.1 reshape.175
  45.8 0.1 mul.54
  45.9 0.1 multiply_reduce_fusion.1
  46.0 0.1 fusion.4
  46.1 0.2 copy.85
  46.3 0.1 convert_reduce_fusion.3
  46.4 0.2 copy.86
  46.6 0.0 collective-permute-done.22.refs_5_.refs_7_
  46.6 0.2 collective-permute-start.25
  46.9 0.1 slice.66.refs_19_
  47.0 0.1 copy.94.refs_21_
  47.1 0.1 copy.87.refs_12_.refs_20_
  47.2 0.7 collective-permute-done.26.refs_8_.refs_11_
  47.9 1.0 %copy-done.6 = bf16[176,1024]{1,0:T(8,128)(2,1)S(1)} copy-done((bf16[176,1024]{1,0:T(8,128)(2,1)S(1)}, bf16[176,1024]{1,0:T(8,128)(2,1)}, u32[]{:S(2)}) %copy-start.6) | copy-done | bytes 360472
  48.9 7.2 %shard_map.59.refs_17_ = f32[4,528]{1,0:T(4,128)S(1)} custom-call(bf16[176,1024]{1,0:T(8,128)(2,1)S(1)} %get-tuple-element.60.refs_0_.refs_1_, bf16[176,1024]{1,0:T(8,128)(2,1)S(1)} %collective-permute-done.15.refs_1_.refs_2_, bf16[176,1024]{1,0:T(8,128)(2,1)S(1)} %collective-permute-done.20.refs_2_.refs_3_, ...), custom_call_target="tpu_custom_call" | custom-call | flops 2854748160 | bytes 4325376 | tf_op jit(solution)/shard_map/pallas_call | solution.py:351
  56.1 0.0 collective-permute-done.27.refs_12_
  56.1 0.0 collective-permute-done.25.refs_8_
  56.1 7.8 %shard_map.60 = f32[4,8,4,128]{3,2,1,0:T(4,128)} custom-call(s32[1]{0:T(128)} %bitcast.13.plane_ref.refs_0_, bf16[176,1024]{1,0:T(8,128)(2,1)S(1)} %get-tuple-element.60.refs_0_.refs_1_, bf16[176,1024]{1,0:T(8,128)(2,1)S(1)} %collective-permute-done.15.refs_1_.refs_2_, bf16[176,1024]{1,0:T(8,128)(2,1)S(1)} %collective-permute-done.20.refs_2_.refs_3_, ...), custom_call_target="tpu_custom_call" | custom-call | tf_op jit(solution)/shard_map/pallas_call | solution.py:362
  64.0 4.6 %all-to-all-start.3 = ((f32[32,4,128]{2,1,0:T(4,128)}), f32[32,4,128]{2,1,0:T(4,128)S(1)}, u32[]{:S(2)}, u32[]{:S(2)}) async-start(f32[32,4,128]{2,1,0:T(4,128)} %bitcast.19), calls=%async_computation.3 | async-start | bytes 131072 | tf_op jit(solution)/shard_map/all_to_all | solution.py:380
  68.6 0.7 slice_reduce_fusion
  69.9 5.9 %all-to-all-done.3 = f32[32,4,128]{2,1,0:T(4,128)S(1)} async-done(((f32[32,4,128]{2,1,0:T(4,128)}), f32[32,4,128]{2,1,0:T(4,128)S(1)}, u32[]{:S(2)}, u32[]{:S(2)}) %all-to-all-start.3) | async-done | bytes 65568 | tf_op jit(solution)/shard_map/all_to_all | solution.py:380
  75.8 0.3 conditional.1
  76.1 0.0 copy-start.13
  76.1 0.6 copy-done.13
  (38 shorter events, 0.3 us)
Async XLA Ops:
  0.0 24.6 %copy-start.12 = (s32[4,8]{1,0:T(4,128)S(1)}, s32[4,8]{1,0:T(4,128)}, u32[]{:S(2)}) copy-start(s32[4,8]{1,0:T(4,128)} %constant.109.clone) | copy-start | bytes 388
  0.0 9.0 %copy-start.10 = (s32[512]{0:T(512)S(1)}, s32[512]{0:T(512)}, u32[]{:S(2)}) copy-start(s32[512]{0:T(512)} %param.8) | copy-start | bytes 6148
  0.0 12.5 %copy-start.11 = (s32[1,512]{1,0:T(1,128)S(1)}, s32[1,512]{1,0:T(1,128)}, u32[]{:S(2)}) copy-start(s32[1,512]{1,0:T(1,128)} %param.9) | copy-start | bytes 6148
  3.4 5.6 %collective-permute-start.16 = (bf16[176,1024]{1,0:T(8,128)(2,1)S(1)}, bf16[176,1024]{1,0:T(8,128)(2,1)S(1)}, u32[]{:S(2)}, u32[]{:S(2)}) collective-permute-start(bf16[176,1024]{1,0:T(8,128)(2,1)S(1)} %get-tuple-element.60.refs_0_.refs_1_), channel_id=1, source_target_pairs={{8,0},{9,1},{0,8},{1,9},{24,16},{25,17},{16,24},{17,25},{10,2},{11... | collective-permute-start | bytes 1081352 | tf_op jit(solution)/shard_map/ppermute | solution.py:279
  3.8 19.5 %collective-permute-start.15 = (bf16[176,1024]{1,0:T(8,128)(2,1)}, bf16[176,1024]{1,0:T(8,128)(2,1)S(1)}, u32[]{:S(2)}, u32[]{:S(2)}) collective-permute-start(bf16[176,1024]{1,0:T(8,128)(2,1)} %get-tuple-element.58), channel_id=1, source_target_pairs={{2,0},{3,1},{10,8},{11,9},{18,16},{19,17},{26,24},{27,25},{0,2},{1... | collective-permute-start | bytes 1081352 | tf_op jit(solution)/shard_map/ppermute | solution.py:276
  6.4 28.2 %collective-permute-start.20 = (bf16[176,1024]{1,0:T(8,128)(2,1)}, bf16[176,1024]{1,0:T(8,128)(2,1)S(1)}, u32[]{:S(2)}, u32[]{:S(2)}) collective-permute-start(bf16[176,1024]{1,0:T(8,128)(2,1)} %get-tuple-element.63), channel_id=1, source_target_pairs={{4,0},{5,1},{12,8},{13,9},{20,16},{21,17},{28,24},{29,25},{6,2},{7... | collective-permute-start | bytes 1081352 | tf_op jit(solution)/shard_map/ppermute | solution.py:276
  9.0 14.3 %collective-permute-start.18 = (bf16[176,1024]{1,0:T(8,128)(2,1)S(1)}, bf16[176,1024]{1,0:T(8,128)(2,1)S(1)}, u32[]{:S(2)}, u32[]{:S(2)}) collective-permute-start(bf16[176,1024]{1,0:T(8,128)(2,1)S(1)} %get-tuple-element.60.refs_0_.refs_1_), channel_id=1, source_target_pairs={{16,0},{8,1},{24,8},{0,9},{17,16},{9,17},{25,24},{1,25},{18,2},{10... | collective-permute-start | bytes 1081352 | tf_op jit(solution)/shard_map/ppermute | solution.py:279
  10.1 13.2 %collective-permute-start.17 = (bf16[176,1024]{1,0:T(8,128)(2,1)S(1)}, bf16[176,1024]{1,0:T(8,128)(2,1)S(1)}, u32[]{:S(2)}, u32[]{:S(2)}) collective-permute-start(bf16[176,1024]{1,0:T(8,128)(2,1)S(1)} %get-tuple-element.60.refs_0_.refs_1_), channel_id=1, source_target_pairs={{1,0},{17,1},{9,8},{25,9},{0,16},{16,17},{8,24},{24,25},{3,2},{19,... | collective-permute-start | bytes 1081352 | tf_op jit(solution)/shard_map/ppermute | solution.py:279
  23.3 6.2 %collective-permute-start.19 = (bf16[176,1024]{1,0:T(8,128)(2,1)S(1)}, bf16[176,1024]{1,0:T(8,128)(2,1)S(1)}, u32[]{:S(2)}, u32[]{:S(2)}) collective-permute-start(bf16[176,1024]{1,0:T(8,128)(2,1)S(1)} %collective-permute-done.15.refs_1_.refs_2_), channel_id=1, source_target_pairs={{8,0},{9,1},{0,8},{1,9},{24,16},{25,17},{16,24},{17,25},{10,2},{11... | collective-permute-start | bytes 1081352 | tf_op jit(solution)/shard_map/ppermute | solution.py:279
  24.8 13.1 %collective-permute-start.21 = (bf16[176,1024]{1,0:T(8,128)(2,1)}, bf16[176,1024]{1,0:T(8,128)(2,1)}, u32[]{:S(2)}, u32[]{:S(2)}) collective-permute-start(bf16[176,1024]{1,0:T(8,128)(2,1)} %get-tuple-element.65), channel_id=1, source_target_pairs={{6,0},{7,1},{14,8},{15,9},{22,16},{23,17},{30,24},{31,25},{4,2},{5... | collective-permute-start | bytes 1081352 | tf_op jit(solution)/shard_map/ppermute | solution.py:276
  27.5 11.1 %collective-permute-start.24 = (bf16[176,1024]{1,0:T(8,128)(2,1)S(1)}, bf16[176,1024]{1,0:T(8,128)(2,1)S(1)}, u32[]{:S(2)}, u32[]{:S(2)}) collective-permute-start(bf16[176,1024]{1,0:T(8,128)(2,1)S(1)} %collective-permute-done.15.refs_1_.refs_2_), channel_id=1, source_target_pairs={{16,0},{8,1},{24,8},{0,9},{17,16},{9,17},{25,24},{1,25},{18,2},{10... | collective-permute-start | bytes 1081352 | tf_op jit(solution)/shard_map/ppermute | solution.py:279
  28.8 11.1 %collective-permute-start.23 = (bf16[176,1024]{1,0:T(8,128)(2,1)S(1)}, bf16[176,1024]{1,0:T(8,128)(2,1)}, u32[]{:S(2)}, u32[]{:S(2)}) collective-permute-start(bf16[176,1024]{1,0:T(8,128)(2,1)S(1)} %collective-permute-done.15.refs_1_.refs_2_), channel_id=1, source_target_pairs={{1,0},{17,1},{9,8},{25,9},{0,16},{16,17},{8,24},{24,25},{3,2},{19,... | collective-permute-start | bytes 1081352 | tf_op jit(solution)/shard_map/ppermute | solution.py:279
  29.5 0.7 copy-start.3
  30.2 17.7 %copy-start.4 = (bf16[176,1024]{1,0:T(8,128)(2,1)S(1)}, bf16[176,1024]{1,0:T(8,128)(2,1)}, u32[]{:S(2)}) copy-start(bf16[176,1024]{1,0:T(8,128)(2,1)} %copy-done.3) | copy-start | bytes 1081348
  31.1 14.1 %all-to-all-start.2 = ((s32[32,1,256]{2,1,0:T(1,128)}), s32[32,1,256]{2,1,0:T(1,128)S(1)}, u32[]{:S(2)}, u32[]{:S(2)}) async-start(s32[32,1,256]{2,1,0:T(1,128)} %all_to_all.21), calls=%async_computation.2 | async-start | bytes 65536 | tf_op jit(solution)/shard_map/all_to_all | solution.py:320
  34.6 12.6 %collective-permute-start.28 = (bf16[176,1024]{1,0:T(8,128)(2,1)S(1)}, bf16[176,1024]{1,0:T(8,128)(2,1)}, u32[]{:S(2)}, u32[]{:S(2)}) collective-permute-start(bf16[176,1024]{1,0:T(8,128)(2,1)S(1)} %collective-permute-done.20.refs_2_.refs_3_), channel_id=1, source_target_pairs={{16,0},{8,1},{24,8},{0,9},{17,16},{9,17},{25,24},{1,25},{18,2},{10... | collective-permute-start | bytes 1081352 | tf_op jit(solution)/shard_map/ppermute | solution.py:279
  36.2 11.8 %collective-permute-start.26 = (bf16[176,1024]{1,0:T(8,128)(2,1)S(1)}, bf16[176,1024]{1,0:T(8,128)(2,1)}, u32[]{:S(2)}, u32[]{:S(2)}) collective-permute-start(bf16[176,1024]{1,0:T(8,128)(2,1)S(1)} %collective-permute-done.20.refs_2_.refs_3_), channel_id=1, source_target_pairs={{1,0},{17,1},{9,8},{25,9},{0,16},{16,17},{8,24},{24,25},{3,2},{19,... | collective-permute-start | bytes 1081352 | tf_op jit(solution)/shard_map/ppermute | solution.py:279
  38.6 8.1 %copy-start.5 = (bf16[176,1024]{1,0:T(8,128)(2,1)}, bf16[176,1024]{1,0:T(8,128)(2,1)S(1)}, u32[]{:S(2)}) copy-start(bf16[176,1024]{1,0:T(8,128)(2,1)S(1)} %collective-permute-done.24.refs_10_.refs_14_) | copy-start | bytes 1081348
  39.9 16.2 %collective-permute-start.29 = (bf16[176,1024]{1,0:T(8,128)(2,1)}, bf16[176,1024]{1,0:T(8,128)(2,1)}, u32[]{:S(2)}, u32[]{:S(2)}) collective-permute-start(bf16[176,1024]{1,0:T(8,128)(2,1)} %collective-permute-done.21.refs_4_), channel_id=1, source_target_pairs={{16,0},{8,1},{24,8},{0,9},{17,16},{9,17},{25,24},{1,25},{18,2},{10... | collective-permute-start | bytes 1081352 | tf_op jit(solution)/shard_map/ppermute | solution.py:279
  40.1 16.0 %collective-permute-start.27 = (bf16[176,1024]{1,0:T(8,128)(2,1)}, bf16[176,1024]{1,0:T(8,128)(2,1)}, u32[]{:S(2)}, u32[]{:S(2)}) collective-permute-start(bf16[176,1024]{1,0:T(8,128)(2,1)} %collective-permute-done.21.refs_4_), channel_id=1, source_target_pairs={{1,0},{17,1},{9,8},{25,9},{0,16},{16,17},{8,24},{24,25},{3,2},{19,... | collective-permute-start | bytes 1081352 | tf_op jit(solution)/shard_map/ppermute | solution.py:279
  42.0 4.7 %collective-permute-start.22 = (bf16[176,1024]{1,0:T(8,128)(2,1)S(1)}, bf16[176,1024]{1,0:T(8,128)(2,1)}, u32[]{:S(2)}, u32[]{:S(2)}) collective-permute-start(bf16[176,1024]{1,0:T(8,128)(2,1)S(1)} %collective-permute-done.20.refs_2_.refs_3_), channel_id=1, source_target_pairs={{8,0},{9,1},{0,8},{1,9},{24,16},{25,17},{16,24},{17,25},{10,2},{11... | collective-permute-start | bytes 1081352 | tf_op jit(solution)/shard_map/ppermute | solution.py:279
  46.6 9.5 %collective-permute-start.25 = (bf16[176,1024]{1,0:T(8,128)(2,1)}, bf16[176,1024]{1,0:T(8,128)(2,1)}, u32[]{:S(2)}, u32[]{:S(2)}) collective-permute-start(bf16[176,1024]{1,0:T(8,128)(2,1)} %collective-permute-done.21.refs_4_), channel_id=1, source_target_pairs={{8,0},{9,1},{0,8},{1,9},{24,16},{25,17},{16,24},{17,25},{10,2},{11... | collective-permute-start | bytes 1081352 | tf_op jit(solution)/shard_map/ppermute | solution.py:279
  47.9 1.0 %copy-start.6 = (bf16[176,1024]{1,0:T(8,128)(2,1)S(1)}, bf16[176,1024]{1,0:T(8,128)(2,1)}, u32[]{:S(2)}) copy-start(bf16[176,1024]{1,0:T(8,128)(2,1)} %copy-done.5) | copy-start | bytes 1081348
  48.9 7.2 %copy-start.7 = (bf16[176,1024]{1,0:T(8,128)(2,1)S(1)}, bf16[176,1024]{1,0:T(8,128)(2,1)}, u32[]{:S(2)}) copy-start(bf16[176,1024]{1,0:T(8,128)(2,1)} %copy-done.5) | copy-start | bytes 1081348
  64.0 11.9 %all-to-all-start.3 = ((f32[32,4,128]{2,1,0:T(4,128)}), f32[32,4,128]{2,1,0:T(4,128)S(1)}, u32[]{:S(2)}, u32[]{:S(2)}) async-start(f32[32,4,128]{2,1,0:T(4,128)} %bitcast.19), calls=%async_computation.3 | async-start | bytes 131072 | tf_op jit(solution)/shard_map/all_to_all | solution.py:380
  76.1 0.6 copy-start.13

commit v5 on v4

--- a/solution.py
+++ b/solution.py
@@ -162,14 +162,18 @@
     return need
 
 
-def early_kernel(pairs, count, *refs):
+def early_kernel(pairs, count, early, *refs):
     *chunks, label_ref, label_col_ref, out_ref, blocks, sems = refs
     need = loader(chunks, count, blocks, sems)
-    best = [Best(jnp.full((1, blocks.shape[1]), -1.0, jnp.float32)) for _ in range(count)]
+    best = [Best(jnp.full((1, early), -1.0, jnp.float32)) for _ in range(count)]
     for j, k in pairs:
         need(j, k)
         sims = similar(
-            blocks[j], blocks[k], label_col_ref[:, j : j + 1], label_ref[k : k + 1, :], 0 if j == k else None
+            blocks[j, :early],
+            blocks[k, :early],
+            label_col_ref[:, j : j + 1],
+            label_ref[k : k + 1, :],
+            0 if j == k else None,
         )
         best[k].add_row(column_max(sims))
         if j != k:
@@ -178,13 +182,15 @@
         out_ref[j : j + 1, :] = best[j].as_row()
 
 
-def late_kernel(pairs, count, group_size, *refs):
-    plane_ref, *chunks, best_ref, place_ref, last_place_ref, label_ref, last_label_ref, label_col_ref, out_ref, blocks, sems = refs
+def late_kernel(pairs, count, number, group_size, *refs):
+    index_ref, *chunks = refs[: 1 + number]
+    best_ref, place_ref, last_place_ref, label_ref, last_label_ref, label_col_ref, *out_refs = refs[1 + number : -3]
+    whole, blocks, sems = refs[-3:]
     need = loader(chunks, count, blocks, sems)
-    cap = chunks[0].shape[0]
-    first = blocks.shape[1] - cap
+    first = best_ref.shape[1]
+    rest = blocks.shape[1] - first
     early = [Best(best_ref[j : j + 1, :]) for j in range(count)]
-    late = [Best(jnp.full((1, cap), -1.0, jnp.float32)) for _ in range(count)]
+    late = [Best(jnp.full((1, rest), -1.0, jnp.float32)) for _ in range(count)]
     for j, k in pairs:
         need(j, k)
         sims = similar(
@@ -223,11 +229,11 @@
         spread += lax.dot_general(stack, low.astype(jnp.bfloat16), NT, preferred_element_type=jnp.float32)
     value = spread[:tall] + spread[tall : 2 * tall] + spread[2 * tall : 3 * tall]
     value = jnp.where(spread[3 * tall :] > 0.5, value, -1.0)
-    n_row, n_col, lines, _ = out_ref.shape
-    for r in range(n_row):
-        here = jnp.where(plane_ref[0] == r, value, -1.0)
-        for c in range(n_col):
-            out_ref[r, c] = here[c * lines : (c + 1) * lines]
+    parts_of, lines = len(out_refs), value.shape[0] // len(out_refs)
+    for c in range(parts_of):
+        whole[c] = value[c * lines : (c + 1) * lines]
+    for k, ref in enumerate(out_refs):
+        ref[...] = whole[lax.rem(index_ref[0] + k, parts_of)]
 
 
 def best_matches(cap, embeddings, dest_pos, cluster_ids):
@@ -292,8 +298,6 @@
         near = after(part, own[k + 1]) if k > 1 else part
         rounds.append([inside(near, 1), *[inside(part, j) for j in range(2, count)]])
 
-    last = after(own[-1], *rounds[-2])
-    rounds.append([inside(after(last, rounds[-1][0]), 1), *[inside(last, j) for j in range(2, count)]])
     place = after(place, rounds[1][0])
 
     planes_i = jnp.arange(groups, dtype=jnp.int32)
@@ -318,6 +322,8 @@
     )
     facts = jnp.broadcast_to(facts[None, :, None, :], (n_row, groups, wide, length)).reshape(devs, length)
     facts = lax.all_to_all(facts, AXES, split_axis=0, concat_axis=0, tiled=True)
+    last = after(own[-1], facts, *rounds[-2])
+    rounds.append([inside(after(last, rounds[-1][0]), 1), *[inside(last, j) for j in range(2, count)]])
     over = jnp.max(facts[:, cap + LEVELS]) > 0
     facts = facts.reshape(n_row, groups, wide, length)
 
@@ -333,7 +339,7 @@
     labels = jnp.sum((places[:, None, :] >= ends[None, :, None]).astype(jnp.int32), axis=1)
     labels = jnp.where(places < group_size, labels, -1)
 
-    early = slots - cap
+    early = (slots - cap) // 256 * 256
     label_cols = labels.T
     facts = places[:, :early], places[:, early:], labels[:, :early], labels[:, early:], label_cols[:early], label_cols
     place, last_place, label, last_label, label_col, label_cols = facts
@@ -349,7 +355,7 @@
 
     limit = 8 + (2 * count * slots * width + 5 * area) // 2**20
     first_best = pl.pallas_call(
-        functools.partial(early_kernel, pairs, count),
+        functools.partial(early_kernel, pairs, count, early),
         out_shape=jax.ShapeDtypeStruct((count, early), jnp.float32),
         in_specs=[any_space] * (count * (groups - 1)) + [VMEM] * 2,
         out_specs=VMEM,
@@ -360,14 +366,14 @@
         ),
     )(*[part for block in blocks for part in block[:-1]], label, label_col)
     best = pl.pallas_call(
-        functools.partial(late_kernel, pairs, count, group_size),
-        out_shape=jax.ShapeDtypeStruct((n_row, n_col, rows_dev // 128, 128), jnp.float32),
+        functools.partial(late_kernel, pairs, count, count * groups, group_size),
+        out_shape=[jax.ShapeDtypeStruct((rows_dev // 128, 128), jnp.float32)] * n_col,
         in_specs=[pl.BlockSpec(memory_space=pltpu.SMEM)] + [any_space] * (count * groups) + [VMEM] * 6,
-        out_specs=VMEM,
-        scratch_shapes=scratch(groups),
+        out_specs=[VMEM] * n_col,
+        scratch_shapes=[pltpu.VMEM((n_col, rows_dev // 128, 128), jnp.float32), *scratch(groups)],
         compiler_params=kernel_params(limit),
     )(
-        plane_ref,
+        index.astype(jnp.int32).reshape(1),
         *itertools.chain(*blocks),
         first_best,
         place,
@@ -377,8 +383,12 @@
         label_cols,
     )
 
-    best = lax.all_to_all(best.reshape(devs, -1, 128), AXES, split_axis=0, concat_axis=0, tiled=True)
-    return jnp.max(best, axis=0).reshape(1, rows_dev), over
+    out = None
+    for k, part in enumerate(best):
+        moves = [(device(i, h), h * n_col + (i + k) % n_col) for i, h in planes]
+        part = lax.ppermute(part, AXES, moves)
+        out = part if out is None else jnp.maximum(out, part)
+    return out.reshape(1, rows_dev), over
 
 
 def shards(embeddings, dest_pos, cluster_ids):

time: 77 us -> 84.2 us (1.094)
  the two profiles are of different devices: /device:TPU:0 before, /device:TPU:3 now
where the time goes in v5:
time: 84.2 us; the launch traced here: 84 us
  starting transfers between devices  34.3 us (41%)
  waiting for transfers between devices  24.8 us (29%)
  Pallas kernels  16.3 us (19%)
  local copies, waits for them, and re-layouts  3.61 us (4%)
  other arithmetic  3.21 us (4%)
  between operations  1.64 us (2%)
    ppermute x8, starting transfers between devices, best_matches(): part = lax.ppermute(part, AXES, moves)  14.9 us
    ppermute x3, waiting for transfers between devices, across(): lax.ppermute(part, AXES, [(device(i, h ^ k), device(i, h)) for i, h in pl...  12.3 us
    ppermute x12, starting transfers between devices, inside(): lax.ppermute(part, AXES, [(device(int(held[j, i]), h), device(i, h)) for...  9.47 us
    pallas_call x1, Pallas kernels, best_matches(): pl.pallas_call(functools.partial(late_kernel, pairs, count, count * group...  6.81 us
    ppermute x8, waiting for transfers between devices, best_matches(): part = lax.ppermute(part, AXES, moves)  6.25 us
    all_to_all x1, waiting for transfers between devices, best_matches(): facts = lax.all_to_all(facts, AXES, split_axis=0, concat_axis=0, tiled=True)  5.9 us
    ppermute x3, starting transfers between devices, across(): lax.ppermute(part, AXES, [(device(i, h ^ k), device(i, h)) for i, h in pl...  5.8 us
    pallas_call x1, Pallas kernels, best_matches(): pl.pallas_call(functools.partial(early_kernel, pairs, count, early), out_...  5.1 us
  transfers between devices with their start and end apart: 24, of which 6 were waited for; matrix products, arithmetic and copies ran while one was open for 5% of the time, Pallas kernels for 7%

profile of v5, /device:TPU:3, one launch (start us, length us, event | category | flops | bytes accessed | tf_op | source)
XLA Modules:
  0.0 84.0 jit_solution(6292729995757656635)
XLA Ops:
  0.0 3.3 %shard_map.57 = (bf16[512,1024]{1,0:T(8,128)(2,1)S(1)}, s32[1,512]{1,0:T(1,128)S(1)}, bf16[176,1024]{1,0:T(8,128)(2,1)S(1)}, bf16[176,1024]{1,0:T(8,128)(2,1)}, bf16[176,1024]{1,0:T(8,128)(2,1)}) custom-call(s32[1]{0:T(128)} %bitcast.13.plane_ref, s32[1,512]{1,0:T(1,128)} %bitcast.37, f32[512,1024]{1,0:T(8,128)} %emb_ref.1), custom_call_target="tpu_custom_call" | custom-call | tf_op jit(solution)/shard_map/pallas_call | solution.py:261
  3.3 0.7 collective-permute-start.24
  4.0 1.3 %collective-permute-start.23 = (bf16[176,1024]{1,0:T(8,128)(2,1)}, bf16[176,1024]{1,0:T(8,128)(2,1)S(1)}, u32[]{:S(2)}, u32[]{:S(2)}) collective-permute-start(bf16[176,1024]{1,0:T(8,128)(2,1)} %get-tuple-element.102), channel_id=1, source_target_pairs={{2,0},{3,1},{10,8},{11,9},{18,16},{19,17},{26,24},{27,25},{0,2},{1... | collective-permute-start | bytes 1081352 | tf_op jit(solution)/shard_map/ppermute | solution.py:282
  5.3 2.3 %collective-permute-start.28 = (bf16[176,1024]{1,0:T(8,128)(2,1)}, bf16[176,1024]{1,0:T(8,128)(2,1)S(1)}, u32[]{:S(2)}, u32[]{:S(2)}) collective-permute-start(bf16[176,1024]{1,0:T(8,128)(2,1)} %get-tuple-element.107), channel_id=1, source_target_pairs={{4,0},{5,1},{12,8},{13,9},{20,16},{21,17},{28,24},{29,25},{6,2},{7... | collective-permute-start | bytes 1081352 | tf_op jit(solution)/shard_map/ppermute | solution.py:282
  7.6 0.3 collective-permute-start.26
  8.0 1.2 %collective-permute-start.25 = (bf16[176,1024]{1,0:T(8,128)(2,1)S(1)}, bf16[176,1024]{1,0:T(8,128)(2,1)S(1)}, u32[]{:S(2)}, u32[]{:S(2)}) collective-permute-start(bf16[176,1024]{1,0:T(8,128)(2,1)S(1)} %get-tuple-element.104.refs_0_.refs_1_), channel_id=1, source_target_pairs={{1,0},{17,1},{9,8},{25,9},{0,16},{16,17},{8,24},{24,25},{3,2},{19,... | collective-permute-start | bytes 1081352 | tf_op jit(solution)/shard_map/ppermute | solution.py:285
  9.2 0.1 convert_reduce_fusion.5
  9.3 0.7 reduce_max.27
  10.7 0.1 convert_reduce_fusion.4
  10.8 11.1 %collective-permute-done.23.refs_1_.refs_2_ = bf16[176,1024]{1,0:T(8,128)(2,1)S(1)} collective-permute-done((bf16[176,1024]{1,0:T(8,128)(2,1)}, bf16[176,1024]{1,0:T(8,128)(2,1)S(1)}, u32[]{:S(2)}, u32[]{:S(2)}) %collective-permute-start.23) | collective-permute-done | bytes 360480 | tf_op jit(solution)/shard_map/ppermute | solution.py:282
  21.9 0.0 collective-permute-done.26.refs_9_.refs_13_
  21.9 0.0 collective-permute-done.25.refs_6_.refs_9_
  21.9 0.8 collective-permute-start.27
  22.7 0.1 pad_add_fusion.1
  22.8 0.1 pad.7.clone
  22.8 0.1 pad.6.clone
  22.9 1.1 %shard_map.58 = (s32[1,704]{1,0:T(1,128)S(1)}, bf16[176,1024]{1,0:T(8,128)(2,1)}) custom-call(s32[1,512]{1,0:T(1,128)S(1)} %bitcast.38, s32[1,512]{1,0:T(1,128)S(1)} %get-tuple-element.99.slot_ref, bf16[512,1024]{1,0:T(8,128)(2,1)S(1)} %get-tuple-element.100.unit_ref), custom_call_target="tpu_custom_call" | custom-call | tf_op jit(solution)/shard_map/pallas_call | solution.py:272
  24.0 0.1 select_reduce_fusion.5
  24.1 0.1 fusion.7
  24.2 2.2 %collective-permute-start.29 = (bf16[176,1024]{1,0:T(8,128)(2,1)}, bf16[176,1024]{1,0:T(8,128)(2,1)}, u32[]{:S(2)}, u32[]{:S(2)}) collective-permute-start(bf16[176,1024]{1,0:T(8,128)(2,1)} %get-tuple-element.109), channel_id=1, source_target_pairs={{6,0},{7,1},{14,8},{15,9},{22,16},{23,17},{30,24},{31,25},{4,2},{5... | collective-permute-start | bytes 1081352 | tf_op jit(solution)/shard_map/ppermute | solution.py:282
  26.4 0.3 collective-permute-start.32
  26.7 1.2 %collective-permute-start.31 = (bf16[176,1024]{1,0:T(8,128)(2,1)S(1)}, bf16[176,1024]{1,0:T(8,128)(2,1)}, u32[]{:S(2)}, u32[]{:S(2)}) collective-permute-start(bf16[176,1024]{1,0:T(8,128)(2,1)S(1)} %collective-permute-done.23.refs_1_.refs_2_), channel_id=1, source_target_pairs={{1,0},{17,1},{9,8},{25,9},{0,16},{16,17},{8,24},{24,25},{3,2},{19,... | collective-permute-start | bytes 1081352 | tf_op jit(solution)/shard_map/ppermute | solution.py:285
  27.9 0.7 copy-done.2
  28.6 0.1 broadcast_in_dim.172
  28.7 0.1 select_reduce_fusion.4
  28.8 0.6 all_to_all.14
  29.5 4.2 %all-to-all-start.1 = ((s32[32,1,256]{2,1,0:T(1,128)}), s32[32,1,256]{2,1,0:T(1,128)S(1)}, u32[]{:S(2)}, u32[]{:S(2)}) async-start(s32[32,1,256]{2,1,0:T(1,128)} %all_to_all.14), calls=%async_computation.1 | async-start | bytes 65536 | tf_op jit(solution)/shard_map/all_to_all | solution.py:324
  33.7 0.0 collective-permute-done.28.refs_2_.refs_3_
  33.7 0.1 collective-permute-start.36
  33.8 1.4 %collective-permute-start.34 = (bf16[176,1024]{1,0:T(8,128)(2,1)S(1)}, bf16[176,1024]{1,0:T(8,128)(2,1)}, u32[]{:S(2)}, u32[]{:S(2)}) collective-permute-start(bf16[176,1024]{1,0:T(8,128)(2,1)S(1)} %collective-permute-done.28.refs_2_.refs_3_), channel_id=1, source_target_pairs={{1,0},{17,1},{9,8},{25,9},{0,16},{16,17},{8,24},{24,25},{3,2},{19,... | collective-permute-start | bytes 1081352 | tf_op jit(solution)/shard_map/ppermute | solution.py:285
  35.2 1.2 %collective-permute-done.29.refs_4_ = bf16[176,1024]{1,0:T(8,128)(2,1)} collective-permute-done((bf16[176,1024]{1,0:T(8,128)(2,1)}, bf16[176,1024]{1,0:T(8,128)(2,1)}, u32[]{:S(2)}, u32[]{:S(2)}) %collective-permute-start.29) | collective-permute-done | bytes 360480 | tf_op jit(solution)/shard_map/ppermute | solution.py:282
  36.4 0.9 %collective-permute-start.30 = (bf16[176,1024]{1,0:T(8,128)(2,1)S(1)}, bf16[176,1024]{1,0:T(8,128)(2,1)}, u32[]{:S(2)}, u32[]{:S(2)}) collective-permute-start(bf16[176,1024]{1,0:T(8,128)(2,1)S(1)} %collective-permute-done.28.refs_2_.refs_3_), channel_id=1, source_target_pairs={{8,0},{9,1},{0,8},{1,9},{24,16},{25,17},{16,24},{17,25},{10,2},{11... | collective-permute-start | bytes 1081352 | tf_op jit(solution)/shard_map/ppermute | solution.py:285
  37.3 5.9 %all-to-all-done.1 = s32[32,1,256]{2,1,0:T(1,128)S(1)} async-done(((s32[32,1,256]{2,1,0:T(1,128)}), s32[32,1,256]{2,1,0:T(1,128)S(1)}, u32[]{:S(2)}, u32[]{:S(2)}) %all-to-all-start.1) | async-done | bytes 32800 | tf_op jit(solution)/shard_map/all_to_all | solution.py:324
  43.2 1.2 %collective-permute-start.37 = (bf16[176,1024]{1,0:T(8,128)(2,1)}, bf16[176,1024]{1,0:T(8,128)(2,1)}, u32[]{:S(2)}, u32[]{:S(2)}) collective-permute-start(bf16[176,1024]{1,0:T(8,128)(2,1)} %collective-permute-done.29.refs_4_), channel_id=1, source_target_pairs={{16,0},{8,1},{24,8},{0,9},{17,16},{9,17},{25,24},{1,25},{18,2},{10... | collective-permute-start | bytes 1081352 | tf_op jit(solution)/shard_map/ppermute | solution.py:285
  44.4 0.3 collective-permute-start.35
  44.8 0.1 reduce.4
  44.9 0.1 broadcast_in_dim.181
  45.0 0.1 select_reduce_fusion.3
  45.1 0.1 reshape.176
  45.3 0.1 mul.54
  45.3 0.1 multiply_reduce_fusion.1
  45.5 0.1 fusion.4
  45.6 0.2 copy.85
  45.8 0.1 convert_reduce_fusion.3
  45.9 0.2 copy.86
  46.1 1.1 %collective-permute-start.33 = (bf16[176,1024]{1,0:T(8,128)(2,1)}, bf16[176,1024]{1,0:T(8,128)(2,1)}, u32[]{:S(2)}, u32[]{:S(2)}) collective-permute-start(bf16[176,1024]{1,0:T(8,128)(2,1)} %collective-permute-done.29.refs_4_), channel_id=1, source_target_pairs={{8,0},{9,1},{0,8},{1,9},{24,16},{25,17},{16,24},{17,25},{10,2},{11... | collective-permute-start | bytes 1081352 | tf_op jit(solution)/shard_map/ppermute | solution.py:285
  47.3 0.1 copy.94.refs_21_
  47.4 0.1 copy.87.refs_12_.refs_20_
  47.5 0.0 copy-done.3
  47.6 1.0 %copy-done.5 = bf16[176,1024]{1,0:T(8,128)(2,1)S(1)} copy-done((bf16[176,1024]{1,0:T(8,128)(2,1)S(1)}, bf16[176,1024]{1,0:T(8,128)(2,1)}, u32[]{:S(2)}) %copy-start.5) | copy-done | bytes 360472
  48.5 5.1 %shard_map.59.refs_17_ = f32[4,512]{1,0:T(4,128)S(1)} custom-call(bf16[176,1024]{1,0:T(8,128)(2,1)S(1)} %get-tuple-element.104.refs_0_.refs_1_, bf16[176,1024]{1,0:T(8,128)(2,1)S(1)} %collective-permute-done.23.refs_1_.refs_2_, bf16[176,1024]{1,0:T(8,128)(2,1)S(1)} %collective-permute-done.28.refs_2_.refs_3_, ...), custom_call_target="tpu_custom_call" | custom-call | flops 2684354560 | bytes 4194304 | tf_op jit(solution)/shard_map/pallas_call | solution.py:357
  53.7 0.4 collective-permute-done.35.refs_12_
  54.0 6.8 %shard_map.60 = (f32[4,128]{1,0:T(4,128)S(1)}, f32[4,128]{1,0:T(4,128)S(1)}, f32[4,128]{1,0:T(4,128)S(1)}, f32[4,128]{1,0:T(4,128)S(1)}, f32[4,128]{1,0:T(4,128)...) custom-call(s32[1]{0:T(128)} %bitcast.16.refs_0_, ...), custom_call_target="tpu_custom_call" | custom-call | tf_op jit(solution)/shard_map/pallas_call | solution.py:368
  60.8 6.0 %collective-permute-start.38 = (f32[4,128]{1,0:T(4,128)S(1)}, f32[4,128]{1,0:T(4,128)S(1)}, u32[]{:S(2)}, u32[]{:S(2)}) collective-permute-start(f32[4,128]{1,0:T(4,128)S(1)} %get-tuple-element.114), channel_id=1, source_target_pairs={{0,0},{1,1},{8,2},{9,3},{16,4},{17,5},{24,6},{25,7},{2,8},{3,9},{1... | collective-permute-start | bytes 6152 | tf_op jit(solution)/shard_map/ppermute | solution.py:389
  66.8 1.0 %collective-permute-start.39 = (f32[4,128]{1,0:T(4,128)S(1)}, f32[4,128]{1,0:T(4,128)S(1)}, u32[]{:S(2)}, u32[]{:S(2)}) collective-permute-start(f32[4,128]{1,0:T(4,128)S(1)} %get-tuple-element.115), channel_id=1, source_target_pairs={{0,1},{1,2},{8,3},{9,4},{16,5},{17,6},{24,7},{25,0},{2,9},{3,10},{... | collective-permute-start | bytes 6152 | tf_op jit(solution)/shard_map/ppermute | solution.py:389
  67.8 0.9 %collective-permute-start.42 = (f32[4,128]{1,0:T(4,128)S(1)}, f32[4,128]{1,0:T(4,128)S(1)}, u32[]{:S(2)}, u32[]{:S(2)}) collective-permute-start(f32[4,128]{1,0:T(4,128)S(1)} %get-tuple-element.118), channel_id=1, source_target_pairs={{0,4},{1,5},{8,6},{9,7},{16,0},{17,1},{24,2},{25,3},{2,12},{3,13},... | collective-permute-start | bytes 6152 | tf_op jit(solution)/shard_map/ppermute | solution.py:389
  68.7 2.3 %collective-permute-start.43 = (f32[4,128]{1,0:T(4,128)S(1)}, f32[4,128]{1,0:T(4,128)S(1)}, u32[]{:S(2)}, u32[]{:S(2)}) collective-permute-start(f32[4,128]{1,0:T(4,128)S(1)} %get-tuple-element.119), channel_id=1, source_target_pairs={{0,5},{1,6},{8,7},{9,0},{16,1},{17,2},{24,3},{25,4},{2,13},{3,14},... | collective-permute-start | bytes 6152 | tf_op jit(solution)/shard_map/ppermute | solution.py:389
  71.0 1.2 %collective-permute-done.39 = f32[4,128]{1,0:T(4,128)S(1)} collective-permute-done((f32[4,128]{1,0:T(4,128)S(1)}, f32[4,128]{1,0:T(4,128)S(1)}, u32[]{:S(2)}, u32[]{:S(2)}) %collective-permute-start.39) | collective-permute-done | bytes 2080 | tf_op jit(solution)/shard_map/ppermute | solution.py:389
  72.2 4.6 %collective-permute-start.44 = (f32[4,128]{1,0:T(4,128)S(1)}, f32[4,128]{1,0:T(4,128)S(1)}, u32[]{:S(2)}, u32[]{:S(2)}) collective-permute-start(f32[4,128]{1,0:T(4,128)S(1)} %get-tuple-element.120), channel_id=1, source_target_pairs={{0,6},{1,7},{8,0},{9,1},{16,2},{17,3},{24,4},{25,5},{2,14},{3,15},... | collective-permute-start | bytes 6152 | tf_op jit(solution)/shard_map/ppermute | solution.py:389
  76.8 0.1 collective-permute-start.45
  76.9 0.7 slice_reduce_fusion
  78.3 5.1 %collective-permute-done.45 = f32[4,128]{1,0:T(4,128)S(1)} collective-permute-done((f32[4,128]{1,0:T(4,128)S(1)}, f32[4,128]{1,0:T(4,128)S(1)}, u32[]{:S(2)}, u32[]{:S(2)}) %collective-permute-start.45) | collective-permute-done | bytes 2080 | tf_op jit(solution)/shard_map/ppermute | solution.py:389
  83.4 0.6 conditional.1
  83.4 0.6 maximum_maximum_fusion
  (48 shorter events, 0.3 us)
Async XLA Ops:
  0.0 24.0 %copy-start.10 = (s32[4,8]{1,0:T(4,128)S(1)}, s32[4,8]{1,0:T(4,128)}, u32[]{:S(2)}) copy-start(s32[4,8]{1,0:T(4,128)} %constant.104.clone) | copy-start | bytes 388
  0.0 7.6 %copy-start.8 = (s32[512]{0:T(512)S(1)}, s32[512]{0:T(512)}, u32[]{:S(2)}) copy-start(s32[512]{0:T(512)} %param.8) | copy-start | bytes 6148
  0.0 10.7 %copy-start.9 = (s32[1,512]{1,0:T(1,128)S(1)}, s32[1,512]{1,0:T(1,128)}, u32[]{:S(2)}) copy-start(s32[1,512]{1,0:T(1,128)} %param.9) | copy-start | bytes 6148
  3.3 4.3 %collective-permute-start.24 = (bf16[176,1024]{1,0:T(8,128)(2,1)S(1)}, bf16[176,1024]{1,0:T(8,128)(2,1)S(1)}, u32[]{:S(2)}, u32[]{:S(2)}) collective-permute-start(bf16[176,1024]{1,0:T(8,128)(2,1)S(1)} %get-tuple-element.104.refs_0_.refs_1_), channel_id=1, source_target_pairs={{8,0},{9,1},{0,8},{1,9},{24,16},{25,17},{16,24},{17,25},{10,2},{11... | collective-permute-start | bytes 1081352 | tf_op jit(solution)/shard_map/ppermute | solution.py:285
  4.0 17.9 %collective-permute-start.23 = (bf16[176,1024]{1,0:T(8,128)(2,1)}, bf16[176,1024]{1,0:T(8,128)(2,1)S(1)}, u32[]{:S(2)}, u32[]{:S(2)}) collective-permute-start(bf16[176,1024]{1,0:T(8,128)(2,1)} %get-tuple-element.102), channel_id=1, source_target_pairs={{2,0},{3,1},{10,8},{11,9},{18,16},{19,17},{26,24},{27,25},{0,2},{1... | collective-permute-start | bytes 1081352 | tf_op jit(solution)/shard_map/ppermute | solution.py:282
  5.3 28.4 %collective-permute-start.28 = (bf16[176,1024]{1,0:T(8,128)(2,1)}, bf16[176,1024]{1,0:T(8,128)(2,1)S(1)}, u32[]{:S(2)}, u32[]{:S(2)}) collective-permute-start(bf16[176,1024]{1,0:T(8,128)(2,1)} %get-tuple-element.107), channel_id=1, source_target_pairs={{4,0},{5,1},{12,8},{13,9},{20,16},{21,17},{28,24},{29,25},{6,2},{7... | collective-permute-start | bytes 1081352 | tf_op jit(solution)/shard_map/ppermute | solution.py:282
  7.6 14.2 %collective-permute-start.26 = (bf16[176,1024]{1,0:T(8,128)(2,1)S(1)}, bf16[176,1024]{1,0:T(8,128)(2,1)S(1)}, u32[]{:S(2)}, u32[]{:S(2)}) collective-permute-start(bf16[176,1024]{1,0:T(8,128)(2,1)S(1)} %get-tuple-element.104.refs_0_.refs_1_), channel_id=1, source_target_pairs={{16,0},{8,1},{24,8},{0,9},{17,16},{9,17},{25,24},{1,25},{18,2},{10... | collective-permute-start | bytes 1081352 | tf_op jit(solution)/shard_map/ppermute | solution.py:285
  8.0 13.9 %collective-permute-start.25 = (bf16[176,1024]{1,0:T(8,128)(2,1)S(1)}, bf16[176,1024]{1,0:T(8,128)(2,1)S(1)}, u32[]{:S(2)}, u32[]{:S(2)}) collective-permute-start(bf16[176,1024]{1,0:T(8,128)(2,1)S(1)} %get-tuple-element.104.refs_0_.refs_1_), channel_id=1, source_target_pairs={{1,0},{17,1},{9,8},{25,9},{0,16},{16,17},{8,24},{24,25},{3,2},{19,... | collective-permute-start | bytes 1081352 | tf_op jit(solution)/shard_map/ppermute | solution.py:285
  21.9 6.0 %collective-permute-start.27 = (bf16[176,1024]{1,0:T(8,128)(2,1)S(1)}, bf16[176,1024]{1,0:T(8,128)(2,1)S(1)}, u32[]{:S(2)}, u32[]{:S(2)}) collective-permute-start(bf16[176,1024]{1,0:T(8,128)(2,1)S(1)} %collective-permute-done.23.refs_1_.refs_2_), channel_id=1, source_target_pairs={{8,0},{9,1},{0,8},{1,9},{24,16},{25,17},{16,24},{17,25},{10,2},{11... | collective-permute-start | bytes 1081352 | tf_op jit(solution)/shard_map/ppermute | solution.py:285
  24.2 12.2 %collective-permute-start.29 = (bf16[176,1024]{1,0:T(8,128)(2,1)}, bf16[176,1024]{1,0:T(8,128)(2,1)}, u32[]{:S(2)}, u32[]{:S(2)}) collective-permute-start(bf16[176,1024]{1,0:T(8,128)(2,1)} %get-tuple-element.109), channel_id=1, source_target_pairs={{6,0},{7,1},{14,8},{15,9},{22,16},{23,17},{30,24},{31,25},{4,2},{5... | collective-permute-start | bytes 1081352 | tf_op jit(solution)/shard_map/ppermute | solution.py:282
  26.4 16.8 %collective-permute-start.32 = (bf16[176,1024]{1,0:T(8,128)(2,1)S(1)}, bf16[176,1024]{1,0:T(8,128)(2,1)S(1)}, u32[]{:S(2)}, u32[]{:S(2)}) collective-permute-start(bf16[176,1024]{1,0:T(8,128)(2,1)S(1)} %collective-permute-done.23.refs_1_.refs_2_), channel_id=1, source_target_pairs={{16,0},{8,1},{24,8},{0,9},{17,16},{9,17},{25,24},{1,25},{18,2},{10... | collective-permute-start | bytes 1081352 | tf_op jit(solution)/shard_map/ppermute | solution.py:285
  26.7 16.6 %collective-permute-start.31 = (bf16[176,1024]{1,0:T(8,128)(2,1)S(1)}, bf16[176,1024]{1,0:T(8,128)(2,1)}, u32[]{:S(2)}, u32[]{:S(2)}) collective-permute-start(bf16[176,1024]{1,0:T(8,128)(2,1)S(1)} %collective-permute-done.23.refs_1_.refs_2_), channel_id=1, source_target_pairs={{1,0},{17,1},{9,8},{25,9},{0,16},{16,17},{8,24},{24,25},{3,2},{19,... | collective-permute-start | bytes 1081352 | tf_op jit(solution)/shard_map/ppermute | solution.py:285
  27.9 0.7 copy-start.2
  28.6 18.9 %copy-start.3 = (bf16[176,1024]{1,0:T(8,128)(2,1)S(1)}, bf16[176,1024]{1,0:T(8,128)(2,1)}, u32[]{:S(2)}) copy-start(bf16[176,1024]{1,0:T(8,128)(2,1)} %copy-done.2) | copy-start | bytes 1081348
  29.5 13.7 %all-to-all-start.1 = ((s32[32,1,256]{2,1,0:T(1,128)}), s32[32,1,256]{2,1,0:T(1,128)S(1)}, u32[]{:S(2)}, u32[]{:S(2)}) async-start(s32[32,1,256]{2,1,0:T(1,128)} %all_to_all.14), calls=%async_computation.1 | async-start | bytes 65536 | tf_op jit(solution)/shard_map/all_to_all | solution.py:324
  33.7 13.8 %collective-permute-start.36 = (bf16[176,1024]{1,0:T(8,128)(2,1)S(1)}, bf16[176,1024]{1,0:T(8,128)(2,1)}, u32[]{:S(2)}, u32[]{:S(2)}) collective-permute-start(bf16[176,1024]{1,0:T(8,128)(2,1)S(1)} %collective-permute-done.28.refs_2_.refs_3_), channel_id=1, source_target_pairs={{16,0},{8,1},{24,8},{0,9},{17,16},{9,17},{25,24},{1,25},{18,2},{10... | collective-permute-start | bytes 1081352 | tf_op jit(solution)/shard_map/ppermute | solution.py:285
  33.8 13.7 %collective-permute-start.34 = (bf16[176,1024]{1,0:T(8,128)(2,1)S(1)}, bf16[176,1024]{1,0:T(8,128)(2,1)}, u32[]{:S(2)}, u32[]{:S(2)}) collective-permute-start(bf16[176,1024]{1,0:T(8,128)(2,1)S(1)} %collective-permute-done.28.refs_2_.refs_3_), channel_id=1, source_target_pairs={{1,0},{17,1},{9,8},{25,9},{0,16},{16,17},{8,24},{24,25},{3,2},{19,... | collective-permute-start | bytes 1081352 | tf_op jit(solution)/shard_map/ppermute | solution.py:285
  36.4 9.7 %collective-permute-start.30 = (bf16[176,1024]{1,0:T(8,128)(2,1)S(1)}, bf16[176,1024]{1,0:T(8,128)(2,1)}, u32[]{:S(2)}, u32[]{:S(2)}) collective-permute-start(bf16[176,1024]{1,0:T(8,128)(2,1)S(1)} %collective-permute-done.28.refs_2_.refs_3_), channel_id=1, source_target_pairs={{8,0},{9,1},{0,8},{1,9},{24,16},{25,17},{16,24},{17,25},{10,2},{11... | collective-permute-start | bytes 1081352 | tf_op jit(solution)/shard_map/ppermute | solution.py:285
  43.2 2.9 %copy-start.4 = (bf16[176,1024]{1,0:T(8,128)(2,1)}, bf16[176,1024]{1,0:T(8,128)(2,1)S(1)}, u32[]{:S(2)}) copy-start(bf16[176,1024]{1,0:T(8,128)(2,1)S(1)} %collective-permute-done.32.refs_10_.refs_14_) | copy-start | bytes 1081348
  43.2 10.4 %collective-permute-start.37 = (bf16[176,1024]{1,0:T(8,128)(2,1)}, bf16[176,1024]{1,0:T(8,128)(2,1)}, u32[]{:S(2)}, u32[]{:S(2)}) collective-permute-start(bf16[176,1024]{1,0:T(8,128)(2,1)} %collective-permute-done.29.refs_4_), channel_id=1, source_target_pairs={{16,0},{8,1},{24,8},{0,9},{17,16},{9,17},{25,24},{1,25},{18,2},{10... | collective-permute-start | bytes 1081352 | tf_op jit(solution)/shard_map/ppermute | solution.py:285
  44.4 9.6 %collective-permute-start.35 = (bf16[176,1024]{1,0:T(8,128)(2,1)}, bf16[176,1024]{1,0:T(8,128)(2,1)}, u32[]{:S(2)}, u32[]{:S(2)}) collective-permute-start(bf16[176,1024]{1,0:T(8,128)(2,1)} %collective-permute-done.29.refs_4_), channel_id=1, source_target_pairs={{1,0},{17,1},{9,8},{25,9},{0,16},{16,17},{8,24},{24,25},{3,2},{19,... | collective-permute-start | bytes 1081352 | tf_op jit(solution)/shard_map/ppermute | solution.py:285
  46.1 7.9 %collective-permute-start.33 = (bf16[176,1024]{1,0:T(8,128)(2,1)}, bf16[176,1024]{1,0:T(8,128)(2,1)}, u32[]{:S(2)}, u32[]{:S(2)}) collective-permute-start(bf16[176,1024]{1,0:T(8,128)(2,1)} %collective-permute-done.29.refs_4_), channel_id=1, source_target_pairs={{8,0},{9,1},{0,8},{1,9},{24,16},{25,17},{16,24},{17,25},{10,2},{11... | collective-permute-start | bytes 1081352 | tf_op jit(solution)/shard_map/ppermute | solution.py:285
  47.5 1.0 %copy-start.5 = (bf16[176,1024]{1,0:T(8,128)(2,1)S(1)}, bf16[176,1024]{1,0:T(8,128)(2,1)}, u32[]{:S(2)}) copy-start(bf16[176,1024]{1,0:T(8,128)(2,1)} %copy-done.4) | copy-start | bytes 1081348
  60.8 7.8 %collective-permute-start.38 = (f32[4,128]{1,0:T(4,128)S(1)}, f32[4,128]{1,0:T(4,128)S(1)}, u32[]{:S(2)}, u32[]{:S(2)}) collective-permute-start(f32[4,128]{1,0:T(4,128)S(1)} %get-tuple-element.114), channel_id=1, source_target_pairs={{0,0},{1,1},{8,2},{9,3},{16,4},{17,5},{24,6},{25,7},{2,8},{3,9},{1... | collective-permute-start | bytes 6152 | tf_op jit(solution)/shard_map/ppermute | solution.py:389
  66.8 5.4 %collective-permute-start.39 = (f32[4,128]{1,0:T(4,128)S(1)}, f32[4,128]{1,0:T(4,128)S(1)}, u32[]{:S(2)}, u32[]{:S(2)}) collective-permute-start(f32[4,128]{1,0:T(4,128)S(1)} %get-tuple-element.115), channel_id=1, source_target_pairs={{0,1},{1,2},{8,3},{9,4},{16,5},{17,6},{24,7},{25,0},{2,9},{3,10},{... | collective-permute-start | bytes 6152 | tf_op jit(solution)/shard_map/ppermute | solution.py:389
  67.8 8.9 %collective-permute-start.40 = (f32[4,128]{1,0:T(4,128)S(1)}, f32[4,128]{1,0:T(4,128)S(1)}, u32[]{:S(2)}, u32[]{:S(2)}) collective-permute-start(f32[4,128]{1,0:T(4,128)S(1)} %get-tuple-element.116), channel_id=1, source_target_pairs={{0,2},{1,3},{8,4},{9,5},{16,6},{17,7},{24,0},{25,1},{2,10},{3,11},... | collective-permute-start | bytes 6152 | tf_op jit(solution)/shard_map/ppermute | solution.py:389
  67.8 10.4 %collective-permute-start.41 = (f32[4,128]{1,0:T(4,128)S(1)}, f32[4,128]{1,0:T(4,128)S(1)}, u32[]{:S(2)}, u32[]{:S(2)}) collective-permute-start(f32[4,128]{1,0:T(4,128)S(1)} %get-tuple-element.117), channel_id=1, source_target_pairs={{0,3},{1,4},{8,5},{9,6},{16,7},{17,0},{24,1},{25,2},{2,11},{3,12},... | collective-permute-start | bytes 6152 | tf_op jit(solution)/shard_map/ppermute | solution.py:389
  67.8 10.5 %collective-permute-start.42 = (f32[4,128]{1,0:T(4,128)S(1)}, f32[4,128]{1,0:T(4,128)S(1)}, u32[]{:S(2)}, u32[]{:S(2)}) collective-permute-start(f32[4,128]{1,0:T(4,128)S(1)} %get-tuple-element.118), channel_id=1, source_target_pairs={{0,4},{1,5},{8,6},{9,7},{16,0},{17,1},{24,2},{25,3},{2,12},{3,13},... | collective-permute-start | bytes 6152 | tf_op jit(solution)/shard_map/ppermute | solution.py:389
  68.7 9.6 %collective-permute-start.43 = (f32[4,128]{1,0:T(4,128)S(1)}, f32[4,128]{1,0:T(4,128)S(1)}, u32[]{:S(2)}, u32[]{:S(2)}) collective-permute-start(f32[4,128]{1,0:T(4,128)S(1)} %get-tuple-element.119), channel_id=1, source_target_pairs={{0,5},{1,6},{8,7},{9,0},{16,1},{17,2},{24,3},{25,4},{2,13},{3,14},... | collective-permute-start | bytes 6152 | tf_op jit(solution)/shard_map/ppermute | solution.py:389
  72.2 6.1 %collective-permute-start.44 = (f32[4,128]{1,0:T(4,128)S(1)}, f32[4,128]{1,0:T(4,128)S(1)}, u32[]{:S(2)}, u32[]{:S(2)}) collective-permute-start(f32[4,128]{1,0:T(4,128)S(1)} %get-tuple-element.120), channel_id=1, source_target_pairs={{0,6},{1,7},{8,0},{9,1},{16,2},{17,3},{24,4},{25,5},{2,14},{3,15},... | collective-permute-start | bytes 6152 | tf_op jit(solution)/shard_map/ppermute | solution.py:389
  76.8 6.6 %collective-permute-start.45 = (f32[4,128]{1,0:T(4,128)S(1)}, f32[4,128]{1,0:T(4,128)S(1)}, u32[]{:S(2)}, u32[]{:S(2)}) collective-permute-start(f32[4,128]{1,0:T(4,128)S(1)} %get-tuple-element.121), channel_id=1, source_target_pairs={{0,7},{1,0},{8,1},{9,2},{16,3},{17,4},{24,5},{25,6},{2,15},{3,8},{... | collective-permute-start | bytes 6152 | tf_op jit(solution)/shard_map/ppermute | solution.py:389

commit v6 on v4

--- a/solution.py
+++ b/solution.py
@@ -162,14 +162,18 @@
     return need
 
 
-def early_kernel(pairs, count, *refs):
+def early_kernel(pairs, count, early, *refs):
     *chunks, label_ref, label_col_ref, out_ref, blocks, sems = refs
     need = loader(chunks, count, blocks, sems)
-    best = [Best(jnp.full((1, blocks.shape[1]), -1.0, jnp.float32)) for _ in range(count)]
+    best = [Best(jnp.full((1, early), -1.0, jnp.float32)) for _ in range(count)]
     for j, k in pairs:
         need(j, k)
         sims = similar(
-            blocks[j], blocks[k], label_col_ref[:, j : j + 1], label_ref[k : k + 1, :], 0 if j == k else None
+            blocks[j, :early],
+            blocks[k, :early],
+            label_col_ref[:, j : j + 1],
+            label_ref[k : k + 1, :],
+            0 if j == k else None,
         )
         best[k].add_row(column_max(sims))
         if j != k:
@@ -181,10 +185,10 @@
 def late_kernel(pairs, count, group_size, *refs):
     plane_ref, *chunks, best_ref, place_ref, last_place_ref, label_ref, last_label_ref, label_col_ref, out_ref, blocks, sems = refs
     need = loader(chunks, count, blocks, sems)
-    cap = chunks[0].shape[0]
-    first = blocks.shape[1] - cap
+    first = best_ref.shape[1]
+    rest = blocks.shape[1] - first
     early = [Best(best_ref[j : j + 1, :]) for j in range(count)]
-    late = [Best(jnp.full((1, cap), -1.0, jnp.float32)) for _ in range(count)]
+    late = [Best(jnp.full((1, rest), -1.0, jnp.float32)) for _ in range(count)]
     for j, k in pairs:
         need(j, k)
         sims = similar(
@@ -292,9 +296,7 @@
         near = after(part, own[k + 1]) if k > 1 else part
         rounds.append([inside(near, 1), *[inside(part, j) for j in range(2, count)]])
 
-    last = after(own[-1], *rounds[-2])
-    rounds.append([inside(after(last, rounds[-1][0]), 1), *[inside(last, j) for j in range(2, count)]])
-    place = after(place, rounds[1][0])
+    place = after(place, *rounds[0])
 
     planes_i = jnp.arange(groups, dtype=jnp.int32)
     swap = (planes_i[:, None] ^ planes_i[None, :]) == plane
@@ -318,6 +320,8 @@
     )
     facts = jnp.broadcast_to(facts[None, :, None, :], (n_row, groups, wide, length)).reshape(devs, length)
     facts = lax.all_to_all(facts, AXES, split_axis=0, concat_axis=0, tiled=True)
+    last = after(own[-1], *rounds[-2], rounds[-1][1])
+    rounds.append([inside(after(last, rounds[-1][0], facts), 1), *[inside(last, j) for j in range(2, count)]])
     over = jnp.max(facts[:, cap + LEVELS]) > 0
     facts = facts.reshape(n_row, groups, wide, length)
 
@@ -333,7 +337,7 @@
     labels = jnp.sum((places[:, None, :] >= ends[None, :, None]).astype(jnp.int32), axis=1)
     labels = jnp.where(places < group_size, labels, -1)
 
-    early = slots - cap
+    early = (slots - cap) // 256 * 256
     label_cols = labels.T
     facts = places[:, :early], places[:, early:], labels[:, :early], labels[:, early:], label_cols[:early], label_cols
     place, last_place, label, last_label, label_col, label_cols = facts
@@ -349,7 +353,7 @@
 
     limit = 8 + (2 * count * slots * width + 5 * area) // 2**20
     first_best = pl.pallas_call(
-        functools.partial(early_kernel, pairs, count),
+        functools.partial(early_kernel, pairs, count, early),
         out_shape=jax.ShapeDtypeStruct((count, early), jnp.float32),
         in_specs=[any_space] * (count * (groups - 1)) + [VMEM] * 2,
         out_specs=VMEM,

time: 77 us -> 83.2 us (1.081)
  waiting for transfers between devices: 23.9 us -> 30.7 us
  Pallas kernels: 19.4 us -> 16.1 us
  starting transfers between devices: 24.7 us -> 27 us
    ppermute x12, waiting for transfers between devices: 2.78 us -> 19.4 us  [inside(): lax.ppermute(part, AXES, [(device(int(held[j, i]), h), device(i, h)) for...]
    ppermute x3, waiting for transfers between devices: 11.9 us -> 4.01 us  [across(): lax.ppermute(part, AXES, [(device(i, h ^ k), device(i, h)) for i, h in pl...]
    pallas_call x1, Pallas kernels: 7.16 us -> 4.95 us  [best_matches(): pl.pallas_call(functools.partial(early_kernel, pairs, count, early), out_...]
    all_to_all x1, starting transfers between devices: 4.57 us -> 6.43 us  [best_matches(): lax.all_to_all(best.reshape(devs, -1, 128), AXES, split_axis=0, concat_ax...]
    all_to_all x1, waiting for transfers between devices: 3.31 us -> 1.57 us  [best_matches(): facts = lax.all_to_all(facts, AXES, split_axis=0, concat_axis=0, tiled=True)]
    ppermute x3, starting transfers between devices: 7.81 us -> 9.3 us  [across(): lax.ppermute(part, AXES, [(device(i, h ^ k), device(i, h)) for i, h in pl...]
    all_to_all x1, starting transfers between devices: 3.42 us -> 2.55 us  [best_matches(): facts = lax.all_to_all(facts, AXES, split_axis=0, concat_axis=0, tiled=True)]
    unnamed x20 -> x16, local copies, waits for them, and re-layouts: 2.4 us -> 3.13 us
  transfers between devices with their start and end apart: 17 -> 17, of which waited for: 7 -> 9; matrix products, arithmetic and copies ran while one was open for 5% -> 5% of each run, Pallas kernels for 11% -> 7%
where the time goes in v6:
time: 83.2 us; the launch traced here: 83 us
  waiting for transfers between devices  30.7 us (37%)
  starting transfers between devices  27 us (32%)
  Pallas kernels  16.1 us (19%)
  local copies, waits for them, and re-layouts  4.93 us (6%)
  other arithmetic  2.62 us (3%)
  between operations  1.59 us (2%)
    ppermute x12, waiting for transfers between devices, inside(): lax.ppermute(part, AXES, [(device(int(held[j, i]), h), device(i, h)) for...  19.4 us
    ppermute x3, starting transfers between devices, across(): lax.ppermute(part, AXES, [(device(i, h ^ k), device(i, h)) for i, h in pl...  9.3 us
    ppermute x12, starting transfers between devices, inside(): lax.ppermute(part, AXES, [(device(int(held[j, i]), h), device(i, h)) for...  8.76 us
    pallas_call x1, Pallas kernels, best_matches(): pl.pallas_call(functools.partial(late_kernel, pairs, count, group_size),...  7.27 us
    all_to_all x1, starting transfers between devices, best_matches(): lax.all_to_all(best.reshape(devs, -1, 128), AXES, split_axis=0, concat_ax...  6.43 us
    all_to_all x1, waiting for transfers between devices, best_matches(): lax.all_to_all(best.reshape(devs, -1, 128), AXES, split_axis=0, concat_ax...  5.74 us
    pallas_call x1, Pallas kernels, best_matches(): pl.pallas_call(functools.partial(early_kernel, pairs, count, early), out_...  4.95 us
    ppermute x3, waiting for transfers between devices, across(): lax.ppermute(part, AXES, [(device(i, h ^ k), device(i, h)) for i, h in pl...  4.01 us
  transfers between devices with their start and end apart: 17, of which 9 were waited for; matrix products, arithmetic and copies ran while one was open for 5% of the time, Pallas kernels for 7%

profile of v6, /device:TPU:0, one launch (start us, length us, event | category | flops | bytes accessed | tf_op | source)
XLA Modules:
  0.0 83.0 jit_solution(2129879695156104451)
XLA Ops:
  0.0 3.3 %shard_map.57 = (bf16[512,1024]{1,0:T(8,128)(2,1)S(1)}, s32[1,512]{1,0:T(1,128)S(1)}, bf16[176,1024]{1,0:T(8,128)(2,1)S(1)}, bf16[176,1024]{1,0:T(8,128)(2,1)}, bf16[176,1024]{1,0:T(8,128)(2,1)}) custom-call(s32[1]{0:T(128)} %bitcast.13.plane_ref.refs_0_, s32[1,512]{1,0:T(1,128)} %bitcast.38, f32[512,1024]{1,0:T(8,128)} %emb_ref.1), custom_call_target="tpu_custom_call" | custom-call | tf_op jit(solution)/shard_map/pallas_call | solution.py:259
  3.4 3.0 %collective-permute-start.18 = (bf16[176,1024]{1,0:T(8,128)(2,1)}, bf16[176,1024]{1,0:T(8,128)(2,1)S(1)}, u32[]{:S(2)}, u32[]{:S(2)}) collective-permute-start(bf16[176,1024]{1,0:T(8,128)(2,1)} %get-tuple-element.61), channel_id=1, source_target_pairs={{2,0},{3,1},{10,8},{11,9},{18,16},{19,17},{26,24},{27,25},{0,2},{1... | collective-permute-start | bytes 1081352 | tf_op jit(solution)/shard_map/ppermute | solution.py:280
  6.4 2.6 %collective-permute-start.19 = (bf16[176,1024]{1,0:T(8,128)(2,1)}, bf16[176,1024]{1,0:T(8,128)(2,1)S(1)}, u32[]{:S(2)}, u32[]{:S(2)}) collective-permute-start(bf16[176,1024]{1,0:T(8,128)(2,1)} %get-tuple-element.62), channel_id=1, source_target_pairs={{4,0},{5,1},{12,8},{13,9},{20,16},{21,17},{28,24},{29,25},{6,2},{7... | collective-permute-start | bytes 1081352 | tf_op jit(solution)/shard_map/ppermute | solution.py:280
  9.0 0.0 collective-permute-start.15
  9.0 0.1 convert_reduce_fusion.5
  9.1 0.6 reduce_max.46
  10.4 0.1 convert_reduce_fusion.4
  10.6 0.1 collective-permute-done.15.refs_3_.refs_5_
  10.6 1.6 %collective-permute-start.17 = (bf16[176,1024]{1,0:T(8,128)(2,1)S(1)}, bf16[176,1024]{1,0:T(8,128)(2,1)S(1)}, u32[]{:S(2)}, u32[]{:S(2)}) collective-permute-start(bf16[176,1024]{1,0:T(8,128)(2,1)S(1)} %get-tuple-element.59.refs_0_.refs_1_), channel_id=1, source_target_pairs={{16,0},{8,1},{24,8},{0,9},{17,16},{9,17},{25,24},{1,25},{18,2},{10... | collective-permute-start | bytes 1081352 | tf_op jit(solution)/shard_map/ppermute | solution.py:283
  12.2 0.4 collective-permute-start.16
  12.7 0.1 pad_add_fusion.1
  12.8 0.1 pad.7.clone
  12.8 0.1 pad.6.clone
  12.9 0.5 shard_map.58
  13.4 0.7 copy-done.9
  14.2 0.1 select_reduce_fusion.5
  14.3 0.1 fusion.7
  14.3 7.1 %collective-permute-done.17.refs_9_.refs_13_ = bf16[176,1024]{1,0:T(8,128)(2,1)S(1)} collective-permute-done((bf16[176,1024]{1,0:T(8,128)(2,1)S(1)}, bf16[176,1024]{1,0:T(8,128)(2,1)S(1)}, u32[]{:S(2)}, u32[]{:S(2)}) %collective-permute-start.17) | collective-permute-done | bytes 360480 | tf_op jit(solution)/shard_map/ppermute | solution.py:283
  21.4 1.2 %collective-permute-done.16.refs_6_.refs_9_ = bf16[176,1024]{1,0:T(8,128)(2,1)S(1)} collective-permute-done((bf16[176,1024]{1,0:T(8,128)(2,1)S(1)}, bf16[176,1024]{1,0:T(8,128)(2,1)S(1)}, u32[]{:S(2)}, u32[]{:S(2)}) %collective-permute-start.16) | collective-permute-done | bytes 360480 | tf_op jit(solution)/shard_map/ppermute | solution.py:283
  22.6 0.1 broadcast_in_dim.172
  22.7 0.1 select_reduce_fusion.4
  22.8 0.6 all_to_all.21
  23.5 2.5 %all-to-all-start.2 = ((s32[32,1,256]{2,1,0:T(1,128)}), s32[32,1,256]{2,1,0:T(1,128)S(1)}, u32[]{:S(2)}, u32[]{:S(2)}) async-start(s32[32,1,256]{2,1,0:T(1,128)} %all_to_all.21), calls=%async_computation.2 | async-start | bytes 65536 | tf_op jit(solution)/shard_map/all_to_all | solution.py:322
  26.0 3.7 %collective-permute-start.20 = (bf16[176,1024]{1,0:T(8,128)(2,1)}, bf16[176,1024]{1,0:T(8,128)(2,1)S(1)}, u32[]{:S(2)}, u32[]{:S(2)}) collective-permute-start(bf16[176,1024]{1,0:T(8,128)(2,1)} %copy-done.9), channel_id=1, source_target_pairs={{6,0},{7,1},{14,8},{15,9},{22,16},{23,17},{30,24},{31,25},{4,2},{5... | collective-permute-start | bytes 1081352 | tf_op jit(solution)/shard_map/ppermute | solution.py:280
  29.7 0.0 collective-permute-done.18.refs_1_.refs_2_
  29.7 1.0 %collective-permute-start.24 = (bf16[176,1024]{1,0:T(8,128)(2,1)S(1)}, bf16[176,1024]{1,0:T(8,128)(2,1)S(1)}, u32[]{:S(2)}, u32[]{:S(2)}) collective-permute-start(bf16[176,1024]{1,0:T(8,128)(2,1)S(1)} %collective-permute-done.18.refs_1_.refs_2_), channel_id=1, source_target_pairs={{16,0},{8,1},{24,8},{0,9},{17,16},{9,17},{25,24},{1,25},{18,2},{10... | collective-permute-start | bytes 1081352 | tf_op jit(solution)/shard_map/ppermute | solution.py:283
  30.7 1.1 %collective-permute-start.23 = (bf16[176,1024]{1,0:T(8,128)(2,1)S(1)}, bf16[176,1024]{1,0:T(8,128)(2,1)}, u32[]{:S(2)}, u32[]{:S(2)}) collective-permute-start(bf16[176,1024]{1,0:T(8,128)(2,1)S(1)} %collective-permute-done.18.refs_1_.refs_2_), channel_id=1, source_target_pairs={{1,0},{17,1},{9,8},{25,9},{0,16},{16,17},{8,24},{24,25},{3,2},{19,... | collective-permute-start | bytes 1081352 | tf_op jit(solution)/shard_map/ppermute | solution.py:283
  31.8 0.0 collective-permute-start.21
  31.8 1.6 %all-to-all-done.2 = s32[32,1,256]{2,1,0:T(1,128)S(1)} async-done(((s32[32,1,256]{2,1,0:T(1,128)}), s32[32,1,256]{2,1,0:T(1,128)S(1)}, u32[]{:S(2)}, u32[]{:S(2)}) %all-to-all-start.2) | async-done | bytes 32800 | tf_op jit(solution)/shard_map/all_to_all | solution.py:322
  33.3 0.1 reduce.4
  33.5 0.1 broadcast_in_dim.181
  33.6 0.1 select_reduce_fusion.3
  33.7 0.1 reshape.175
  33.8 0.1 mul.54
  33.9 0.1 multiply_reduce_fusion.1
  34.0 0.0 collective-permute-done.19.refs_2_.refs_3_
  34.0 0.0 collective-permute-done.21.refs_4_.refs_6_
  34.0 1.0 %collective-permute-start.25 = (bf16[176,1024]{1,0:T(8,128)(2,1)S(1)}, bf16[176,1024]{1,0:T(8,128)(2,1)}, u32[]{:S(2)}, u32[]{:S(2)}) collective-permute-start(bf16[176,1024]{1,0:T(8,128)(2,1)S(1)} %collective-permute-done.19.refs_2_.refs_3_), channel_id=1, source_target_pairs={{1,0},{17,1},{9,8},{25,9},{0,16},{16,17},{8,24},{24,25},{3,2},{19,... | collective-permute-start | bytes 1081352 | tf_op jit(solution)/shard_map/ppermute | solution.py:283
  35.0 4.0 %collective-permute-done.20.refs_4_ = bf16[176,1024]{1,0:T(8,128)(2,1)S(1)} collective-permute-done((bf16[176,1024]{1,0:T(8,128)(2,1)}, bf16[176,1024]{1,0:T(8,128)(2,1)S(1)}, u32[]{:S(2)}, u32[]{:S(2)}) %collective-permute-start.20) | collective-permute-done | bytes 360480 | tf_op jit(solution)/shard_map/ppermute | solution.py:280
  39.0 0.0 collective-permute-start.22
  39.1 0.2 copy.85
  39.3 0.1 fusion.4
  39.4 1.7 %collective-permute-start.28 = (bf16[176,1024]{1,0:T(8,128)(2,1)S(1)}, bf16[176,1024]{1,0:T(8,128)(2,1)}, u32[]{:S(2)}, u32[]{:S(2)}) collective-permute-start(bf16[176,1024]{1,0:T(8,128)(2,1)S(1)} %collective-permute-done.19.refs_2_.refs_3_), channel_id=1, source_target_pairs={{16,0},{8,1},{24,8},{0,9},{17,16},{9,17},{25,24},{1,25},{18,2},{10... | collective-permute-start | bytes 1081352 | tf_op jit(solution)/shard_map/ppermute | solution.py:283
  41.1 0.1 convert_reduce_fusion.3
  41.2 0.2 copy.86
  41.4 0.0 collective-permute-done.24.refs_10_.refs_14_
  41.4 0.7 copy-done.5
  42.2 0.0 collective-permute-done.23.refs_7_.refs_10_
  42.2 7.3 %collective-permute-done.25.refs_8_.refs_11_ = bf16[176,1024]{1,0:T(8,128)(2,1)} collective-permute-done((bf16[176,1024]{1,0:T(8,128)(2,1)S(1)}, bf16[176,1024]{1,0:T(8,128)(2,1)}, u32[]{:S(2)}, u32[]{:S(2)}) %collective-permute-start.25) | collective-permute-done | bytes 360480 | tf_op jit(solution)/shard_map/ppermute | solution.py:283
  49.5 0.9 %collective-permute-start.29 = (bf16[176,1024]{1,0:T(8,128)(2,1)S(1)}, bf16[176,1024]{1,0:T(8,128)(2,1)}, u32[]{:S(2)}, u32[]{:S(2)}) collective-permute-start(bf16[176,1024]{1,0:T(8,128)(2,1)S(1)} %collective-permute-done.20.refs_4_), channel_id=1, source_target_pairs={{16,0},{8,1},{24,8},{0,9},{17,16},{9,17},{25,24},{1,25},{18,2},{10... | collective-permute-start | bytes 1081352 | tf_op jit(solution)/shard_map/ppermute | solution.py:283
  50.4 1.2 %collective-permute-start.27 = (bf16[176,1024]{1,0:T(8,128)(2,1)S(1)}, bf16[176,1024]{1,0:T(8,128)(2,1)}, u32[]{:S(2)}, u32[]{:S(2)}) collective-permute-start(bf16[176,1024]{1,0:T(8,128)(2,1)S(1)} %collective-permute-done.20.refs_4_), channel_id=1, source_target_pairs={{1,0},{17,1},{9,8},{25,9},{0,16},{16,17},{8,24},{24,25},{3,2},{19,... | collective-permute-start | bytes 1081352 | tf_op jit(solution)/shard_map/ppermute | solution.py:283
  51.5 0.0 collective-permute-done.22.refs_5_.refs_7_
  51.5 0.0 collective-permute-start.26
  51.6 0.1 copy.94.refs_21_
  51.7 0.1 copy.87.refs_12_.refs_20_
  51.9 1.0 %copy-done.6 = bf16[176,1024]{1,0:T(8,128)(2,1)S(1)} copy-done((bf16[176,1024]{1,0:T(8,128)(2,1)S(1)}, bf16[176,1024]{1,0:T(8,128)(2,1)}, u32[]{:S(2)}) %copy-start.6) | copy-done | bytes 360472
  52.9 5.0 %shard_map.59.refs_17_ = f32[4,512]{1,0:T(4,128)S(1)} custom-call(bf16[176,1024]{1,0:T(8,128)(2,1)S(1)} %get-tuple-element.59.refs_0_.refs_1_, bf16[176,1024]{1,0:T(8,128)(2,1)S(1)} %collective-permute-done.18.refs_1_.refs_2_, bf16[176,1024]{1,0:T(8,128)(2,1)S(1)} %collective-permute-done.19.refs_2_.refs_3_, ...), custom_call_target="tpu_custom_call" | custom-call | flops 2684354560 | bytes 4194304 | tf_op jit(solution)/shard_map/pallas_call | solution.py:355
  57.8 1.9 %collective-permute-done.29.refs_16_ = bf16[176,1024]{1,0:T(8,128)(2,1)} collective-permute-done((bf16[176,1024]{1,0:T(8,128)(2,1)S(1)}, bf16[176,1024]{1,0:T(8,128)(2,1)}, u32[]{:S(2)}, u32[]{:S(2)}) %collective-permute-start.29) | collective-permute-done | bytes 360480 | tf_op jit(solution)/shard_map/ppermute | solution.py:283
  59.7 1.8 %collective-permute-done.27.refs_12_ = bf16[176,1024]{1,0:T(8,128)(2,1)} collective-permute-done((bf16[176,1024]{1,0:T(8,128)(2,1)S(1)}, bf16[176,1024]{1,0:T(8,128)(2,1)}, u32[]{:S(2)}, u32[]{:S(2)}) %collective-permute-start.27) | collective-permute-done | bytes 360480 | tf_op jit(solution)/shard_map/ppermute | solution.py:283
  61.5 7.3 %shard_map.60 = f32[4,8,4,128]{3,2,1,0:T(4,128)} custom-call(s32[1]{0:T(128)} %bitcast.13.plane_ref.refs_0_, bf16[176,1024]{1,0:T(8,128)(2,1)S(1)} %get-tuple-element.59.refs_0_.refs_1_, bf16[176,1024]{1,0:T(8,128)(2,1)S(1)} %collective-permute-done.18.refs_1_.refs_2_, bf16[176,1024]{1,0:T(8,128)(2,1)S(1)} %collective-permute-done.19.refs_2_.refs_3_, ...), custom_call_target="tpu_custom_call" | custom-call | tf_op jit(solution)/shard_map/pallas_call | solution.py:366
  68.8 6.4 %all-to-all-start.3 = ((f32[32,4,128]{2,1,0:T(4,128)}), f32[32,4,128]{2,1,0:T(4,128)S(1)}, u32[]{:S(2)}, u32[]{:S(2)}) async-start(f32[32,4,128]{2,1,0:T(4,128)} %bitcast.19), calls=%async_computation.3 | async-start | bytes 131072 | tf_op jit(solution)/shard_map/all_to_all | solution.py:384
  75.2 0.7 slice_reduce_fusion
  76.6 5.7 %all-to-all-done.3 = f32[32,4,128]{2,1,0:T(4,128)S(1)} async-done(((f32[32,4,128]{2,1,0:T(4,128)}), f32[32,4,128]{2,1,0:T(4,128)S(1)}, u32[]{:S(2)}, u32[]{:S(2)}) %all-to-all-start.3) | async-done | bytes 65568 | tf_op jit(solution)/shard_map/all_to_all | solution.py:384
  82.4 0.6 copy-done.13
  (34 shorter events, 0.3 us)
Async XLA Ops:
  0.0 14.2 %copy-start.12 = (s32[4,8]{1,0:T(4,128)S(1)}, s32[4,8]{1,0:T(4,128)}, u32[]{:S(2)}) copy-start(s32[4,8]{1,0:T(4,128)} %constant.109.clone) | copy-start | bytes 388
  0.0 9.0 %copy-start.10 = (s32[512]{0:T(512)S(1)}, s32[512]{0:T(512)}, u32[]{:S(2)}) copy-start(s32[512]{0:T(512)} %param.8) | copy-start | bytes 6148
  0.0 10.4 %copy-start.11 = (s32[1,512]{1,0:T(1,128)S(1)}, s32[1,512]{1,0:T(1,128)}, u32[]{:S(2)}) copy-start(s32[1,512]{1,0:T(1,128)} %param.9) | copy-start | bytes 6148
  3.4 26.4 %collective-permute-start.18 = (bf16[176,1024]{1,0:T(8,128)(2,1)}, bf16[176,1024]{1,0:T(8,128)(2,1)S(1)}, u32[]{:S(2)}, u32[]{:S(2)}) collective-permute-start(bf16[176,1024]{1,0:T(8,128)(2,1)} %get-tuple-element.61), channel_id=1, source_target_pairs={{2,0},{3,1},{10,8},{11,9},{18,16},{19,17},{26,24},{27,25},{0,2},{1... | collective-permute-start | bytes 1081352 | tf_op jit(solution)/shard_map/ppermute | solution.py:280
  6.4 27.7 %collective-permute-start.19 = (bf16[176,1024]{1,0:T(8,128)(2,1)}, bf16[176,1024]{1,0:T(8,128)(2,1)S(1)}, u32[]{:S(2)}, u32[]{:S(2)}) collective-permute-start(bf16[176,1024]{1,0:T(8,128)(2,1)} %get-tuple-element.62), channel_id=1, source_target_pairs={{4,0},{5,1},{12,8},{13,9},{20,16},{21,17},{28,24},{29,25},{6,2},{7... | collective-permute-start | bytes 1081352 | tf_op jit(solution)/shard_map/ppermute | solution.py:280
  9.0 1.7 %collective-permute-start.15 = (bf16[176,1024]{1,0:T(8,128)(2,1)S(1)}, bf16[176,1024]{1,0:T(8,128)(2,1)S(1)}, u32[]{:S(2)}, u32[]{:S(2)}) collective-permute-start(bf16[176,1024]{1,0:T(8,128)(2,1)S(1)} %get-tuple-element.59.refs_0_.refs_1_), channel_id=1, source_target_pairs={{8,0},{9,1},{0,8},{1,9},{24,16},{25,17},{16,24},{17,25},{10,2},{11... | collective-permute-start | bytes 1081352 | tf_op jit(solution)/shard_map/ppermute | solution.py:283
  10.6 10.8 %collective-permute-start.17 = (bf16[176,1024]{1,0:T(8,128)(2,1)S(1)}, bf16[176,1024]{1,0:T(8,128)(2,1)S(1)}, u32[]{:S(2)}, u32[]{:S(2)}) collective-permute-start(bf16[176,1024]{1,0:T(8,128)(2,1)S(1)} %get-tuple-element.59.refs_0_.refs_1_), channel_id=1, source_target_pairs={{16,0},{8,1},{24,8},{0,9},{17,16},{9,17},{25,24},{1,25},{18,2},{10... | collective-permute-start | bytes 1081352 | tf_op jit(solution)/shard_map/ppermute | solution.py:283
  12.2 10.4 %collective-permute-start.16 = (bf16[176,1024]{1,0:T(8,128)(2,1)S(1)}, bf16[176,1024]{1,0:T(8,128)(2,1)S(1)}, u32[]{:S(2)}, u32[]{:S(2)}) collective-permute-start(bf16[176,1024]{1,0:T(8,128)(2,1)S(1)} %get-tuple-element.59.refs_0_.refs_1_), channel_id=1, source_target_pairs={{1,0},{17,1},{9,8},{25,9},{0,16},{16,17},{8,24},{24,25},{3,2},{19,... | collective-permute-start | bytes 1081352 | tf_op jit(solution)/shard_map/ppermute | solution.py:283
  13.4 0.7 copy-start.9
  23.5 9.9 %all-to-all-start.2 = ((s32[32,1,256]{2,1,0:T(1,128)}), s32[32,1,256]{2,1,0:T(1,128)S(1)}, u32[]{:S(2)}, u32[]{:S(2)}) async-start(s32[32,1,256]{2,1,0:T(1,128)} %all_to_all.21), calls=%async_computation.2 | async-start | bytes 65536 | tf_op jit(solution)/shard_map/all_to_all | solution.py:322
  26.0 13.0 %collective-permute-start.20 = (bf16[176,1024]{1,0:T(8,128)(2,1)}, bf16[176,1024]{1,0:T(8,128)(2,1)S(1)}, u32[]{:S(2)}, u32[]{:S(2)}) collective-permute-start(bf16[176,1024]{1,0:T(8,128)(2,1)} %copy-done.9), channel_id=1, source_target_pairs={{6,0},{7,1},{14,8},{15,9},{22,16},{23,17},{30,24},{31,25},{4,2},{5... | collective-permute-start | bytes 1081352 | tf_op jit(solution)/shard_map/ppermute | solution.py:280
  29.7 11.7 %collective-permute-start.24 = (bf16[176,1024]{1,0:T(8,128)(2,1)S(1)}, bf16[176,1024]{1,0:T(8,128)(2,1)S(1)}, u32[]{:S(2)}, u32[]{:S(2)}) collective-permute-start(bf16[176,1024]{1,0:T(8,128)(2,1)S(1)} %collective-permute-done.18.refs_1_.refs_2_), channel_id=1, source_target_pairs={{16,0},{8,1},{24,8},{0,9},{17,16},{9,17},{25,24},{1,25},{18,2},{10... | collective-permute-start | bytes 1081352 | tf_op jit(solution)/shard_map/ppermute | solution.py:283
  30.7 11.5 %collective-permute-start.23 = (bf16[176,1024]{1,0:T(8,128)(2,1)S(1)}, bf16[176,1024]{1,0:T(8,128)(2,1)}, u32[]{:S(2)}, u32[]{:S(2)}) collective-permute-start(bf16[176,1024]{1,0:T(8,128)(2,1)S(1)} %collective-permute-done.18.refs_1_.refs_2_), channel_id=1, source_target_pairs={{1,0},{17,1},{9,8},{25,9},{0,16},{16,17},{8,24},{24,25},{3,2},{19,... | collective-permute-start | bytes 1081352 | tf_op jit(solution)/shard_map/ppermute | solution.py:283
  31.8 2.3 %collective-permute-start.21 = (bf16[176,1024]{1,0:T(8,128)(2,1)S(1)}, bf16[176,1024]{1,0:T(8,128)(2,1)}, u32[]{:S(2)}, u32[]{:S(2)}) collective-permute-start(bf16[176,1024]{1,0:T(8,128)(2,1)S(1)} %collective-permute-done.18.refs_1_.refs_2_), channel_id=1, source_target_pairs={{8,0},{9,1},{0,8},{1,9},{24,16},{25,17},{16,24},{17,25},{10,2},{11... | collective-permute-start | bytes 1081352 | tf_op jit(solution)/shard_map/ppermute | solution.py:283
  34.0 15.4 %collective-permute-start.25 = (bf16[176,1024]{1,0:T(8,128)(2,1)S(1)}, bf16[176,1024]{1,0:T(8,128)(2,1)}, u32[]{:S(2)}, u32[]{:S(2)}) collective-permute-start(bf16[176,1024]{1,0:T(8,128)(2,1)S(1)} %collective-permute-done.19.refs_2_.refs_3_), channel_id=1, source_target_pairs={{1,0},{17,1},{9,8},{25,9},{0,16},{16,17},{8,24},{24,25},{3,2},{19,... | collective-permute-start | bytes 1081352 | tf_op jit(solution)/shard_map/ppermute | solution.py:283
  39.0 12.5 %collective-permute-start.22 = (bf16[176,1024]{1,0:T(8,128)(2,1)S(1)}, bf16[176,1024]{1,0:T(8,128)(2,1)}, u32[]{:S(2)}, u32[]{:S(2)}) collective-permute-start(bf16[176,1024]{1,0:T(8,128)(2,1)S(1)} %collective-permute-done.19.refs_2_.refs_3_), channel_id=1, source_target_pairs={{8,0},{9,1},{0,8},{1,9},{24,16},{25,17},{16,24},{17,25},{10,2},{11... | collective-permute-start | bytes 1081352 | tf_op jit(solution)/shard_map/ppermute | solution.py:283
  39.4 12.5 %collective-permute-start.28 = (bf16[176,1024]{1,0:T(8,128)(2,1)S(1)}, bf16[176,1024]{1,0:T(8,128)(2,1)}, u32[]{:S(2)}, u32[]{:S(2)}) collective-permute-start(bf16[176,1024]{1,0:T(8,128)(2,1)S(1)} %collective-permute-done.19.refs_2_.refs_3_), channel_id=1, source_target_pairs={{16,0},{8,1},{24,8},{0,9},{17,16},{9,17},{25,24},{1,25},{18,2},{10... | collective-permute-start | bytes 1081352 | tf_op jit(solution)/shard_map/ppermute | solution.py:283
  41.4 0.8 copy-start.5
  49.5 10.2 %collective-permute-start.29 = (bf16[176,1024]{1,0:T(8,128)(2,1)S(1)}, bf16[176,1024]{1,0:T(8,128)(2,1)}, u32[]{:S(2)}, u32[]{:S(2)}) collective-permute-start(bf16[176,1024]{1,0:T(8,128)(2,1)S(1)} %collective-permute-done.20.refs_4_), channel_id=1, source_target_pairs={{16,0},{8,1},{24,8},{0,9},{17,16},{9,17},{25,24},{1,25},{18,2},{10... | collective-permute-start | bytes 1081352 | tf_op jit(solution)/shard_map/ppermute | solution.py:283
  50.4 11.1 %collective-permute-start.27 = (bf16[176,1024]{1,0:T(8,128)(2,1)S(1)}, bf16[176,1024]{1,0:T(8,128)(2,1)}, u32[]{:S(2)}, u32[]{:S(2)}) collective-permute-start(bf16[176,1024]{1,0:T(8,128)(2,1)S(1)} %collective-permute-done.20.refs_4_), channel_id=1, source_target_pairs={{1,0},{17,1},{9,8},{25,9},{0,16},{16,17},{8,24},{24,25},{3,2},{19,... | collective-permute-start | bytes 1081352 | tf_op jit(solution)/shard_map/ppermute | solution.py:283
  51.5 6.3 %collective-permute-start.26 = (bf16[176,1024]{1,0:T(8,128)(2,1)S(1)}, bf16[176,1024]{1,0:T(8,128)(2,1)}, u32[]{:S(2)}, u32[]{:S(2)}) collective-permute-start(bf16[176,1024]{1,0:T(8,128)(2,1)S(1)} %collective-permute-done.20.refs_4_), channel_id=1, source_target_pairs={{8,0},{9,1},{0,8},{1,9},{24,16},{25,17},{16,24},{17,25},{10,2},{11... | collective-permute-start | bytes 1081352 | tf_op jit(solution)/shard_map/ppermute | solution.py:283
  51.9 1.0 %copy-start.6 = (bf16[176,1024]{1,0:T(8,128)(2,1)S(1)}, bf16[176,1024]{1,0:T(8,128)(2,1)}, u32[]{:S(2)}) copy-start(bf16[176,1024]{1,0:T(8,128)(2,1)} %copy-done.5) | copy-start | bytes 1081348
  68.8 13.5 %all-to-all-start.3 = ((f32[32,4,128]{2,1,0:T(4,128)}), f32[32,4,128]{2,1,0:T(4,128)S(1)}, u32[]{:S(2)}, u32[]{:S(2)}) async-start(f32[32,4,128]{2,1,0:T(4,128)} %bitcast.19), calls=%async_computation.3 | async-start | bytes 131072 | tf_op jit(solution)/shard_map/all_to_all | solution.py:384
  82.4 0.6 copy-start.13

commit v7 on v6

--- a/solution.py
+++ b/solution.py
@@ -296,7 +296,9 @@
         near = after(part, own[k + 1]) if k > 1 else part
         rounds.append([inside(near, 1), *[inside(part, j) for j in range(2, count)]])
 
-    place = after(place, *rounds[0])
+    last = after(own[-1], *rounds[-2])
+    rounds.append([inside(after(last, rounds[-1][0]), 1), *[inside(last, j) for j in range(2, count)]])
+    place = after(place, rounds[1][0])
 
     planes_i = jnp.arange(groups, dtype=jnp.int32)
     swap = (planes_i[:, None] ^ planes_i[None, :]) == plane
@@ -320,8 +322,6 @@
     )
     facts = jnp.broadcast_to(facts[None, :, None, :], (n_row, groups, wide, length)).reshape(devs, length)
     facts = lax.all_to_all(facts, AXES, split_axis=0, concat_axis=0, tiled=True)
-    last = after(own[-1], *rounds[-2], rounds[-1][1])
-    rounds.append([inside(after(last, rounds[-1][0], facts), 1), *[inside(last, j) for j in range(2, count)]])
     over = jnp.max(facts[:, cap + LEVELS]) > 0
     facts = facts.reshape(n_row, groups, wide, length)
 

time: 83.2 us -> 75.1 us (0.903)
  waiting for transfers between devices: 30.7 us -> 25.2 us
  starting transfers between devices: 27 us -> 24.1 us
  Pallas kernels: 16.1 us -> 17 us
    ppermute x12, waiting for transfers between devices: 19.4 us -> 4.13 us  [inside(): lax.ppermute(part, AXES, [(device(int(held[j, i]), h), device(i, h)) for...]
    ppermute x3, waiting for transfers between devices: 4.01 us -> 11.9 us  [across(): lax.ppermute(part, AXES, [(device(i, h ^ k), device(i, h)) for i, h in pl...]
    all_to_all x1, starting transfers between devices: 6.43 us -> 4.06 us  [best_matches(): lax.all_to_all(best.reshape(devs, -1, 128), AXES, split_axis=0, concat_ax...]
    all_to_all x1, waiting for transfers between devices: 1.57 us -> 3.31 us  [best_matches(): facts = lax.all_to_all(facts, AXES, split_axis=0, concat_axis=0, tiled=True)]
    ppermute x3, starting transfers between devices: 9.3 us -> 7.81 us  [across(): lax.ppermute(part, AXES, [(device(i, h ^ k), device(i, h)) for i, h in pl...]
    all_to_all x1, starting transfers between devices: 2.55 us -> 3.42 us  [best_matches(): facts = lax.all_to_all(facts, AXES, split_axis=0, concat_axis=0, tiled=True)]
    unnamed x16 -> x20, local copies, waits for them, and re-layouts: 3.13 us -> 2.4 us
  transfers between devices with their start and end apart: 17 -> 17, of which waited for: 9 -> 8; matrix products, arithmetic and copies ran while one was open for 5% -> 5% of each run, Pallas kernels for 7% -> 8%
where the time goes in v7:
time: 75.1 us; the launch traced here: 74.8 us
  waiting for transfers between devices  25.2 us (34%)
  starting transfers between devices  24.1 us (32%)
  Pallas kernels  17 us (23%)
  local copies, waits for them, and re-layouts  4.21 us (6%)
  other arithmetic  2.62 us (3%)
  between operations  1.58 us (2%)
    ppermute x3, waiting for transfers between devices, across(): lax.ppermute(part, AXES, [(device(i, h ^ k), device(i, h)) for i, h in pl...  11.9 us
    ppermute x12, starting transfers between devices, inside(): lax.ppermute(part, AXES, [(device(int(held[j, i]), h), device(i, h)) for...  8.86 us
    ppermute x3, starting transfers between devices, across(): lax.ppermute(part, AXES, [(device(i, h ^ k), device(i, h)) for i, h in pl...  7.81 us
    pallas_call x1, Pallas kernels, best_matches(): pl.pallas_call(functools.partial(late_kernel, pairs, count, group_size),...  7.48 us
    all_to_all x1, waiting for transfers between devices, best_matches(): lax.all_to_all(best.reshape(devs, -1, 128), AXES, split_axis=0, concat_ax...  5.9 us
    pallas_call x1, Pallas kernels, best_matches(): pl.pallas_call(functools.partial(early_kernel, pairs, count, early), out_...  5.1 us
    ppermute x12, waiting for transfers between devices, inside(): lax.ppermute(part, AXES, [(device(int(held[j, i]), h), device(i, h)) for...  4.13 us
    all_to_all x1, starting transfers between devices, best_matches(): lax.all_to_all(best.reshape(devs, -1, 128), AXES, split_axis=0, concat_ax...  4.06 us
  transfers between devices with their start and end apart: 17, of which 8 were waited for; matrix products, arithmetic and copies ran while one was open for 5% of the time, Pallas kernels for 8%

profile of v7, /device:TPU:0, one launch (start us, length us, event | category | flops | bytes accessed | tf_op | source)
XLA Modules:
  0.0 74.8 jit_solution(7540935944593093292)
XLA Ops:
  0.0 3.3 %shard_map.57 = (bf16[512,1024]{1,0:T(8,128)(2,1)S(1)}, s32[1,512]{1,0:T(1,128)S(1)}, bf16[176,1024]{1,0:T(8,128)(2,1)S(1)}, bf16[176,1024]{1,0:T(8,128)(2,1)}, bf16[176,1024]{1,0:T(8,128)(2,1)}) custom-call(s32[1]{0:T(128)} %bitcast.13.plane_ref.refs_0_, s32[1,512]{1,0:T(1,128)} %bitcast.38, f32[512,1024]{1,0:T(8,128)} %emb_ref.1), custom_call_target="tpu_custom_call" | custom-call | tf_op jit(solution)/shard_map/pallas_call | solution.py:259
  3.4 0.5 collective-permute-start.16
  3.8 2.6 %collective-permute-start.15 = (bf16[176,1024]{1,0:T(8,128)(2,1)}, bf16[176,1024]{1,0:T(8,128)(2,1)S(1)}, u32[]{:S(2)}, u32[]{:S(2)}) collective-permute-start(bf16[176,1024]{1,0:T(8,128)(2,1)} %get-tuple-element.58), channel_id=1, source_target_pairs={{2,0},{3,1},{10,8},{11,9},{18,16},{19,17},{26,24},{27,25},{0,2},{1... | collective-permute-start | bytes 1081352 | tf_op jit(solution)/shard_map/ppermute | solution.py:280
  6.4 2.6 %collective-permute-start.20 = (bf16[176,1024]{1,0:T(8,128)(2,1)}, bf16[176,1024]{1,0:T(8,128)(2,1)S(1)}, u32[]{:S(2)}, u32[]{:S(2)}) collective-permute-start(bf16[176,1024]{1,0:T(8,128)(2,1)} %get-tuple-element.63), channel_id=1, source_target_pairs={{4,0},{5,1},{12,8},{13,9},{20,16},{21,17},{28,24},{29,25},{6,2},{7... | collective-permute-start | bytes 1081352 | tf_op jit(solution)/shard_map/ppermute | solution.py:280
  9.0 0.0 collective-permute-done.16.refs_3_.refs_5_
  9.0 1.1 %collective-permute-start.18 = (bf16[176,1024]{1,0:T(8,128)(2,1)S(1)}, bf16[176,1024]{1,0:T(8,128)(2,1)S(1)}, u32[]{:S(2)}, u32[]{:S(2)}) collective-permute-start(bf16[176,1024]{1,0:T(8,128)(2,1)S(1)} %get-tuple-element.60.refs_0_.refs_1_), channel_id=1, source_target_pairs={{16,0},{8,1},{24,8},{0,9},{17,16},{9,17},{25,24},{1,25},{18,2},{10... | collective-permute-start | bytes 1081352 | tf_op jit(solution)/shard_map/ppermute | solution.py:283
  10.1 1.0 %collective-permute-start.17 = (bf16[176,1024]{1,0:T(8,128)(2,1)S(1)}, bf16[176,1024]{1,0:T(8,128)(2,1)S(1)}, u32[]{:S(2)}, u32[]{:S(2)}) collective-permute-start(bf16[176,1024]{1,0:T(8,128)(2,1)S(1)} %get-tuple-element.60.refs_0_.refs_1_), channel_id=1, source_target_pairs={{1,0},{17,1},{9,8},{25,9},{0,16},{16,17},{8,24},{24,25},{3,2},{19,... | collective-permute-start | bytes 1081352 | tf_op jit(solution)/shard_map/ppermute | solution.py:283
  11.1 0.1 convert_reduce_fusion.5
  11.2 0.6 reduce_max.46
  12.5 0.1 convert_reduce_fusion.4
  12.6 10.6 %collective-permute-done.15.refs_1_.refs_2_ = bf16[176,1024]{1,0:T(8,128)(2,1)S(1)} collective-permute-done((bf16[176,1024]{1,0:T(8,128)(2,1)}, bf16[176,1024]{1,0:T(8,128)(2,1)S(1)}, u32[]{:S(2)}, u32[]{:S(2)}) %collective-permute-start.15) | collective-permute-done | bytes 360480 | tf_op jit(solution)/shard_map/ppermute | solution.py:280
  23.3 0.0 collective-permute-done.18.refs_9_.refs_13_
  23.3 0.0 collective-permute-done.17.refs_6_.refs_9_
  23.3 0.0 collective-permute-start.19
  23.3 0.1 pad_add_fusion.1
  23.4 0.1 pad.7.clone
  23.5 0.1 pad.6.clone
  23.5 1.1 %shard_map.58 = (s32[1,704]{1,0:T(1,128)S(1)}, bf16[176,1024]{1,0:T(8,128)(2,1)}) custom-call(s32[1,512]{1,0:T(1,128)S(1)} %bitcast.39, s32[1,512]{1,0:T(1,128)S(1)} %get-tuple-element.55.slot_ref, bf16[512,1024]{1,0:T(8,128)(2,1)S(1)} %get-tuple-element.56.unit_ref), custom_call_target="tpu_custom_call" | custom-call | tf_op jit(solution)/shard_map/pallas_call | solution.py:270
  24.6 0.1 select_reduce_fusion.5
  24.7 0.1 fusion.7
  24.8 2.6 %collective-permute-start.21 = (bf16[176,1024]{1,0:T(8,128)(2,1)}, bf16[176,1024]{1,0:T(8,128)(2,1)}, u32[]{:S(2)}, u32[]{:S(2)}) collective-permute-start(bf16[176,1024]{1,0:T(8,128)(2,1)} %get-tuple-element.65), channel_id=1, source_target_pairs={{6,0},{7,1},{14,8},{15,9},{22,16},{23,17},{30,24},{31,25},{4,2},{5... | collective-permute-start | bytes 1081352 | tf_op jit(solution)/shard_map/ppermute | solution.py:280
  27.5 1.3 %collective-permute-start.24 = (bf16[176,1024]{1,0:T(8,128)(2,1)S(1)}, bf16[176,1024]{1,0:T(8,128)(2,1)S(1)}, u32[]{:S(2)}, u32[]{:S(2)}) collective-permute-start(bf16[176,1024]{1,0:T(8,128)(2,1)S(1)} %collective-permute-done.15.refs_1_.refs_2_), channel_id=1, source_target_pairs={{16,0},{8,1},{24,8},{0,9},{17,16},{9,17},{25,24},{1,25},{18,2},{10... | collective-permute-start | bytes 1081352 | tf_op jit(solution)/shard_map/ppermute | solution.py:283
  28.8 0.7 collective-permute-start.23
  29.5 0.0 collective-permute-done.19.refs_4_.refs_6_
  29.5 0.7 copy-done.3
  30.3 0.1 broadcast_in_dim.172
  30.3 0.1 select_reduce_fusion.4
  30.5 0.6 all_to_all.21
  31.1 3.4 %all-to-all-start.2 = ((s32[32,1,256]{2,1,0:T(1,128)}), s32[32,1,256]{2,1,0:T(1,128)S(1)}, u32[]{:S(2)}, u32[]{:S(2)}) async-start(s32[32,1,256]{2,1,0:T(1,128)} %all_to_all.21), calls=%async_computation.2 | async-start | bytes 65536 | tf_op jit(solution)/shard_map/all_to_all | solution.py:324
  34.6 0.0 collective-permute-done.20.refs_2_.refs_3_
  34.6 1.6 %collective-permute-start.28 = (bf16[176,1024]{1,0:T(8,128)(2,1)S(1)}, bf16[176,1024]{1,0:T(8,128)(2,1)}, u32[]{:S(2)}, u32[]{:S(2)}) collective-permute-start(bf16[176,1024]{1,0:T(8,128)(2,1)S(1)} %collective-permute-done.20.refs_2_.refs_3_), channel_id=1, source_target_pairs={{16,0},{8,1},{24,8},{0,9},{17,16},{9,17},{25,24},{1,25},{18,2},{10... | collective-permute-start | bytes 1081352 | tf_op jit(solution)/shard_map/ppermute | solution.py:283
  36.2 0.5 collective-permute-start.26
  36.7 1.2 %collective-permute-done.21.refs_4_ = bf16[176,1024]{1,0:T(8,128)(2,1)} collective-permute-done((bf16[176,1024]{1,0:T(8,128)(2,1)}, bf16[176,1024]{1,0:T(8,128)(2,1)}, u32[]{:S(2)}, u32[]{:S(2)}) %collective-permute-start.21) | collective-permute-done | bytes 360480 | tf_op jit(solution)/shard_map/ppermute | solution.py:280
  37.9 0.7 collective-permute-done.24.refs_10_.refs_14_
  38.6 1.4 %collective-permute-done.23.refs_7_.refs_10_ = bf16[176,1024]{1,0:T(8,128)(2,1)} collective-permute-done((bf16[176,1024]{1,0:T(8,128)(2,1)S(1)}, bf16[176,1024]{1,0:T(8,128)(2,1)}, u32[]{:S(2)}, u32[]{:S(2)}) %collective-permute-start.23) | collective-permute-done | bytes 360480 | tf_op jit(solution)/shard_map/ppermute | solution.py:283
  39.9 0.2 collective-permute-start.29
  40.1 1.8 %collective-permute-start.27 = (bf16[176,1024]{1,0:T(8,128)(2,1)}, bf16[176,1024]{1,0:T(8,128)(2,1)}, u32[]{:S(2)}, u32[]{:S(2)}) collective-permute-start(bf16[176,1024]{1,0:T(8,128)(2,1)} %collective-permute-done.21.refs_4_), channel_id=1, source_target_pairs={{1,0},{17,1},{9,8},{25,9},{0,16},{16,17},{8,24},{24,25},{3,2},{19,... | collective-permute-start | bytes 1081352 | tf_op jit(solution)/shard_map/ppermute | solution.py:283
  41.9 0.0 collective-permute-start.22
  42.0 3.3 %all-to-all-done.2 = s32[32,1,256]{2,1,0:T(1,128)S(1)} async-done(((s32[32,1,256]{2,1,0:T(1,128)}), s32[32,1,256]{2,1,0:T(1,128)S(1)}, u32[]{:S(2)}, u32[]{:S(2)}) %all-to-all-start.2) | async-done | bytes 32800 | tf_op jit(solution)/shard_map/all_to_all | solution.py:324
  45.3 0.1 reduce.4
  45.4 0.1 broadcast_in_dim.181
  45.5 0.1 select_reduce_fusion.3
  45.7 0.1 reshape.175
  45.8 0.1 mul.54
  45.9 0.1 multiply_reduce_fusion.1
  46.0 0.1 fusion.4
  46.1 0.2 copy.85
  46.3 0.1 convert_reduce_fusion.3
  46.4 0.2 copy.86
  46.6 0.0 collective-permute-done.22.refs_5_.refs_7_
  46.6 0.2 collective-permute-start.25
  46.9 0.1 copy.94.refs_21_
  47.0 0.1 copy.87.refs_12_.refs_20_
  47.1 0.0 collective-permute-done.28.refs_11_.refs_15_
  47.1 0.8 %collective-permute-done.26.refs_8_.refs_11_ = bf16[176,1024]{1,0:T(8,128)(2,1)} collective-permute-done((bf16[176,1024]{1,0:T(8,128)(2,1)S(1)}, bf16[176,1024]{1,0:T(8,128)(2,1)}, u32[]{:S(2)}, u32[]{:S(2)}) %collective-permute-start.26) | collective-permute-done | bytes 360480 | tf_op jit(solution)/shard_map/ppermute | solution.py:283
  47.9 1.0 %copy-done.6 = bf16[176,1024]{1,0:T(8,128)(2,1)S(1)} copy-done((bf16[176,1024]{1,0:T(8,128)(2,1)S(1)}, bf16[176,1024]{1,0:T(8,128)(2,1)}, u32[]{:S(2)}) %copy-start.6) | copy-done | bytes 360472
  48.9 5.1 %shard_map.59.refs_17_ = f32[4,512]{1,0:T(4,128)S(1)} custom-call(bf16[176,1024]{1,0:T(8,128)(2,1)S(1)} %get-tuple-element.60.refs_0_.refs_1_, bf16[176,1024]{1,0:T(8,128)(2,1)S(1)} %collective-permute-done.15.refs_1_.refs_2_, bf16[176,1024]{1,0:T(8,128)(2,1)S(1)} %collective-permute-done.20.refs_2_.refs_3_, ...), custom_call_target="tpu_custom_call" | custom-call | flops 2684354560 | bytes 4194304 | tf_op jit(solution)/shard_map/pallas_call | solution.py:355
  54.0 0.0 collective-permute-done.29.refs_16_
  54.0 1.3 %collective-permute-done.27.refs_12_ = bf16[176,1024]{1,0:T(8,128)(2,1)} collective-permute-done((bf16[176,1024]{1,0:T(8,128)(2,1)}, bf16[176,1024]{1,0:T(8,128)(2,1)}, u32[]{:S(2)}, u32[]{:S(2)}) %collective-permute-start.27) | collective-permute-done | bytes 360480 | tf_op jit(solution)/shard_map/ppermute | solution.py:283
  55.3 7.5 %shard_map.60 = f32[4,8,4,128]{3,2,1,0:T(4,128)} custom-call(s32[1]{0:T(128)} %bitcast.13.plane_ref.refs_0_, bf16[176,1024]{1,0:T(8,128)(2,1)S(1)} %get-tuple-element.60.refs_0_.refs_1_, bf16[176,1024]{1,0:T(8,128)(2,1)S(1)} %collective-permute-done.15.refs_1_.refs_2_, bf16[176,1024]{1,0:T(8,128)(2,1)S(1)} %collective-permute-done.20.refs_2_.refs_3_, ...), custom_call_target="tpu_custom_call" | custom-call | tf_op jit(solution)/shard_map/pallas_call | solution.py:366
  62.8 4.1 %all-to-all-start.3 = ((f32[32,4,128]{2,1,0:T(4,128)}), f32[32,4,128]{2,1,0:T(4,128)S(1)}, u32[]{:S(2)}, u32[]{:S(2)}) async-start(f32[32,4,128]{2,1,0:T(4,128)} %bitcast.19), calls=%async_computation.3 | async-start | bytes 131072 | tf_op jit(solution)/shard_map/all_to_all | solution.py:384
  66.9 0.7 slice_reduce_fusion
  68.3 5.9 %all-to-all-done.3 = f32[32,4,128]{2,1,0:T(4,128)S(1)} async-done(((f32[32,4,128]{2,1,0:T(4,128)}), f32[32,4,128]{2,1,0:T(4,128)S(1)}, u32[]{:S(2)}, u32[]{:S(2)}) %all-to-all-start.3) | async-done | bytes 65568 | tf_op jit(solution)/shard_map/all_to_all | solution.py:384
  74.2 0.6 copy-done.13
  (38 shorter events, 0.3 us)
Async XLA Ops:
  0.0 24.6 %copy-start.12 = (s32[4,8]{1,0:T(4,128)S(1)}, s32[4,8]{1,0:T(4,128)}, u32[]{:S(2)}) copy-start(s32[4,8]{1,0:T(4,128)} %constant.109.clone) | copy-start | bytes 388
  0.0 9.0 %copy-start.10 = (s32[512]{0:T(512)S(1)}, s32[512]{0:T(512)}, u32[]{:S(2)}) copy-start(s32[512]{0:T(512)} %param.8) | copy-start | bytes 6148
  0.0 12.5 %copy-start.11 = (s32[1,512]{1,0:T(1,128)S(1)}, s32[1,512]{1,0:T(1,128)}, u32[]{:S(2)}) copy-start(s32[1,512]{1,0:T(1,128)} %param.9) | copy-start | bytes 6148
  3.4 5.6 %collective-permute-start.16 = (bf16[176,1024]{1,0:T(8,128)(2,1)S(1)}, bf16[176,1024]{1,0:T(8,128)(2,1)S(1)}, u32[]{:S(2)}, u32[]{:S(2)}) collective-permute-start(bf16[176,1024]{1,0:T(8,128)(2,1)S(1)} %get-tuple-element.60.refs_0_.refs_1_), channel_id=1, source_target_pairs={{8,0},{9,1},{0,8},{1,9},{24,16},{25,17},{16,24},{17,25},{10,2},{11... | collective-permute-start | bytes 1081352 | tf_op jit(solution)/shard_map/ppermute | solution.py:283
  3.8 19.5 %collective-permute-start.15 = (bf16[176,1024]{1,0:T(8,128)(2,1)}, bf16[176,1024]{1,0:T(8,128)(2,1)S(1)}, u32[]{:S(2)}, u32[]{:S(2)}) collective-permute-start(bf16[176,1024]{1,0:T(8,128)(2,1)} %get-tuple-element.58), channel_id=1, source_target_pairs={{2,0},{3,1},{10,8},{11,9},{18,16},{19,17},{26,24},{27,25},{0,2},{1... | collective-permute-start | bytes 1081352 | tf_op jit(solution)/shard_map/ppermute | solution.py:280
  6.4 28.2 %collective-permute-start.20 = (bf16[176,1024]{1,0:T(8,128)(2,1)}, bf16[176,1024]{1,0:T(8,128)(2,1)S(1)}, u32[]{:S(2)}, u32[]{:S(2)}) collective-permute-start(bf16[176,1024]{1,0:T(8,128)(2,1)} %get-tuple-element.63), channel_id=1, source_target_pairs={{4,0},{5,1},{12,8},{13,9},{20,16},{21,17},{28,24},{29,25},{6,2},{7... | collective-permute-start | bytes 1081352 | tf_op jit(solution)/shard_map/ppermute | solution.py:280
  9.0 14.3 %collective-permute-start.18 = (bf16[176,1024]{1,0:T(8,128)(2,1)S(1)}, bf16[176,1024]{1,0:T(8,128)(2,1)S(1)}, u32[]{:S(2)}, u32[]{:S(2)}) collective-permute-start(bf16[176,1024]{1,0:T(8,128)(2,1)S(1)} %get-tuple-element.60.refs_0_.refs_1_), channel_id=1, source_target_pairs={{16,0},{8,1},{24,8},{0,9},{17,16},{9,17},{25,24},{1,25},{18,2},{10... | collective-permute-start | bytes 1081352 | tf_op jit(solution)/shard_map/ppermute | solution.py:283
  10.1 13.2 %collective-permute-start.17 = (bf16[176,1024]{1,0:T(8,128)(2,1)S(1)}, bf16[176,1024]{1,0:T(8,128)(2,1)S(1)}, u32[]{:S(2)}, u32[]{:S(2)}) collective-permute-start(bf16[176,1024]{1,0:T(8,128)(2,1)S(1)} %get-tuple-element.60.refs_0_.refs_1_), channel_id=1, source_target_pairs={{1,0},{17,1},{9,8},{25,9},{0,16},{16,17},{8,24},{24,25},{3,2},{19,... | collective-permute-start | bytes 1081352 | tf_op jit(solution)/shard_map/ppermute | solution.py:283
  23.3 6.2 %collective-permute-start.19 = (bf16[176,1024]{1,0:T(8,128)(2,1)S(1)}, bf16[176,1024]{1,0:T(8,128)(2,1)S(1)}, u32[]{:S(2)}, u32[]{:S(2)}) collective-permute-start(bf16[176,1024]{1,0:T(8,128)(2,1)S(1)} %collective-permute-done.15.refs_1_.refs_2_), channel_id=1, source_target_pairs={{8,0},{9,1},{0,8},{1,9},{24,16},{25,17},{16,24},{17,25},{10,2},{11... | collective-permute-start | bytes 1081352 | tf_op jit(solution)/shard_map/ppermute | solution.py:283
  24.8 13.1 %collective-permute-start.21 = (bf16[176,1024]{1,0:T(8,128)(2,1)}, bf16[176,1024]{1,0:T(8,128)(2,1)}, u32[]{:S(2)}, u32[]{:S(2)}) collective-permute-start(bf16[176,1024]{1,0:T(8,128)(2,1)} %get-tuple-element.65), channel_id=1, source_target_pairs={{6,0},{7,1},{14,8},{15,9},{22,16},{23,17},{30,24},{31,25},{4,2},{5... | collective-permute-start | bytes 1081352 | tf_op jit(solution)/shard_map/ppermute | solution.py:280
  27.5 11.1 %collective-permute-start.24 = (bf16[176,1024]{1,0:T(8,128)(2,1)S(1)}, bf16[176,1024]{1,0:T(8,128)(2,1)S(1)}, u32[]{:S(2)}, u32[]{:S(2)}) collective-permute-start(bf16[176,1024]{1,0:T(8,128)(2,1)S(1)} %collective-permute-done.15.refs_1_.refs_2_), channel_id=1, source_target_pairs={{16,0},{8,1},{24,8},{0,9},{17,16},{9,17},{25,24},{1,25},{18,2},{10... | collective-permute-start | bytes 1081352 | tf_op jit(solution)/shard_map/ppermute | solution.py:283
  28.8 11.1 %collective-permute-start.23 = (bf16[176,1024]{1,0:T(8,128)(2,1)S(1)}, bf16[176,1024]{1,0:T(8,128)(2,1)}, u32[]{:S(2)}, u32[]{:S(2)}) collective-permute-start(bf16[176,1024]{1,0:T(8,128)(2,1)S(1)} %collective-permute-done.15.refs_1_.refs_2_), channel_id=1, source_target_pairs={{1,0},{17,1},{9,8},{25,9},{0,16},{16,17},{8,24},{24,25},{3,2},{19,... | collective-permute-start | bytes 1081352 | tf_op jit(solution)/shard_map/ppermute | solution.py:283
  29.5 0.7 copy-start.3
  30.2 17.7 %copy-start.4 = (bf16[176,1024]{1,0:T(8,128)(2,1)S(1)}, bf16[176,1024]{1,0:T(8,128)(2,1)}, u32[]{:S(2)}) copy-start(bf16[176,1024]{1,0:T(8,128)(2,1)} %copy-done.3) | copy-start | bytes 1081348
  31.1 14.1 %all-to-all-start.2 = ((s32[32,1,256]{2,1,0:T(1,128)}), s32[32,1,256]{2,1,0:T(1,128)S(1)}, u32[]{:S(2)}, u32[]{:S(2)}) async-start(s32[32,1,256]{2,1,0:T(1,128)} %all_to_all.21), calls=%async_computation.2 | async-start | bytes 65536 | tf_op jit(solution)/shard_map/all_to_all | solution.py:324
  34.6 12.6 %collective-permute-start.28 = (bf16[176,1024]{1,0:T(8,128)(2,1)S(1)}, bf16[176,1024]{1,0:T(8,128)(2,1)}, u32[]{:S(2)}, u32[]{:S(2)}) collective-permute-start(bf16[176,1024]{1,0:T(8,128)(2,1)S(1)} %collective-permute-done.20.refs_2_.refs_3_), channel_id=1, source_target_pairs={{16,0},{8,1},{24,8},{0,9},{17,16},{9,17},{25,24},{1,25},{18,2},{10... | collective-permute-start | bytes 1081352 | tf_op jit(solution)/shard_map/ppermute | solution.py:283
  36.2 11.8 %collective-permute-start.26 = (bf16[176,1024]{1,0:T(8,128)(2,1)S(1)}, bf16[176,1024]{1,0:T(8,128)(2,1)}, u32[]{:S(2)}, u32[]{:S(2)}) collective-permute-start(bf16[176,1024]{1,0:T(8,128)(2,1)S(1)} %collective-permute-done.20.refs_2_.refs_3_), channel_id=1, source_target_pairs={{1,0},{17,1},{9,8},{25,9},{0,16},{16,17},{8,24},{24,25},{3,2},{19,... | collective-permute-start | bytes 1081352 | tf_op jit(solution)/shard_map/ppermute | solution.py:283
  38.6 8.1 %copy-start.5 = (bf16[176,1024]{1,0:T(8,128)(2,1)}, bf16[176,1024]{1,0:T(8,128)(2,1)S(1)}, u32[]{:S(2)}) copy-start(bf16[176,1024]{1,0:T(8,128)(2,1)S(1)} %collective-permute-done.24.refs_10_.refs_14_) | copy-start | bytes 1081348
  39.9 14.1 %collective-permute-start.29 = (bf16[176,1024]{1,0:T(8,128)(2,1)}, bf16[176,1024]{1,0:T(8,128)(2,1)}, u32[]{:S(2)}, u32[]{:S(2)}) collective-permute-start(bf16[176,1024]{1,0:T(8,128)(2,1)} %collective-permute-done.21.refs_4_), channel_id=1, source_target_pairs={{16,0},{8,1},{24,8},{0,9},{17,16},{9,17},{25,24},{1,25},{18,2},{10... | collective-permute-start | bytes 1081352 | tf_op jit(solution)/shard_map/ppermute | solution.py:283
  40.1 15.2 %collective-permute-start.27 = (bf16[176,1024]{1,0:T(8,128)(2,1)}, bf16[176,1024]{1,0:T(8,128)(2,1)}, u32[]{:S(2)}, u32[]{:S(2)}) collective-permute-start(bf16[176,1024]{1,0:T(8,128)(2,1)} %collective-permute-done.21.refs_4_), channel_id=1, source_target_pairs={{1,0},{17,1},{9,8},{25,9},{0,16},{16,17},{8,24},{24,25},{3,2},{19,... | collective-permute-start | bytes 1081352 | tf_op jit(solution)/shard_map/ppermute | solution.py:283
  41.9 4.7 %collective-permute-start.22 = (bf16[176,1024]{1,0:T(8,128)(2,1)S(1)}, bf16[176,1024]{1,0:T(8,128)(2,1)}, u32[]{:S(2)}, u32[]{:S(2)}) collective-permute-start(bf16[176,1024]{1,0:T(8,128)(2,1)S(1)} %collective-permute-done.20.refs_2_.refs_3_), channel_id=1, source_target_pairs={{8,0},{9,1},{0,8},{1,9},{24,16},{25,17},{16,24},{17,25},{10,2},{11... | collective-permute-start | bytes 1081352 | tf_op jit(solution)/shard_map/ppermute | solution.py:283
  46.6 8.7 %collective-permute-start.25 = (bf16[176,1024]{1,0:T(8,128)(2,1)}, bf16[176,1024]{1,0:T(8,128)(2,1)}, u32[]{:S(2)}, u32[]{:S(2)}) collective-permute-start(bf16[176,1024]{1,0:T(8,128)(2,1)} %collective-permute-done.21.refs_4_), channel_id=1, source_target_pairs={{8,0},{9,1},{0,8},{1,9},{24,16},{25,17},{16,24},{17,25},{10,2},{11... | collective-permute-start | bytes 1081352 | tf_op jit(solution)/shard_map/ppermute | solution.py:283
  47.9 1.0 %copy-start.6 = (bf16[176,1024]{1,0:T(8,128)(2,1)S(1)}, bf16[176,1024]{1,0:T(8,128)(2,1)}, u32[]{:S(2)}) copy-start(bf16[176,1024]{1,0:T(8,128)(2,1)} %copy-done.5) | copy-start | bytes 1081348
  48.9 6.4 %copy-start.7 = (bf16[176,1024]{1,0:T(8,128)(2,1)S(1)}, bf16[176,1024]{1,0:T(8,128)(2,1)}, u32[]{:S(2)}) copy-start(bf16[176,1024]{1,0:T(8,128)(2,1)} %copy-done.5) | copy-start | bytes 1081348
  62.8 11.3 %all-to-all-start.3 = ((f32[32,4,128]{2,1,0:T(4,128)}), f32[32,4,128]{2,1,0:T(4,128)S(1)}, u32[]{:S(2)}, u32[]{:S(2)}) async-start(f32[32,4,128]{2,1,0:T(4,128)} %bitcast.19), calls=%async_computation.3 | async-start | bytes 131072 | tf_op jit(solution)/shard_map/all_to_all | solution.py:384
  74.2 0.6 copy-start.13

commit v8 on v7

--- a/solution.py
+++ b/solution.py
@@ -60,19 +60,14 @@
     return held, pairs
 
 
-def write_chunks(slot, unit, cap, chunk_refs, numbers):
-    for ref, k in zip(chunk_refs, numbers):
-        index = lax.broadcasted_iota(jnp.int32, (cap, unit.shape[0]), 0) + k * cap
-        pick = (index == slot).astype(jnp.bfloat16)
-        ref[...] = jnp.dot(pick, unit, preferred_element_type=jnp.float32).astype(jnp.bfloat16)
-
-
-def unit_kernel(groups, cap, group_size, numbers, plane_ref, dest_ref, emb_ref, unit_ref, slot_ref, *chunk_refs):
+def pack_kernel(groups, cap, group_size, plane_ref, dest_ref, emb_ref, place_ref, *chunk_refs):
     rows_dev = emb_ref.shape[0]
     dest = dest_ref[...]
-    group = jnp.zeros_like(dest)
+    group, place = jnp.zeros_like(dest), dest
     for g in range(1, groups):
-        group += (dest >= g * group_size).astype(jnp.int32)
+        above = dest >= g * group_size
+        group += above.astype(jnp.int32)
+        place -= jnp.where(above, group_size, 0)
     group = jnp.bitwise_xor(group, plane_ref[0])
     pad = -(-groups // 16) * 16
     member = lax.broadcasted_iota(jnp.int32, (pad, rows_dev), 0) == group
@@ -82,27 +77,17 @@
     before = jnp.dot(member.astype(jnp.bfloat16), earlier.astype(jnp.bfloat16), preferred_element_type=jnp.float32)
     rank = jnp.sum(jnp.where(member, before, 0.0), axis=0, keepdims=True).astype(jnp.int32)
     slot = jnp.where(rank < cap, group * cap + rank, groups * cap)
-    slot_ref[...] = slot
+    pick = (lax.broadcasted_iota(jnp.int32, (groups * cap, rows_dev), 0) == slot).astype(jnp.bfloat16)
     x = emb_ref[...]
     unit = (x * lax.rsqrt(jnp.sum(x * x, axis=1, keepdims=True) + 1e-06)).astype(jnp.bfloat16)
-    unit_ref[...] = unit
-    write_chunks(slot, unit, cap, chunk_refs, numbers)
-
-
-def rest_kernel(groups, cap, group_size, numbers, dest_ref, slot_ref, unit_ref, place_ref, *chunk_refs):
-    rows_dev = unit_ref.shape[0]
-    slot = slot_ref[...]
-    write_chunks(slot, unit_ref[...], cap, chunk_refs, numbers)
-    dest = dest_ref[...]
-    place = dest
-    for g in range(1, groups):
-        place -= jnp.where(dest >= g * group_size, group_size, 0)
+    for k, ref in enumerate(chunk_refs):
+        chunk = jnp.dot(pick[k * cap : (k + 1) * cap], unit, preferred_element_type=jnp.float32)
+        ref[...] = chunk.astype(jnp.bfloat16)
     high = lax.shift_right_logical(place, 7)
     low = jnp.bitwise_and(place, 127)
     kind = lax.broadcasted_iota(jnp.int32, (16, rows_dev), 0)
     facts = jnp.where(kind == 0, high, jnp.where(kind == 1, low, jnp.where(kind == 2, 1, 0)))
     facts = facts.astype(jnp.float32).astype(jnp.bfloat16)
-    pick = (lax.broadcasted_iota(jnp.int32, (groups * cap, rows_dev), 0) == slot).astype(jnp.bfloat16)
     got = lax.dot_general(facts, pick, NT, preferred_element_type=jnp.float32).astype(jnp.int32)
     there = got[2:3, :] > 0
     place_ref[...] = jnp.where(there, got[0:1, :] * 128 + got[1:2, :], group_size)
@@ -227,11 +212,8 @@
         spread += lax.dot_general(stack, low.astype(jnp.bfloat16), NT, preferred_element_type=jnp.float32)
     value = spread[:tall] + spread[tall : 2 * tall] + spread[2 * tall : 3 * tall]
     value = jnp.where(spread[3 * tall :] > 0.5, value, -1.0)
-    n_row, n_col, lines, _ = out_ref.shape
-    for r in range(n_row):
-        here = jnp.where(plane_ref[0] == r, value, -1.0)
-        for c in range(n_col):
-            out_ref[r, c] = here[c * lines : (c + 1) * lines]
+    for r in range(out_ref.shape[0]):
+        out_ref[r] = jnp.where(plane_ref[0] == r, value, -1.0)
 
 
 def best_matches(cap, embeddings, dest_pos, cluster_ids):
@@ -252,29 +234,18 @@
         return (i // wide) * n_col + h * wide + i % wide
 
     planes = [(i, h) for h in range(groups) for i in range(n_row * wide)]
-    numbers, others = tuple(range(min(3, groups))), tuple(range(3, groups))
-    chunk_shape = jax.ShapeDtypeStruct((cap, width), jnp.bfloat16)
     dest_row = dest_pos.reshape(1, rows_dev)
     plane_ref = plane.astype(jnp.int32).reshape(1)
-    unit, slot, *made = pl.pallas_call(
-        functools.partial(unit_kernel, groups, cap, group_size, numbers),
+    place, *parts = pl.pallas_call(
+        functools.partial(pack_kernel, groups, cap, group_size),
         out_shape=[
-            jax.ShapeDtypeStruct((rows_dev, width), jnp.bfloat16),
-            jax.ShapeDtypeStruct((1, rows_dev), jnp.int32),
-            *[chunk_shape] * len(numbers),
+            jax.ShapeDtypeStruct((1, slots), jnp.int32),
+            *[jax.ShapeDtypeStruct((cap, width), jnp.bfloat16)] * groups,
         ],
         in_specs=[pl.BlockSpec(memory_space=pltpu.SMEM), VMEM, VMEM],
-        out_specs=[VMEM] * (2 + len(numbers)),
+        out_specs=[VMEM] * (1 + groups),
         compiler_params=kernel_params(20),
     )(plane_ref, dest_row, embeddings)
-    place, *more = pl.pallas_call(
-        functools.partial(rest_kernel, groups, cap, group_size, others),
-        out_shape=[jax.ShapeDtypeStruct((1, slots), jnp.int32), *[chunk_shape] * len(others)],
-        in_specs=[VMEM] * 3,
-        out_specs=[VMEM] * (1 + len(others)),
-        compiler_params=kernel_params(20),
-    )(dest_row, slot, unit)
-    parts = dict(zip(numbers + others, made + more))
 
     def across(part, k):
         return lax.ppermute(part, AXES, [(device(i, h ^ k), device(i, h)) for i, h in planes])
@@ -365,7 +336,7 @@
     )(*[part for block in blocks for part in block[:-1]], label, label_col)
     best = pl.pallas_call(
         functools.partial(late_kernel, pairs, count, group_size),
-        out_shape=jax.ShapeDtypeStruct((n_row, n_col, rows_dev // 128, 128), jnp.float32),
+        out_shape=jax.ShapeDtypeStruct((n_row, group_size // 128, 128), jnp.float32),
         in_specs=[pl.BlockSpec(memory_space=pltpu.SMEM)] + [any_space] * (count * groups) + [VMEM] * 6,
         out_specs=VMEM,
         scratch_shapes=scratch(groups),

time: 75.1 us -> 74.9 us (level)
  waiting for transfers between devices: 25.2 us -> 23.1 us
  local copies, waits for them, and re-layouts: 4.21 us -> 5.89 us
  other arithmetic: 2.62 us -> 3.68 us
  Pallas kernels: 17 us -> 16.1 us
    ppermute x12, waiting for transfers between devices: 4.13 us -> 2.46 us  [inside(): lax.ppermute(part, AXES, [(device(int(held[j, i]), h), device(i, h)) for...]
    slice x2, local copies, waits for them, and re-layouts: 0.13 us -> 1.79 us  [best_matches(): labels[:, :early]]
    select_n x1, other arithmetic: 0.04 us -> 1.02 us  [best_matches(): labels = jnp.where(places < group_size, labels, -1)]
    pallas_call x2 -> x1, Pallas kernels: 4.45 us -> 3.54 us  [best_matches(): pl.pallas_call(functools.partial(pack_kernel, groups, cap, group_size), o...]
    reduce_sum x1, local copies, waits for them, and re-layouts: 0.18 us -> 0.94 us  [best_matches(): jnp.sum((places[:, None, :] >= ends[None, :, None]).astype(jnp.int32), ax...]
  transfers between devices with their start and end apart: 17 -> 17, of which waited for: 8 -> 6; matrix products, arithmetic and copies ran while one was open for 5% -> 10% of each run, Pallas kernels for 8% -> 7%
where the time goes in v8:
time: 74.9 us; the launch traced here: 74.5 us
  starting transfers between devices  24 us (32%)
  waiting for transfers between devices  23.1 us (31%)
  Pallas kernels  16.1 us (21%)
  local copies, waits for them, and re-layouts  5.89 us (8%)
  other arithmetic  3.68 us (5%)
  between operations  1.68 us (2%)
    ppermute x3, waiting for transfers between devices, across(): lax.ppermute(part, AXES, [(device(i, h ^ k), device(i, h)) for i, h in pl...  12 us
    ppermute x12, starting transfers between devices, inside(): lax.ppermute(part, AXES, [(device(int(held[j, i]), h), device(i, h)) for...  8.79 us
    ppermute x3, starting transfers between devices, across(): lax.ppermute(part, AXES, [(device(i, h ^ k), device(i, h)) for i, h in pl...  7.83 us
    pallas_call x1, Pallas kernels, best_matches(): pl.pallas_call(functools.partial(late_kernel, pairs, count, group_size),...  7.47 us
    all_to_all x1, waiting for transfers between devices, best_matches(): lax.all_to_all(best.reshape(devs, -1, 128), AXES, split_axis=0, concat_ax...  5.71 us
    pallas_call x1, Pallas kernels, best_matches(): pl.pallas_call(functools.partial(early_kernel, pairs, count, early), out_...  5.1 us
    all_to_all x1, starting transfers between devices, best_matches(): lax.all_to_all(best.reshape(devs, -1, 128), AXES, split_axis=0, concat_ax...  4.03 us
    pallas_call x1, Pallas kernels, best_matches(): pl.pallas_call(functools.partial(pack_kernel, groups, cap, group_size), o...  3.54 us
  transfers between devices with their start and end apart: 17, of which 6 were waited for; matrix products, arithmetic and copies ran while one was open for 10% of the time, Pallas kernels for 7%

profile of v8, /device:TPU:0, one launch (start us, length us, event | category | flops | bytes accessed | tf_op | source)
XLA Modules:
  0.0 74.5 jit_solution(12737986466160223444)
XLA Ops:
  0.0 3.5 %shard_map.57 = (s32[1,704]{1,0:T(1,128)S(1)}, bf16[176,1024]{1,0:T(8,128)(2,1)S(1)}, bf16[176,1024]{1,0:T(8,128)(2,1)S(1)}, bf16[176,1024]{1,0:T(8,128)(2,1)}, bf16[176,1024]{1,0:T(8,128)(2,1)}) custom-call(s32[1]{0:T(128)} %bitcast.12.plane_ref.refs_0_, s32[1,512]{1,0:T(1,128)} %bitcast.38, f32[512,1024]{1,0:T(8,128)} %emb_ref.1), custom_call_target="tpu_custom_call" | custom-call | tf_op jit(solution)/shard_map/pallas_call | solution.py:239
  3.5 0.5 collective-permute-start.16
  4.0 2.6 %collective-permute-start.15 = (bf16[176,1024]{1,0:T(8,128)(2,1)S(1)}, bf16[176,1024]{1,0:T(8,128)(2,1)S(1)}, u32[]{:S(2)}, u32[]{:S(2)}) collective-permute-start(bf16[176,1024]{1,0:T(8,128)(2,1)S(1)} %get-tuple-element.52), channel_id=1, source_target_pairs={{2,0},{3,1},{10,8},{11,9},{18,16},{19,17},{26,24},{27,25},{0,2},{1... | collective-permute-start | bytes 1081352 | tf_op jit(solution)/shard_map/ppermute | solution.py:251
  6.6 2.6 %collective-permute-start.20 = (bf16[176,1024]{1,0:T(8,128)(2,1)}, bf16[176,1024]{1,0:T(8,128)(2,1)S(1)}, u32[]{:S(2)}, u32[]{:S(2)}) collective-permute-start(bf16[176,1024]{1,0:T(8,128)(2,1)} %get-tuple-element.57), channel_id=1, source_target_pairs={{4,0},{5,1},{12,8},{13,9},{20,16},{21,17},{28,24},{29,25},{6,2},{7... | collective-permute-start | bytes 1081352 | tf_op jit(solution)/shard_map/ppermute | solution.py:251
  9.2 0.0 collective-permute-done.16.refs_3_.refs_5_
  9.2 1.1 %collective-permute-start.18 = (bf16[176,1024]{1,0:T(8,128)(2,1)S(1)}, bf16[176,1024]{1,0:T(8,128)(2,1)S(1)}, u32[]{:S(2)}, u32[]{:S(2)}) collective-permute-start(bf16[176,1024]{1,0:T(8,128)(2,1)S(1)} %get-tuple-element.54.refs_0_.refs_1_), channel_id=1, source_target_pairs={{16,0},{8,1},{24,8},{0,9},{17,16},{9,17},{25,24},{1,25},{18,2},{10... | collective-permute-start | bytes 1081352 | tf_op jit(solution)/shard_map/ppermute | solution.py:254
  10.3 1.0 %collective-permute-start.17 = (bf16[176,1024]{1,0:T(8,128)(2,1)S(1)}, bf16[176,1024]{1,0:T(8,128)(2,1)S(1)}, u32[]{:S(2)}, u32[]{:S(2)}) collective-permute-start(bf16[176,1024]{1,0:T(8,128)(2,1)S(1)} %get-tuple-element.54.refs_0_.refs_1_), channel_id=1, source_target_pairs={{1,0},{17,1},{9,8},{25,9},{0,16},{16,17},{8,24},{24,25},{3,2},{19,... | collective-permute-start | bytes 1081352 | tf_op jit(solution)/shard_map/ppermute | solution.py:254
  11.3 0.1 convert_reduce_fusion.5
  11.4 0.7 reduce_max.46
  12.9 0.1 convert_reduce_fusion.4
  13.0 10.1 %collective-permute-done.15.refs_1_.refs_2_ = bf16[176,1024]{1,0:T(8,128)(2,1)S(1)} collective-permute-done((bf16[176,1024]{1,0:T(8,128)(2,1)S(1)}, bf16[176,1024]{1,0:T(8,128)(2,1)S(1)}, u32[]{:S(2)}, u32[]{:S(2)}) %collective-permute-start.15) | collective-permute-done | bytes 360480 | tf_op jit(solution)/shard_map/ppermute | solution.py:251
  23.1 0.0 collective-permute-done.18.refs_9_.refs_13_
  23.1 0.0 collective-permute-done.17.refs_6_.refs_9_
  23.1 0.0 collective-permute-start.19
  23.1 0.1 pad_add_fusion.1
  23.1 0.1 pad.7.clone
  23.2 0.1 pad.6.clone
  23.3 0.1 select_reduce_fusion.5
  23.4 0.1 fusion.7
  23.5 2.7 %collective-permute-start.21 = (bf16[176,1024]{1,0:T(8,128)(2,1)}, bf16[176,1024]{1,0:T(8,128)(2,1)S(1)}, u32[]{:S(2)}, u32[]{:S(2)}) collective-permute-start(bf16[176,1024]{1,0:T(8,128)(2,1)} %get-tuple-element.59), channel_id=1, source_target_pairs={{6,0},{7,1},{14,8},{15,9},{22,16},{23,17},{30,24},{31,25},{4,2},{5... | collective-permute-start | bytes 1081352 | tf_op jit(solution)/shard_map/ppermute | solution.py:251
  26.2 1.3 %collective-permute-start.24 = (bf16[176,1024]{1,0:T(8,128)(2,1)S(1)}, bf16[176,1024]{1,0:T(8,128)(2,1)S(1)}, u32[]{:S(2)}, u32[]{:S(2)}) collective-permute-start(bf16[176,1024]{1,0:T(8,128)(2,1)S(1)} %collective-permute-done.15.refs_1_.refs_2_), channel_id=1, source_target_pairs={{16,0},{8,1},{24,8},{0,9},{17,16},{9,17},{25,24},{1,25},{18,2},{10... | collective-permute-start | bytes 1081352 | tf_op jit(solution)/shard_map/ppermute | solution.py:254
  27.5 0.7 collective-permute-start.23
  28.2 0.0 collective-permute-done.19.refs_4_.refs_6_
  28.2 0.1 broadcast_in_dim.172
  28.3 0.1 select_reduce_fusion.4
  28.4 0.6 all_to_all.21
  29.1 3.4 %all-to-all-start.2 = ((s32[32,1,256]{2,1,0:T(1,128)}), s32[32,1,256]{2,1,0:T(1,128)S(1)}, u32[]{:S(2)}, u32[]{:S(2)}) async-start(s32[32,1,256]{2,1,0:T(1,128)} %all_to_all.21), calls=%async_computation.2 | async-start | bytes 65536 | tf_op jit(solution)/shard_map/all_to_all | solution.py:295
  32.5 0.0 collective-permute-done.20.refs_2_.refs_3_
  32.5 1.6 %collective-permute-start.28 = (bf16[176,1024]{1,0:T(8,128)(2,1)S(1)}, bf16[176,1024]{1,0:T(8,128)(2,1)}, u32[]{:S(2)}, u32[]{:S(2)}) collective-permute-start(bf16[176,1024]{1,0:T(8,128)(2,1)S(1)} %collective-permute-done.20.refs_2_.refs_3_), channel_id=1, source_target_pairs={{16,0},{8,1},{24,8},{0,9},{17,16},{9,17},{25,24},{1,25},{18,2},{10... | collective-permute-start | bytes 1081352 | tf_op jit(solution)/shard_map/ppermute | solution.py:254
  34.1 0.5 collective-permute-start.26
  34.6 2.0 %collective-permute-done.21.refs_4_ = bf16[176,1024]{1,0:T(8,128)(2,1)S(1)} collective-permute-done((bf16[176,1024]{1,0:T(8,128)(2,1)}, bf16[176,1024]{1,0:T(8,128)(2,1)S(1)}, u32[]{:S(2)}, u32[]{:S(2)}) %collective-permute-start.21) | collective-permute-done | bytes 360480 | tf_op jit(solution)/shard_map/ppermute | solution.py:251
  36.5 0.9 %collective-permute-done.24.refs_10_.refs_14_ = bf16[176,1024]{1,0:T(8,128)(2,1)S(1)} collective-permute-done((bf16[176,1024]{1,0:T(8,128)(2,1)S(1)}, bf16[176,1024]{1,0:T(8,128)(2,1)S(1)}, u32[]{:S(2)}, u32[]{:S(2)}) %collective-permute-start.24) | collective-permute-done | bytes 360480 | tf_op jit(solution)/shard_map/ppermute | solution.py:254
  37.5 1.5 %collective-permute-done.23.refs_7_.refs_10_ = bf16[176,1024]{1,0:T(8,128)(2,1)} collective-permute-done((bf16[176,1024]{1,0:T(8,128)(2,1)S(1)}, bf16[176,1024]{1,0:T(8,128)(2,1)}, u32[]{:S(2)}, u32[]{:S(2)}) %collective-permute-start.23) | collective-permute-done | bytes 360480 | tf_op jit(solution)/shard_map/ppermute | solution.py:254
  39.0 0.0 collective-permute-start.29
  39.0 2.0 %collective-permute-start.27 = (bf16[176,1024]{1,0:T(8,128)(2,1)S(1)}, bf16[176,1024]{1,0:T(8,128)(2,1)}, u32[]{:S(2)}, u32[]{:S(2)}) collective-permute-start(bf16[176,1024]{1,0:T(8,128)(2,1)S(1)} %collective-permute-done.21.refs_4_), channel_id=1, source_target_pairs={{1,0},{17,1},{9,8},{25,9},{0,16},{16,17},{8,24},{24,25},{3,2},{19,... | collective-permute-start | bytes 1081352 | tf_op jit(solution)/shard_map/ppermute | solution.py:254
  41.0 0.0 collective-permute-start.22
  41.0 2.9 %all-to-all-done.2 = s32[32,1,256]{2,1,0:T(1,128)S(1)} async-done(((s32[32,1,256]{2,1,0:T(1,128)}), s32[32,1,256]{2,1,0:T(1,128)S(1)}, u32[]{:S(2)}, u32[]{:S(2)}) %all-to-all-start.2) | async-done | bytes 32800 | tf_op jit(solution)/shard_map/all_to_all | solution.py:295
  43.9 0.1 reduce.4
  44.0 0.1 broadcast_in_dim.181
  44.2 0.1 select_reduce_fusion.3
  44.3 0.1 reshape.175
  44.4 0.1 mul.54
  44.5 0.1 multiply_reduce_fusion.1
  44.6 0.1 fusion.4
  44.7 0.2 copy.85
  45.0 0.1 convert_reduce_fusion.3
  45.1 0.9 %copy.86 = s32[4,704]{0,1:T(8,128)} copy(s32[4,704]{1,0:T(4,128)S(1)} %convert_reduce_fusion.3) | data formatting | bytes 22528 | tf_op jit(solution)/shard_map/reduce_sum | solution.py:308
  46.0 0.0 collective-permute-done.22.refs_5_.refs_7_
  46.0 0.1 collective-permute-start.25
  46.1 1.0 %broadcast_select_fusion.1 = s32[4,704]{0,1:T(8,128)S(1)} fusion(pred[4,704]{0,1:T(8,128)(4,1)S(1)} %copy.85, s32[4,704]{0,1:T(8,128)} %copy.86), kind=kLoop, calls=%fused_computation.30 | loop fusion | flops 2816 | bytes 25344 | tf_op jit(solution)/shard_map/jit(_where)/select_n | solution.py:309
  47.2 0.7 slice.63
  47.9 0.1 copy.94.refs_21_
  48.0 1.1 %copy.87.refs_12_.refs_20_ = s32[4,512]{1,0:T(4,128)S(1)} copy(s32[4,512]{0,1:T(8,128)} %slice.63) | data formatting | bytes 16384 | tf_op jit(solution)/shard_map/slice | solution.py:313
  49.1 0.0 collective-permute-done.26.refs_8_.refs_11_
  49.1 0.0 copy-start.7
  49.1 1.0 %copy-done.7 = bf16[176,1024]{1,0:T(8,128)(2,1)S(1)} copy-done((bf16[176,1024]{1,0:T(8,128)(2,1)S(1)}, bf16[176,1024]{1,0:T(8,128)(2,1)}, u32[]{:S(2)}) %copy-start.7) | copy-done | bytes 360472
  50.1 5.1 %shard_map.58.refs_17_ = f32[4,512]{1,0:T(4,128)S(1)} custom-call(bf16[176,1024]{1,0:T(8,128)(2,1)S(1)} %get-tuple-element.54.refs_0_.refs_1_, bf16[176,1024]{1,0:T(8,128)(2,1)S(1)} %collective-permute-done.15.refs_1_.refs_2_, bf16[176,1024]{1,0:T(8,128)(2,1)S(1)} %collective-permute-done.20.refs_2_.refs_3_, ...), custom_call_target="tpu_custom_call" | custom-call | flops 2684354560 | bytes 4194304 | tf_op jit(solution)/shard_map/pallas_call | solution.py:326
  55.2 0.0 collective-permute-done.29.refs_16_
  55.3 0.0 collective-permute-done.25.refs_8_
  55.3 7.5 %shard_map.59 = f32[4,32,128]{2,1,0:T(8,128)} custom-call(s32[1]{0:T(128)} %bitcast.12.plane_ref.refs_0_, bf16[176,1024]{1,0:T(8,128)(2,1)S(1)} %get-tuple-element.54.refs_0_.refs_1_, bf16[176,1024]{1,0:T(8,128)(2,1)S(1)} %collective-permute-done.15.refs_1_.refs_2_, bf16[176,1024]{1,0:T(8,128)(2,1)S(1)} %collective-permute-done.20.refs_2_.refs_3_, ...), custom_call_target="tpu_custom_call" | custom-call | tf_op jit(solution)/shard_map/pallas_call | solution.py:337
  62.8 4.0 %all-to-all-start.3 = ((f32[32,4,128]{2,1,0:T(4,128)}), f32[32,4,128]{2,1,0:T(4,128)S(1)}, u32[]{:S(2)}, u32[]{:S(2)}) async-start(f32[32,4,128]{2,1,0:T(4,128)} %bitcast.19), calls=%async_computation.3 | async-start | bytes 131072 | tf_op jit(solution)/shard_map/all_to_all | solution.py:355
  66.8 0.7 slice_reduce_fusion
  68.2 5.7 %all-to-all-done.3 = f32[32,4,128]{2,1,0:T(4,128)S(1)} async-done(((f32[32,4,128]{2,1,0:T(4,128)}), f32[32,4,128]{2,1,0:T(4,128)S(1)}, u32[]{:S(2)}, u32[]{:S(2)}) %all-to-all-start.3) | async-done | bytes 65568 | tf_op jit(solution)/shard_map/all_to_all | solution.py:355
  73.9 0.6 copy-done.17
  (37 shorter events, 0.3 us)
Async XLA Ops:
  0.0 23.3 %copy-start.16 = (s32[4,8]{1,0:T(4,128)S(1)}, s32[4,8]{1,0:T(4,128)}, u32[]{:S(2)}) copy-start(s32[4,8]{1,0:T(4,128)} %constant.109.clone) | copy-start | bytes 388
  0.0 9.2 %copy-start.14 = (s32[512]{0:T(512)S(1)}, s32[512]{0:T(512)}, u32[]{:S(2)}) copy-start(s32[512]{0:T(512)} %param.8) | copy-start | bytes 6148
  0.0 12.8 %copy-start.15 = (s32[1,512]{1,0:T(1,128)S(1)}, s32[1,512]{1,0:T(1,128)}, u32[]{:S(2)}) copy-start(s32[1,512]{1,0:T(1,128)} %param.9) | copy-start | bytes 6148
  3.5 5.6 %collective-permute-start.16 = (bf16[176,1024]{1,0:T(8,128)(2,1)S(1)}, bf16[176,1024]{1,0:T(8,128)(2,1)S(1)}, u32[]{:S(2)}, u32[]{:S(2)}) collective-permute-start(bf16[176,1024]{1,0:T(8,128)(2,1)S(1)} %get-tuple-element.54.refs_0_.refs_1_), channel_id=1, source_target_pairs={{8,0},{9,1},{0,8},{1,9},{24,16},{25,17},{16,24},{17,25},{10,2},{11... | collective-permute-start | bytes 1081352 | tf_op jit(solution)/shard_map/ppermute | solution.py:254
  4.0 19.1 %collective-permute-start.15 = (bf16[176,1024]{1,0:T(8,128)(2,1)S(1)}, bf16[176,1024]{1,0:T(8,128)(2,1)S(1)}, u32[]{:S(2)}, u32[]{:S(2)}) collective-permute-start(bf16[176,1024]{1,0:T(8,128)(2,1)S(1)} %get-tuple-element.52), channel_id=1, source_target_pairs={{2,0},{3,1},{10,8},{11,9},{18,16},{19,17},{26,24},{27,25},{0,2},{1... | collective-permute-start | bytes 1081352 | tf_op jit(solution)/shard_map/ppermute | solution.py:251
  6.6 25.9 %collective-permute-start.20 = (bf16[176,1024]{1,0:T(8,128)(2,1)}, bf16[176,1024]{1,0:T(8,128)(2,1)S(1)}, u32[]{:S(2)}, u32[]{:S(2)}) collective-permute-start(bf16[176,1024]{1,0:T(8,128)(2,1)} %get-tuple-element.57), channel_id=1, source_target_pairs={{4,0},{5,1},{12,8},{13,9},{20,16},{21,17},{28,24},{29,25},{6,2},{7... | collective-permute-start | bytes 1081352 | tf_op jit(solution)/shard_map/ppermute | solution.py:251
  9.2 13.9 %collective-permute-start.18 = (bf16[176,1024]{1,0:T(8,128)(2,1)S(1)}, bf16[176,1024]{1,0:T(8,128)(2,1)S(1)}, u32[]{:S(2)}, u32[]{:S(2)}) collective-permute-start(bf16[176,1024]{1,0:T(8,128)(2,1)S(1)} %get-tuple-element.54.refs_0_.refs_1_), channel_id=1, source_target_pairs={{16,0},{8,1},{24,8},{0,9},{17,16},{9,17},{25,24},{1,25},{18,2},{10... | collective-permute-start | bytes 1081352 | tf_op jit(solution)/shard_map/ppermute | solution.py:254
  10.3 12.7 %collective-permute-start.17 = (bf16[176,1024]{1,0:T(8,128)(2,1)S(1)}, bf16[176,1024]{1,0:T(8,128)(2,1)S(1)}, u32[]{:S(2)}, u32[]{:S(2)}) collective-permute-start(bf16[176,1024]{1,0:T(8,128)(2,1)S(1)} %get-tuple-element.54.refs_0_.refs_1_), channel_id=1, source_target_pairs={{1,0},{17,1},{9,8},{25,9},{0,16},{16,17},{8,24},{24,25},{3,2},{19,... | collective-permute-start | bytes 1081352 | tf_op jit(solution)/shard_map/ppermute | solution.py:254
  23.1 5.1 %collective-permute-start.19 = (bf16[176,1024]{1,0:T(8,128)(2,1)S(1)}, bf16[176,1024]{1,0:T(8,128)(2,1)S(1)}, u32[]{:S(2)}, u32[]{:S(2)}) collective-permute-start(bf16[176,1024]{1,0:T(8,128)(2,1)S(1)} %collective-permute-done.15.refs_1_.refs_2_), channel_id=1, source_target_pairs={{8,0},{9,1},{0,8},{1,9},{24,16},{25,17},{16,24},{17,25},{10,2},{11... | collective-permute-start | bytes 1081352 | tf_op jit(solution)/shard_map/ppermute | solution.py:254
  23.5 13.0 %collective-permute-start.21 = (bf16[176,1024]{1,0:T(8,128)(2,1)}, bf16[176,1024]{1,0:T(8,128)(2,1)S(1)}, u32[]{:S(2)}, u32[]{:S(2)}) collective-permute-start(bf16[176,1024]{1,0:T(8,128)(2,1)} %get-tuple-element.59), channel_id=1, source_target_pairs={{6,0},{7,1},{14,8},{15,9},{22,16},{23,17},{30,24},{31,25},{4,2},{5... | collective-permute-start | bytes 1081352 | tf_op jit(solution)/shard_map/ppermute | solution.py:251
  26.2 11.3 %collective-permute-start.24 = (bf16[176,1024]{1,0:T(8,128)(2,1)S(1)}, bf16[176,1024]{1,0:T(8,128)(2,1)S(1)}, u32[]{:S(2)}, u32[]{:S(2)}) collective-permute-start(bf16[176,1024]{1,0:T(8,128)(2,1)S(1)} %collective-permute-done.15.refs_1_.refs_2_), channel_id=1, source_target_pairs={{16,0},{8,1},{24,8},{0,9},{17,16},{9,17},{25,24},{1,25},{18,2},{10... | collective-permute-start | bytes 1081352 | tf_op jit(solution)/shard_map/ppermute | solution.py:254
  27.5 11.5 %collective-permute-start.23 = (bf16[176,1024]{1,0:T(8,128)(2,1)S(1)}, bf16[176,1024]{1,0:T(8,128)(2,1)}, u32[]{:S(2)}, u32[]{:S(2)}) collective-permute-start(bf16[176,1024]{1,0:T(8,128)(2,1)S(1)} %collective-permute-done.15.refs_1_.refs_2_), channel_id=1, source_target_pairs={{1,0},{17,1},{9,8},{25,9},{0,16},{16,17},{8,24},{24,25},{3,2},{19,... | collective-permute-start | bytes 1081352 | tf_op jit(solution)/shard_map/ppermute | solution.py:254
  29.1 14.8 %all-to-all-start.2 = ((s32[32,1,256]{2,1,0:T(1,128)}), s32[32,1,256]{2,1,0:T(1,128)S(1)}, u32[]{:S(2)}, u32[]{:S(2)}) async-start(s32[32,1,256]{2,1,0:T(1,128)} %all_to_all.21), calls=%async_computation.2 | async-start | bytes 65536 | tf_op jit(solution)/shard_map/all_to_all | solution.py:295
  32.5 16.6 %collective-permute-start.28 = (bf16[176,1024]{1,0:T(8,128)(2,1)S(1)}, bf16[176,1024]{1,0:T(8,128)(2,1)}, u32[]{:S(2)}, u32[]{:S(2)}) collective-permute-start(bf16[176,1024]{1,0:T(8,128)(2,1)S(1)} %collective-permute-done.20.refs_2_.refs_3_), channel_id=1, source_target_pairs={{16,0},{8,1},{24,8},{0,9},{17,16},{9,17},{25,24},{1,25},{18,2},{10... | collective-permute-start | bytes 1081352 | tf_op jit(solution)/shard_map/ppermute | solution.py:254
  34.1 15.1 %collective-permute-start.26 = (bf16[176,1024]{1,0:T(8,128)(2,1)S(1)}, bf16[176,1024]{1,0:T(8,128)(2,1)}, u32[]{:S(2)}, u32[]{:S(2)}) collective-permute-start(bf16[176,1024]{1,0:T(8,128)(2,1)S(1)} %collective-permute-done.20.refs_2_.refs_3_), channel_id=1, source_target_pairs={{1,0},{17,1},{9,8},{25,9},{0,16},{16,17},{8,24},{24,25},{3,2},{19,... | collective-permute-start | bytes 1081352 | tf_op jit(solution)/shard_map/ppermute | solution.py:254
  37.5 8.6 %copy-start.6 = (bf16[176,1024]{1,0:T(8,128)(2,1)}, bf16[176,1024]{1,0:T(8,128)(2,1)S(1)}, u32[]{:S(2)}) copy-start(bf16[176,1024]{1,0:T(8,128)(2,1)S(1)} %collective-permute-done.24.refs_10_.refs_14_) | copy-start | bytes 1081348
  39.0 16.3 %collective-permute-start.29 = (bf16[176,1024]{1,0:T(8,128)(2,1)S(1)}, bf16[176,1024]{1,0:T(8,128)(2,1)}, u32[]{:S(2)}, u32[]{:S(2)}) collective-permute-start(bf16[176,1024]{1,0:T(8,128)(2,1)S(1)} %collective-permute-done.21.refs_4_), channel_id=1, source_target_pairs={{16,0},{8,1},{24,8},{0,9},{17,16},{9,17},{25,24},{1,25},{18,2},{10... | collective-permute-start | bytes 1081352 | tf_op jit(solution)/shard_map/ppermute | solution.py:254
  39.0 16.3 %collective-permute-start.27 = (bf16[176,1024]{1,0:T(8,128)(2,1)S(1)}, bf16[176,1024]{1,0:T(8,128)(2,1)}, u32[]{:S(2)}, u32[]{:S(2)}) collective-permute-start(bf16[176,1024]{1,0:T(8,128)(2,1)S(1)} %collective-permute-done.21.refs_4_), channel_id=1, source_target_pairs={{1,0},{17,1},{9,8},{25,9},{0,16},{16,17},{8,24},{24,25},{3,2},{19,... | collective-permute-start | bytes 1081352 | tf_op jit(solution)/shard_map/ppermute | solution.py:254
  41.0 5.0 %collective-permute-start.22 = (bf16[176,1024]{1,0:T(8,128)(2,1)S(1)}, bf16[176,1024]{1,0:T(8,128)(2,1)}, u32[]{:S(2)}, u32[]{:S(2)}) collective-permute-start(bf16[176,1024]{1,0:T(8,128)(2,1)S(1)} %collective-permute-done.20.refs_2_.refs_3_), channel_id=1, source_target_pairs={{8,0},{9,1},{0,8},{1,9},{24,16},{25,17},{16,24},{17,25},{10,2},{11... | collective-permute-start | bytes 1081352 | tf_op jit(solution)/shard_map/ppermute | solution.py:254
  43.9 0.8 %copy-start.12 = (s32[32,1,256]{2,1,0:T(1,128)}, s32[32,1,256]{2,1,0:T(1,128)S(1)}, u32[]{:S(2)}) copy-start(s32[32,1,256]{2,1,0:T(1,128)S(1)} %all-to-all-done.2) | copy-start | bytes 98308
  46.0 9.2 %collective-permute-start.25 = (bf16[176,1024]{1,0:T(8,128)(2,1)S(1)}, bf16[176,1024]{1,0:T(8,128)(2,1)}, u32[]{:S(2)}, u32[]{:S(2)}) collective-permute-start(bf16[176,1024]{1,0:T(8,128)(2,1)S(1)} %collective-permute-done.21.refs_4_), channel_id=1, source_target_pairs={{8,0},{9,1},{0,8},{1,9},{24,16},{25,17},{16,24},{17,25},{10,2},{11... | collective-permute-start | bytes 1081352 | tf_op jit(solution)/shard_map/ppermute | solution.py:254
  49.1 1.0 %copy-start.7 = (bf16[176,1024]{1,0:T(8,128)(2,1)S(1)}, bf16[176,1024]{1,0:T(8,128)(2,1)}, u32[]{:S(2)}) copy-start(bf16[176,1024]{1,0:T(8,128)(2,1)} %copy-done.6) | copy-start | bytes 1081348
  50.1 5.2 %copy-start.8 = (bf16[176,1024]{1,0:T(8,128)(2,1)S(1)}, bf16[176,1024]{1,0:T(8,128)(2,1)}, u32[]{:S(2)}) copy-start(bf16[176,1024]{1,0:T(8,128)(2,1)} %copy-done.6) | copy-start | bytes 1081348
  55.2 11.6 %copy-start.13 = (s32[32,1,256]{2,1,0:T(1,128)S(1)}, s32[32,1,256]{2,1,0:T(1,128)}, u32[]{:S(2)}) copy-start(s32[32,1,256]{2,1,0:T(1,128)} %copy-done.12) | copy-start | bytes 98308
  62.8 11.1 %all-to-all-start.3 = ((f32[32,4,128]{2,1,0:T(4,128)}), f32[32,4,128]{2,1,0:T(4,128)S(1)}, u32[]{:S(2)}, u32[]{:S(2)}) async-start(f32[32,4,128]{2,1,0:T(4,128)} %bitcast.19), calls=%async_computation.3 | async-start | bytes 131072 | tf_op jit(solution)/shard_map/all_to_all | solution.py:355
  73.9 0.6 copy-start.17

commit v9 on v8

--- a/solution.py
+++ b/solution.py
@@ -93,6 +93,14 @@
     place_ref[...] = jnp.where(there, got[0:1, :] * 128 + got[1:2, :], group_size)
 
 
+def diagonal(n):
+    return lax.broadcasted_iota(jnp.int32, (n, n), 0) == lax.broadcasted_iota(jnp.int32, (n, n), 1)
+
+
+def as_column(row):
+    return jnp.max(jnp.where(diagonal(row.shape[1]), row, -2.0), axis=1, keepdims=True)
+
+
 class Best:
     def __init__(self, start):
         self.row, self.column = start, None
@@ -106,8 +114,7 @@
     def as_row(self):
         if self.column is None:
             return self.row
-        n = self.column.shape[0]
-        eye = lax.broadcasted_iota(jnp.int32, (n, n), 0) == lax.broadcasted_iota(jnp.int32, (n, n), 1)
+        eye = diagonal(self.column.shape[0])
         return jnp.maximum(self.row, jnp.max(jnp.where(eye, self.column, -1.0), axis=0, keepdims=True))
 
 
@@ -148,15 +155,18 @@
 
 
 def early_kernel(pairs, count, early, *refs):
-    *chunks, label_ref, label_col_ref, out_ref, blocks, sems = refs
+    *chunks, label_ref, last_label_ref, out_ref, label_col_ref, blocks, sems = refs
     need = loader(chunks, count, blocks, sems)
+    for j in sorted({j for j, _ in pairs}):
+        label_col_ref[:early, j : j + 1] = as_column(label_ref[j : j + 1, :])
+        label_col_ref[early:, j : j + 1] = as_column(last_label_ref[j : j + 1, :])
     best = [Best(jnp.full((1, early), -1.0, jnp.float32)) for _ in range(count)]
     for j, k in pairs:
         need(j, k)
         sims = similar(
             blocks[j, :early],
             blocks[k, :early],
-            label_col_ref[:, j : j + 1],
+            label_col_ref[:early, j : j + 1],
             label_ref[k : k + 1, :],
             0 if j == k else None,
         )
@@ -306,12 +316,10 @@
     mine = (mine[:, None] == jnp.arange(n_row * wide)[None, :]).astype(jnp.int32)
     places = jnp.sum(mine[:, :, None] * places[None, :, :], axis=1)
     labels = jnp.sum((places[:, None, :] >= ends[None, :, None]).astype(jnp.int32), axis=1)
-    labels = jnp.where(places < group_size, labels, -1)
+    labels = jnp.where(places < group_size, labels, -1).astype(jnp.float32)
 
     early = (slots - cap) // 256 * 256
-    label_cols = labels.T
-    facts = places[:, :early], places[:, early:], labels[:, :early], labels[:, early:], label_cols[:early], label_cols
-    place, last_place, label, last_label, label_col, label_cols = facts
+    label, last_label = labels[:, :early], labels[:, early:]
     blocks = [own] + [[moved[j - 1] for moved in rounds] for j in range(1, count)]
     any_space = pl.BlockSpec(memory_space=pltpu.HBM)
     area = 4 * slots * slots
@@ -323,17 +331,20 @@
         ]
 
     limit = 8 + (2 * count * slots * width + 5 * area) // 2**20
-    first_best = pl.pallas_call(
+    first_best, label_cols = pl.pallas_call(
         functools.partial(early_kernel, pairs, count, early),
-        out_shape=jax.ShapeDtypeStruct((count, early), jnp.float32),
+        out_shape=[
+            jax.ShapeDtypeStruct((count, early), jnp.float32),
+            jax.ShapeDtypeStruct((slots, count), jnp.float32),
+        ],
         in_specs=[any_space] * (count * (groups - 1)) + [VMEM] * 2,
-        out_specs=VMEM,
+        out_specs=[VMEM] * 2,
         scratch_shapes=scratch(groups - 1),
         compiler_params=kernel_params(limit),
         cost_estimate=pl.CostEstimate(
             flops=2 * len(pairs) * early * early * width, bytes_accessed=2 * count * early * width, transcendentals=0
         ),
-    )(*[part for block in blocks for part in block[:-1]], label, label_col)
+    )(*[part for block in blocks for part in block[:-1]], label, last_label)
     best = pl.pallas_call(
         functools.partial(late_kernel, pairs, count, group_size),
         out_shape=jax.ShapeDtypeStruct((n_row, group_size // 128, 128), jnp.float32),
@@ -345,8 +356,8 @@
         plane_ref,
         *itertools.chain(*blocks),
         first_best,
-        place,
-        last_place,
+        places[:, :early],
+        places[:, early:],
         label,
         last_label,
         label_cols,

time: 74.9 us -> 73.3 us (0.979)
  local copies, waits for them, and re-layouts: 5.89 us -> 1.82 us
  waiting for transfers between devices: 23.1 us -> 26.8 us
  other arithmetic: 3.68 us -> 2.66 us
    ppermute x12, waiting for transfers between devices: 2.46 us -> 5.91 us  [inside(): lax.ppermute(part, AXES, [(device(int(held[j, i]), h), device(i, h)) for...]
    slice x4 -> x2, local copies, waits for them, and re-layouts: 1.83 us -> 0.01 us  [best_matches(): label, last_label = (labels[:, :early], labels[:, early:])]
    unnamed x20 -> x9, local copies, waits for them, and re-layouts: 1.66 us -> 0.59 us
    select_n x1 -> x0, other arithmetic: 1.02 us -> none  [best_matches(): labels = jnp.where(places < group_size, labels, -1)]
    reduce_sum x1 -> x0, local copies, waits for them, and re-layouts: 0.94 us -> none  [best_matches(): jnp.sum((places[:, None, :] >= ends[None, :, None]).astype(jnp.int32), ax...]
  transfers between devices with their start and end apart: 17 -> 17, of which waited for: 6 -> 10; matrix products, arithmetic and copies ran while one was open for 10% -> 4% of each run, Pallas kernels for 7% -> 7%
where the time goes in v9:
time: 73.3 us; the launch traced here: 73.1 us
  waiting for transfers between devices  26.8 us (37%)
  starting transfers between devices  23.4 us (32%)
  Pallas kernels  16.6 us (23%)
  other arithmetic  2.66 us (4%)
  local copies, waits for them, and re-layouts  1.82 us (2%)
  between operations  1.6 us (2%)
    ppermute x3, waiting for transfers between devices, across(): lax.ppermute(part, AXES, [(device(i, h ^ k), device(i, h)) for i, h in pl...  12 us
    ppermute x12, starting transfers between devices, inside(): lax.ppermute(part, AXES, [(device(int(held[j, i]), h), device(i, h)) for...  8.86 us
    ppermute x3, starting transfers between devices, across(): lax.ppermute(part, AXES, [(device(i, h ^ k), device(i, h)) for i, h in pl...  7.83 us
    pallas_call x1, Pallas kernels, best_matches(): pl.pallas_call(functools.partial(late_kernel, pairs, count, group_size),...  7.61 us
    ppermute x12, waiting for transfers between devices, inside(): lax.ppermute(part, AXES, [(device(int(held[j, i]), h), device(i, h)) for...  5.91 us
    all_to_all x1, waiting for transfers between devices, best_matches(): lax.all_to_all(best.reshape(devs, -1, 128), AXES, split_axis=0, concat_ax...  5.9 us
    pallas_call x1, Pallas kernels, best_matches(): pl.pallas_call(functools.partial(early_kernel, pairs, count, early), out_...  5.45 us
    pallas_call x1, Pallas kernels, best_matches(): pl.pallas_call(functools.partial(pack_kernel, groups, cap, group_size), o...  3.53 us
  transfers between devices with their start and end apart: 17, of which 10 were waited for; matrix products, arithmetic and copies ran while one was open for 4% of the time, Pallas kernels for 7%

profile of v9, /device:TPU:0, one launch (start us, length us, event | category | flops | bytes accessed | tf_op | source)
XLA Modules:
  0.0 73.1 jit_solution(5835674999253324565)
XLA Ops:
  0.0 0.0 copy-start.6
  0.0 3.5 %shard_map.57 = (s32[1,704]{1,0:T(1,128)S(1)}, bf16[176,1024]{1,0:T(8,128)(2,1)S(1)}, bf16[176,1024]{1,0:T(8,128)(2,1)S(1)}, bf16[176,1024]{1,0:T(8,128)(2,1)}, bf16[176,1024]{1,0:T(8,128)(2,1)}) custom-call(s32[1]{0:T(128)} %bitcast.11.plane_ref.refs_0_, s32[1,512]{1,0:T(1,128)} %bitcast.32, f32[512,1024]{1,0:T(8,128)} %emb_ref.1), custom_call_target="tpu_custom_call" | custom-call | tf_op jit(solution)/shard_map/pallas_call | solution.py:249
  3.5 0.5 collective-permute-start.16
  4.0 2.6 %collective-permute-start.15 = (bf16[176,1024]{1,0:T(8,128)(2,1)S(1)}, bf16[176,1024]{1,0:T(8,128)(2,1)S(1)}, u32[]{:S(2)}, u32[]{:S(2)}) collective-permute-start(bf16[176,1024]{1,0:T(8,128)(2,1)S(1)} %get-tuple-element.56), channel_id=1, source_target_pairs={{2,0},{3,1},{10,8},{11,9},{18,16},{19,17},{26,24},{27,25},{0,2},{1... | collective-permute-start | bytes 1081352 | tf_op jit(solution)/shard_map/ppermute | solution.py:261
  6.6 2.6 %collective-permute-start.20 = (bf16[176,1024]{1,0:T(8,128)(2,1)}, bf16[176,1024]{1,0:T(8,128)(2,1)S(1)}, u32[]{:S(2)}, u32[]{:S(2)}) collective-permute-start(bf16[176,1024]{1,0:T(8,128)(2,1)} %get-tuple-element.61), channel_id=1, source_target_pairs={{4,0},{5,1},{12,8},{13,9},{20,16},{21,17},{28,24},{29,25},{6,2},{7... | collective-permute-start | bytes 1081352 | tf_op jit(solution)/shard_map/ppermute | solution.py:261
  9.2 0.0 copy-done.4
  9.2 0.0 collective-permute-done.16.refs_3_.refs_5_
  9.2 1.1 %collective-permute-start.18 = (bf16[176,1024]{1,0:T(8,128)(2,1)S(1)}, bf16[176,1024]{1,0:T(8,128)(2,1)S(1)}, u32[]{:S(2)}, u32[]{:S(2)}) collective-permute-start(bf16[176,1024]{1,0:T(8,128)(2,1)S(1)} %get-tuple-element.58.refs_0_.refs_1_), channel_id=1, source_target_pairs={{16,0},{8,1},{24,8},{0,9},{17,16},{9,17},{25,24},{1,25},{18,2},{10... | collective-permute-start | bytes 1081352 | tf_op jit(solution)/shard_map/ppermute | solution.py:264
  10.3 1.0 %collective-permute-start.17 = (bf16[176,1024]{1,0:T(8,128)(2,1)S(1)}, bf16[176,1024]{1,0:T(8,128)(2,1)S(1)}, u32[]{:S(2)}, u32[]{:S(2)}) collective-permute-start(bf16[176,1024]{1,0:T(8,128)(2,1)S(1)} %get-tuple-element.58.refs_0_.refs_1_), channel_id=1, source_target_pairs={{1,0},{17,1},{9,8},{25,9},{0,16},{16,17},{8,24},{24,25},{3,2},{19,... | collective-permute-start | bytes 1081352 | tf_op jit(solution)/shard_map/ppermute | solution.py:264
  11.3 0.1 convert_reduce_fusion.5
  11.4 0.7 reduce_max.46
  12.8 0.0 copy-done.5
  12.8 0.1 convert_reduce_fusion.4
  13.0 10.1 %collective-permute-done.15.refs_1_.refs_2_ = bf16[176,1024]{1,0:T(8,128)(2,1)S(1)} collective-permute-done((bf16[176,1024]{1,0:T(8,128)(2,1)S(1)}, bf16[176,1024]{1,0:T(8,128)(2,1)S(1)}, u32[]{:S(2)}, u32[]{:S(2)}) %collective-permute-start.15) | collective-permute-done | bytes 360480 | tf_op jit(solution)/shard_map/ppermute | solution.py:261
  23.0 0.0 collective-permute-done.18.refs_9_.refs_13_
  23.1 0.0 collective-permute-done.17.refs_6_.refs_9_
  23.1 0.0 collective-permute-start.19
  23.1 0.1 pad_add_fusion.1
  23.1 0.1 pad.7.clone
  23.2 0.1 pad.6.clone
  23.3 0.0 copy-done.6
  23.3 0.1 select_reduce_fusion.5
  23.4 0.1 fusion.7
  23.5 2.7 %collective-permute-start.21 = (bf16[176,1024]{1,0:T(8,128)(2,1)}, bf16[176,1024]{1,0:T(8,128)(2,1)S(1)}, u32[]{:S(2)}, u32[]{:S(2)}) collective-permute-start(bf16[176,1024]{1,0:T(8,128)(2,1)} %get-tuple-element.63), channel_id=1, source_target_pairs={{6,0},{7,1},{14,8},{15,9},{22,16},{23,17},{30,24},{31,25},{4,2},{5... | collective-permute-start | bytes 1081352 | tf_op jit(solution)/shard_map/ppermute | solution.py:261
  26.2 1.3 %collective-permute-start.24 = (bf16[176,1024]{1,0:T(8,128)(2,1)S(1)}, bf16[176,1024]{1,0:T(8,128)(2,1)S(1)}, u32[]{:S(2)}, u32[]{:S(2)}) collective-permute-start(bf16[176,1024]{1,0:T(8,128)(2,1)S(1)} %collective-permute-done.15.refs_1_.refs_2_), channel_id=1, source_target_pairs={{16,0},{8,1},{24,8},{0,9},{17,16},{9,17},{25,24},{1,25},{18,2},{10... | collective-permute-start | bytes 1081352 | tf_op jit(solution)/shard_map/ppermute | solution.py:264
  27.5 0.7 collective-permute-start.23
  28.2 0.0 collective-permute-done.19.refs_4_.refs_6_
  28.2 0.1 broadcast_in_dim.172
  28.3 0.1 select_reduce_fusion.4
  28.4 0.6 all_to_all.21
  29.1 3.4 %all-to-all-start.2 = ((s32[32,1,256]{2,1,0:T(1,128)}), s32[32,1,256]{2,1,0:T(1,128)S(1)}, u32[]{:S(2)}, u32[]{:S(2)}) async-start(s32[32,1,256]{2,1,0:T(1,128)} %all_to_all.21), calls=%async_computation.2 | async-start | bytes 65536 | tf_op jit(solution)/shard_map/all_to_all | solution.py:305
  32.5 0.0 collective-permute-done.20.refs_2_.refs_3_
  32.5 1.6 %collective-permute-start.28 = (bf16[176,1024]{1,0:T(8,128)(2,1)S(1)}, bf16[176,1024]{1,0:T(8,128)(2,1)}, u32[]{:S(2)}, u32[]{:S(2)}) collective-permute-start(bf16[176,1024]{1,0:T(8,128)(2,1)S(1)} %collective-permute-done.20.refs_2_.refs_3_), channel_id=1, source_target_pairs={{16,0},{8,1},{24,8},{0,9},{17,16},{9,17},{25,24},{1,25},{18,2},{10... | collective-permute-start | bytes 1081352 | tf_op jit(solution)/shard_map/ppermute | solution.py:264
  34.0 0.5 collective-permute-start.26
  34.6 2.0 %collective-permute-done.21.refs_4_ = bf16[176,1024]{1,0:T(8,128)(2,1)S(1)} collective-permute-done((bf16[176,1024]{1,0:T(8,128)(2,1)}, bf16[176,1024]{1,0:T(8,128)(2,1)S(1)}, u32[]{:S(2)}, u32[]{:S(2)}) %collective-permute-start.21) | collective-permute-done | bytes 360480 | tf_op jit(solution)/shard_map/ppermute | solution.py:261
  36.5 0.9 %collective-permute-done.24.refs_10_.refs_14_ = bf16[176,1024]{1,0:T(8,128)(2,1)S(1)} collective-permute-done((bf16[176,1024]{1,0:T(8,128)(2,1)S(1)}, bf16[176,1024]{1,0:T(8,128)(2,1)S(1)}, u32[]{:S(2)}, u32[]{:S(2)}) %collective-permute-start.24) | collective-permute-done | bytes 360480 | tf_op jit(solution)/shard_map/ppermute | solution.py:264
  37.5 1.5 %collective-permute-done.23.refs_7_.refs_10_ = bf16[176,1024]{1,0:T(8,128)(2,1)} collective-permute-done((bf16[176,1024]{1,0:T(8,128)(2,1)S(1)}, bf16[176,1024]{1,0:T(8,128)(2,1)}, u32[]{:S(2)}, u32[]{:S(2)}) %collective-permute-start.23) | collective-permute-done | bytes 360480 | tf_op jit(solution)/shard_map/ppermute | solution.py:264
  39.0 0.0 collective-permute-start.29
  39.0 2.0 %collective-permute-start.27 = (bf16[176,1024]{1,0:T(8,128)(2,1)S(1)}, bf16[176,1024]{1,0:T(8,128)(2,1)}, u32[]{:S(2)}, u32[]{:S(2)}) collective-permute-start(bf16[176,1024]{1,0:T(8,128)(2,1)S(1)} %collective-permute-done.21.refs_4_), channel_id=1, source_target_pairs={{1,0},{17,1},{9,8},{25,9},{0,16},{16,17},{8,24},{24,25},{3,2},{19,... | collective-permute-start | bytes 1081352 | tf_op jit(solution)/shard_map/ppermute | solution.py:264
  41.0 0.0 collective-permute-start.22
  41.0 2.9 %all-to-all-done.2 = s32[32,1,256]{2,1,0:T(1,128)S(1)} async-done(((s32[32,1,256]{2,1,0:T(1,128)}), s32[32,1,256]{2,1,0:T(1,128)S(1)}, u32[]{:S(2)}, u32[]{:S(2)}) %all-to-all-start.2) | async-done | bytes 32800 | tf_op jit(solution)/shard_map/all_to_all | solution.py:305
  43.9 0.1 reduce.4
  44.0 0.1 broadcast_in_dim.181
  44.1 0.1 select_reduce_fusion.3
  44.3 0.1 reshape.175
  44.4 0.1 mul.54
  44.5 0.1 multiply_reduce_fusion.1
  44.6 0.1 fusion.4
  44.7 0.1 convert_reduce_fusion.3
  44.8 0.0 collective-permute-done.22.refs_5_.refs_7_
  44.8 0.2 collective-permute-start.25
  45.1 0.5 collective-permute-done.28.refs_11_.refs_15_
  45.6 1.3 %collective-permute-done.26.refs_8_.refs_11_ = bf16[176,1024]{1,0:T(8,128)(2,1)} collective-permute-done((bf16[176,1024]{1,0:T(8,128)(2,1)S(1)}, bf16[176,1024]{1,0:T(8,128)(2,1)}, u32[]{:S(2)}, u32[]{:S(2)}) %collective-permute-start.26) | collective-permute-done | bytes 360480 | tf_op jit(solution)/shard_map/ppermute | solution.py:264
  46.9 5.5 %shard_map.58 = (f32[4,512]{1,0:T(4,128)S(1)}, f32[704,4]{1,0:T(8,128)S(1)}) custom-call(bf16[176,1024]{1,0:T(8,128)(2,1)S(1)} %get-tuple-element.58.refs_0_.refs_1_, bf16[176,1024]{1,0:T(8,128)(2,1)S(1)} %collective-permute-done.15.refs_1_.refs_2_, bf16[176,1024]{1,0:T(8,128)(2,1)S(1)} %collective-permute-done.20.refs_2_.refs_3_, ...), custom_call_target="tpu_custom_call" | custom-call | flops 2684354560 | bytes 4194304 | tf_op jit(solution)/shard_map/pallas_call | solution.py:334
  52.3 0.3 collective-permute-done.29.refs_16_
  52.6 1.4 %collective-permute-done.27.refs_12_ = bf16[176,1024]{1,0:T(8,128)(2,1)} collective-permute-done((bf16[176,1024]{1,0:T(8,128)(2,1)S(1)}, bf16[176,1024]{1,0:T(8,128)(2,1)}, u32[]{:S(2)}, u32[]{:S(2)}) %collective-permute-start.27) | collective-permute-done | bytes 360480 | tf_op jit(solution)/shard_map/ppermute | solution.py:264
  54.0 0.0 collective-permute-done.25.refs_8_
  54.0 7.6 %shard_map.59 = f32[4,32,128]{2,1,0:T(8,128)} custom-call(s32[1]{0:T(128)} %bitcast.11.plane_ref.refs_0_, bf16[176,1024]{1,0:T(8,128)(2,1)S(1)} %get-tuple-element.58.refs_0_.refs_1_, bf16[176,1024]{1,0:T(8,128)(2,1)S(1)} %collective-permute-done.15.refs_1_.refs_2_, bf16[176,1024]{1,0:T(8,128)(2,1)S(1)} %collective-permute-done.20.refs_2_.refs_3_, ...), custom_call_target="tpu_custom_call" | custom-call | tf_op jit(solution)/shard_map/pallas_call | solution.py:348
  61.6 3.3 %all-to-all-start.3 = ((f32[32,4,128]{2,1,0:T(4,128)}), f32[32,4,128]{2,1,0:T(4,128)S(1)}, u32[]{:S(2)}, u32[]{:S(2)}) async-start(f32[32,4,128]{2,1,0:T(4,128)} %bitcast.17), calls=%async_computation.3 | async-start | bytes 131072 | tf_op jit(solution)/shard_map/all_to_all | solution.py:366
  64.9 0.7 slice_reduce_fusion
  66.3 5.9 %all-to-all-done.3 = f32[32,4,128]{2,1,0:T(4,128)S(1)} async-done(((f32[32,4,128]{2,1,0:T(4,128)}), f32[32,4,128]{2,1,0:T(4,128)S(1)}, u32[]{:S(2)}, u32[]{:S(2)}) %all-to-all-start.3) | async-done | bytes 65568 | tf_op jit(solution)/shard_map/all_to_all | solution.py:366
  72.2 0.3 conditional.1
  72.5 0.0 copy-start.7
  72.5 0.6 copy-done.7
  (21 shorter events, 0.2 us)
Async XLA Ops:
  0.0 23.3 %copy-start.6 = (s32[4,8]{1,0:T(4,128)S(1)}, s32[4,8]{1,0:T(4,128)}, u32[]{:S(2)}) copy-start(s32[4,8]{1,0:T(4,128)} %constant.109.clone) | copy-start | bytes 388
  0.0 9.2 %copy-start.4 = (s32[512]{0:T(512)S(1)}, s32[512]{0:T(512)}, u32[]{:S(2)}) copy-start(s32[512]{0:T(512)} %param.8) | copy-start | bytes 6148
  0.0 12.8 %copy-start.5 = (s32[1,512]{1,0:T(1,128)S(1)}, s32[1,512]{1,0:T(1,128)}, u32[]{:S(2)}) copy-start(s32[1,512]{1,0:T(1,128)} %param.9) | copy-start | bytes 6148
  3.5 5.6 %collective-permute-start.16 = (bf16[176,1024]{1,0:T(8,128)(2,1)S(1)}, bf16[176,1024]{1,0:T(8,128)(2,1)S(1)}, u32[]{:S(2)}, u32[]{:S(2)}) collective-permute-start(bf16[176,1024]{1,0:T(8,128)(2,1)S(1)} %get-tuple-element.58.refs_0_.refs_1_), channel_id=1, source_target_pairs={{8,0},{9,1},{0,8},{1,9},{24,16},{25,17},{16,24},{17,25},{10,2},{11... | collective-permute-start | bytes 1081352 | tf_op jit(solution)/shard_map/ppermute | solution.py:264
  4.0 19.1 %collective-permute-start.15 = (bf16[176,1024]{1,0:T(8,128)(2,1)S(1)}, bf16[176,1024]{1,0:T(8,128)(2,1)S(1)}, u32[]{:S(2)}, u32[]{:S(2)}) collective-permute-start(bf16[176,1024]{1,0:T(8,128)(2,1)S(1)} %get-tuple-element.56), channel_id=1, source_target_pairs={{2,0},{3,1},{10,8},{11,9},{18,16},{19,17},{26,24},{27,25},{0,2},{1... | collective-permute-start | bytes 1081352 | tf_op jit(solution)/shard_map/ppermute | solution.py:261
  6.6 25.9 %collective-permute-start.20 = (bf16[176,1024]{1,0:T(8,128)(2,1)}, bf16[176,1024]{1,0:T(8,128)(2,1)S(1)}, u32[]{:S(2)}, u32[]{:S(2)}) collective-permute-start(bf16[176,1024]{1,0:T(8,128)(2,1)} %get-tuple-element.61), channel_id=1, source_target_pairs={{4,0},{5,1},{12,8},{13,9},{20,16},{21,17},{28,24},{29,25},{6,2},{7... | collective-permute-start | bytes 1081352 | tf_op jit(solution)/shard_map/ppermute | solution.py:261
  9.2 13.9 %collective-permute-start.18 = (bf16[176,1024]{1,0:T(8,128)(2,1)S(1)}, bf16[176,1024]{1,0:T(8,128)(2,1)S(1)}, u32[]{:S(2)}, u32[]{:S(2)}) collective-permute-start(bf16[176,1024]{1,0:T(8,128)(2,1)S(1)} %get-tuple-element.58.refs_0_.refs_1_), channel_id=1, source_target_pairs={{16,0},{8,1},{24,8},{0,9},{17,16},{9,17},{25,24},{1,25},{18,2},{10... | collective-permute-start | bytes 1081352 | tf_op jit(solution)/shard_map/ppermute | solution.py:264
  10.3 12.7 %collective-permute-start.17 = (bf16[176,1024]{1,0:T(8,128)(2,1)S(1)}, bf16[176,1024]{1,0:T(8,128)(2,1)S(1)}, u32[]{:S(2)}, u32[]{:S(2)}) collective-permute-start(bf16[176,1024]{1,0:T(8,128)(2,1)S(1)} %get-tuple-element.58.refs_0_.refs_1_), channel_id=1, source_target_pairs={{1,0},{17,1},{9,8},{25,9},{0,16},{16,17},{8,24},{24,25},{3,2},{19,... | collective-permute-start | bytes 1081352 | tf_op jit(solution)/shard_map/ppermute | solution.py:264
  23.1 5.1 %collective-permute-start.19 = (bf16[176,1024]{1,0:T(8,128)(2,1)S(1)}, bf16[176,1024]{1,0:T(8,128)(2,1)S(1)}, u32[]{:S(2)}, u32[]{:S(2)}) collective-permute-start(bf16[176,1024]{1,0:T(8,128)(2,1)S(1)} %collective-permute-done.15.refs_1_.refs_2_), channel_id=1, source_target_pairs={{8,0},{9,1},{0,8},{1,9},{24,16},{25,17},{16,24},{17,25},{10,2},{11... | collective-permute-start | bytes 1081352 | tf_op jit(solution)/shard_map/ppermute | solution.py:264
  23.5 13.0 %collective-permute-start.21 = (bf16[176,1024]{1,0:T(8,128)(2,1)}, bf16[176,1024]{1,0:T(8,128)(2,1)S(1)}, u32[]{:S(2)}, u32[]{:S(2)}) collective-permute-start(bf16[176,1024]{1,0:T(8,128)(2,1)} %get-tuple-element.63), channel_id=1, source_target_pairs={{6,0},{7,1},{14,8},{15,9},{22,16},{23,17},{30,24},{31,25},{4,2},{5... | collective-permute-start | bytes 1081352 | tf_op jit(solution)/shard_map/ppermute | solution.py:261
  26.2 11.3 %collective-permute-start.24 = (bf16[176,1024]{1,0:T(8,128)(2,1)S(1)}, bf16[176,1024]{1,0:T(8,128)(2,1)S(1)}, u32[]{:S(2)}, u32[]{:S(2)}) collective-permute-start(bf16[176,1024]{1,0:T(8,128)(2,1)S(1)} %collective-permute-done.15.refs_1_.refs_2_), channel_id=1, source_target_pairs={{16,0},{8,1},{24,8},{0,9},{17,16},{9,17},{25,24},{1,25},{18,2},{10... | collective-permute-start | bytes 1081352 | tf_op jit(solution)/shard_map/ppermute | solution.py:264
  27.5 11.5 %collective-permute-start.23 = (bf16[176,1024]{1,0:T(8,128)(2,1)S(1)}, bf16[176,1024]{1,0:T(8,128)(2,1)}, u32[]{:S(2)}, u32[]{:S(2)}) collective-permute-start(bf16[176,1024]{1,0:T(8,128)(2,1)S(1)} %collective-permute-done.15.refs_1_.refs_2_), channel_id=1, source_target_pairs={{1,0},{17,1},{9,8},{25,9},{0,16},{16,17},{8,24},{24,25},{3,2},{19,... | collective-permute-start | bytes 1081352 | tf_op jit(solution)/shard_map/ppermute | solution.py:264
  29.1 14.8 %all-to-all-start.2 = ((s32[32,1,256]{2,1,0:T(1,128)}), s32[32,1,256]{2,1,0:T(1,128)S(1)}, u32[]{:S(2)}, u32[]{:S(2)}) async-start(s32[32,1,256]{2,1,0:T(1,128)} %all_to_all.21), calls=%async_computation.2 | async-start | bytes 65536 | tf_op jit(solution)/shard_map/all_to_all | solution.py:305
  32.5 13.1 %collective-permute-start.28 = (bf16[176,1024]{1,0:T(8,128)(2,1)S(1)}, bf16[176,1024]{1,0:T(8,128)(2,1)}, u32[]{:S(2)}, u32[]{:S(2)}) collective-permute-start(bf16[176,1024]{1,0:T(8,128)(2,1)S(1)} %collective-permute-done.20.refs_2_.refs_3_), channel_id=1, source_target_pairs={{16,0},{8,1},{24,8},{0,9},{17,16},{9,17},{25,24},{1,25},{18,2},{10... | collective-permute-start | bytes 1081352 | tf_op jit(solution)/shard_map/ppermute | solution.py:264
  34.0 12.8 %collective-permute-start.26 = (bf16[176,1024]{1,0:T(8,128)(2,1)S(1)}, bf16[176,1024]{1,0:T(8,128)(2,1)}, u32[]{:S(2)}, u32[]{:S(2)}) collective-permute-start(bf16[176,1024]{1,0:T(8,128)(2,1)S(1)} %collective-permute-done.20.refs_2_.refs_3_), channel_id=1, source_target_pairs={{1,0},{17,1},{9,8},{25,9},{0,16},{16,17},{8,24},{24,25},{3,2},{19,... | collective-permute-start | bytes 1081352 | tf_op jit(solution)/shard_map/ppermute | solution.py:264
  39.0 13.6 %collective-permute-start.29 = (bf16[176,1024]{1,0:T(8,128)(2,1)S(1)}, bf16[176,1024]{1,0:T(8,128)(2,1)}, u32[]{:S(2)}, u32[]{:S(2)}) collective-permute-start(bf16[176,1024]{1,0:T(8,128)(2,1)S(1)} %collective-permute-done.21.refs_4_), channel_id=1, source_target_pairs={{16,0},{8,1},{24,8},{0,9},{17,16},{9,17},{25,24},{1,25},{18,2},{10... | collective-permute-start | bytes 1081352 | tf_op jit(solution)/shard_map/ppermute | solution.py:264
  39.0 15.0 %collective-permute-start.27 = (bf16[176,1024]{1,0:T(8,128)(2,1)S(1)}, bf16[176,1024]{1,0:T(8,128)(2,1)}, u32[]{:S(2)}, u32[]{:S(2)}) collective-permute-start(bf16[176,1024]{1,0:T(8,128)(2,1)S(1)} %collective-permute-done.21.refs_4_), channel_id=1, source_target_pairs={{1,0},{17,1},{9,8},{25,9},{0,16},{16,17},{8,24},{24,25},{3,2},{19,... | collective-permute-start | bytes 1081352 | tf_op jit(solution)/shard_map/ppermute | solution.py:264
  41.0 3.8 %collective-permute-start.22 = (bf16[176,1024]{1,0:T(8,128)(2,1)S(1)}, bf16[176,1024]{1,0:T(8,128)(2,1)}, u32[]{:S(2)}, u32[]{:S(2)}) collective-permute-start(bf16[176,1024]{1,0:T(8,128)(2,1)S(1)} %collective-permute-done.20.refs_2_.refs_3_), channel_id=1, source_target_pairs={{8,0},{9,1},{0,8},{1,9},{24,16},{25,17},{16,24},{17,25},{10,2},{11... | collective-permute-start | bytes 1081352 | tf_op jit(solution)/shard_map/ppermute | solution.py:264
  44.8 9.1 %collective-permute-start.25 = (bf16[176,1024]{1,0:T(8,128)(2,1)S(1)}, bf16[176,1024]{1,0:T(8,128)(2,1)S(1)}, u32[]{:S(2)}, u32[]{:S(2)}) collective-permute-start(bf16[176,1024]{1,0:T(8,128)(2,1)S(1)} %collective-permute-done.21.refs_4_), channel_id=1, source_target_pairs={{8,0},{9,1},{0,8},{1,9},{24,16},{25,17},{16,24},{17,25},{10,2},{11... | collective-permute-start | bytes 1081352 | tf_op jit(solution)/shard_map/ppermute | solution.py:264
  61.6 10.6 %all-to-all-start.3 = ((f32[32,4,128]{2,1,0:T(4,128)}), f32[32,4,128]{2,1,0:T(4,128)S(1)}, u32[]{:S(2)}, u32[]{:S(2)}) async-start(f32[32,4,128]{2,1,0:T(4,128)} %bitcast.17), calls=%async_computation.3 | async-start | bytes 131072 | tf_op jit(solution)/shard_map/all_to_all | solution.py:366
  72.5 0.6 copy-start.7

commit v10 on v9

--- a/solution.py
+++ b/solution.py
@@ -177,13 +177,8 @@
         out_ref[j : j + 1, :] = best[j].as_row()
 
 
-def late_kernel(pairs, count, group_size, *refs):
-    plane_ref, *chunks, best_ref, place_ref, last_place_ref, label_ref, last_label_ref, label_col_ref, out_ref, blocks, sems = refs
-    need = loader(chunks, count, blocks, sems)
-    first = best_ref.shape[1]
-    rest = blocks.shape[1] - first
-    early = [Best(best_ref[j : j + 1, :]) for j in range(count)]
-    late = [Best(jnp.full((1, rest), -1.0, jnp.float32)) for _ in range(count)]
+def meet_last(pairs, blocks, early, late, need, label_ref, last_label_ref, label_col_ref):
+    first = label_ref.shape[1]
     for j, k in pairs:
         need(j, k)
         sims = similar(
@@ -203,6 +198,27 @@
             )
             early[k].add_row(column_max(sims))
             late[j].add_column(row_max(sims))
+
+
+def near_kernel(pairs, count, *refs):
+    *chunks, best_ref, label_ref, last_label_ref, label_col_ref, early_ref, late_ref, blocks, sems = refs
+    need = loader(chunks, count, blocks, sems)
+    rest = last_label_ref.shape[1]
+    early = [Best(best_ref[j : j + 1, :]) for j in range(best_ref.shape[0])]
+    late = [Best(jnp.full((1, rest), -1.0, jnp.float32)) for _ in early]
+    meet_last(pairs, blocks, early, late, need, label_ref, last_label_ref, label_col_ref)
+    for j, (one, other) in enumerate(zip(early, late)):
+        early_ref[j : j + 1, :] = one.as_row()
+        late_ref[j : j + 1, :] = other.as_row()
+
+
+def late_kernel(pairs, count, group_size, *refs):
+    plane_ref, *chunks, best_ref, last_best_ref, place_ref, last_place_ref = refs[:-6]
+    label_ref, last_label_ref, label_col_ref, out_ref, blocks, sems = refs[-6:]
+    need = loader(chunks, count, blocks, sems)
+    early = [Best(best_ref[j : j + 1, :]) for j in range(count)]
+    late = [Best(last_best_ref[j : j + 1, :]) for j in range(count)]
+    meet_last(pairs, blocks, early, late, need, label_ref, last_label_ref, label_col_ref)
     tall = group_size // 128
     pieces = [(early[j], place_ref[j : j + 1, :]) for j in range(count)]
     pieces += [(late[j], last_place_ref[j : j + 1, :]) for j in range(count)]
@@ -345,10 +361,30 @@
             flops=2 * len(pairs) * early * early * width, bytes_accessed=2 * count * early * width, transcendentals=0
         ),
     )(*[part for block in blocks for part in block[:-1]], label, last_label)
+    near = [pair for pair in pairs if max(pair) < 2]
+    first_best, last_best = pl.pallas_call(
+        functools.partial(near_kernel, near, 2),
+        out_shape=[
+            jax.ShapeDtypeStruct((count, early), jnp.float32),
+            jax.ShapeDtypeStruct((count, slots - early), jnp.float32),
+        ],
+        in_specs=[any_space] * (2 * groups) + [VMEM] * 4,
+        out_specs=[VMEM] * 2,
+        scratch_shapes=[
+            pltpu.VMEM((2, slots, width), jnp.bfloat16),
+            pltpu.SemaphoreType.DMA((2, groups)),
+        ],
+        compiler_params=kernel_params(limit),
+        cost_estimate=pl.CostEstimate(
+            flops=2 * len(near) * (slots * slots - early * early) * width,
+            bytes_accessed=4 * slots * width,
+            transcendentals=0,
+        ),
+    )(*blocks[0], *blocks[1], first_best, label, last_label, label_cols)
     best = pl.pallas_call(
-        functools.partial(late_kernel, pairs, count, group_size),
+        functools.partial(late_kernel, [pair for pair in pairs if pair not in near], count, group_size),
         out_shape=jax.ShapeDtypeStruct((n_row, group_size // 128, 128), jnp.float32),
-        in_specs=[pl.BlockSpec(memory_space=pltpu.SMEM)] + [any_space] * (count * groups) + [VMEM] * 6,
+        in_specs=[pl.BlockSpec(memory_space=pltpu.SMEM)] + [any_space] * (count * groups) + [VMEM] * 7,
         out_specs=VMEM,
         scratch_shapes=scratch(groups),
         compiler_params=kernel_params(limit),
@@ -356,6 +392,7 @@
         plane_ref,
         *itertools.chain(*blocks),
         first_best,
+        last_best,
         places[:, :early],
         places[:, early:],
         label,

time: 73.3 us -> 74.5 us (1.016)
  Pallas kernels: 16.6 us -> 19.2 us
  waiting for transfers between devices: 26.8 us -> 25.1 us
    pallas_call x1 -> x2, Pallas kernels: 7.61 us -> 10.2 us  [the longest x1 6.85 us: best_matches(): pl.pallas_call(functools.partial(late_kernel, [pair for pair in pairs if...]
    ppermute x12, waiting for transfers between devices: 5.91 us -> 4.28 us  [inside(): lax.ppermute(part, AXES, [(device(int(held[j, i]), h), device(i, h)) for...]
  transfers between devices with their start and end apart: 17 -> 17, of which waited for: 10 -> 8; matrix products, arithmetic and copies ran while one was open for 4% -> 4% of each run, Pallas kernels for 7% -> 12%
where the time goes in v10:
time: 74.5 us; the launch traced here: 74.3 us
  waiting for transfers between devices  25.1 us (34%)
  starting transfers between devices  23.6 us (32%)
  Pallas kernels  19.2 us (26%)
  other arithmetic  2.66 us (4%)
  local copies, waits for them, and re-layouts  1.82 us (2%)
  between operations  1.63 us (2%)
    ppermute x3, waiting for transfers between devices, across(): lax.ppermute(part, AXES, [(device(i, h ^ k), device(i, h)) for i, h in pl...  12 us
    ppermute x12, starting transfers between devices, inside(): lax.ppermute(part, AXES, [(device(int(held[j, i]), h), device(i, h)) for...  8.86 us
    ppermute x3, starting transfers between devices, across(): lax.ppermute(part, AXES, [(device(i, h ^ k), device(i, h)) for i, h in pl...  7.83 us
    pallas_call x1, Pallas kernels, best_matches(): pl.pallas_call(functools.partial(late_kernel, [pair for pair in pairs if...  6.85 us
    all_to_all x1, waiting for transfers between devices, best_matches(): lax.all_to_all(best.reshape(devs, -1, 128), AXES, split_axis=0, concat_ax...  5.9 us
    pallas_call x1, Pallas kernels, best_matches(): pl.pallas_call(functools.partial(early_kernel, pairs, count, early), out_...  5.45 us
    ppermute x12, waiting for transfers between devices, inside(): lax.ppermute(part, AXES, [(device(int(held[j, i]), h), device(i, h)) for...  4.28 us
    pallas_call x1, Pallas kernels, best_matches(): pl.pallas_call(functools.partial(pack_kernel, groups, cap, group_size), o...  3.53 us
  transfers between devices with their start and end apart: 17, of which 8 were waited for; matrix products, arithmetic and copies ran while one was open for 4% of the time, Pallas kernels for 12%

profile of v10, /device:TPU:0, one launch (start us, length us, event | category | flops | bytes accessed | tf_op | source)
XLA Modules:
  0.0 74.3 jit_solution(18241406888127446725)
XLA Ops:
  0.0 3.5 %shard_map.57 = (s32[1,704]{1,0:T(1,128)S(1)}, bf16[176,1024]{1,0:T(8,128)(2,1)S(1)}, bf16[176,1024]{1,0:T(8,128)(2,1)S(1)}, bf16[176,1024]{1,0:T(8,128)(2,1)}, bf16[176,1024]{1,0:T(8,128)(2,1)}) custom-call(s32[1]{0:T(128)} %bitcast.11.plane_ref.refs_0_, s32[1,512]{1,0:T(1,128)} %bitcast.32, f32[512,1024]{1,0:T(8,128)} %emb_ref.1), custom_call_target="tpu_custom_call" | custom-call | tf_op jit(solution)/shard_map/pallas_call | solution.py:265
  3.5 0.5 collective-permute-start.16
  4.0 2.6 %collective-permute-start.15 = (bf16[176,1024]{1,0:T(8,128)(2,1)S(1)}, bf16[176,1024]{1,0:T(8,128)(2,1)S(1)}, u32[]{:S(2)}, u32[]{:S(2)}) collective-permute-start(bf16[176,1024]{1,0:T(8,128)(2,1)S(1)} %get-tuple-element.60), channel_id=1, source_target_pairs={{2,0},{3,1},{10,8},{11,9},{18,16},{19,17},{26,24},{27,25},{0,2},{1... | collective-permute-start | bytes 1081352 | tf_op jit(solution)/shard_map/ppermute | solution.py:277
  6.6 2.6 %collective-permute-start.20 = (bf16[176,1024]{1,0:T(8,128)(2,1)}, bf16[176,1024]{1,0:T(8,128)(2,1)S(1)}, u32[]{:S(2)}, u32[]{:S(2)}) collective-permute-start(bf16[176,1024]{1,0:T(8,128)(2,1)} %get-tuple-element.65), channel_id=1, source_target_pairs={{4,0},{5,1},{12,8},{13,9},{20,16},{21,17},{28,24},{29,25},{6,2},{7... | collective-permute-start | bytes 1081352 | tf_op jit(solution)/shard_map/ppermute | solution.py:277
  9.2 0.0 copy-done.4
  9.2 0.0 collective-permute-done.16.refs_3_.refs_4_.refs_5_
  9.2 1.1 %collective-permute-start.18 = (bf16[176,1024]{1,0:T(8,128)(2,1)S(1)}, bf16[176,1024]{1,0:T(8,128)(2,1)S(1)}, u32[]{:S(2)}, u32[]{:S(2)}) collective-permute-start(bf16[176,1024]{1,0:T(8,128)(2,1)S(1)} %get-tuple-element.62.refs_0_.refs_1_), channel_id=1, source_target_pairs={{16,0},{8,1},{24,8},{0,9},{17,16},{9,17},{25,24},{1,25},{18,2},{10... | collective-permute-start | bytes 1081352 | tf_op jit(solution)/shard_map/ppermute | solution.py:280
  10.3 1.0 %collective-permute-start.17 = (bf16[176,1024]{1,0:T(8,128)(2,1)S(1)}, bf16[176,1024]{1,0:T(8,128)(2,1)S(1)}, u32[]{:S(2)}, u32[]{:S(2)}) collective-permute-start(bf16[176,1024]{1,0:T(8,128)(2,1)S(1)} %get-tuple-element.62.refs_0_.refs_1_), channel_id=1, source_target_pairs={{1,0},{17,1},{9,8},{25,9},{0,16},{16,17},{8,24},{24,25},{3,2},{19,... | collective-permute-start | bytes 1081352 | tf_op jit(solution)/shard_map/ppermute | solution.py:280
  11.3 0.1 convert_reduce_fusion.5
  11.4 0.7 reduce_max.46
  12.8 0.0 copy-done.5
  12.8 0.1 convert_reduce_fusion.4
  13.0 10.1 %collective-permute-done.15.refs_1_.refs_2_ = bf16[176,1024]{1,0:T(8,128)(2,1)S(1)} collective-permute-done((bf16[176,1024]{1,0:T(8,128)(2,1)S(1)}, bf16[176,1024]{1,0:T(8,128)(2,1)S(1)}, u32[]{:S(2)}, u32[]{:S(2)}) %collective-permute-start.15) | collective-permute-done | bytes 360480 | tf_op jit(solution)/shard_map/ppermute | solution.py:277
  23.0 0.0 collective-permute-done.18.refs_9_.refs_13_
  23.1 0.0 collective-permute-done.17.refs_6_.refs_9_
  23.1 0.0 collective-permute-start.19
  23.1 0.1 pad_add_fusion.1
  23.1 0.1 pad.7.clone
  23.2 0.1 pad.6.clone
  23.3 0.0 copy-done.6
  23.3 0.1 select_reduce_fusion.5
  23.4 0.1 fusion.7
  23.5 2.7 %collective-permute-start.21 = (bf16[176,1024]{1,0:T(8,128)(2,1)}, bf16[176,1024]{1,0:T(8,128)(2,1)S(1)}, u32[]{:S(2)}, u32[]{:S(2)}) collective-permute-start(bf16[176,1024]{1,0:T(8,128)(2,1)} %get-tuple-element.67), channel_id=1, source_target_pairs={{6,0},{7,1},{14,8},{15,9},{22,16},{23,17},{30,24},{31,25},{4,2},{5... | collective-permute-start | bytes 1081352 | tf_op jit(solution)/shard_map/ppermute | solution.py:277
  26.2 1.3 %collective-permute-start.24 = (bf16[176,1024]{1,0:T(8,128)(2,1)S(1)}, bf16[176,1024]{1,0:T(8,128)(2,1)S(1)}, u32[]{:S(2)}, u32[]{:S(2)}) collective-permute-start(bf16[176,1024]{1,0:T(8,128)(2,1)S(1)} %collective-permute-done.15.refs_1_.refs_2_), channel_id=1, source_target_pairs={{16,0},{8,1},{24,8},{0,9},{17,16},{9,17},{25,24},{1,25},{18,2},{10... | collective-permute-start | bytes 1081352 | tf_op jit(solution)/shard_map/ppermute | solution.py:280
  27.5 0.7 collective-permute-start.23
  28.2 0.0 collective-permute-done.19.refs_4_.refs_5_.refs_6_
  28.2 0.1 broadcast_in_dim.172
  28.3 0.1 select_reduce_fusion.4
  28.4 0.6 all_to_all.21
  29.1 3.4 %all-to-all-start.2 = ((s32[32,1,256]{2,1,0:T(1,128)}), s32[32,1,256]{2,1,0:T(1,128)S(1)}, u32[]{:S(2)}, u32[]{:S(2)}) async-start(s32[32,1,256]{2,1,0:T(1,128)} %all_to_all.21), calls=%async_computation.2 | async-start | bytes 65536 | tf_op jit(solution)/shard_map/all_to_all | solution.py:321
  32.5 0.0 collective-permute-done.20.refs_2_.refs_3_
  32.5 1.6 %collective-permute-start.28 = (bf16[176,1024]{1,0:T(8,128)(2,1)S(1)}, bf16[176,1024]{1,0:T(8,128)(2,1)}, u32[]{:S(2)}, u32[]{:S(2)}) collective-permute-start(bf16[176,1024]{1,0:T(8,128)(2,1)S(1)} %collective-permute-done.20.refs_2_.refs_3_), channel_id=1, source_target_pairs={{16,0},{8,1},{24,8},{0,9},{17,16},{9,17},{25,24},{1,25},{18,2},{10... | collective-permute-start | bytes 1081352 | tf_op jit(solution)/shard_map/ppermute | solution.py:280
  34.0 0.5 collective-permute-start.26
  34.6 2.0 %collective-permute-done.21.refs_3_.refs_4_ = bf16[176,1024]{1,0:T(8,128)(2,1)S(1)} collective-permute-done((bf16[176,1024]{1,0:T(8,128)(2,1)}, bf16[176,1024]{1,0:T(8,128)(2,1)S(1)}, u32[]{:S(2)}, u32[]{:S(2)}) %collective-permute-start.21) | collective-permute-done | bytes 360480 | tf_op jit(solution)/shard_map/ppermute | solution.py:277
  36.5 0.9 %collective-permute-done.24.refs_10_.refs_14_ = bf16[176,1024]{1,0:T(8,128)(2,1)S(1)} collective-permute-done((bf16[176,1024]{1,0:T(8,128)(2,1)S(1)}, bf16[176,1024]{1,0:T(8,128)(2,1)S(1)}, u32[]{:S(2)}, u32[]{:S(2)}) %collective-permute-start.24) | collective-permute-done | bytes 360480 | tf_op jit(solution)/shard_map/ppermute | solution.py:280
  37.5 1.5 %collective-permute-done.23.refs_7_.refs_10_ = bf16[176,1024]{1,0:T(8,128)(2,1)} collective-permute-done((bf16[176,1024]{1,0:T(8,128)(2,1)S(1)}, bf16[176,1024]{1,0:T(8,128)(2,1)}, u32[]{:S(2)}, u32[]{:S(2)}) %collective-permute-start.23) | collective-permute-done | bytes 360480 | tf_op jit(solution)/shard_map/ppermute | solution.py:280
  39.0 0.0 collective-permute-start.29
  39.0 2.0 %collective-permute-start.27 = (bf16[176,1024]{1,0:T(8,128)(2,1)S(1)}, bf16[176,1024]{1,0:T(8,128)(2,1)}, u32[]{:S(2)}, u32[]{:S(2)}) collective-permute-start(bf16[176,1024]{1,0:T(8,128)(2,1)S(1)} %collective-permute-done.21.refs_3_.refs_4_), channel_id=1, source_target_pairs={{1,0},{17,1},{9,8},{25,9},{0,16},{16,17},{8,24},{24,25},{3,2},{19,... | collective-permute-start | bytes 1081352 | tf_op jit(solution)/shard_map/ppermute | solution.py:280
  41.0 0.0 collective-permute-start.22
  41.0 2.9 %all-to-all-done.2 = s32[32,1,256]{2,1,0:T(1,128)S(1)} async-done(((s32[32,1,256]{2,1,0:T(1,128)}), s32[32,1,256]{2,1,0:T(1,128)S(1)}, u32[]{:S(2)}, u32[]{:S(2)}) %all-to-all-start.2) | async-done | bytes 32800 | tf_op jit(solution)/shard_map/all_to_all | solution.py:321
  43.9 0.1 reduce.4
  44.0 0.1 broadcast_in_dim.181
  44.1 0.1 select_reduce_fusion.3
  44.3 0.1 reshape.175
  44.4 0.1 mul.54
  44.5 0.1 multiply_reduce_fusion.1
  44.6 0.1 fusion.4
  44.7 0.1 convert_reduce_fusion.3
  44.8 0.0 collective-permute-done.22.refs_5_.refs_6_.refs_7_
  44.8 0.2 collective-permute-start.25
  45.1 0.5 collective-permute-done.28.refs_11_.refs_15_
  45.6 1.3 %collective-permute-done.26.refs_8_.refs_11_ = bf16[176,1024]{1,0:T(8,128)(2,1)} collective-permute-done((bf16[176,1024]{1,0:T(8,128)(2,1)S(1)}, bf16[176,1024]{1,0:T(8,128)(2,1)}, u32[]{:S(2)}, u32[]{:S(2)}) %collective-permute-start.26) | collective-permute-done | bytes 360480 | tf_op jit(solution)/shard_map/ppermute | solution.py:280
  46.9 5.5 %shard_map.58 = (f32[4,512]{1,0:T(4,128)S(1)}, f32[704,4]{1,0:T(8,128)S(1)}) custom-call(bf16[176,1024]{1,0:T(8,128)(2,1)S(1)} %get-tuple-element.62.refs_0_.refs_1_, bf16[176,1024]{1,0:T(8,128)(2,1)S(1)} %collective-permute-done.15.refs_1_.refs_2_, bf16[176,1024]{1,0:T(8,128)(2,1)S(1)} %collective-permute-done.20.refs_2_.refs_3_, ...), custom_call_target="tpu_custom_call" | custom-call | flops 2684354560 | bytes 4194304 | tf_op jit(solution)/shard_map/pallas_call | solution.py:350
  52.3 0.0 collective-permute-done.25.refs_7_.refs_8_
  52.3 3.3 %shard_map.59 = (f32[4,512]{1,0:T(4,128)S(1)}, f32[4,192]{1,0:T(4,128)S(1)}) custom-call(bf16[176,1024]{1,0:T(8,128)(2,1)S(1)} %get-tuple-element.62.refs_0_.refs_1_, bf16[176,1024]{1,0:T(8,128)(2,1)S(1)} %collective-permute-done.15.refs_1_.refs_2_, bf16[176,1024]{1,0:T(8,128)(2,1)S(1)} %collective-permute-done.20.refs_2_.refs_3_, ...), custom_call_target="tpu_custom_call" | custom-call | flops 956301312 | bytes 2883584 | tf_op jit(solution)/shard_map/pallas_call | solution.py:365
  55.7 0.0 collective-permute-done.29.refs_16_
  55.7 0.0 collective-permute-done.27.refs_12_
  55.7 6.8 %shard_map.60 = f32[4,32,128]{2,1,0:T(8,128)} custom-call(s32[1]{0:T(128)} %bitcast.11.plane_ref.refs_0_, bf16[176,1024]{1,0:T(8,128)(2,1)S(1)} %get-tuple-element.62.refs_0_.refs_1_, bf16[176,1024]{1,0:T(8,128)(2,1)S(1)} %collective-permute-done.15.refs_1_.refs_2_, bf16[176,1024]{1,0:T(8,128)(2,1)S(1)} %collective-permute-done.20.refs_2_.refs_3_, ...), custom_call_target="tpu_custom_call" | custom-call | tf_op jit(solution)/shard_map/pallas_call | solution.py:384
  62.6 3.5 %all-to-all-start.3 = ((f32[32,4,128]{2,1,0:T(4,128)}), f32[32,4,128]{2,1,0:T(4,128)S(1)}, u32[]{:S(2)}, u32[]{:S(2)}) async-start(f32[32,4,128]{2,1,0:T(4,128)} %bitcast.17), calls=%async_computation.3 | async-start | bytes 131072 | tf_op jit(solution)/shard_map/all_to_all | solution.py:403
  66.1 0.7 slice_reduce_fusion
  67.5 5.9 %all-to-all-done.3 = f32[32,4,128]{2,1,0:T(4,128)S(1)} async-done(((f32[32,4,128]{2,1,0:T(4,128)}), f32[32,4,128]{2,1,0:T(4,128)S(1)}, u32[]{:S(2)}, u32[]{:S(2)}) %all-to-all-start.3) | async-done | bytes 65568 | tf_op jit(solution)/shard_map/all_to_all | solution.py:403
  73.4 0.3 conditional.1
  73.7 0.0 copy-start.7
  73.7 0.6 copy-done.7
  (22 shorter events, 0.2 us)
Async XLA Ops:
  0.0 23.3 %copy-start.6 = (s32[4,8]{1,0:T(4,128)S(1)}, s32[4,8]{1,0:T(4,128)}, u32[]{:S(2)}) copy-start(s32[4,8]{1,0:T(4,128)} %constant.109.clone) | copy-start | bytes 388
  0.0 9.2 %copy-start.4 = (s32[512]{0:T(512)S(1)}, s32[512]{0:T(512)}, u32[]{:S(2)}) copy-start(s32[512]{0:T(512)} %param.8) | copy-start | bytes 6148
  0.0 12.8 %copy-start.5 = (s32[1,512]{1,0:T(1,128)S(1)}, s32[1,512]{1,0:T(1,128)}, u32[]{:S(2)}) copy-start(s32[1,512]{1,0:T(1,128)} %param.9) | copy-start | bytes 6148
  3.5 5.6 %collective-permute-start.16 = (bf16[176,1024]{1,0:T(8,128)(2,1)S(1)}, bf16[176,1024]{1,0:T(8,128)(2,1)S(1)}, u32[]{:S(2)}, u32[]{:S(2)}) collective-permute-start(bf16[176,1024]{1,0:T(8,128)(2,1)S(1)} %get-tuple-element.62.refs_0_.refs_1_), channel_id=1, source_target_pairs={{8,0},{9,1},{0,8},{1,9},{24,16},{25,17},{16,24},{17,25},{10,2},{11... | collective-permute-start | bytes 1081352 | tf_op jit(solution)/shard_map/ppermute | solution.py:280
  4.0 19.1 %collective-permute-start.15 = (bf16[176,1024]{1,0:T(8,128)(2,1)S(1)}, bf16[176,1024]{1,0:T(8,128)(2,1)S(1)}, u32[]{:S(2)}, u32[]{:S(2)}) collective-permute-start(bf16[176,1024]{1,0:T(8,128)(2,1)S(1)} %get-tuple-element.60), channel_id=1, source_target_pairs={{2,0},{3,1},{10,8},{11,9},{18,16},{19,17},{26,24},{27,25},{0,2},{1... | collective-permute-start | bytes 1081352 | tf_op jit(solution)/shard_map/ppermute | solution.py:277
  6.6 25.9 %collective-permute-start.20 = (bf16[176,1024]{1,0:T(8,128)(2,1)}, bf16[176,1024]{1,0:T(8,128)(2,1)S(1)}, u32[]{:S(2)}, u32[]{:S(2)}) collective-permute-start(bf16[176,1024]{1,0:T(8,128)(2,1)} %get-tuple-element.65), channel_id=1, source_target_pairs={{4,0},{5,1},{12,8},{13,9},{20,16},{21,17},{28,24},{29,25},{6,2},{7... | collective-permute-start | bytes 1081352 | tf_op jit(solution)/shard_map/ppermute | solution.py:277
  9.2 13.9 %collective-permute-start.18 = (bf16[176,1024]{1,0:T(8,128)(2,1)S(1)}, bf16[176,1024]{1,0:T(8,128)(2,1)S(1)}, u32[]{:S(2)}, u32[]{:S(2)}) collective-permute-start(bf16[176,1024]{1,0:T(8,128)(2,1)S(1)} %get-tuple-element.62.refs_0_.refs_1_), channel_id=1, source_target_pairs={{16,0},{8,1},{24,8},{0,9},{17,16},{9,17},{25,24},{1,25},{18,2},{10... | collective-permute-start | bytes 1081352 | tf_op jit(solution)/shard_map/ppermute | solution.py:280
  10.3 12.7 %collective-permute-start.17 = (bf16[176,1024]{1,0:T(8,128)(2,1)S(1)}, bf16[176,1024]{1,0:T(8,128)(2,1)S(1)}, u32[]{:S(2)}, u32[]{:S(2)}) collective-permute-start(bf16[176,1024]{1,0:T(8,128)(2,1)S(1)} %get-tuple-element.62.refs_0_.refs_1_), channel_id=1, source_target_pairs={{1,0},{17,1},{9,8},{25,9},{0,16},{16,17},{8,24},{24,25},{3,2},{19,... | collective-permute-start | bytes 1081352 | tf_op jit(solution)/shard_map/ppermute | solution.py:280
  23.1 5.1 %collective-permute-start.19 = (bf16[176,1024]{1,0:T(8,128)(2,1)S(1)}, bf16[176,1024]{1,0:T(8,128)(2,1)S(1)}, u32[]{:S(2)}, u32[]{:S(2)}) collective-permute-start(bf16[176,1024]{1,0:T(8,128)(2,1)S(1)} %collective-permute-done.15.refs_1_.refs_2_), channel_id=1, source_target_pairs={{8,0},{9,1},{0,8},{1,9},{24,16},{25,17},{16,24},{17,25},{10,2},{11... | collective-permute-start | bytes 1081352 | tf_op jit(solution)/shard_map/ppermute | solution.py:280
  23.5 13.0 %collective-permute-start.21 = (bf16[176,1024]{1,0:T(8,128)(2,1)}, bf16[176,1024]{1,0:T(8,128)(2,1)S(1)}, u32[]{:S(2)}, u32[]{:S(2)}) collective-permute-start(bf16[176,1024]{1,0:T(8,128)(2,1)} %get-tuple-element.67), channel_id=1, source_target_pairs={{6,0},{7,1},{14,8},{15,9},{22,16},{23,17},{30,24},{31,25},{4,2},{5... | collective-permute-start | bytes 1081352 | tf_op jit(solution)/shard_map/ppermute | solution.py:277
  26.2 11.3 %collective-permute-start.24 = (bf16[176,1024]{1,0:T(8,128)(2,1)S(1)}, bf16[176,1024]{1,0:T(8,128)(2,1)S(1)}, u32[]{:S(2)}, u32[]{:S(2)}) collective-permute-start(bf16[176,1024]{1,0:T(8,128)(2,1)S(1)} %collective-permute-done.15.refs_1_.refs_2_), channel_id=1, source_target_pairs={{16,0},{8,1},{24,8},{0,9},{17,16},{9,17},{25,24},{1,25},{18,2},{10... | collective-permute-start | bytes 1081352 | tf_op jit(solution)/shard_map/ppermute | solution.py:280
  27.5 11.5 %collective-permute-start.23 = (bf16[176,1024]{1,0:T(8,128)(2,1)S(1)}, bf16[176,1024]{1,0:T(8,128)(2,1)}, u32[]{:S(2)}, u32[]{:S(2)}) collective-permute-start(bf16[176,1024]{1,0:T(8,128)(2,1)S(1)} %collective-permute-done.15.refs_1_.refs_2_), channel_id=1, source_target_pairs={{1,0},{17,1},{9,8},{25,9},{0,16},{16,17},{8,24},{24,25},{3,2},{19,... | collective-permute-start | bytes 1081352 | tf_op jit(solution)/shard_map/ppermute | solution.py:280
  29.1 14.8 %all-to-all-start.2 = ((s32[32,1,256]{2,1,0:T(1,128)}), s32[32,1,256]{2,1,0:T(1,128)S(1)}, u32[]{:S(2)}, u32[]{:S(2)}) async-start(s32[32,1,256]{2,1,0:T(1,128)} %all_to_all.21), calls=%async_computation.2 | async-start | bytes 65536 | tf_op jit(solution)/shard_map/all_to_all | solution.py:321
  32.5 13.1 %collective-permute-start.28 = (bf16[176,1024]{1,0:T(8,128)(2,1)S(1)}, bf16[176,1024]{1,0:T(8,128)(2,1)}, u32[]{:S(2)}, u32[]{:S(2)}) collective-permute-start(bf16[176,1024]{1,0:T(8,128)(2,1)S(1)} %collective-permute-done.20.refs_2_.refs_3_), channel_id=1, source_target_pairs={{16,0},{8,1},{24,8},{0,9},{17,16},{9,17},{25,24},{1,25},{18,2},{10... | collective-permute-start | bytes 1081352 | tf_op jit(solution)/shard_map/ppermute | solution.py:280
  34.0 12.8 %collective-permute-start.26 = (bf16[176,1024]{1,0:T(8,128)(2,1)S(1)}, bf16[176,1024]{1,0:T(8,128)(2,1)}, u32[]{:S(2)}, u32[]{:S(2)}) collective-permute-start(bf16[176,1024]{1,0:T(8,128)(2,1)S(1)} %collective-permute-done.20.refs_2_.refs_3_), channel_id=1, source_target_pairs={{1,0},{17,1},{9,8},{25,9},{0,16},{16,17},{8,24},{24,25},{3,2},{19,... | collective-permute-start | bytes 1081352 | tf_op jit(solution)/shard_map/ppermute | solution.py:280
  39.0 16.7 %collective-permute-start.29 = (bf16[176,1024]{1,0:T(8,128)(2,1)S(1)}, bf16[176,1024]{1,0:T(8,128)(2,1)}, u32[]{:S(2)}, u32[]{:S(2)}) collective-permute-start(bf16[176,1024]{1,0:T(8,128)(2,1)S(1)} %collective-permute-done.21.refs_3_.refs_4_), channel_id=1, source_target_pairs={{16,0},{8,1},{24,8},{0,9},{17,16},{9,17},{25,24},{1,25},{18,2},{10... | collective-permute-start | bytes 1081352 | tf_op jit(solution)/shard_map/ppermute | solution.py:280
  39.0 16.7 %collective-permute-start.27 = (bf16[176,1024]{1,0:T(8,128)(2,1)S(1)}, bf16[176,1024]{1,0:T(8,128)(2,1)}, u32[]{:S(2)}, u32[]{:S(2)}) collective-permute-start(bf16[176,1024]{1,0:T(8,128)(2,1)S(1)} %collective-permute-done.21.refs_3_.refs_4_), channel_id=1, source_target_pairs={{1,0},{17,1},{9,8},{25,9},{0,16},{16,17},{8,24},{24,25},{3,2},{19,... | collective-permute-start | bytes 1081352 | tf_op jit(solution)/shard_map/ppermute | solution.py:280
  41.0 3.8 %collective-permute-start.22 = (bf16[176,1024]{1,0:T(8,128)(2,1)S(1)}, bf16[176,1024]{1,0:T(8,128)(2,1)}, u32[]{:S(2)}, u32[]{:S(2)}) collective-permute-start(bf16[176,1024]{1,0:T(8,128)(2,1)S(1)} %collective-permute-done.20.refs_2_.refs_3_), channel_id=1, source_target_pairs={{8,0},{9,1},{0,8},{1,9},{24,16},{25,17},{16,24},{17,25},{10,2},{11... | collective-permute-start | bytes 1081352 | tf_op jit(solution)/shard_map/ppermute | solution.py:280
  44.8 7.5 %collective-permute-start.25 = (bf16[176,1024]{1,0:T(8,128)(2,1)S(1)}, bf16[176,1024]{1,0:T(8,128)(2,1)S(1)}, u32[]{:S(2)}, u32[]{:S(2)}) collective-permute-start(bf16[176,1024]{1,0:T(8,128)(2,1)S(1)} %collective-permute-done.21.refs_3_.refs_4_), channel_id=1, source_target_pairs={{8,0},{9,1},{0,8},{1,9},{24,16},{25,17},{16,24},{17,25},{10,2},{11... | collective-permute-start | bytes 1081352 | tf_op jit(solution)/shard_map/ppermute | solution.py:280
  62.6 10.8 %all-to-all-start.3 = ((f32[32,4,128]{2,1,0:T(4,128)}), f32[32,4,128]{2,1,0:T(4,128)S(1)}, u32[]{:S(2)}, u32[]{:S(2)}) async-start(f32[32,4,128]{2,1,0:T(4,128)} %bitcast.17), calls=%async_computation.3 | async-start | bytes 131072 | tf_op jit(solution)/shard_map/all_to_all | solution.py:403
  73.7 0.6 copy-start.7

commit v11 on v9

--- a/solution.py
+++ b/solution.py
@@ -10,6 +10,7 @@
 from jax.sharding import PartitionSpec as P
 
 AXES = ("row", "col")
+PIECES = 4
 LEVELS = 16
 NT = (((1,), (1,)), ((), ()))
 VMEM = pl.BlockSpec(memory_space=pltpu.VMEM)
@@ -60,8 +61,13 @@
     return held, pairs
 
 
-def pack_kernel(groups, cap, group_size, plane_ref, dest_ref, emb_ref, place_ref, *chunk_refs):
+def pack_kernel(groups, cap, group_size, plane_ref, dest_ref, emb_ref, place_ref, *refs):
+    *chunk_refs, emb, unit, sems = refs
     rows_dev = emb_ref.shape[0]
+    pieces = [pl.ds(start, rows_dev // PIECES) for start in range(0, rows_dev, rows_dev // PIECES)]
+    loads = [pltpu.make_async_copy(emb_ref.at[piece], emb.at[piece], sems.at[i]) for i, piece in enumerate(pieces)]
+    for load in loads:
+        load.start()
     dest = dest_ref[...]
     group, place = jnp.zeros_like(dest), dest
     for g in range(1, groups):
@@ -78,10 +84,13 @@
     rank = jnp.sum(jnp.where(member, before, 0.0), axis=0, keepdims=True).astype(jnp.int32)
     slot = jnp.where(rank < cap, group * cap + rank, groups * cap)
     pick = (lax.broadcasted_iota(jnp.int32, (groups * cap, rows_dev), 0) == slot).astype(jnp.bfloat16)
-    x = emb_ref[...]
-    unit = (x * lax.rsqrt(jnp.sum(x * x, axis=1, keepdims=True) + 1e-06)).astype(jnp.bfloat16)
+    for load, piece in zip(loads, pieces):
+        load.wait()
+        x = emb[piece]
+        scale = lax.rsqrt(jnp.sum(x * x, axis=1, keepdims=True) + 1e-06)
+        unit[piece] = (x * scale).astype(jnp.bfloat16)
     for k, ref in enumerate(chunk_refs):
-        chunk = jnp.dot(pick[k * cap : (k + 1) * cap], unit, preferred_element_type=jnp.float32)
+        chunk = jnp.dot(pick[k * cap : (k + 1) * cap], unit[...], preferred_element_type=jnp.float32)
         ref[...] = chunk.astype(jnp.bfloat16)
     high = lax.shift_right_logical(place, 7)
     low = jnp.bitwise_and(place, 127)
@@ -177,14 +186,30 @@
         out_ref[j : j + 1, :] = best[j].as_row()
 
 
+def by_place(best, place, tall):
+    slots = best.shape[1]
+    high = lax.broadcasted_iota(jnp.int32, (tall, slots), 0) == lax.shift_right_logical(place, 7)
+    low = lax.broadcasted_iota(jnp.int32, (128, slots), 0) == jnp.bitwise_and(place, 127)
+    parts, rest = [], best
+    for _ in range(3):
+        part = rest.astype(jnp.bfloat16).astype(jnp.float32)
+        rest = rest - part
+        parts.append(part)
+    parts.append(jnp.ones_like(best))
+    stack = jnp.concatenate([jnp.where(high, part, 0.0) for part in parts], axis=0).astype(jnp.bfloat16)
+    return lax.dot_general(stack, low.astype(jnp.bfloat16), NT, preferred_element_type=jnp.float32)
+
+
 def late_kernel(pairs, count, group_size, *refs):
     plane_ref, *chunks, best_ref, place_ref, last_place_ref, label_ref, last_label_ref, label_col_ref, out_ref, blocks, sems = refs
     need = loader(chunks, count, blocks, sems)
     first = best_ref.shape[1]
     rest = blocks.shape[1] - first
+    tall = group_size // 128
     early = [Best(best_ref[j : j + 1, :]) for j in range(count)]
     late = [Best(jnp.full((1, rest), -1.0, jnp.float32)) for _ in range(count)]
-    for j, k in pairs:
+    spread = jnp.zeros((4 * tall, 128), jnp.float32)
+    for number, (j, k) in enumerate(pairs):
         need(j, k)
         sims = similar(
             blocks[j],
@@ -203,23 +228,10 @@
             )
             early[k].add_row(column_max(sims))
             late[j].add_column(row_max(sims))
-    tall = group_size // 128
-    pieces = [(early[j], place_ref[j : j + 1, :]) for j in range(count)]
-    pieces += [(late[j], last_place_ref[j : j + 1, :]) for j in range(count)]
-    spread = jnp.zeros((4 * tall, 128), jnp.float32)
-    for best, place in pieces:
-        best = best.as_row()
-        slots = best.shape[1]
-        high = lax.broadcasted_iota(jnp.int32, (tall, slots), 0) == lax.shift_right_logical(place, 7)
-        low = lax.broadcasted_iota(jnp.int32, (128, slots), 0) == jnp.bitwise_and(place, 127)
-        parts, rest = [], best
-        for _ in range(3):
-            part = rest.astype(jnp.bfloat16).astype(jnp.float32)
-            rest = rest - part
-            parts.append(part)
-        parts.append(jnp.ones_like(best))
-        stack = jnp.concatenate([jnp.where(high, part, 0.0) for part in parts], axis=0).astype(jnp.bfloat16)
-        spread += lax.dot_general(stack, low.astype(jnp.bfloat16), NT, preferred_element_type=jnp.float32)
+        ahead = {block for pair in pairs[number + 1 :] for block in pair}
+        for block in sorted({j, k} - ahead):
+            spread += by_place(early[block].as_row(), place_ref[block : block + 1, :], tall)
+            spread += by_place(late[block].as_row(), last_place_ref[block : block + 1, :], tall)
     value = spread[:tall] + spread[tall : 2 * tall] + spread[2 * tall : 3 * tall]
     value = jnp.where(spread[3 * tall :] > 0.5, value, -1.0)
     for r in range(out_ref.shape[0]):
@@ -252,8 +264,13 @@
             jax.ShapeDtypeStruct((1, slots), jnp.int32),
             *[jax.ShapeDtypeStruct((cap, width), jnp.bfloat16)] * groups,
         ],
-        in_specs=[pl.BlockSpec(memory_space=pltpu.SMEM), VMEM, VMEM],
+        in_specs=[pl.BlockSpec(memory_space=pltpu.SMEM), VMEM, pl.BlockSpec(memory_space=pltpu.HBM)],
         out_specs=[VMEM] * (1 + groups),
+        scratch_shapes=[
+            pltpu.VMEM((rows_dev, width), jnp.float32),
+            pltpu.VMEM((rows_dev, width), jnp.bfloat16),
+            pltpu.SemaphoreType.DMA((PIECES,)),
+        ],
         compiler_params=kernel_params(20),
     )(plane_ref, dest_row, embeddings)
 

time: 73.3 us -> 74.4 us (1.015)
  Pallas kernels: 16.6 us -> 17.5 us
where the time goes in v11:
time: 74.4 us; the launch traced here: 74.2 us
  waiting for transfers between devices  26.7 us (36%)
  starting transfers between devices  23.6 us (32%)
  Pallas kernels  17.5 us (24%)
  other arithmetic  2.66 us (4%)
  local copies, waits for them, and re-layouts  1.82 us (2%)
  between operations  1.61 us (2%)
    ppermute x3, waiting for transfers between devices, across(): lax.ppermute(part, AXES, [(device(i, h ^ k), device(i, h)) for i, h in pl...  11.9 us
    ppermute x12, starting transfers between devices, inside(): lax.ppermute(part, AXES, [(device(int(held[j, i]), h), device(i, h)) for...  8.92 us
    pallas_call x1, Pallas kernels, best_matches(): pl.pallas_call(functools.partial(late_kernel, pairs, count, group_size),...  8.04 us
    ppermute x3, starting transfers between devices, across(): lax.ppermute(part, AXES, [(device(i, h ^ k), device(i, h)) for i, h in pl...  7.9 us
    ppermute x12, waiting for transfers between devices, inside(): lax.ppermute(part, AXES, [(device(int(held[j, i]), h), device(i, h)) for...  5.99 us
    all_to_all x1, waiting for transfers between devices, best_matches(): lax.all_to_all(best.reshape(devs, -1, 128), AXES, split_axis=0, concat_ax...  5.9 us
    pallas_call x1, Pallas kernels, best_matches(): pl.pallas_call(functools.partial(early_kernel, pairs, count, early), out_...  5.46 us
    pallas_call x1, Pallas kernels, best_matches(): pl.pallas_call(functools.partial(pack_kernel, groups, cap, group_size), o...  4.04 us
  transfers between devices with their start and end apart: 17, of which 10 were waited for; matrix products, arithmetic and copies ran while one was open for 4% of the time, Pallas kernels for 7%

profile of v11, /device:TPU:0, one launch (start us, length us, event | category | flops | bytes accessed | tf_op | source)
XLA Modules:
  0.0 74.2 jit_solution(2570702409255298018)
XLA Ops:
  0.0 0.0 copy-start.6
  0.0 4.0 %shard_map.57 = (s32[1,704]{1,0:T(1,128)S(1)}, bf16[176,1024]{1,0:T(8,128)(2,1)S(1)}, bf16[176,1024]{1,0:T(8,128)(2,1)S(1)}, bf16[176,1024]{1,0:T(8,128)(2,1)}, bf16[176,1024]{1,0:T(8,128)(2,1)}) custom-call(s32[1]{0:T(128)} %bitcast.11.plane_ref.refs_0_, s32[1,512]{1,0:T(1,128)} %bitcast.32, f32[512,1024]{1,0:T(8,128)} %emb_ref.1), custom_call_target="tpu_custom_call" | custom-call | tf_op jit(solution)/shard_map/pallas_call | solution.py:261
  4.1 0.5 collective-permute-start.16
  4.6 2.7 %collective-permute-start.15 = (bf16[176,1024]{1,0:T(8,128)(2,1)S(1)}, bf16[176,1024]{1,0:T(8,128)(2,1)S(1)}, u32[]{:S(2)}, u32[]{:S(2)}) collective-permute-start(bf16[176,1024]{1,0:T(8,128)(2,1)S(1)} %get-tuple-element.56), channel_id=1, source_target_pairs={{2,0},{3,1},{10,8},{11,9},{18,16},{19,17},{26,24},{27,25},{0,2},{1... | collective-permute-start | bytes 1081352 | tf_op jit(solution)/shard_map/ppermute | solution.py:278
  7.2 2.6 %collective-permute-start.20 = (bf16[176,1024]{1,0:T(8,128)(2,1)}, bf16[176,1024]{1,0:T(8,128)(2,1)S(1)}, u32[]{:S(2)}, u32[]{:S(2)}) collective-permute-start(bf16[176,1024]{1,0:T(8,128)(2,1)} %get-tuple-element.61), channel_id=1, source_target_pairs={{4,0},{5,1},{12,8},{13,9},{20,16},{21,17},{28,24},{29,25},{6,2},{7... | collective-permute-start | bytes 1081352 | tf_op jit(solution)/shard_map/ppermute | solution.py:278
  9.8 0.0 copy-done.4
  9.8 0.0 collective-permute-done.16.refs_3_.refs_5_
  9.8 1.1 %collective-permute-start.18 = (bf16[176,1024]{1,0:T(8,128)(2,1)S(1)}, bf16[176,1024]{1,0:T(8,128)(2,1)S(1)}, u32[]{:S(2)}, u32[]{:S(2)}) collective-permute-start(bf16[176,1024]{1,0:T(8,128)(2,1)S(1)} %get-tuple-element.58.refs_0_.refs_1_), channel_id=1, source_target_pairs={{16,0},{8,1},{24,8},{0,9},{17,16},{9,17},{25,24},{1,25},{18,2},{10... | collective-permute-start | bytes 1081352 | tf_op jit(solution)/shard_map/ppermute | solution.py:281
  10.9 1.0 %collective-permute-start.17 = (bf16[176,1024]{1,0:T(8,128)(2,1)S(1)}, bf16[176,1024]{1,0:T(8,128)(2,1)S(1)}, u32[]{:S(2)}, u32[]{:S(2)}) collective-permute-start(bf16[176,1024]{1,0:T(8,128)(2,1)S(1)} %get-tuple-element.58.refs_0_.refs_1_), channel_id=1, source_target_pairs={{1,0},{17,1},{9,8},{25,9},{0,16},{16,17},{8,24},{24,25},{3,2},{19,... | collective-permute-start | bytes 1081352 | tf_op jit(solution)/shard_map/ppermute | solution.py:281
  11.9 0.1 convert_reduce_fusion.5
  12.0 0.7 reduce_max.46
  13.5 0.0 copy-done.5
  13.5 0.1 convert_reduce_fusion.4
  13.6 10.0 %collective-permute-done.15.refs_1_.refs_2_ = bf16[176,1024]{1,0:T(8,128)(2,1)S(1)} collective-permute-done((bf16[176,1024]{1,0:T(8,128)(2,1)S(1)}, bf16[176,1024]{1,0:T(8,128)(2,1)S(1)}, u32[]{:S(2)}, u32[]{:S(2)}) %collective-permute-start.15) | collective-permute-done | bytes 360480 | tf_op jit(solution)/shard_map/ppermute | solution.py:278
  23.6 0.0 collective-permute-done.18.refs_9_.refs_13_
  23.6 0.0 collective-permute-done.17.refs_6_.refs_9_
  23.6 0.0 collective-permute-start.19
  23.6 0.1 pad_add_fusion.1
  23.7 0.1 pad.7.clone
  23.8 0.1 pad.6.clone
  23.9 0.0 copy-done.6
  23.9 0.1 select_reduce_fusion.5
  24.0 0.1 fusion.7
  24.1 2.7 %collective-permute-start.21 = (bf16[176,1024]{1,0:T(8,128)(2,1)}, bf16[176,1024]{1,0:T(8,128)(2,1)S(1)}, u32[]{:S(2)}, u32[]{:S(2)}) collective-permute-start(bf16[176,1024]{1,0:T(8,128)(2,1)} %get-tuple-element.63), channel_id=1, source_target_pairs={{6,0},{7,1},{14,8},{15,9},{22,16},{23,17},{30,24},{31,25},{4,2},{5... | collective-permute-start | bytes 1081352 | tf_op jit(solution)/shard_map/ppermute | solution.py:278
  26.7 1.3 %collective-permute-start.24 = (bf16[176,1024]{1,0:T(8,128)(2,1)S(1)}, bf16[176,1024]{1,0:T(8,128)(2,1)S(1)}, u32[]{:S(2)}, u32[]{:S(2)}) collective-permute-start(bf16[176,1024]{1,0:T(8,128)(2,1)S(1)} %collective-permute-done.15.refs_1_.refs_2_), channel_id=1, source_target_pairs={{16,0},{8,1},{24,8},{0,9},{17,16},{9,17},{25,24},{1,25},{18,2},{10... | collective-permute-start | bytes 1081352 | tf_op jit(solution)/shard_map/ppermute | solution.py:281
  28.1 0.7 collective-permute-start.23
  28.8 0.0 collective-permute-done.19.refs_4_.refs_6_
  28.8 0.1 broadcast_in_dim.172
  28.9 0.1 select_reduce_fusion.4
  29.0 0.6 all_to_all.21
  29.6 3.4 %all-to-all-start.2 = ((s32[32,1,256]{2,1,0:T(1,128)}), s32[32,1,256]{2,1,0:T(1,128)S(1)}, u32[]{:S(2)}, u32[]{:S(2)}) async-start(s32[32,1,256]{2,1,0:T(1,128)} %all_to_all.21), calls=%async_computation.2 | async-start | bytes 65536 | tf_op jit(solution)/shard_map/all_to_all | solution.py:322
  33.1 0.0 collective-permute-done.20.refs_2_.refs_3_
  33.1 1.6 %collective-permute-start.28 = (bf16[176,1024]{1,0:T(8,128)(2,1)S(1)}, bf16[176,1024]{1,0:T(8,128)(2,1)}, u32[]{:S(2)}, u32[]{:S(2)}) collective-permute-start(bf16[176,1024]{1,0:T(8,128)(2,1)S(1)} %collective-permute-done.20.refs_2_.refs_3_), channel_id=1, source_target_pairs={{16,0},{8,1},{24,8},{0,9},{17,16},{9,17},{25,24},{1,25},{18,2},{10... | collective-permute-start | bytes 1081352 | tf_op jit(solution)/shard_map/ppermute | solution.py:281
  34.7 0.5 collective-permute-start.26
  35.2 1.9 %collective-permute-done.21.refs_4_ = bf16[176,1024]{1,0:T(8,128)(2,1)S(1)} collective-permute-done((bf16[176,1024]{1,0:T(8,128)(2,1)}, bf16[176,1024]{1,0:T(8,128)(2,1)S(1)}, u32[]{:S(2)}, u32[]{:S(2)}) %collective-permute-start.21) | collective-permute-done | bytes 360480 | tf_op jit(solution)/shard_map/ppermute | solution.py:278
  37.1 0.9 %collective-permute-done.24.refs_10_.refs_14_ = bf16[176,1024]{1,0:T(8,128)(2,1)S(1)} collective-permute-done((bf16[176,1024]{1,0:T(8,128)(2,1)S(1)}, bf16[176,1024]{1,0:T(8,128)(2,1)S(1)}, u32[]{:S(2)}, u32[]{:S(2)}) %collective-permute-start.24) | collective-permute-done | bytes 360480 | tf_op jit(solution)/shard_map/ppermute | solution.py:281
  38.0 1.5 %collective-permute-done.23.refs_7_.refs_10_ = bf16[176,1024]{1,0:T(8,128)(2,1)} collective-permute-done((bf16[176,1024]{1,0:T(8,128)(2,1)S(1)}, bf16[176,1024]{1,0:T(8,128)(2,1)}, u32[]{:S(2)}, u32[]{:S(2)}) %collective-permute-start.23) | collective-permute-done | bytes 360480 | tf_op jit(solution)/shard_map/ppermute | solution.py:281
  39.6 0.0 collective-permute-start.29
  39.6 2.0 %collective-permute-start.27 = (bf16[176,1024]{1,0:T(8,128)(2,1)S(1)}, bf16[176,1024]{1,0:T(8,128)(2,1)}, u32[]{:S(2)}, u32[]{:S(2)}) collective-permute-start(bf16[176,1024]{1,0:T(8,128)(2,1)S(1)} %collective-permute-done.21.refs_4_), channel_id=1, source_target_pairs={{1,0},{17,1},{9,8},{25,9},{0,16},{16,17},{8,24},{24,25},{3,2},{19,... | collective-permute-start | bytes 1081352 | tf_op jit(solution)/shard_map/ppermute | solution.py:281
  41.6 0.0 collective-permute-start.22
  41.6 2.9 %all-to-all-done.2 = s32[32,1,256]{2,1,0:T(1,128)S(1)} async-done(((s32[32,1,256]{2,1,0:T(1,128)}), s32[32,1,256]{2,1,0:T(1,128)S(1)}, u32[]{:S(2)}, u32[]{:S(2)}) %all-to-all-start.2) | async-done | bytes 32800 | tf_op jit(solution)/shard_map/all_to_all | solution.py:322
  44.5 0.1 reduce.4
  44.6 0.1 broadcast_in_dim.181
  44.7 0.1 select_reduce_fusion.3
  44.8 0.1 reshape.175
  45.0 0.1 mul.54
  45.1 0.1 multiply_reduce_fusion.1
  45.2 0.1 fusion.4
  45.3 0.1 convert_reduce_fusion.3
  45.4 0.0 collective-permute-done.22.refs_5_.refs_7_
  45.4 0.2 collective-permute-start.25
  45.6 0.5 collective-permute-done.28.refs_11_.refs_15_
  46.2 1.3 %collective-permute-done.26.refs_8_.refs_11_ = bf16[176,1024]{1,0:T(8,128)(2,1)} collective-permute-done((bf16[176,1024]{1,0:T(8,128)(2,1)S(1)}, bf16[176,1024]{1,0:T(8,128)(2,1)}, u32[]{:S(2)}, u32[]{:S(2)}) %collective-permute-start.26) | collective-permute-done | bytes 360480 | tf_op jit(solution)/shard_map/ppermute | solution.py:281
  47.5 5.5 %shard_map.58 = (f32[4,512]{1,0:T(4,128)S(1)}, f32[704,4]{1,0:T(8,128)S(1)}) custom-call(bf16[176,1024]{1,0:T(8,128)(2,1)S(1)} %get-tuple-element.58.refs_0_.refs_1_, bf16[176,1024]{1,0:T(8,128)(2,1)S(1)} %collective-permute-done.15.refs_1_.refs_2_, bf16[176,1024]{1,0:T(8,128)(2,1)S(1)} %collective-permute-done.20.refs_2_.refs_3_, ...), custom_call_target="tpu_custom_call" | custom-call | flops 2684354560 | bytes 4194304 | tf_op jit(solution)/shard_map/pallas_call | solution.py:351
  53.0 0.2 collective-permute-done.29.refs_16_
  53.2 1.4 %collective-permute-done.27.refs_12_ = bf16[176,1024]{1,0:T(8,128)(2,1)} collective-permute-done((bf16[176,1024]{1,0:T(8,128)(2,1)S(1)}, bf16[176,1024]{1,0:T(8,128)(2,1)}, u32[]{:S(2)}, u32[]{:S(2)}) %collective-permute-start.27) | collective-permute-done | bytes 360480 | tf_op jit(solution)/shard_map/ppermute | solution.py:281
  54.6 0.0 collective-permute-done.25.refs_8_
  54.6 8.0 %shard_map.59 = f32[4,32,128]{2,1,0:T(8,128)} custom-call(s32[1]{0:T(128)} %bitcast.11.plane_ref.refs_0_, bf16[176,1024]{1,0:T(8,128)(2,1)S(1)} %get-tuple-element.58.refs_0_.refs_1_, bf16[176,1024]{1,0:T(8,128)(2,1)S(1)} %collective-permute-done.15.refs_1_.refs_2_, bf16[176,1024]{1,0:T(8,128)(2,1)S(1)} %collective-permute-done.20.refs_2_.refs_3_, ...), custom_call_target="tpu_custom_call" | custom-call | tf_op jit(solution)/shard_map/pallas_call | solution.py:365
  62.6 3.3 %all-to-all-start.3 = ((f32[32,4,128]{2,1,0:T(4,128)}), f32[32,4,128]{2,1,0:T(4,128)S(1)}, u32[]{:S(2)}, u32[]{:S(2)}) async-start(f32[32,4,128]{2,1,0:T(4,128)} %bitcast.17), calls=%async_computation.3 | async-start | bytes 131072 | tf_op jit(solution)/shard_map/all_to_all | solution.py:383
  66.0 0.7 slice_reduce_fusion
  67.4 5.9 %all-to-all-done.3 = f32[32,4,128]{2,1,0:T(4,128)S(1)} async-done(((f32[32,4,128]{2,1,0:T(4,128)}), f32[32,4,128]{2,1,0:T(4,128)S(1)}, u32[]{:S(2)}, u32[]{:S(2)}) %all-to-all-start.3) | async-done | bytes 65568 | tf_op jit(solution)/shard_map/all_to_all | solution.py:383
  73.3 0.3 conditional.1
  73.6 0.0 copy-start.7
  73.6 0.6 copy-done.7
  (21 shorter events, 0.2 us)
Async XLA Ops:
  0.0 23.9 %copy-start.6 = (s32[4,8]{1,0:T(4,128)S(1)}, s32[4,8]{1,0:T(4,128)}, u32[]{:S(2)}) copy-start(s32[4,8]{1,0:T(4,128)} %constant.109.clone) | copy-start | bytes 388
  0.0 9.8 %copy-start.4 = (s32[512]{0:T(512)S(1)}, s32[512]{0:T(512)}, u32[]{:S(2)}) copy-start(s32[512]{0:T(512)} %param.8) | copy-start | bytes 6148
  0.0 13.5 %copy-start.5 = (s32[1,512]{1,0:T(1,128)S(1)}, s32[1,512]{1,0:T(1,128)}, u32[]{:S(2)}) copy-start(s32[1,512]{1,0:T(1,128)} %param.9) | copy-start | bytes 6148
  4.1 5.8 %collective-permute-start.16 = (bf16[176,1024]{1,0:T(8,128)(2,1)S(1)}, bf16[176,1024]{1,0:T(8,128)(2,1)S(1)}, u32[]{:S(2)}, u32[]{:S(2)}) collective-permute-start(bf16[176,1024]{1,0:T(8,128)(2,1)S(1)} %get-tuple-element.58.refs_0_.refs_1_), channel_id=1, source_target_pairs={{8,0},{9,1},{0,8},{1,9},{24,16},{25,17},{16,24},{17,25},{10,2},{11... | collective-permute-start | bytes 1081352 | tf_op jit(solution)/shard_map/ppermute | solution.py:281
  4.6 19.1 %collective-permute-start.15 = (bf16[176,1024]{1,0:T(8,128)(2,1)S(1)}, bf16[176,1024]{1,0:T(8,128)(2,1)S(1)}, u32[]{:S(2)}, u32[]{:S(2)}) collective-permute-start(bf16[176,1024]{1,0:T(8,128)(2,1)S(1)} %get-tuple-element.56), channel_id=1, source_target_pairs={{2,0},{3,1},{10,8},{11,9},{18,16},{19,17},{26,24},{27,25},{0,2},{1... | collective-permute-start | bytes 1081352 | tf_op jit(solution)/shard_map/ppermute | solution.py:278
  7.2 25.9 %collective-permute-start.20 = (bf16[176,1024]{1,0:T(8,128)(2,1)}, bf16[176,1024]{1,0:T(8,128)(2,1)S(1)}, u32[]{:S(2)}, u32[]{:S(2)}) collective-permute-start(bf16[176,1024]{1,0:T(8,128)(2,1)} %get-tuple-element.61), channel_id=1, source_target_pairs={{4,0},{5,1},{12,8},{13,9},{20,16},{21,17},{28,24},{29,25},{6,2},{7... | collective-permute-start | bytes 1081352 | tf_op jit(solution)/shard_map/ppermute | solution.py:278
  9.8 13.8 %collective-permute-start.18 = (bf16[176,1024]{1,0:T(8,128)(2,1)S(1)}, bf16[176,1024]{1,0:T(8,128)(2,1)S(1)}, u32[]{:S(2)}, u32[]{:S(2)}) collective-permute-start(bf16[176,1024]{1,0:T(8,128)(2,1)S(1)} %get-tuple-element.58.refs_0_.refs_1_), channel_id=1, source_target_pairs={{16,0},{8,1},{24,8},{0,9},{17,16},{9,17},{25,24},{1,25},{18,2},{10... | collective-permute-start | bytes 1081352 | tf_op jit(solution)/shard_map/ppermute | solution.py:281
  10.9 12.7 %collective-permute-start.17 = (bf16[176,1024]{1,0:T(8,128)(2,1)S(1)}, bf16[176,1024]{1,0:T(8,128)(2,1)S(1)}, u32[]{:S(2)}, u32[]{:S(2)}) collective-permute-start(bf16[176,1024]{1,0:T(8,128)(2,1)S(1)} %get-tuple-element.58.refs_0_.refs_1_), channel_id=1, source_target_pairs={{1,0},{17,1},{9,8},{25,9},{0,16},{16,17},{8,24},{24,25},{3,2},{19,... | collective-permute-start | bytes 1081352 | tf_op jit(solution)/shard_map/ppermute | solution.py:281
  23.6 5.1 %collective-permute-start.19 = (bf16[176,1024]{1,0:T(8,128)(2,1)S(1)}, bf16[176,1024]{1,0:T(8,128)(2,1)S(1)}, u32[]{:S(2)}, u32[]{:S(2)}) collective-permute-start(bf16[176,1024]{1,0:T(8,128)(2,1)S(1)} %collective-permute-done.15.refs_1_.refs_2_), channel_id=1, source_target_pairs={{8,0},{9,1},{0,8},{1,9},{24,16},{25,17},{16,24},{17,25},{10,2},{11... | collective-permute-start | bytes 1081352 | tf_op jit(solution)/shard_map/ppermute | solution.py:281
  24.1 13.0 %collective-permute-start.21 = (bf16[176,1024]{1,0:T(8,128)(2,1)}, bf16[176,1024]{1,0:T(8,128)(2,1)S(1)}, u32[]{:S(2)}, u32[]{:S(2)}) collective-permute-start(bf16[176,1024]{1,0:T(8,128)(2,1)} %get-tuple-element.63), channel_id=1, source_target_pairs={{6,0},{7,1},{14,8},{15,9},{22,16},{23,17},{30,24},{31,25},{4,2},{5... | collective-permute-start | bytes 1081352 | tf_op jit(solution)/shard_map/ppermute | solution.py:278
  26.7 11.3 %collective-permute-start.24 = (bf16[176,1024]{1,0:T(8,128)(2,1)S(1)}, bf16[176,1024]{1,0:T(8,128)(2,1)S(1)}, u32[]{:S(2)}, u32[]{:S(2)}) collective-permute-start(bf16[176,1024]{1,0:T(8,128)(2,1)S(1)} %collective-permute-done.15.refs_1_.refs_2_), channel_id=1, source_target_pairs={{16,0},{8,1},{24,8},{0,9},{17,16},{9,17},{25,24},{1,25},{18,2},{10... | collective-permute-start | bytes 1081352 | tf_op jit(solution)/shard_map/ppermute | solution.py:281
  28.1 11.5 %collective-permute-start.23 = (bf16[176,1024]{1,0:T(8,128)(2,1)S(1)}, bf16[176,1024]{1,0:T(8,128)(2,1)}, u32[]{:S(2)}, u32[]{:S(2)}) collective-permute-start(bf16[176,1024]{1,0:T(8,128)(2,1)S(1)} %collective-permute-done.15.refs_1_.refs_2_), channel_id=1, source_target_pairs={{1,0},{17,1},{9,8},{25,9},{0,16},{16,17},{8,24},{24,25},{3,2},{19,... | collective-permute-start | bytes 1081352 | tf_op jit(solution)/shard_map/ppermute | solution.py:281
  29.6 14.8 %all-to-all-start.2 = ((s32[32,1,256]{2,1,0:T(1,128)}), s32[32,1,256]{2,1,0:T(1,128)S(1)}, u32[]{:S(2)}, u32[]{:S(2)}) async-start(s32[32,1,256]{2,1,0:T(1,128)} %all_to_all.21), calls=%async_computation.2 | async-start | bytes 65536 | tf_op jit(solution)/shard_map/all_to_all | solution.py:322
  33.1 13.1 %collective-permute-start.28 = (bf16[176,1024]{1,0:T(8,128)(2,1)S(1)}, bf16[176,1024]{1,0:T(8,128)(2,1)}, u32[]{:S(2)}, u32[]{:S(2)}) collective-permute-start(bf16[176,1024]{1,0:T(8,128)(2,1)S(1)} %collective-permute-done.20.refs_2_.refs_3_), channel_id=1, source_target_pairs={{16,0},{8,1},{24,8},{0,9},{17,16},{9,17},{25,24},{1,25},{18,2},{10... | collective-permute-start | bytes 1081352 | tf_op jit(solution)/shard_map/ppermute | solution.py:281
  34.7 12.8 %collective-permute-start.26 = (bf16[176,1024]{1,0:T(8,128)(2,1)S(1)}, bf16[176,1024]{1,0:T(8,128)(2,1)}, u32[]{:S(2)}, u32[]{:S(2)}) collective-permute-start(bf16[176,1024]{1,0:T(8,128)(2,1)S(1)} %collective-permute-done.20.refs_2_.refs_3_), channel_id=1, source_target_pairs={{1,0},{17,1},{9,8},{25,9},{0,16},{16,17},{8,24},{24,25},{3,2},{19,... | collective-permute-start | bytes 1081352 | tf_op jit(solution)/shard_map/ppermute | solution.py:281
  39.6 13.6 %collective-permute-start.29 = (bf16[176,1024]{1,0:T(8,128)(2,1)S(1)}, bf16[176,1024]{1,0:T(8,128)(2,1)}, u32[]{:S(2)}, u32[]{:S(2)}) collective-permute-start(bf16[176,1024]{1,0:T(8,128)(2,1)S(1)} %collective-permute-done.21.refs_4_), channel_id=1, source_target_pairs={{16,0},{8,1},{24,8},{0,9},{17,16},{9,17},{25,24},{1,25},{18,2},{10... | collective-permute-start | bytes 1081352 | tf_op jit(solution)/shard_map/ppermute | solution.py:281
  39.6 15.0 %collective-permute-start.27 = (bf16[176,1024]{1,0:T(8,128)(2,1)S(1)}, bf16[176,1024]{1,0:T(8,128)(2,1)}, u32[]{:S(2)}, u32[]{:S(2)}) collective-permute-start(bf16[176,1024]{1,0:T(8,128)(2,1)S(1)} %collective-permute-done.21.refs_4_), channel_id=1, source_target_pairs={{1,0},{17,1},{9,8},{25,9},{0,16},{16,17},{8,24},{24,25},{3,2},{19,... | collective-permute-start | bytes 1081352 | tf_op jit(solution)/shard_map/ppermute | solution.py:281
  41.6 3.8 %collective-permute-start.22 = (bf16[176,1024]{1,0:T(8,128)(2,1)S(1)}, bf16[176,1024]{1,0:T(8,128)(2,1)}, u32[]{:S(2)}, u32[]{:S(2)}) collective-permute-start(bf16[176,1024]{1,0:T(8,128)(2,1)S(1)} %collective-permute-done.20.refs_2_.refs_3_), channel_id=1, source_target_pairs={{8,0},{9,1},{0,8},{1,9},{24,16},{25,17},{16,24},{17,25},{10,2},{11... | collective-permute-start | bytes 1081352 | tf_op jit(solution)/shard_map/ppermute | solution.py:281
  45.4 9.2 %collective-permute-start.25 = (bf16[176,1024]{1,0:T(8,128)(2,1)S(1)}, bf16[176,1024]{1,0:T(8,128)(2,1)S(1)}, u32[]{:S(2)}, u32[]{:S(2)}) collective-permute-start(bf16[176,1024]{1,0:T(8,128)(2,1)S(1)} %collective-permute-done.21.refs_4_), channel_id=1, source_target_pairs={{8,0},{9,1},{0,8},{1,9},{24,16},{25,17},{16,24},{17,25},{10,2},{11... | collective-permute-start | bytes 1081352 | tf_op jit(solution)/shard_map/ppermute | solution.py:281
  62.6 10.6 %all-to-all-start.3 = ((f32[32,4,128]{2,1,0:T(4,128)}), f32[32,4,128]{2,1,0:T(4,128)S(1)}, u32[]{:S(2)}, u32[]{:S(2)}) async-start(f32[32,4,128]{2,1,0:T(4,128)} %bitcast.17), calls=%async_computation.3 | async-start | bytes 131072 | tf_op jit(solution)/shard_map/all_to_all | solution.py:383
  73.6 0.6 copy-start.7

commit v12 on v9

--- a/solution.py
+++ b/solution.py
@@ -157,8 +157,9 @@
 def early_kernel(pairs, count, early, *refs):
     *chunks, label_ref, last_label_ref, out_ref, label_col_ref, blocks, sems = refs
     need = loader(chunks, count, blocks, sems)
-    for j in sorted({j for j, _ in pairs}):
-        label_col_ref[:early, j : j + 1] = as_column(label_ref[j : j + 1, :])
+    for j in range(count):
+        if any(j == left for left, _ in pairs):
+            label_col_ref[:early, j : j + 1] = as_column(label_ref[j : j + 1, :])
         label_col_ref[early:, j : j + 1] = as_column(last_label_ref[j : j + 1, :])
     best = [Best(jnp.full((1, early), -1.0, jnp.float32)) for _ in range(count)]
     for j, k in pairs:
@@ -178,7 +179,7 @@
 
 
 def late_kernel(pairs, count, group_size, *refs):
-    plane_ref, *chunks, best_ref, place_ref, last_place_ref, label_ref, last_label_ref, label_col_ref, out_ref, blocks, sems = refs
+    plane_ref, *chunks, best_ref, place_ref, last_place_ref, label_ref, label_col_ref, out_ref, blocks, sems = refs
     need = loader(chunks, count, blocks, sems)
     first = best_ref.shape[1]
     rest = blocks.shape[1] - first
@@ -187,19 +188,22 @@
     for j, k in pairs:
         need(j, k)
         sims = similar(
+            blocks[k, first:],
             blocks[j],
-            blocks[k, first:],
-            label_col_ref[:, j : j + 1],
-            last_label_ref[k : k + 1, :],
-            first if j == k else None,
+            label_col_ref[first:, k : k + 1],
+            label_ref[j : j + 1, :],
+            -first if j == k else None,
         )
-        column = row_max(sims)
-        early[j].add_column(column[:first])
-        late[k].add_row(column_max(sims))
+        row = column_max(sims)
+        early[j].add_row(row[:, :first])
+        late[j].add_row(row[:, first:])
+        late[k].add_column(row_max(sims))
         if j != k:
-            late[j].add_column(column[first:])
             sims = similar(
-                blocks[j, first:], blocks[k, :first], label_col_ref[first:, j : j + 1], label_ref[k : k + 1, :]
+                blocks[j, first:],
+                blocks[k, :first],
+                label_col_ref[first:, j : j + 1],
+                label_ref[k : k + 1, :first],
             )
             early[k].add_row(column_max(sims))
             late[j].add_column(row_max(sims))
@@ -348,7 +352,7 @@
     best = pl.pallas_call(
         functools.partial(late_kernel, pairs, count, group_size),
         out_shape=jax.ShapeDtypeStruct((n_row, group_size // 128, 128), jnp.float32),
-        in_specs=[pl.BlockSpec(memory_space=pltpu.SMEM)] + [any_space] * (count * groups) + [VMEM] * 6,
+        in_specs=[pl.BlockSpec(memory_space=pltpu.SMEM)] + [any_space] * (count * groups) + [VMEM] * 5,
         out_specs=VMEM,
         scratch_shapes=scratch(groups),
         compiler_params=kernel_params(limit),
@@ -358,8 +362,7 @@
         first_best,
         places[:, :early],
         places[:, early:],
-        label,
-        last_label,
+        labels,
         label_cols,
     )
 

time: 73.3 us -> 73.2 us (level)
  transfers between devices with their start and end apart: 17 -> 17, of which waited for: 10 -> 10; matrix products, arithmetic and copies ran while one was open for 4% -> 4% of each run, Pallas kernels for 7% -> 8%
where the time goes in v12:
time: 73.2 us; the launch traced here: 72.9 us
  waiting for transfers between devices  26.7 us (36%)
  starting transfers between devices  23.4 us (32%)
  Pallas kernels  16.5 us (23%)
  other arithmetic  2.66 us (4%)
  local copies, waits for them, and re-layouts  1.82 us (2%)
  between operations  1.6 us (2%)
    ppermute x3, waiting for transfers between devices, across(): lax.ppermute(part, AXES, [(device(i, h ^ k), device(i, h)) for i, h in pl...  12 us
    ppermute x12, starting transfers between devices, inside(): lax.ppermute(part, AXES, [(device(int(held[j, i]), h), device(i, h)) for...  8.86 us
    ppermute x3, starting transfers between devices, across(): lax.ppermute(part, AXES, [(device(i, h ^ k), device(i, h)) for i, h in pl...  7.83 us
    pallas_call x1, Pallas kernels, best_matches(): pl.pallas_call(functools.partial(late_kernel, pairs, count, group_size),...  7.49 us
    all_to_all x1, waiting for transfers between devices, best_matches(): lax.all_to_all(best.reshape(devs, -1, 128), AXES, split_axis=0, concat_ax...  5.9 us
    ppermute x12, waiting for transfers between devices, inside(): lax.ppermute(part, AXES, [(device(int(held[j, i]), h), device(i, h)) for...  5.88 us
    pallas_call x1, Pallas kernels, best_matches(): pl.pallas_call(functools.partial(early_kernel, pairs, count, early), out_...  5.48 us
    pallas_call x1, Pallas kernels, best_matches(): pl.pallas_call(functools.partial(pack_kernel, groups, cap, group_size), o...  3.53 us
  transfers between devices with their start and end apart: 17, of which 10 were waited for; matrix products, arithmetic and copies ran while one was open for 4% of the time, Pallas kernels for 8%

profile of v12, /device:TPU:0, one launch (start us, length us, event | category | flops | bytes accessed | tf_op | source)
XLA Modules:
  0.0 72.9 jit_solution(15787118599812379324)
XLA Ops:
  0.0 0.0 copy-start.6
  0.0 3.5 %shard_map.57 = (s32[1,704]{1,0:T(1,128)S(1)}, bf16[176,1024]{1,0:T(8,128)(2,1)S(1)}, bf16[176,1024]{1,0:T(8,128)(2,1)S(1)}, bf16[176,1024]{1,0:T(8,128)(2,1)}, bf16[176,1024]{1,0:T(8,128)(2,1)}) custom-call(s32[1]{0:T(128)} %bitcast.11.plane_ref.refs_0_, s32[1,512]{1,0:T(1,128)} %bitcast.32, f32[512,1024]{1,0:T(8,128)} %emb_ref.1), custom_call_target="tpu_custom_call" | custom-call | tf_op jit(solution)/shard_map/pallas_call | solution.py:253
  3.5 0.5 collective-permute-start.16
  4.0 2.6 %collective-permute-start.15 = (bf16[176,1024]{1,0:T(8,128)(2,1)S(1)}, bf16[176,1024]{1,0:T(8,128)(2,1)S(1)}, u32[]{:S(2)}, u32[]{:S(2)}) collective-permute-start(bf16[176,1024]{1,0:T(8,128)(2,1)S(1)} %get-tuple-element.56), channel_id=1, source_target_pairs={{2,0},{3,1},{10,8},{11,9},{18,16},{19,17},{26,24},{27,25},{0,2},{1... | collective-permute-start | bytes 1081352 | tf_op jit(solution)/shard_map/ppermute | solution.py:265
  6.6 2.6 %collective-permute-start.20 = (bf16[176,1024]{1,0:T(8,128)(2,1)}, bf16[176,1024]{1,0:T(8,128)(2,1)S(1)}, u32[]{:S(2)}, u32[]{:S(2)}) collective-permute-start(bf16[176,1024]{1,0:T(8,128)(2,1)} %get-tuple-element.61), channel_id=1, source_target_pairs={{4,0},{5,1},{12,8},{13,9},{20,16},{21,17},{28,24},{29,25},{6,2},{7... | collective-permute-start | bytes 1081352 | tf_op jit(solution)/shard_map/ppermute | solution.py:265
  9.2 0.0 copy-done.4
  9.2 0.0 collective-permute-done.16.refs_3_.refs_5_
  9.2 1.1 %collective-permute-start.18 = (bf16[176,1024]{1,0:T(8,128)(2,1)S(1)}, bf16[176,1024]{1,0:T(8,128)(2,1)S(1)}, u32[]{:S(2)}, u32[]{:S(2)}) collective-permute-start(bf16[176,1024]{1,0:T(8,128)(2,1)S(1)} %get-tuple-element.58.refs_0_.refs_1_), channel_id=1, source_target_pairs={{16,0},{8,1},{24,8},{0,9},{17,16},{9,17},{25,24},{1,25},{18,2},{10... | collective-permute-start | bytes 1081352 | tf_op jit(solution)/shard_map/ppermute | solution.py:268
  10.3 1.0 %collective-permute-start.17 = (bf16[176,1024]{1,0:T(8,128)(2,1)S(1)}, bf16[176,1024]{1,0:T(8,128)(2,1)S(1)}, u32[]{:S(2)}, u32[]{:S(2)}) collective-permute-start(bf16[176,1024]{1,0:T(8,128)(2,1)S(1)} %get-tuple-element.58.refs_0_.refs_1_), channel_id=1, source_target_pairs={{1,0},{17,1},{9,8},{25,9},{0,16},{16,17},{8,24},{24,25},{3,2},{19,... | collective-permute-start | bytes 1081352 | tf_op jit(solution)/shard_map/ppermute | solution.py:268
  11.3 0.1 convert_reduce_fusion.5
  11.4 0.7 reduce_max.46
  12.8 0.0 copy-done.5
  12.8 0.1 convert_reduce_fusion.4
  13.0 10.1 %collective-permute-done.15.refs_1_.refs_2_ = bf16[176,1024]{1,0:T(8,128)(2,1)S(1)} collective-permute-done((bf16[176,1024]{1,0:T(8,128)(2,1)S(1)}, bf16[176,1024]{1,0:T(8,128)(2,1)S(1)}, u32[]{:S(2)}, u32[]{:S(2)}) %collective-permute-start.15) | collective-permute-done | bytes 360480 | tf_op jit(solution)/shard_map/ppermute | solution.py:265
  23.0 0.0 collective-permute-done.18.refs_9_.refs_13_
  23.1 0.0 collective-permute-done.17.refs_6_.refs_9_
  23.1 0.0 collective-permute-start.19
  23.1 0.1 pad_add_fusion.1
  23.1 0.1 pad.7.clone
  23.2 0.1 pad.6.clone
  23.3 0.0 copy-done.6
  23.3 0.1 select_reduce_fusion.5
  23.4 0.1 fusion.7
  23.5 2.7 %collective-permute-start.21 = (bf16[176,1024]{1,0:T(8,128)(2,1)}, bf16[176,1024]{1,0:T(8,128)(2,1)S(1)}, u32[]{:S(2)}, u32[]{:S(2)}) collective-permute-start(bf16[176,1024]{1,0:T(8,128)(2,1)} %get-tuple-element.63), channel_id=1, source_target_pairs={{6,0},{7,1},{14,8},{15,9},{22,16},{23,17},{30,24},{31,25},{4,2},{5... | collective-permute-start | bytes 1081352 | tf_op jit(solution)/shard_map/ppermute | solution.py:265
  26.2 1.3 %collective-permute-start.24 = (bf16[176,1024]{1,0:T(8,128)(2,1)S(1)}, bf16[176,1024]{1,0:T(8,128)(2,1)S(1)}, u32[]{:S(2)}, u32[]{:S(2)}) collective-permute-start(bf16[176,1024]{1,0:T(8,128)(2,1)S(1)} %collective-permute-done.15.refs_1_.refs_2_), channel_id=1, source_target_pairs={{16,0},{8,1},{24,8},{0,9},{17,16},{9,17},{25,24},{1,25},{18,2},{10... | collective-permute-start | bytes 1081352 | tf_op jit(solution)/shard_map/ppermute | solution.py:268
  27.5 0.7 collective-permute-start.23
  28.2 0.0 collective-permute-done.19.refs_4_.refs_6_
  28.2 0.1 broadcast_in_dim.172
  28.3 0.1 select_reduce_fusion.4
  28.4 0.6 all_to_all.21
  29.1 3.4 %all-to-all-start.2 = ((s32[32,1,256]{2,1,0:T(1,128)}), s32[32,1,256]{2,1,0:T(1,128)S(1)}, u32[]{:S(2)}, u32[]{:S(2)}) async-start(s32[32,1,256]{2,1,0:T(1,128)} %all_to_all.21), calls=%async_computation.2 | async-start | bytes 65536 | tf_op jit(solution)/shard_map/all_to_all | solution.py:309
  32.5 0.0 collective-permute-done.20.refs_2_.refs_3_
  32.5 1.6 %collective-permute-start.28 = (bf16[176,1024]{1,0:T(8,128)(2,1)S(1)}, bf16[176,1024]{1,0:T(8,128)(2,1)}, u32[]{:S(2)}, u32[]{:S(2)}) collective-permute-start(bf16[176,1024]{1,0:T(8,128)(2,1)S(1)} %collective-permute-done.20.refs_2_.refs_3_), channel_id=1, source_target_pairs={{16,0},{8,1},{24,8},{0,9},{17,16},{9,17},{25,24},{1,25},{18,2},{10... | collective-permute-start | bytes 1081352 | tf_op jit(solution)/shard_map/ppermute | solution.py:268
  34.0 0.5 collective-permute-start.26
  34.6 2.0 %collective-permute-done.21.refs_4_ = bf16[176,1024]{1,0:T(8,128)(2,1)S(1)} collective-permute-done((bf16[176,1024]{1,0:T(8,128)(2,1)}, bf16[176,1024]{1,0:T(8,128)(2,1)S(1)}, u32[]{:S(2)}, u32[]{:S(2)}) %collective-permute-start.21) | collective-permute-done | bytes 360480 | tf_op jit(solution)/shard_map/ppermute | solution.py:265
  36.5 0.9 %collective-permute-done.24.refs_10_.refs_14_ = bf16[176,1024]{1,0:T(8,128)(2,1)S(1)} collective-permute-done((bf16[176,1024]{1,0:T(8,128)(2,1)S(1)}, bf16[176,1024]{1,0:T(8,128)(2,1)S(1)}, u32[]{:S(2)}, u32[]{:S(2)}) %collective-permute-start.24) | collective-permute-done | bytes 360480 | tf_op jit(solution)/shard_map/ppermute | solution.py:268
  37.5 1.5 %collective-permute-done.23.refs_7_.refs_10_ = bf16[176,1024]{1,0:T(8,128)(2,1)} collective-permute-done((bf16[176,1024]{1,0:T(8,128)(2,1)S(1)}, bf16[176,1024]{1,0:T(8,128)(2,1)}, u32[]{:S(2)}, u32[]{:S(2)}) %collective-permute-start.23) | collective-permute-done | bytes 360480 | tf_op jit(solution)/shard_map/ppermute | solution.py:268
  39.0 0.0 collective-permute-start.29
  39.0 2.0 %collective-permute-start.27 = (bf16[176,1024]{1,0:T(8,128)(2,1)S(1)}, bf16[176,1024]{1,0:T(8,128)(2,1)}, u32[]{:S(2)}, u32[]{:S(2)}) collective-permute-start(bf16[176,1024]{1,0:T(8,128)(2,1)S(1)} %collective-permute-done.21.refs_4_), channel_id=1, source_target_pairs={{1,0},{17,1},{9,8},{25,9},{0,16},{16,17},{8,24},{24,25},{3,2},{19,... | collective-permute-start | bytes 1081352 | tf_op jit(solution)/shard_map/ppermute | solution.py:268
  41.0 0.0 collective-permute-start.22
  41.0 2.9 %all-to-all-done.2 = s32[32,1,256]{2,1,0:T(1,128)S(1)} async-done(((s32[32,1,256]{2,1,0:T(1,128)}), s32[32,1,256]{2,1,0:T(1,128)S(1)}, u32[]{:S(2)}, u32[]{:S(2)}) %all-to-all-start.2) | async-done | bytes 32800 | tf_op jit(solution)/shard_map/all_to_all | solution.py:309
  43.9 0.1 reduce.4
  44.0 0.1 broadcast_in_dim.181
  44.1 0.1 select_reduce_fusion.3
  44.3 0.1 reshape.175
  44.4 0.1 mul.54
  44.5 0.1 multiply_reduce_fusion.1
  44.6 0.1 fusion.4
  44.7 0.1 convert_reduce_fusion.3
  44.8 0.0 collective-permute-done.22.refs_5_.refs_7_
  44.8 0.2 collective-permute-start.25
  45.1 0.5 collective-permute-done.28.refs_11_.refs_15_
  45.6 1.3 %collective-permute-done.26.refs_8_.refs_11_ = bf16[176,1024]{1,0:T(8,128)(2,1)} collective-permute-done((bf16[176,1024]{1,0:T(8,128)(2,1)S(1)}, bf16[176,1024]{1,0:T(8,128)(2,1)}, u32[]{:S(2)}, u32[]{:S(2)}) %collective-permute-start.26) | collective-permute-done | bytes 360480 | tf_op jit(solution)/shard_map/ppermute | solution.py:268
  46.9 5.5 %shard_map.58 = (f32[4,512]{1,0:T(4,128)S(1)}, f32[704,4]{1,0:T(8,128)S(1)}) custom-call(bf16[176,1024]{1,0:T(8,128)(2,1)S(1)} %get-tuple-element.58.refs_0_.refs_1_, bf16[176,1024]{1,0:T(8,128)(2,1)S(1)} %collective-permute-done.15.refs_1_.refs_2_, bf16[176,1024]{1,0:T(8,128)(2,1)S(1)} %collective-permute-done.20.refs_2_.refs_3_, ...), custom_call_target="tpu_custom_call" | custom-call | flops 2684354560 | bytes 4194304 | tf_op jit(solution)/shard_map/pallas_call | solution.py:338
  52.4 0.2 collective-permute-done.29.refs_16_
  52.6 1.4 %collective-permute-done.27.refs_12_ = bf16[176,1024]{1,0:T(8,128)(2,1)} collective-permute-done((bf16[176,1024]{1,0:T(8,128)(2,1)S(1)}, bf16[176,1024]{1,0:T(8,128)(2,1)}, u32[]{:S(2)}, u32[]{:S(2)}) %collective-permute-start.27) | collective-permute-done | bytes 360480 | tf_op jit(solution)/shard_map/ppermute | solution.py:268
  54.0 0.0 collective-permute-done.25.refs_8_
  54.0 7.5 %shard_map.59 = f32[4,32,128]{2,1,0:T(8,128)} custom-call(s32[1]{0:T(128)} %bitcast.11.plane_ref.refs_0_, bf16[176,1024]{1,0:T(8,128)(2,1)S(1)} %get-tuple-element.58.refs_0_.refs_1_, bf16[176,1024]{1,0:T(8,128)(2,1)S(1)} %collective-permute-done.15.refs_1_.refs_2_, bf16[176,1024]{1,0:T(8,128)(2,1)S(1)} %collective-permute-done.20.refs_2_.refs_3_, ...), custom_call_target="tpu_custom_call" | custom-call | tf_op jit(solution)/shard_map/pallas_call | solution.py:352
  61.5 3.3 %all-to-all-start.3 = ((f32[32,4,128]{2,1,0:T(4,128)}), f32[32,4,128]{2,1,0:T(4,128)S(1)}, u32[]{:S(2)}, u32[]{:S(2)}) async-start(f32[32,4,128]{2,1,0:T(4,128)} %bitcast.17), calls=%async_computation.3 | async-start | bytes 131072 | tf_op jit(solution)/shard_map/all_to_all | solution.py:369
  64.8 0.7 slice_reduce_fusion
  66.2 5.9 %all-to-all-done.3 = f32[32,4,128]{2,1,0:T(4,128)S(1)} async-done(((f32[32,4,128]{2,1,0:T(4,128)}), f32[32,4,128]{2,1,0:T(4,128)S(1)}, u32[]{:S(2)}, u32[]{:S(2)}) %all-to-all-start.3) | async-done | bytes 65568 | tf_op jit(solution)/shard_map/all_to_all | solution.py:369
  72.1 0.3 conditional.1
  72.4 0.0 copy-start.7
  72.4 0.6 copy-done.7
  (21 shorter events, 0.2 us)
Async XLA Ops:
  0.0 23.3 %copy-start.6 = (s32[4,8]{1,0:T(4,128)S(1)}, s32[4,8]{1,0:T(4,128)}, u32[]{:S(2)}) copy-start(s32[4,8]{1,0:T(4,128)} %constant.109.clone) | copy-start | bytes 388
  0.0 9.2 %copy-start.4 = (s32[512]{0:T(512)S(1)}, s32[512]{0:T(512)}, u32[]{:S(2)}) copy-start(s32[512]{0:T(512)} %param.8) | copy-start | bytes 6148
  0.0 12.8 %copy-start.5 = (s32[1,512]{1,0:T(1,128)S(1)}, s32[1,512]{1,0:T(1,128)}, u32[]{:S(2)}) copy-start(s32[1,512]{1,0:T(1,128)} %param.9) | copy-start | bytes 6148
  3.5 5.6 %collective-permute-start.16 = (bf16[176,1024]{1,0:T(8,128)(2,1)S(1)}, bf16[176,1024]{1,0:T(8,128)(2,1)S(1)}, u32[]{:S(2)}, u32[]{:S(2)}) collective-permute-start(bf16[176,1024]{1,0:T(8,128)(2,1)S(1)} %get-tuple-element.58.refs_0_.refs_1_), channel_id=1, source_target_pairs={{8,0},{9,1},{0,8},{1,9},{24,16},{25,17},{16,24},{17,25},{10,2},{11... | collective-permute-start | bytes 1081352 | tf_op jit(solution)/shard_map/ppermute | solution.py:268
  4.0 19.1 %collective-permute-start.15 = (bf16[176,1024]{1,0:T(8,128)(2,1)S(1)}, bf16[176,1024]{1,0:T(8,128)(2,1)S(1)}, u32[]{:S(2)}, u32[]{:S(2)}) collective-permute-start(bf16[176,1024]{1,0:T(8,128)(2,1)S(1)} %get-tuple-element.56), channel_id=1, source_target_pairs={{2,0},{3,1},{10,8},{11,9},{18,16},{19,17},{26,24},{27,25},{0,2},{1... | collective-permute-start | bytes 1081352 | tf_op jit(solution)/shard_map/ppermute | solution.py:265
  6.6 25.9 %collective-permute-start.20 = (bf16[176,1024]{1,0:T(8,128)(2,1)}, bf16[176,1024]{1,0:T(8,128)(2,1)S(1)}, u32[]{:S(2)}, u32[]{:S(2)}) collective-permute-start(bf16[176,1024]{1,0:T(8,128)(2,1)} %get-tuple-element.61), channel_id=1, source_target_pairs={{4,0},{5,1},{12,8},{13,9},{20,16},{21,17},{28,24},{29,25},{6,2},{7... | collective-permute-start | bytes 1081352 | tf_op jit(solution)/shard_map/ppermute | solution.py:265
  9.2 13.9 %collective-permute-start.18 = (bf16[176,1024]{1,0:T(8,128)(2,1)S(1)}, bf16[176,1024]{1,0:T(8,128)(2,1)S(1)}, u32[]{:S(2)}, u32[]{:S(2)}) collective-permute-start(bf16[176,1024]{1,0:T(8,128)(2,1)S(1)} %get-tuple-element.58.refs_0_.refs_1_), channel_id=1, source_target_pairs={{16,0},{8,1},{24,8},{0,9},{17,16},{9,17},{25,24},{1,25},{18,2},{10... | collective-permute-start | bytes 1081352 | tf_op jit(solution)/shard_map/ppermute | solution.py:268
  10.3 12.7 %collective-permute-start.17 = (bf16[176,1024]{1,0:T(8,128)(2,1)S(1)}, bf16[176,1024]{1,0:T(8,128)(2,1)S(1)}, u32[]{:S(2)}, u32[]{:S(2)}) collective-permute-start(bf16[176,1024]{1,0:T(8,128)(2,1)S(1)} %get-tuple-element.58.refs_0_.refs_1_), channel_id=1, source_target_pairs={{1,0},{17,1},{9,8},{25,9},{0,16},{16,17},{8,24},{24,25},{3,2},{19,... | collective-permute-start | bytes 1081352 | tf_op jit(solution)/shard_map/ppermute | solution.py:268
  23.1 5.1 %collective-permute-start.19 = (bf16[176,1024]{1,0:T(8,128)(2,1)S(1)}, bf16[176,1024]{1,0:T(8,128)(2,1)S(1)}, u32[]{:S(2)}, u32[]{:S(2)}) collective-permute-start(bf16[176,1024]{1,0:T(8,128)(2,1)S(1)} %collective-permute-done.15.refs_1_.refs_2_), channel_id=1, source_target_pairs={{8,0},{9,1},{0,8},{1,9},{24,16},{25,17},{16,24},{17,25},{10,2},{11... | collective-permute-start | bytes 1081352 | tf_op jit(solution)/shard_map/ppermute | solution.py:268
  23.5 13.0 %collective-permute-start.21 = (bf16[176,1024]{1,0:T(8,128)(2,1)}, bf16[176,1024]{1,0:T(8,128)(2,1)S(1)}, u32[]{:S(2)}, u32[]{:S(2)}) collective-permute-start(bf16[176,1024]{1,0:T(8,128)(2,1)} %get-tuple-element.63), channel_id=1, source_target_pairs={{6,0},{7,1},{14,8},{15,9},{22,16},{23,17},{30,24},{31,25},{4,2},{5... | collective-permute-start | bytes 1081352 | tf_op jit(solution)/shard_map/ppermute | solution.py:265
  26.2 11.3 %collective-permute-start.24 = (bf16[176,1024]{1,0:T(8,128)(2,1)S(1)}, bf16[176,1024]{1,0:T(8,128)(2,1)S(1)}, u32[]{:S(2)}, u32[]{:S(2)}) collective-permute-start(bf16[176,1024]{1,0:T(8,128)(2,1)S(1)} %collective-permute-done.15.refs_1_.refs_2_), channel_id=1, source_target_pairs={{16,0},{8,1},{24,8},{0,9},{17,16},{9,17},{25,24},{1,25},{18,2},{10... | collective-permute-start | bytes 1081352 | tf_op jit(solution)/shard_map/ppermute | solution.py:268
  27.5 11.5 %collective-permute-start.23 = (bf16[176,1024]{1,0:T(8,128)(2,1)S(1)}, bf16[176,1024]{1,0:T(8,128)(2,1)}, u32[]{:S(2)}, u32[]{:S(2)}) collective-permute-start(bf16[176,1024]{1,0:T(8,128)(2,1)S(1)} %collective-permute-done.15.refs_1_.refs_2_), channel_id=1, source_target_pairs={{1,0},{17,1},{9,8},{25,9},{0,16},{16,17},{8,24},{24,25},{3,2},{19,... | collective-permute-start | bytes 1081352 | tf_op jit(solution)/shard_map/ppermute | solution.py:268
  29.1 14.8 %all-to-all-start.2 = ((s32[32,1,256]{2,1,0:T(1,128)}), s32[32,1,256]{2,1,0:T(1,128)S(1)}, u32[]{:S(2)}, u32[]{:S(2)}) async-start(s32[32,1,256]{2,1,0:T(1,128)} %all_to_all.21), calls=%async_computation.2 | async-start | bytes 65536 | tf_op jit(solution)/shard_map/all_to_all | solution.py:309
  32.5 13.1 %collective-permute-start.28 = (bf16[176,1024]{1,0:T(8,128)(2,1)S(1)}, bf16[176,1024]{1,0:T(8,128)(2,1)}, u32[]{:S(2)}, u32[]{:S(2)}) collective-permute-start(bf16[176,1024]{1,0:T(8,128)(2,1)S(1)} %collective-permute-done.20.refs_2_.refs_3_), channel_id=1, source_target_pairs={{16,0},{8,1},{24,8},{0,9},{17,16},{9,17},{25,24},{1,25},{18,2},{10... | collective-permute-start | bytes 1081352 | tf_op jit(solution)/shard_map/ppermute | solution.py:268
  34.0 12.8 %collective-permute-start.26 = (bf16[176,1024]{1,0:T(8,128)(2,1)S(1)}, bf16[176,1024]{1,0:T(8,128)(2,1)}, u32[]{:S(2)}, u32[]{:S(2)}) collective-permute-start(bf16[176,1024]{1,0:T(8,128)(2,1)S(1)} %collective-permute-done.20.refs_2_.refs_3_), channel_id=1, source_target_pairs={{1,0},{17,1},{9,8},{25,9},{0,16},{16,17},{8,24},{24,25},{3,2},{19,... | collective-permute-start | bytes 1081352 | tf_op jit(solution)/shard_map/ppermute | solution.py:268
  39.0 13.6 %collective-permute-start.29 = (bf16[176,1024]{1,0:T(8,128)(2,1)S(1)}, bf16[176,1024]{1,0:T(8,128)(2,1)}, u32[]{:S(2)}, u32[]{:S(2)}) collective-permute-start(bf16[176,1024]{1,0:T(8,128)(2,1)S(1)} %collective-permute-done.21.refs_4_), channel_id=1, source_target_pairs={{16,0},{8,1},{24,8},{0,9},{17,16},{9,17},{25,24},{1,25},{18,2},{10... | collective-permute-start | bytes 1081352 | tf_op jit(solution)/shard_map/ppermute | solution.py:268
  39.0 15.0 %collective-permute-start.27 = (bf16[176,1024]{1,0:T(8,128)(2,1)S(1)}, bf16[176,1024]{1,0:T(8,128)(2,1)}, u32[]{:S(2)}, u32[]{:S(2)}) collective-permute-start(bf16[176,1024]{1,0:T(8,128)(2,1)S(1)} %collective-permute-done.21.refs_4_), channel_id=1, source_target_pairs={{1,0},{17,1},{9,8},{25,9},{0,16},{16,17},{8,24},{24,25},{3,2},{19,... | collective-permute-start | bytes 1081352 | tf_op jit(solution)/shard_map/ppermute | solution.py:268
  41.0 3.8 %collective-permute-start.22 = (bf16[176,1024]{1,0:T(8,128)(2,1)S(1)}, bf16[176,1024]{1,0:T(8,128)(2,1)}, u32[]{:S(2)}, u32[]{:S(2)}) collective-permute-start(bf16[176,1024]{1,0:T(8,128)(2,1)S(1)} %collective-permute-done.20.refs_2_.refs_3_), channel_id=1, source_target_pairs={{8,0},{9,1},{0,8},{1,9},{24,16},{25,17},{16,24},{17,25},{10,2},{11... | collective-permute-start | bytes 1081352 | tf_op jit(solution)/shard_map/ppermute | solution.py:268
  44.8 9.1 %collective-permute-start.25 = (bf16[176,1024]{1,0:T(8,128)(2,1)S(1)}, bf16[176,1024]{1,0:T(8,128)(2,1)S(1)}, u32[]{:S(2)}, u32[]{:S(2)}) collective-permute-start(bf16[176,1024]{1,0:T(8,128)(2,1)S(1)} %collective-permute-done.21.refs_4_), channel_id=1, source_target_pairs={{8,0},{9,1},{0,8},{1,9},{24,16},{25,17},{16,24},{17,25},{10,2},{11... | collective-permute-start | bytes 1081352 | tf_op jit(solution)/shard_map/ppermute | solution.py:268
  61.5 10.6 %all-to-all-start.3 = ((f32[32,4,128]{2,1,0:T(4,128)}), f32[32,4,128]{2,1,0:T(4,128)S(1)}, u32[]{:S(2)}, u32[]{:S(2)}) async-start(f32[32,4,128]{2,1,0:T(4,128)} %bitcast.17), calls=%async_computation.3 | async-start | bytes 131072 | tf_op jit(solution)/shard_map/all_to_all | solution.py:369
  72.4 0.6 copy-start.7

commit v13 on v12

--- a/solution.py
+++ b/solution.py
@@ -273,7 +273,7 @@
     own = [parts[0]] + [across(parts[k], k) for k in range(1, min(3, groups))]
     near = inside(own[0], 1)
     rounds = [[near] + [inside(after(own[0], near), j) for j in range(2, count)]]
-    rest = after([parts[k] for k in range(3, groups)], near)
+    rest = [parts[k] for k in range(3, groups)]
 
     own += [across(part, k) for k, part in zip(range(3, groups), rest)]
     for k in range(1, groups - 1):

time: 73.2 us -> 73 us (level)
    ppermute x12, waiting for transfers between devices: 5.88 us -> 2.62 us  [inside(): lax.ppermute(part, AXES, [(device(int(held[j, i]), h), device(i, h)) for...]
    ppermute x3, starting transfers between devices: 7.83 us -> 5.16 us  [across(): lax.ppermute(part, AXES, [(device(i, h ^ k), device(i, h)) for i, h in pl...]
    all_to_all x1, waiting for transfers between devices: 2.91 us -> 5.33 us  [best_matches(): facts = lax.all_to_all(facts, AXES, split_axis=0, concat_axis=0, tiled=True)]
    all_to_all x1, starting transfers between devices: 3.38 us -> 5.2 us  [best_matches(): facts = lax.all_to_all(facts, AXES, split_axis=0, concat_axis=0, tiled=True)]
    ppermute x3, waiting for transfers between devices: 12 us -> 12.9 us  [across(): lax.ppermute(part, AXES, [(device(i, h ^ k), device(i, h)) for i, h in pl...]
  transfers between devices with their start and end apart: 17 -> 17, of which waited for: 10 -> 6; matrix products, arithmetic and copies ran while one was open for 4% -> 4% of each run, Pallas kernels for 8% -> 8%
where the time goes in v13:
time: 73 us; the launch traced here: 72.7 us
  waiting for transfers between devices  26.8 us (37%)
  starting transfers between devices  23.2 us (32%)
  Pallas kernels  16.5 us (23%)
  other arithmetic  2.66 us (4%)
  local copies, waits for them, and re-layouts  1.82 us (2%)
  between operations  1.61 us (2%)
    ppermute x3, waiting for transfers between devices, across(): lax.ppermute(part, AXES, [(device(i, h ^ k), device(i, h)) for i, h in pl...  12.9 us
    ppermute x12, starting transfers between devices, inside(): lax.ppermute(part, AXES, [(device(int(held[j, i]), h), device(i, h)) for...  8.86 us
    pallas_call x1, Pallas kernels, best_matches(): pl.pallas_call(functools.partial(late_kernel, pairs, count, group_size),...  7.48 us
    all_to_all x1, waiting for transfers between devices, best_matches(): lax.all_to_all(best.reshape(devs, -1, 128), AXES, split_axis=0, concat_ax...  5.9 us
    pallas_call x1, Pallas kernels, best_matches(): pl.pallas_call(functools.partial(early_kernel, pairs, count, early), out_...  5.48 us
    all_to_all x1, waiting for transfers between devices, best_matches(): facts = lax.all_to_all(facts, AXES, split_axis=0, concat_axis=0, tiled=True)  5.33 us
    all_to_all x1, starting transfers between devices, best_matches(): facts = lax.all_to_all(facts, AXES, split_axis=0, concat_axis=0, tiled=True)  5.2 us
    ppermute x3, starting transfers between devices, across(): lax.ppermute(part, AXES, [(device(i, h ^ k), device(i, h)) for i, h in pl...  5.16 us
  transfers between devices with their start and end apart: 17, of which 6 were waited for; matrix products, arithmetic and copies ran while one was open for 4% of the time, Pallas kernels for 8%

profile of v13, /device:TPU:0, one launch (start us, length us, event | category | flops | bytes accessed | tf_op | source)
XLA Modules:
  0.0 72.7 jit_solution(1315615392411529290)
XLA Ops:
  0.0 0.0 copy-start.5
  0.0 3.5 %shard_map.57 = (s32[1,704]{1,0:T(1,128)S(1)}, bf16[176,1024]{1,0:T(8,128)(2,1)S(1)}, bf16[176,1024]{1,0:T(8,128)(2,1)S(1)}, bf16[176,1024]{1,0:T(8,128)(2,1)}, bf16[176,1024]{1,0:T(8,128)(2,1)}) custom-call(s32[1]{0:T(128)} %bitcast.11.plane_ref.refs_0_, s32[1,512]{1,0:T(1,128)} %bitcast.32, f32[512,1024]{1,0:T(8,128)} %emb_ref.1), custom_call_target="tpu_custom_call" | custom-call | tf_op jit(solution)/shard_map/pallas_call | solution.py:253
  3.5 0.5 collective-permute-start.16
  4.0 2.6 %collective-permute-start.15 = (bf16[176,1024]{1,0:T(8,128)(2,1)S(1)}, bf16[176,1024]{1,0:T(8,128)(2,1)S(1)}, u32[]{:S(2)}, u32[]{:S(2)}) collective-permute-start(bf16[176,1024]{1,0:T(8,128)(2,1)S(1)} %get-tuple-element.54), channel_id=1, source_target_pairs={{2,0},{3,1},{10,8},{11,9},{18,16},{19,17},{26,24},{27,25},{0,2},{1... | collective-permute-start | bytes 1081352 | tf_op jit(solution)/shard_map/ppermute | solution.py:265
  6.6 2.6 %collective-permute-start.20 = (bf16[176,1024]{1,0:T(8,128)(2,1)}, bf16[176,1024]{1,0:T(8,128)(2,1)S(1)}, u32[]{:S(2)}, u32[]{:S(2)}) collective-permute-start(bf16[176,1024]{1,0:T(8,128)(2,1)} %get-tuple-element.59), channel_id=1, source_target_pairs={{4,0},{5,1},{12,8},{13,9},{20,16},{21,17},{28,24},{29,25},{6,2},{7... | collective-permute-start | bytes 1081352 | tf_op jit(solution)/shard_map/ppermute | solution.py:265
  9.2 0.0 collective-permute-start.21
  9.2 0.0 copy-done.3
  9.2 0.0 collective-permute-done.16.refs_3_.refs_5_
  9.2 1.1 %collective-permute-start.18 = (bf16[176,1024]{1,0:T(8,128)(2,1)S(1)}, bf16[176,1024]{1,0:T(8,128)(2,1)S(1)}, u32[]{:S(2)}, u32[]{:S(2)}) collective-permute-start(bf16[176,1024]{1,0:T(8,128)(2,1)S(1)} %get-tuple-element.56.refs_0_.refs_1_), channel_id=1, source_target_pairs={{16,0},{8,1},{24,8},{0,9},{17,16},{9,17},{25,24},{1,25},{18,2},{10... | collective-permute-start | bytes 1081352 | tf_op jit(solution)/shard_map/ppermute | solution.py:268
  10.3 1.0 %collective-permute-start.17 = (bf16[176,1024]{1,0:T(8,128)(2,1)S(1)}, bf16[176,1024]{1,0:T(8,128)(2,1)S(1)}, u32[]{:S(2)}, u32[]{:S(2)}) collective-permute-start(bf16[176,1024]{1,0:T(8,128)(2,1)S(1)} %get-tuple-element.56.refs_0_.refs_1_), channel_id=1, source_target_pairs={{1,0},{17,1},{9,8},{25,9},{0,16},{16,17},{8,24},{24,25},{3,2},{19,... | collective-permute-start | bytes 1081352 | tf_op jit(solution)/shard_map/ppermute | solution.py:268
  11.3 0.1 convert_reduce_fusion.5
  11.4 0.7 reduce_max.46
  12.8 0.0 copy-done.4
  12.9 0.1 convert_reduce_fusion.4
  13.0 9.9 %collective-permute-done.15.refs_1_.refs_2_ = bf16[176,1024]{1,0:T(8,128)(2,1)S(1)} collective-permute-done((bf16[176,1024]{1,0:T(8,128)(2,1)S(1)}, bf16[176,1024]{1,0:T(8,128)(2,1)S(1)}, u32[]{:S(2)}, u32[]{:S(2)}) %collective-permute-start.15) | collective-permute-done | bytes 360480 | tf_op jit(solution)/shard_map/ppermute | solution.py:265
  22.9 0.0 collective-permute-done.18.refs_9_.refs_13_
  22.9 0.0 collective-permute-done.17.refs_6_.refs_9_
  22.9 0.0 collective-permute-start.19
  22.9 0.1 pad_add_fusion.1
  23.0 0.1 pad.7.clone
  23.0 0.1 pad.6.clone
  23.1 0.0 copy-done.5
  23.1 0.1 select_reduce_fusion.5
  23.2 0.1 fusion.7
  23.3 1.8 %collective-permute-start.24 = (bf16[176,1024]{1,0:T(8,128)(2,1)S(1)}, bf16[176,1024]{1,0:T(8,128)(2,1)S(1)}, u32[]{:S(2)}, u32[]{:S(2)}) collective-permute-start(bf16[176,1024]{1,0:T(8,128)(2,1)S(1)} %collective-permute-done.15.refs_1_.refs_2_), channel_id=1, source_target_pairs={{16,0},{8,1},{24,8},{0,9},{17,16},{9,17},{25,24},{1,25},{18,2},{10... | collective-permute-start | bytes 1081352 | tf_op jit(solution)/shard_map/ppermute | solution.py:268
  25.1 0.2 collective-permute-start.23
  25.3 0.0 collective-permute-done.19.refs_4_.refs_6_
  25.4 0.1 broadcast_in_dim.172
  25.4 0.1 select_reduce_fusion.4
  25.6 0.6 all_to_all.21
  26.2 5.2 %all-to-all-start.2 = ((s32[32,1,256]{2,1,0:T(1,128)}), s32[32,1,256]{2,1,0:T(1,128)S(1)}, u32[]{:S(2)}, u32[]{:S(2)}) async-start(s32[32,1,256]{2,1,0:T(1,128)} %all_to_all.21), calls=%async_computation.2 | async-start | bytes 65536 | tf_op jit(solution)/shard_map/all_to_all | solution.py:309
  31.4 3.0 %collective-permute-done.20.refs_2_.refs_3_ = bf16[176,1024]{1,0:T(8,128)(2,1)S(1)} collective-permute-done((bf16[176,1024]{1,0:T(8,128)(2,1)}, bf16[176,1024]{1,0:T(8,128)(2,1)S(1)}, u32[]{:S(2)}, u32[]{:S(2)}) %collective-permute-start.20) | collective-permute-done | bytes 360480 | tf_op jit(solution)/shard_map/ppermute | solution.py:265
  34.4 0.0 collective-permute-start.28
  34.4 2.0 %collective-permute-start.26 = (bf16[176,1024]{1,0:T(8,128)(2,1)S(1)}, bf16[176,1024]{1,0:T(8,128)(2,1)}, u32[]{:S(2)}, u32[]{:S(2)}) collective-permute-start(bf16[176,1024]{1,0:T(8,128)(2,1)S(1)} %collective-permute-done.20.refs_2_.refs_3_), channel_id=1, source_target_pairs={{1,0},{17,1},{9,8},{25,9},{0,16},{16,17},{8,24},{24,25},{3,2},{19,... | collective-permute-start | bytes 1081352 | tf_op jit(solution)/shard_map/ppermute | solution.py:268
  36.5 0.0 collective-permute-done.21.refs_4_
  36.5 0.0 collective-permute-done.24.refs_10_.refs_14_
  36.5 0.0 collective-permute-done.23.refs_7_.refs_10_
  36.5 1.0 %collective-permute-start.29 = (bf16[176,1024]{1,0:T(8,128)(2,1)S(1)}, bf16[176,1024]{1,0:T(8,128)(2,1)}, u32[]{:S(2)}, u32[]{:S(2)}) collective-permute-start(bf16[176,1024]{1,0:T(8,128)(2,1)S(1)} %collective-permute-done.21.refs_4_), channel_id=1, source_target_pairs={{16,0},{8,1},{24,8},{0,9},{17,16},{9,17},{25,24},{1,25},{18,2},{10... | collective-permute-start | bytes 1081352 | tf_op jit(solution)/shard_map/ppermute | solution.py:268
  37.5 1.1 %collective-permute-start.27 = (bf16[176,1024]{1,0:T(8,128)(2,1)S(1)}, bf16[176,1024]{1,0:T(8,128)(2,1)}, u32[]{:S(2)}, u32[]{:S(2)}) collective-permute-start(bf16[176,1024]{1,0:T(8,128)(2,1)S(1)} %collective-permute-done.21.refs_4_), channel_id=1, source_target_pairs={{1,0},{17,1},{9,8},{25,9},{0,16},{16,17},{8,24},{24,25},{3,2},{19,... | collective-permute-start | bytes 1081352 | tf_op jit(solution)/shard_map/ppermute | solution.py:268
  38.6 0.0 collective-permute-start.22
  38.6 5.3 %all-to-all-done.2 = s32[32,1,256]{2,1,0:T(1,128)S(1)} async-done(((s32[32,1,256]{2,1,0:T(1,128)}), s32[32,1,256]{2,1,0:T(1,128)S(1)}, u32[]{:S(2)}, u32[]{:S(2)}) %all-to-all-start.2) | async-done | bytes 32800 | tf_op jit(solution)/shard_map/all_to_all | solution.py:309
  43.9 0.1 reduce.4
  44.0 0.1 broadcast_in_dim.181
  44.1 0.1 select_reduce_fusion.3
  44.3 0.1 reshape.175
  44.4 0.1 mul.54
  44.5 0.1 multiply_reduce_fusion.1
  44.6 0.1 fusion.4
  44.7 0.1 convert_reduce_fusion.3
  44.8 0.0 collective-permute-done.22.refs_5_.refs_7_
  44.8 0.2 collective-permute-start.25
  45.1 0.9 %collective-permute-done.28.refs_11_.refs_15_ = bf16[176,1024]{1,0:T(8,128)(2,1)} collective-permute-done((bf16[176,1024]{1,0:T(8,128)(2,1)S(1)}, bf16[176,1024]{1,0:T(8,128)(2,1)}, u32[]{:S(2)}, u32[]{:S(2)}) %collective-permute-start.28) | collective-permute-done | bytes 360480 | tf_op jit(solution)/shard_map/ppermute | solution.py:268
  46.0 0.0 collective-permute-done.26.refs_8_.refs_11_
  46.0 5.5 %shard_map.58 = (f32[4,512]{1,0:T(4,128)S(1)}, f32[704,4]{1,0:T(8,128)S(1)}) custom-call(bf16[176,1024]{1,0:T(8,128)(2,1)S(1)} %get-tuple-element.56.refs_0_.refs_1_, bf16[176,1024]{1,0:T(8,128)(2,1)S(1)} %collective-permute-done.15.refs_1_.refs_2_, bf16[176,1024]{1,0:T(8,128)(2,1)S(1)} %collective-permute-done.20.refs_2_.refs_3_, ...), custom_call_target="tpu_custom_call" | custom-call | flops 2684354560 | bytes 4194304 | tf_op jit(solution)/shard_map/pallas_call | solution.py:338
  51.5 0.0 collective-permute-done.29.refs_16_
  51.5 1.7 %collective-permute-done.27.refs_12_ = bf16[176,1024]{1,0:T(8,128)(2,1)} collective-permute-done((bf16[176,1024]{1,0:T(8,128)(2,1)S(1)}, bf16[176,1024]{1,0:T(8,128)(2,1)}, u32[]{:S(2)}, u32[]{:S(2)}) %collective-permute-start.27) | collective-permute-done | bytes 360480 | tf_op jit(solution)/shard_map/ppermute | solution.py:268
  53.2 0.0 collective-permute-done.25.refs_8_
  53.2 7.5 %shard_map.59 = f32[4,32,128]{2,1,0:T(8,128)} custom-call(s32[1]{0:T(128)} %bitcast.11.plane_ref.refs_0_, bf16[176,1024]{1,0:T(8,128)(2,1)S(1)} %get-tuple-element.56.refs_0_.refs_1_, bf16[176,1024]{1,0:T(8,128)(2,1)S(1)} %collective-permute-done.15.refs_1_.refs_2_, bf16[176,1024]{1,0:T(8,128)(2,1)S(1)} %collective-permute-done.20.refs_2_.refs_3_, ...), custom_call_target="tpu_custom_call" | custom-call | tf_op jit(solution)/shard_map/pallas_call | solution.py:352
  60.6 4.0 %all-to-all-start.3 = ((f32[32,4,128]{2,1,0:T(4,128)}), f32[32,4,128]{2,1,0:T(4,128)S(1)}, u32[]{:S(2)}, u32[]{:S(2)}) async-start(f32[32,4,128]{2,1,0:T(4,128)} %bitcast.17), calls=%async_computation.3 | async-start | bytes 131072 | tf_op jit(solution)/shard_map/all_to_all | solution.py:369
  64.6 0.7 slice_reduce_fusion
  66.0 5.9 %all-to-all-done.3 = f32[32,4,128]{2,1,0:T(4,128)S(1)} async-done(((f32[32,4,128]{2,1,0:T(4,128)}), f32[32,4,128]{2,1,0:T(4,128)S(1)}, u32[]{:S(2)}, u32[]{:S(2)}) %all-to-all-start.3) | async-done | bytes 65568 | tf_op jit(solution)/shard_map/all_to_all | solution.py:369
  71.9 0.3 conditional.1
  72.1 0.0 copy-start.6
  72.2 0.6 copy-done.6
  (21 shorter events, 0.2 us)
Async XLA Ops:
  0.0 23.1 %copy-start.5 = (s32[4,8]{1,0:T(4,128)S(1)}, s32[4,8]{1,0:T(4,128)}, u32[]{:S(2)}) copy-start(s32[4,8]{1,0:T(4,128)} %constant.109.clone) | copy-start | bytes 388
  0.0 9.2 %copy-start.3 = (s32[512]{0:T(512)S(1)}, s32[512]{0:T(512)}, u32[]{:S(2)}) copy-start(s32[512]{0:T(512)} %param.8) | copy-start | bytes 6148
  0.0 12.8 %copy-start.4 = (s32[1,512]{1,0:T(1,128)S(1)}, s32[1,512]{1,0:T(1,128)}, u32[]{:S(2)}) copy-start(s32[1,512]{1,0:T(1,128)} %param.9) | copy-start | bytes 6148
  3.5 5.6 %collective-permute-start.16 = (bf16[176,1024]{1,0:T(8,128)(2,1)S(1)}, bf16[176,1024]{1,0:T(8,128)(2,1)S(1)}, u32[]{:S(2)}, u32[]{:S(2)}) collective-permute-start(bf16[176,1024]{1,0:T(8,128)(2,1)S(1)} %get-tuple-element.56.refs_0_.refs_1_), channel_id=1, source_target_pairs={{8,0},{9,1},{0,8},{1,9},{24,16},{25,17},{16,24},{17,25},{10,2},{11... | collective-permute-start | bytes 1081352 | tf_op jit(solution)/shard_map/ppermute | solution.py:268
  4.0 18.9 %collective-permute-start.15 = (bf16[176,1024]{1,0:T(8,128)(2,1)S(1)}, bf16[176,1024]{1,0:T(8,128)(2,1)S(1)}, u32[]{:S(2)}, u32[]{:S(2)}) collective-permute-start(bf16[176,1024]{1,0:T(8,128)(2,1)S(1)} %get-tuple-element.54), channel_id=1, source_target_pairs={{2,0},{3,1},{10,8},{11,9},{18,16},{19,17},{26,24},{27,25},{0,2},{1... | collective-permute-start | bytes 1081352 | tf_op jit(solution)/shard_map/ppermute | solution.py:265
  6.6 27.9 %collective-permute-start.20 = (bf16[176,1024]{1,0:T(8,128)(2,1)}, bf16[176,1024]{1,0:T(8,128)(2,1)S(1)}, u32[]{:S(2)}, u32[]{:S(2)}) collective-permute-start(bf16[176,1024]{1,0:T(8,128)(2,1)} %get-tuple-element.59), channel_id=1, source_target_pairs={{4,0},{5,1},{12,8},{13,9},{20,16},{21,17},{28,24},{29,25},{6,2},{7... | collective-permute-start | bytes 1081352 | tf_op jit(solution)/shard_map/ppermute | solution.py:265
  9.2 27.3 %collective-permute-start.21 = (bf16[176,1024]{1,0:T(8,128)(2,1)}, bf16[176,1024]{1,0:T(8,128)(2,1)S(1)}, u32[]{:S(2)}, u32[]{:S(2)}) collective-permute-start(bf16[176,1024]{1,0:T(8,128)(2,1)} %get-tuple-element.60), channel_id=1, source_target_pairs={{6,0},{7,1},{14,8},{15,9},{22,16},{23,17},{30,24},{31,25},{4,2},{5... | collective-permute-start | bytes 1081352 | tf_op jit(solution)/shard_map/ppermute | solution.py:265
  9.2 13.7 %collective-permute-start.18 = (bf16[176,1024]{1,0:T(8,128)(2,1)S(1)}, bf16[176,1024]{1,0:T(8,128)(2,1)S(1)}, u32[]{:S(2)}, u32[]{:S(2)}) collective-permute-start(bf16[176,1024]{1,0:T(8,128)(2,1)S(1)} %get-tuple-element.56.refs_0_.refs_1_), channel_id=1, source_target_pairs={{16,0},{8,1},{24,8},{0,9},{17,16},{9,17},{25,24},{1,25},{18,2},{10... | collective-permute-start | bytes 1081352 | tf_op jit(solution)/shard_map/ppermute | solution.py:268
  10.3 12.6 %collective-permute-start.17 = (bf16[176,1024]{1,0:T(8,128)(2,1)S(1)}, bf16[176,1024]{1,0:T(8,128)(2,1)S(1)}, u32[]{:S(2)}, u32[]{:S(2)}) collective-permute-start(bf16[176,1024]{1,0:T(8,128)(2,1)S(1)} %get-tuple-element.56.refs_0_.refs_1_), channel_id=1, source_target_pairs={{1,0},{17,1},{9,8},{25,9},{0,16},{16,17},{8,24},{24,25},{3,2},{19,... | collective-permute-start | bytes 1081352 | tf_op jit(solution)/shard_map/ppermute | solution.py:268
  22.9 2.5 %collective-permute-start.19 = (bf16[176,1024]{1,0:T(8,128)(2,1)S(1)}, bf16[176,1024]{1,0:T(8,128)(2,1)S(1)}, u32[]{:S(2)}, u32[]{:S(2)}) collective-permute-start(bf16[176,1024]{1,0:T(8,128)(2,1)S(1)} %collective-permute-done.15.refs_1_.refs_2_), channel_id=1, source_target_pairs={{8,0},{9,1},{0,8},{1,9},{24,16},{25,17},{16,24},{17,25},{10,2},{11... | collective-permute-start | bytes 1081352 | tf_op jit(solution)/shard_map/ppermute | solution.py:268
  23.3 13.2 %collective-permute-start.24 = (bf16[176,1024]{1,0:T(8,128)(2,1)S(1)}, bf16[176,1024]{1,0:T(8,128)(2,1)S(1)}, u32[]{:S(2)}, u32[]{:S(2)}) collective-permute-start(bf16[176,1024]{1,0:T(8,128)(2,1)S(1)} %collective-permute-done.15.refs_1_.refs_2_), channel_id=1, source_target_pairs={{16,0},{8,1},{24,8},{0,9},{17,16},{9,17},{25,24},{1,25},{18,2},{10... | collective-permute-start | bytes 1081352 | tf_op jit(solution)/shard_map/ppermute | solution.py:268
  25.1 11.4 %collective-permute-start.23 = (bf16[176,1024]{1,0:T(8,128)(2,1)S(1)}, bf16[176,1024]{1,0:T(8,128)(2,1)}, u32[]{:S(2)}, u32[]{:S(2)}) collective-permute-start(bf16[176,1024]{1,0:T(8,128)(2,1)S(1)} %collective-permute-done.15.refs_1_.refs_2_), channel_id=1, source_target_pairs={{1,0},{17,1},{9,8},{25,9},{0,16},{16,17},{8,24},{24,25},{3,2},{19,... | collective-permute-start | bytes 1081352 | tf_op jit(solution)/shard_map/ppermute | solution.py:268
  26.2 17.7 %all-to-all-start.2 = ((s32[32,1,256]{2,1,0:T(1,128)}), s32[32,1,256]{2,1,0:T(1,128)S(1)}, u32[]{:S(2)}, u32[]{:S(2)}) async-start(s32[32,1,256]{2,1,0:T(1,128)} %all_to_all.21), calls=%async_computation.2 | async-start | bytes 65536 | tf_op jit(solution)/shard_map/all_to_all | solution.py:309
  34.4 11.5 %collective-permute-start.28 = (bf16[176,1024]{1,0:T(8,128)(2,1)S(1)}, bf16[176,1024]{1,0:T(8,128)(2,1)}, u32[]{:S(2)}, u32[]{:S(2)}) collective-permute-start(bf16[176,1024]{1,0:T(8,128)(2,1)S(1)} %collective-permute-done.20.refs_2_.refs_3_), channel_id=1, source_target_pairs={{16,0},{8,1},{24,8},{0,9},{17,16},{9,17},{25,24},{1,25},{18,2},{10... | collective-permute-start | bytes 1081352 | tf_op jit(solution)/shard_map/ppermute | solution.py:268
  34.4 11.5 %collective-permute-start.26 = (bf16[176,1024]{1,0:T(8,128)(2,1)S(1)}, bf16[176,1024]{1,0:T(8,128)(2,1)}, u32[]{:S(2)}, u32[]{:S(2)}) collective-permute-start(bf16[176,1024]{1,0:T(8,128)(2,1)S(1)} %collective-permute-done.20.refs_2_.refs_3_), channel_id=1, source_target_pairs={{1,0},{17,1},{9,8},{25,9},{0,16},{16,17},{8,24},{24,25},{3,2},{19,... | collective-permute-start | bytes 1081352 | tf_op jit(solution)/shard_map/ppermute | solution.py:268
  36.5 15.0 %collective-permute-start.29 = (bf16[176,1024]{1,0:T(8,128)(2,1)S(1)}, bf16[176,1024]{1,0:T(8,128)(2,1)}, u32[]{:S(2)}, u32[]{:S(2)}) collective-permute-start(bf16[176,1024]{1,0:T(8,128)(2,1)S(1)} %collective-permute-done.21.refs_4_), channel_id=1, source_target_pairs={{16,0},{8,1},{24,8},{0,9},{17,16},{9,17},{25,24},{1,25},{18,2},{10... | collective-permute-start | bytes 1081352 | tf_op jit(solution)/shard_map/ppermute | solution.py:268
  37.5 15.7 %collective-permute-start.27 = (bf16[176,1024]{1,0:T(8,128)(2,1)S(1)}, bf16[176,1024]{1,0:T(8,128)(2,1)}, u32[]{:S(2)}, u32[]{:S(2)}) collective-permute-start(bf16[176,1024]{1,0:T(8,128)(2,1)S(1)} %collective-permute-done.21.refs_4_), channel_id=1, source_target_pairs={{1,0},{17,1},{9,8},{25,9},{0,16},{16,17},{8,24},{24,25},{3,2},{19,... | collective-permute-start | bytes 1081352 | tf_op jit(solution)/shard_map/ppermute | solution.py:268
  38.6 6.3 %collective-permute-start.22 = (bf16[176,1024]{1,0:T(8,128)(2,1)S(1)}, bf16[176,1024]{1,0:T(8,128)(2,1)}, u32[]{:S(2)}, u32[]{:S(2)}) collective-permute-start(bf16[176,1024]{1,0:T(8,128)(2,1)S(1)} %collective-permute-done.20.refs_2_.refs_3_), channel_id=1, source_target_pairs={{8,0},{9,1},{0,8},{1,9},{24,16},{25,17},{16,24},{17,25},{10,2},{11... | collective-permute-start | bytes 1081352 | tf_op jit(solution)/shard_map/ppermute | solution.py:268
  44.8 8.3 %collective-permute-start.25 = (bf16[176,1024]{1,0:T(8,128)(2,1)S(1)}, bf16[176,1024]{1,0:T(8,128)(2,1)S(1)}, u32[]{:S(2)}, u32[]{:S(2)}) collective-permute-start(bf16[176,1024]{1,0:T(8,128)(2,1)S(1)} %collective-permute-done.21.refs_4_), channel_id=1, source_target_pairs={{8,0},{9,1},{0,8},{1,9},{24,16},{25,17},{16,24},{17,25},{10,2},{11... | collective-permute-start | bytes 1081352 | tf_op jit(solution)/shard_map/ppermute | solution.py:268
  60.6 11.2 %all-to-all-start.3 = ((f32[32,4,128]{2,1,0:T(4,128)}), f32[32,4,128]{2,1,0:T(4,128)S(1)}, u32[]{:S(2)}, u32[]{:S(2)}) async-start(f32[32,4,128]{2,1,0:T(4,128)} %bitcast.17), calls=%async_computation.3 | async-start | bytes 131072 | tf_op jit(solution)/shard_map/all_to_all | solution.py:369
  72.1 0.6 copy-start.6
